TPU v7x, 32 devices: a whole 2x2x4 slice. The times are simulated.
32 devices in a mesh: dp: 8 (over z, y), tensor: 4 (over x, core).
Axes of the slice: x: 2, y: 2, z: 4, core: 2. Of those that a mesh axis runs over, the one named last changes fastest.
Arguments:
- image_tokens: bfloat16 [18816, 512], P(('dp', 'tensor')), may hold values from -6 to 6
- tag_tokens: bfloat16 [12288, 512], P(('dp', 'tensor')), may hold values from -6 to 6
- image_cotangent: bfloat16 [18816, 512], P(('dp', 'tensor')), may hold values from -6 to 6
- tag_cotangent: bfloat16 [12288, 512], P(('dp', 'tensor')), may hold values from -6 to 6
- tag_lengths: int32 [24], P('dp'), may hold values from 1 to 512, 6144 in all
- slot_blocks: int32 [80], replicated, may hold values from 0 to 79, as said below
- master_blocks: float32 [4, 80, 128, 128], P('tensor', 'dp'), as said below
- left_factor: float32 [4, 80, 128, 128], P('tensor', 'dp'), as said below
- right_factor: float32 [4, 80, 128, 128], P('tensor', 'dp'), as said below
- left_root: float32 [4, 80, 128, 128], P('tensor', 'dp'), as said below
- right_root: float32 [4, 80, 128, 128], P('tensor', 'dp'), as said below
- vector_master: float32 [10, 512], P(None, 'dp'), as said below
- vector_moment: float32 [10, 512], P(None, 'dp'), as said below
Outputs:
- encoder_out: bfloat16 [18816, 512], P(('dp', 'tensor'))
- tag_output: bfloat16 [12288, 512], P(('dp', 'tensor'))
- image_gradient: float32 [18816, 512], P(('dp', 'tensor'))
- tag_gradient: float32 [12288, 512], P(('dp', 'tensor'))
- block_gradient: float32 [4, 80, 128, 128], P('tensor', 'dp')
- left_updated: float32 [4, 80, 128, 128], P('tensor', 'dp')
- right_updated: float32 [4, 80, 128, 128], P('tensor', 'dp')
- master_updated: float32 [4, 80, 128, 128], P('tensor', 'dp')
- master_copy: bfloat16 [4, 80, 128, 128], P('tensor', 'dp')
- vector_gradient: float32 [10, 512], P(None, 'dp')
- moment_updated: float32 [10, 512], P(None, 'dp')
- vector_updated: float32 [10, 512], P(None, 'dp')
Inputs may be any that keep to these rules, and one draw needn't show every extreme that they name: `slot_blocks`: each of 0 to 79 appears once; a slot holding 80 or more holds no tile. `tag_lengths`: one sequence has 512 live tags. `master_blocks`: master weights. `left_factor`: symmetric. `right_factor`: symmetric. `left_root`: symmetric. `right_root`: symmetric. `vector_master`: gains and shifts. `vector_moment`: every entry is positive.
All inputs are finite; a program needn't handle non-finite values. No bound on the sum of `tag_lengths` on one device may be relied on, other than what follows from the above.
Results may differ from a plain program's by a relative error of at most 0.019.
Values may be sent and summed in bfloat16 or wider, within the bound.
No kernel may reach another device: no remote copies, remote signals or barrier semaphores. Data moves between devices by JAX's collectives and lax.ppermute only.
A program may use at most 128 MiB of HBM per device.

v0:
```python
import jax
import jax.numpy as jnp
from jax import lax
from jax.sharding import PartitionSpec as P

D = 512
HEADS = 8
HEAD_DIM = 64
FF = 1024


NORM_EPSILON = 1e-05
MATRIX_RATE = 0.5
VECTOR_RATE = 0.2
STAT_DECAY = 0.5
MASKED_SCORE = -1e30


def for_sending(array):

    def short(part):
        return part.astype(jnp.bfloat16) if part.dtype == jnp.float32 else part

    return jax.tree.map(short, array)


def matmul(former, latter):
    return jnp.dot(former, latter, preferred_element_type=jnp.float32)


def times_transpose(former, latter):
    return lax.dot_general(
        former, latter, (((1,), (1,)), ((), ())), preferred_element_type=jnp.float32
    )


def transpose_times(former, latter):
    return lax.dot_general(
        former, latter, (((0,), (0,)), ((), ())), preferred_element_type=jnp.float32
    )


def smooth_gate(values):
    return jax.nn.gelu(values, approximate=False)


def gate_backward(preact, incoming):
    result, pullback = jax.vjp(smooth_gate, preact)
    return pullback(incoming)[0]


def from_blocks(blocks, row_count, column_count, tile_size):
    return (
        blocks.reshape(row_count // tile_size, column_count // tile_size, tile_size, tile_size)
        .transpose(0, 2, 1, 3)
        .reshape(row_count, column_count)
    )


def to_blocks(matrix, tile_size):
    row_count, column_count = matrix.shape
    return (
        matrix.reshape(row_count // tile_size, tile_size, column_count // tile_size, tile_size)
        .transpose(0, 2, 1, 3)
        .reshape(-1, tile_size, tile_size)
    )


def norm_forward(residual, norm_gain, norm_shift):
    row_mean = jnp.mean(residual, axis=-1, keepdims=True)
    centered = residual - row_mean
    inverse_scale = lax.rsqrt(jnp.mean(centered * centered, axis=-1, keepdims=True) + NORM_EPSILON)
    normed = centered * inverse_scale
    return (normed * norm_gain + norm_shift, (normed, inverse_scale))


def norm_backward(gradient, stored, norm_gain):
    normed, inverse_scale = stored
    scaled = gradient * norm_gain
    adjusted = (
        scaled
        - jnp.mean(scaled, axis=-1, keepdims=True)
        - normed * jnp.mean(scaled * normed, axis=-1, keepdims=True)
    )
    return (inverse_scale * adjusted, jnp.sum(gradient * normed, axis=0), jnp.sum(gradient, axis=0))


def causal_allowed(item_length, live_count):
    row_index = lax.broadcasted_iota(jnp.int32, (item_length, item_length), 0)
    column_index = lax.broadcasted_iota(jnp.int32, (item_length, item_length), 1)
    return (column_index <= row_index) & (column_index < live_count)


def split_heads(matrix):
    return matrix.reshape(matrix.shape[0], matrix.shape[1] // HEAD_DIM, HEAD_DIM)


def head_scores(queries, key_rows, allowed):
    scores = jnp.einsum(
        "qhd,khd->hqk",
        split_heads(queries),
        split_heads(key_rows),
        preferred_element_type=jnp.float32,
    ) * HEAD_DIM ** (-0.5)
    if allowed is None:
        return scores
    return jnp.where(allowed[None], scores, MASKED_SCORE)


def attend(queries, key_rows, value_rows, allowed):
    scores = head_scores(queries, key_rows, allowed)
    row_max = jnp.max(scores, axis=-1, keepdims=True)
    log_total = row_max + jnp.log(jnp.sum(jnp.exp(scores - row_max), axis=-1, keepdims=True))
    attention = jnp.exp(scores - log_total).astype(jnp.bfloat16)
    mixed_rows = jnp.einsum(
        "hqk,khd->qhd", attention, split_heads(value_rows), preferred_element_type=jnp.float32
    )
    return (mixed_rows.reshape(queries.shape).astype(jnp.bfloat16), log_total)


def attend_back(queries, key_rows, value_rows, allowed, log_total, delta_mixed):
    scores = head_scores(queries, key_rows, allowed)
    attention = jnp.exp(scores - log_total)
    delta_heads = split_heads(delta_mixed)
    delta_attention = jnp.einsum(
        "qhd,khd->hqk", delta_heads, split_heads(value_rows), preferred_element_type=jnp.float32
    )
    delta_values = jnp.einsum(
        "hqk,qhd->khd",
        attention.astype(jnp.bfloat16),
        delta_heads,
        preferred_element_type=jnp.float32,
    )
    delta_scores = attention * (
        delta_attention - jnp.sum(attention * delta_attention, axis=-1, keepdims=True)
    )
    delta_scores = delta_scores.astype(jnp.bfloat16)
    delta_queries = jnp.einsum(
        "hqk,khd->qhd", delta_scores, split_heads(key_rows), preferred_element_type=jnp.float32
    ) * HEAD_DIM ** (-0.5)
    delta_keys = jnp.einsum(
        "hqk,qhd->khd", delta_scores, split_heads(queries), preferred_element_type=jnp.float32
    ) * HEAD_DIM ** (-0.5)
    return (
        delta_queries.reshape(queries.shape),
        delta_keys.reshape(key_rows.shape),
        delta_values.reshape(value_rows.shape),
    )


def gather_rows(operand):
    return jax.tree.map(
        lambda part, own: part.astype(own.dtype),
        lax.all_gather(for_sending(operand), "tensor", axis=0, tiled=True),
        operand,
    )


def spread_rows(operand):
    return lax.psum_scatter(operand, "tensor", scatter_dimension=0, tiled=True)


def gather_deltas(operand):
    return lax.all_gather(operand, "tensor", axis=0, tiled=True)


def spread_deltas(operand):
    return lax.psum_scatter(operand, "tensor", scatter_dimension=0, tiled=True)


def self_forward(tokens_low, project_in, project_out, tag_lengths, causal, item_length):
    gathered = gather_rows(tokens_low)
    head_width = project_out.shape[0]
    packed = matmul(gathered, project_in).astype(jnp.bfloat16)
    item_blocks = packed.reshape(tag_lengths.shape[0], item_length, 3 * head_width)

    def one_item(operands):
        item_rows, live_count = operands
        allowed = causal_allowed(item_length, live_count) if causal else None
        return attend(
            item_rows[:, :head_width],
            item_rows[:, head_width : 2 * head_width],
            item_rows[:, 2 * head_width :],
            allowed,
        )

    mixed_rows, log_total = lax.map(one_item, (item_blocks, tag_lengths))
    mixed_rows = mixed_rows.reshape(-1, head_width)
    return (
        spread_rows(matmul(mixed_rows, project_out)),
        (gathered, item_blocks, mixed_rows, log_total),
    )


def self_backward(gradient, stored, project_in, project_out, tag_lengths, causal, item_length):
    gathered, item_blocks, mixed_rows, log_total = stored
    head_width = project_out.shape[0]
    delta_all = gather_deltas(gradient.astype(jnp.bfloat16))
    delta_mixed = times_transpose(delta_all, project_out).astype(jnp.bfloat16)
    delta_out = transpose_times(mixed_rows, delta_all)
    delta_items = delta_mixed.reshape(tag_lengths.shape[0], item_length, head_width)

    def one_item(operands):
        item_rows, live_count, item_total, item_delta = operands
        allowed = causal_allowed(item_length, live_count) if causal else None
        item_deltas = attend_back(
            item_rows[:, :head_width],
            item_rows[:, head_width : 2 * head_width],
            item_rows[:, 2 * head_width :],
            allowed,
            item_total,
            item_delta,
        )
        return jnp.concatenate(item_deltas, axis=1).astype(jnp.bfloat16)

    delta_packed = lax.map(one_item, (item_blocks, tag_lengths, log_total, delta_items)).reshape(
        -1, 3 * head_width
    )
    delta_in = transpose_times(gathered, delta_packed)
    delta_tokens = spread_deltas(times_transpose(delta_packed, project_in))
    return (delta_tokens, delta_in, delta_out)


def cross_forward(
    tags_low, encoded_low, project_query, project_pair, project_out, item_length, image_length
):
    tags_all, encoded_all = gather_rows((tags_low, encoded_low))
    head_width = project_out.shape[0]
    item_count = tags_all.shape[0] // item_length
    queries = (
        matmul(tags_all, project_query)
        .astype(jnp.bfloat16)
        .reshape(item_count, item_length, head_width)
    )
    pairs = (
        matmul(encoded_all, project_pair)
        .astype(jnp.bfloat16)
        .reshape(item_count, image_length, 2 * head_width)
    )

    def one_item(operands):
        item_queries, item_pairs = operands
        return attend(item_queries, item_pairs[:, :head_width], item_pairs[:, head_width:], None)

    mixed_rows, log_total = lax.map(one_item, (queries, pairs))
    mixed_rows = mixed_rows.reshape(-1, head_width)
    return (
        spread_rows(matmul(mixed_rows, project_out)),
        (tags_all, encoded_all, queries, pairs, mixed_rows, log_total),
    )


def cross_backward(gradient, stored, project_query, project_pair, project_out):
    tags_all, encoded_all, queries, pairs, mixed_rows, log_total = stored
    head_width = project_out.shape[0]
    delta_all = gather_deltas(gradient.astype(jnp.bfloat16))
    delta_mixed = times_transpose(delta_all, project_out).astype(jnp.bfloat16)
    delta_out = transpose_times(mixed_rows, delta_all)
    delta_items = delta_mixed.reshape(queries.shape)

    def one_item(operands):
        item_queries, item_pairs, item_total, item_delta = operands
        delta_query, delta_key, delta_value = attend_back(
            item_queries,
            item_pairs[:, :head_width],
            item_pairs[:, head_width:],
            None,
            item_total,
            item_delta,
        )
        return (
            delta_query.astype(jnp.bfloat16),
            jnp.concatenate([delta_key, delta_value], axis=1).astype(jnp.bfloat16),
        )

    delta_queries, delta_pairs = lax.map(one_item, (queries, pairs, log_total, delta_items))
    delta_queries = delta_queries.reshape(-1, head_width)
    delta_pairs = delta_pairs.reshape(-1, 2 * head_width)
    delta_query_weight = transpose_times(tags_all, delta_queries)
    delta_pair_weight = transpose_times(encoded_all, delta_pairs)
    delta_tags, delta_encoded = spread_deltas(
        (times_transpose(delta_queries, project_query), times_transpose(delta_pairs, project_pair))
    )
    return (delta_tags, delta_encoded, delta_query_weight, delta_pair_weight, delta_out)


def ffn_forward(normed_rows, project_up, project_down):
    rows_low = normed_rows.astype(jnp.bfloat16)
    gathered = gather_rows(rows_low)
    preact = matmul(gathered, project_up)
    hidden = smooth_gate(preact).astype(jnp.bfloat16)
    result = spread_rows(matmul(hidden, project_down))
    stored = (gathered, hidden, preact, project_up, project_down)
    return (result, stored)


def ffn_backward(gradient, stored):
    inputs, hidden, preact, project_up, project_down = stored
    delta_low = gradient.astype(jnp.bfloat16)
    delta_all = gather_deltas(delta_low)
    delta_hidden = gate_backward(preact, times_transpose(delta_all, project_down)).astype(
        jnp.bfloat16
    )
    delta_down = transpose_times(hidden, delta_all)
    delta_up = transpose_times(inputs, delta_hidden)
    delta_rows = times_transpose(delta_hidden, project_up)
    delta_rows = spread_deltas(delta_rows)
    return (delta_rows, delta_up, delta_down)


def local(
    image_tokens,
    tag_tokens,
    image_cotangent,
    tag_cotangent,
    tag_lengths,
    slot_blocks,
    master_blocks,
    left_factor,
    right_factor,
    left_root,
    right_root,
    vector_master,
    vector_moment,
):
    shards = lax.axis_size("tensor")
    tile_size = master_blocks.shape[2]
    head_width = HEADS * HEAD_DIM // shards
    hidden_width = FF // shards
    shapes = [
        (D, 3 * head_width),
        (head_width, D),
        (D, hidden_width),
        (hidden_width, D),
        (D, 3 * head_width),
        (head_width, D),
        (D, head_width),
        (D, 2 * head_width),
        (head_width, D),
        (D, hidden_width),
        (hidden_width, D),
    ]
    counts = [
        row_count // tile_size * (column_count // tile_size) for row_count, column_count in shapes
    ]
    block_total = sum(counts)
    slot_total = slot_blocks.shape[0]
    gathered_slots, gathered_vectors = (
        lax.all_gather(master_blocks.astype(jnp.bfloat16), "dp", axis=1, tiled=True),
        lax.all_gather(vector_master.astype(jnp.bfloat16), "dp", axis=1, tiled=True),
    )
    placement = jnp.argsort(slot_blocks)[:block_total]
    ordered = jnp.take(gathered_slots[0], placement, axis=0)
    weights = []
    offset = 0
    for (row_count, column_count), number in zip(shapes, counts):
        weights.append(
            from_blocks(ordered[offset : offset + number], row_count, column_count, tile_size)
        )
        offset = offset + number
    vectors = gathered_vectors.astype(jnp.float32)
    image_count = tag_lengths.shape[0]
    image_length = image_tokens.shape[0] * shards // image_count
    item_length = tag_tokens.shape[0] * shards // image_count
    attended, saved_image = self_forward(
        image_tokens, weights[0], weights[1], tag_lengths, False, image_length
    )
    after_attention, norm_one = norm_forward(
        image_tokens.astype(jnp.float32) + attended, vectors[0], vectors[1]
    )
    ffn_out, saved_ffn = ffn_forward(after_attention, weights[2], weights[3])
    encoded, norm_two = norm_forward(after_attention + ffn_out, vectors[2], vectors[3])
    encoded_low = encoded.astype(jnp.bfloat16)
    attended, saved_tags = self_forward(
        tag_tokens, weights[4], weights[5], tag_lengths, True, item_length
    )
    after_self, norm_three = norm_forward(
        tag_tokens.astype(jnp.float32) + attended, vectors[4], vectors[5]
    )
    crossed, saved_cross = cross_forward(
        after_self.astype(jnp.bfloat16),
        encoded_low,
        weights[6],
        weights[7],
        weights[8],
        item_length,
        image_length,
    )
    after_cross, norm_four = norm_forward(after_self + crossed, vectors[6], vectors[7])
    ffn_tags, saved_ffn_tags = ffn_forward(after_cross, weights[9], weights[10])
    decoded, norm_five = norm_forward(after_cross + ffn_tags, vectors[8], vectors[9])
    local_rows = tag_tokens.shape[0]
    row_index = (
        lax.broadcasted_iota(jnp.int32, (local_rows, 1), 0) + lax.axis_index("tensor") * local_rows
    )
    matches = row_index // item_length == lax.broadcasted_iota(jnp.int32, (1, image_count), 1)
    live_count = jnp.sum(jnp.where(matches, tag_lengths[None, :], 0), axis=1, keepdims=True)
    live_rows = (row_index % item_length < live_count).astype(jnp.float32)
    vector_deltas = [None] * 10
    backflow = tag_cotangent.astype(jnp.float32) * live_rows
    backflow, vector_deltas[8], vector_deltas[9] = norm_backward(backflow, norm_five, vectors[8])
    through, delta_up_tags, delta_down_tags = ffn_backward(backflow, saved_ffn_tags)
    backflow = backflow + through
    backflow, vector_deltas[6], vector_deltas[7] = norm_backward(backflow, norm_four, vectors[6])
    through, delta_encoded, delta_cross_query, delta_cross_pair, delta_cross_out = cross_backward(
        backflow, saved_cross, weights[6], weights[7], weights[8]
    )
    backflow = backflow + through
    backflow, vector_deltas[4], vector_deltas[5] = norm_backward(backflow, norm_three, vectors[4])
    through, delta_tag_in, delta_tag_out = self_backward(
        backflow, saved_tags, weights[4], weights[5], tag_lengths, True, item_length
    )
    tag_gradient = backflow + through
    backflow = image_cotangent.astype(jnp.float32) + delta_encoded
    backflow, vector_deltas[2], vector_deltas[3] = norm_backward(backflow, norm_two, vectors[2])
    through, delta_up, delta_down = ffn_backward(backflow, saved_ffn)
    backflow = backflow + through
    backflow, vector_deltas[0], vector_deltas[1] = norm_backward(backflow, norm_one, vectors[0])
    through, delta_image_in, delta_image_out = self_backward(
        backflow, saved_image, weights[0], weights[1], tag_lengths, False, image_length
    )
    image_gradient = backflow + through
    deltas = [
        delta_image_in,
        delta_image_out,
        delta_up,
        delta_down,
        delta_tag_in,
        delta_tag_out,
        delta_cross_query,
        delta_cross_pair,
        delta_cross_out,
        delta_up_tags,
        delta_down_tags,
    ]
    tile_listing = [to_blocks(part_delta, tile_size) for part_delta in deltas]
    tile_listing.append(jnp.zeros((slot_total - block_total, tile_size, tile_size), jnp.float32))
    outgoing = jnp.take(jnp.concatenate(tile_listing, axis=0), slot_blocks, axis=0)[None]
    dealt_tiles, vector_part = (
        lax.psum_scatter(outgoing, "dp", scatter_dimension=1, tiled=True),
        lax.psum_scatter(jnp.stack(vector_deltas, axis=0), "dp", scatter_dimension=1, tiled=True),
    )
    vector_gradient = lax.psum(vector_part, "tensor")
    highest = lax.Precision.HIGHEST
    left_updated = STAT_DECAY * left_factor + (1.0 - STAT_DECAY) * jnp.einsum(
        "asij,askj->asik", dealt_tiles, dealt_tiles, precision=highest
    )
    right_updated = STAT_DECAY * right_factor + (1.0 - STAT_DECAY) * jnp.einsum(
        "asji,asjk->asik", dealt_tiles, dealt_tiles, precision=highest
    )
    rotated = jnp.einsum("asij,asjk->asik", left_root, dealt_tiles, precision=highest)
    master_updated = master_blocks - MATRIX_RATE * jnp.einsum(
        "asij,asjk->asik", rotated, right_root, precision=highest
    )
    moment_updated = (
        STAT_DECAY * vector_moment + (1.0 - STAT_DECAY) * vector_gradient * vector_gradient
    )
    vector_updated = vector_master - VECTOR_RATE * vector_gradient / (
        jnp.sqrt(moment_updated) + 1e-08
    )
    return (
        encoded_low,
        decoded.astype(jnp.bfloat16),
        image_gradient,
        tag_gradient,
        dealt_tiles,
        left_updated,
        right_updated,
        master_updated,
        master_updated.astype(jnp.bfloat16),
        vector_gradient,
        moment_updated,
        vector_updated,
    )


def solution(mesh):
    in_specs = (
        P(("dp", "tensor"), None),
        P(("dp", "tensor"), None),
        P(("dp", "tensor"), None),
        P(("dp", "tensor"), None),
        P("dp"),
        P(),
        P("tensor", "dp", None, None),
        P("tensor", "dp", None, None),
        P("tensor", "dp", None, None),
        P("tensor", "dp", None, None),
        P("tensor", "dp", None, None),
        P(None, "dp"),
        P(None, "dp"),
    )
    out_specs = (
        P(("dp", "tensor"), None),
        P(("dp", "tensor"), None),
        P(("dp", "tensor"), None),
        P(("dp", "tensor"), None),
        P("tensor", "dp", None, None),
        P("tensor", "dp", None, None),
        P("tensor", "dp", None, None),
        P("tensor", "dp", None, None),
        P("tensor", "dp", None, None),
        P(None, "dp"),
        P(None, "dp"),
        P(None, "dp"),
    )
    return jax.shard_map(local, mesh=mesh, in_specs=in_specs, out_specs=out_specs, check_vma=False)
```

profile of v0, /device:TPU:0, one launch (start us, length us, event | category | flops | bytes accessed | tf_op | source)
XLA Modules:
  0.0 1076.4 jit_solution(10765054131421987231)
XLA Ops:
  13.3 32.2 %all-gather.1 = bf16[8,64,10]{1,2,0:T(8,128)(2,1)S(1)} all-gather(bf16[1,64,10]{1,2,0:T(8,128)(2,1)S(1)} %convert_bitcast_fusion.2), channel_id=1, replica_groups=mesh['dp'=8,'tensor'=4] {'dp'}, dimensions={0}, use_global_device_ids=true | all-gather | bytes 11520 | tf_op jit(solution)/shard_map/all_gather | solution.py:350
  47.5 3.0 reshape.856
  50.5 43.7 %all-gather.19.cloned.1.call-done = bf16[1,80,128,128]{3,2,0,1:T(8,128)(2,1)} async-done(((bf16[1,10,128,128]{3,2,0,1:T(8,128)(2,1)}), bf16[1,80,128,128]{3,2,0,1:T(8,128)(2,1)}) %all-gather.19.cloned.1.call-update) | async-done | bytes 2621456 | tf_op jit(solution)/shard_map/all_gather | solution.py:349
  94.2 2.8 gather_fusion
  101.9 2.7 convolution_convert_fusion.2
  104.6 4.0 copy.287
  108.6 13.5 %while.68 = (s32[]{:T(128)}, bf16[3,784,128]{2,1,0:T(8,128)(2,1)S(1)}, f32[3,2,784,1]{2,1,3,0:T(2,128)S(1)}, bf16[3,784,384]{1,2,0:T(8,128)(2,1)}, s32[]{:T(128)}) while((s32[]{:T(128)}, bf16[3,784,128]{2,1,0:T(8,128)(2,1)S(1)}, f32[3,2,784,1]{2,1,3,0:T(2,128)S(1)}, bf16[3,784,384]{1,2,0:T(8,128)(2,1)}, s32[]{:T(128)}) %tuple.286), condition=%wide.region_4.5_spmd, body=%wide.region_1.0_spmd.sunk | while | flops 324637152 | bytes 18819664 | solution.py:187
  122.2 2.9 fusion.154
  125.1 46.0 %fusion = f32[592,512]{1,0:T(8,128)} fusion(f32[2352,512]{1,0:T(8,128)} %fusion.154), kind=kCustom, calls=%all-reduce-scatter | all-reduce-scatter fusion | flops 1212417 | bytes 6029824
  175.3 3.4 fusion.39
  187.8 3.6 concatenate.53
  195.6 11.0 %while.69 = (s32[]{:T(128)}, bf16[3,512,128]{2,1,0:T(8,128)(2,1)}, f32[3,2,512,1]{2,1,3,0:T(2,128)S(1)}, bf16[3,512,384]{1,2,0:T(8,128)(2,1)S(1)}, s32[3]{0:T(128)S(1)}, /*index=5*/s32[]{:T(128)}) while((s32[]{:T(128)}, bf16[3,512,128]{2,1,0:T(8,128)(2,1)}, f32[3,2,512,1]{2,1,3,0:T(2,128)S(1)}, bf16[3,512,384]{1,2,0:T(8,128)(2,1)S(1)}, ...), condition=%wide.region_14.15_spmd, body=%wide.region_11.14_spmd.sunk | while | flops 138477056 | bytes 9471081 | solution.py:187
  206.6 3.6 fusion.155
  210.3 8.5 all-gather.35.cloned.1.call-done
  218.8 2.9 reshape.860
  221.7 8.2 multiply_convert_fusion.3
  231.1 3.0 fusion.101
  234.1 62.3 %fusion.1 = f32[592,512]{1,0:T(8,128)S(1)} fusion(f32[2352,512]{1,0:T(8,128)} %fusion.101), kind=kCustom, calls=%all-reduce-scatter.1 | all-reduce-scatter fusion | flops 1212417 | bytes 6029824
  298.5 3.6 concatenate.54
  310.7 23.3 %all-gather.37.cloned.1.call-done = bf16[4,588,512]{2,1,0:T(8,128)(2,1)} async-done(((bf16[1,588,512]{2,1,0:T(8,128)(2,1)}), bf16[4,588,512]{2,1,0:T(8,128)(2,1)}) %all-gather.37.cloned.1.call-update) | async-done | bytes 2408464 | tf_op jit(solution)/shard_map/all_gather | solution.py:154
  333.9 3.0 reshape.862
  336.9 3.6 convolution_convert_fusion.3
  343.0 12.8 %all-gather.23.cloned.1.call-done = bf16[1536,512]{1,0:T(8,128)(2,1)} async-done(((bf16[384,512]{1,0:T(8,128)(2,1)}), bf16[1536,512]{1,0:T(8,128)(2,1)}) %all-gather.23.cloned.1.call-update) | async-done | bytes 1572880 | tf_op jit(solution)/shard_map/all_gather | solution.py:154
  360.1 16.0 %while.70 = (s32[]{:T(128)}, bf16[3,512,128]{2,1,0:T(8,128)(2,1)}, f32[3,2,512,1]{2,1,3,0:T(2,128)}, bf16[3,784,256]{1,2,0:T(8,128)(2,1)}, bf16[3,512,128]{1,2,0:T(8,128)(2,1)}, /*index=5*/s32[]{:T(128)}) while((s32[]{:T(128)}, bf16[3,512,128]{2,1,0:T(8,128)(2,1)}, f32[3,2,512,1]{2,1,3,0:T(2,128)}, bf16[3,784,256]{1,2,0:T(8,128)(2,1)}, ...), condition=%wide.region_21.22_spmd, body=%wide.region_18.21_spmd.sunk | while | flops 212007936 | bytes 12722269 | solution.py:245
  376.1 3.3 fusion.156
  379.5 38.0 %reduce-scatter.23.cloned.1.call-done = f32[384,512]{1,0:T(8,128)} async-done(((f32[1536,512]{1,0:T(8,128)}), f32[384,512]{1,0:T(8,128)}) %reduce-scatter.23.cloned.1.call-update) | async-done | bytes 786448 | tf_op jit(solution)/shard_map/reduce_scatter | solution.py:160
  424.0 16.9 %all-gather.25.cloned.1.call-done = bf16[1536,512]{1,0:T(8,128)(2,1)} async-done(((bf16[384,512]{1,0:T(8,128)(2,1)}), bf16[1536,512]{1,0:T(8,128)(2,1)}) %all-gather.25.cloned.1.call-update) | async-done | bytes 1572880 | tf_op jit(solution)/shard_map/all_gather | solution.py:154
  440.9 6.6 multiply_convert_fusion.4
  451.4 37.4 %reduce-scatter.25.cloned.1.call-done = f32[384,512]{1,0:T(8,128)} async-done(((f32[1536,512]{1,0:T(8,128)}), f32[384,512]{1,0:T(8,128)}) %reduce-scatter.25.cloned.1.call-update) | async-done | bytes 786448 | tf_op jit(solution)/shard_map/reduce_scatter | solution.py:160
  493.3 19.4 %all-gather.27.cloned.1.call-done = bf16[1536,512]{1,0:T(8,128)(2,1)} async-done(((bf16[384,512]{1,0:T(8,128)(2,1)}), bf16[1536,512]{1,0:T(8,128)(2,1)}) %all-gather.27.cloned.1.call-update) | async-done | bytes 1572880 | tf_op jit(solution)/shard_map/all_gather | solution.py:164
  512.6 3.3 add_convert_fusion.1
  519.3 38.1 %reduce-scatter.27.cloned.1.call-done = f32[384,512]{1,0:T(8,128)} async-done(((f32[1536,512]{1,0:T(8,128)}), f32[384,512]{1,0:T(8,128)}) %reduce-scatter.27.cloned.1.call-update) | async-done | bytes 786448 | tf_op jit(solution)/shard_map/reduce_scatter | solution.py:168
  557.3 3.7 multiply_reduce_fusion.14
  562.4 19.8 %all-gather.29.cloned.1.call-done = bf16[1536,512]{1,0:T(8,128)(2,1)} async-done(((bf16[384,512]{1,0:T(8,128)(2,1)}), bf16[1536,512]{1,0:T(8,128)(2,1)}) %all-gather.29.cloned.1.call-update) | async-done | bytes 1572880 | tf_op jit(solution)/shard_map/all_gather | solution.py:164
  582.2 2.7 convolution_convert_fusion.7
  585.7 38.9 %while.71 = (s32[]{:T(128)}, bf16[3,512,128]{2,1,0:T(8,128)(2,1)}, bf16[3,784,256]{2,1,0:T(8,128)(2,1)}, bf16[3,784,256]{1,2,0:T(8,128)(2,1)}, bf16[3,512,128]{1...) while((s32[]{:T(128)}, bf16[3,512,128]{2,1,0:T(8,128)(2,1)}, ...), condition=%wide.region_36.37_spmd, body=%wide.region_34.36_spmd.sunk | while | flops 524669952 | bytes 31096948 | solution.py:276
  624.6 4.4 fusion.96
  629.0 46.2 %fusion.2 = f32[592,512]{1,0:T(8,128)} fusion(f32[2352,512]{1,0:T(8,128)} %fusion.96), kind=kCustom, calls=%all-reduce-scatter.2 | all-reduce-scatter fusion | flops 1212417 | bytes 6029824
  678.1 4.6 concatenate.55
  686.6 3.1 fusion.157
  690.0 25.3 %all-gather.39.cloned.1.call-done = bf16[4,588,512]{2,1,0:T(8,128)(2,1)} async-done(((bf16[1,588,512]{2,1,0:T(8,128)(2,1)}), bf16[4,588,512]{2,1,0:T(8,128)(2,1)}) %all-gather.39.cloned.1.call-update) | async-done | bytes 2408464 | tf_op jit(solution)/shard_map/all_gather | solution.py:164
  715.3 2.9 reshape.864
  718.2 4.4 add_convert_fusion
  723.7 3.2 fusion.105
  726.9 62.3 %fusion.3 = f32[592,512]{1,0:T(8,128)S(1)} fusion(f32[2352,512]{1,0:T(8,128)} %fusion.105), kind=kCustom, calls=%all-reduce-scatter.3 | all-reduce-scatter fusion | flops 1212417 | bytes 6029824
  791.4 3.6 concatenate.56
  802.3 4.5 copy.325
  811.7 2.9 fusion.162
  821.8 3.9 fusion.160
  836.1 13.0 %all-gather.31.cloned.1.call-done = bf16[1536,512]{1,0:T(8,128)(2,1)} async-done(((bf16[384,512]{1,0:T(8,128)(2,1)}), bf16[1536,512]{1,0:T(8,128)(2,1)}) %all-gather.31.cloned.1.call-update) | async-done | bytes 1572880 | tf_op jit(solution)/shard_map/all_gather | solution.py:164
  851.2 20.3 %while.73 = (s32[]{:T(128)}, bf16[3,512,384]{2,1,0:T(8,128)(2,1)S(1)}, bf16[3,512,384]{1,2,0:T(8,128)(2,1)}, s32[3]{0:T(128)S(1)}, f32[3,2,512,1]{2,1,3,0:T(2,128)}, /*index=5*/bf16[3,512,128]{2,1,0:T(8,128)(2,1)S(1)}, s32[]{:T(128)}) while((s32[]{:T(128)}, bf16[3,512,384]{2,1,0:T(8,128)(2,1)S(1)}, bf16[3,512,384]{1,2,0:T(8,128)(2,1)}, ...), condition=%wide.region_52.53_spmd, body=%wide.region_50.52_spmd.sunk | while | flops 342294016 | bytes 22041716 | solution.py:216
  871.6 2.7 fusion.76
  874.4 32.0 %while.72 = (s32[]{:T(128)}, bf16[3,784,384]{2,1,0:T(8,128)(2,1)}, bf16[3,784,384]{1,2,0:T(8,128)(2,1)}, f32[3,2,784,1]{2,1,3,0:T(2,128)}, bf16[3,784,128]{2,1,0:T(8,128)(2,1)}, /*index=5*/s32[]{:T(128)}) while((s32[]{:T(128)}, bf16[3,784,384]{2,1,0:T(8,128)(2,1)}, bf16[3,784,384]{1,2,0:T(8,128)(2,1)}, f32[3,2,784,1]{2,1,3,0:T(2,128)}, ...), condition=%wide.region_45.46_spmd, body=%wide.region_43.45_spmd.sunk | while | flops 803817984 | bytes 45754332 | solution.py:216
  906.4 4.3 convolution_bitcast_fusion
  915.5 2.8 copy.317
  920.3 4.2 fusion.58
  932.4 2.8 fusion.60
  940.4 5.8 gather_fusion.1
  946.2 5.2 bitcast_select_fusion
  954.6 6.0 psum.7
  960.6 5.1 fusion.79
  965.7 45.3 %fusion.4 = f32[592,512]{1,0:T(8,128)S(1)} fusion(f32[2352,512]{1,0:T(8,128)} %fusion.79), kind=kCustom, calls=%all-reduce-scatter.4 | all-reduce-scatter fusion | flops 1212417 | bytes 6029824
  1013.8 2.7 dynamic-slice_add_fusion
  1018.8 42.3 %reduce-scatter.33.cloned.1.call-done = f32[1,10,128,128]{3,2,1,0:T(8,128)} async-done(((f32[1,80,128,128]{3,2,1,0:T(8,128)}), f32[1,10,128,128]{3,2,1,0:T(8,128)}) %reduce-scatter.33.cloned.1.call-update) | async-done | bytes 655376 | tf_op jit(solution)/shard_map/reduce_scatter | solution.py:440
  (643 shorter events, 276.6 us)
Async XLA Ops:
  7.2 1055.8 %copy-start = (f32[1,10,128,128]{3,2,1,0:T(8,128)S(1)}, f32[1,10,128,128]{3,2,1,0:T(8,128)}, u32[]{:S(2)}) copy-start(f32[1,10,128,128]{3,2,1,0:T(8,128)} %param.35) | copy-start | bytes 1966084
  7.2 39.0 %copy-start.107 = (u32[32]{0:T(128)S(1)}, u32[32]{0:T(128)}, u32[]{:S(2)}) copy-start(u32[32]{0:T(128)} %constant.313) | copy-start | bytes 388
  7.2 6.1 copy-start.91
  7.2 40.3 %all-gather.33.cloned.1.call-start = ((), (), s32[]{:S(2)}) async-start(), calls=%async_computation.22 | async-start | bytes 3031040 | tf_op jit(solution)/shard_map/all_gather | solution.py:154
  8.0 86.3 %all-gather.19.cloned.1.call-start = ((), (), s32[]{:S(2)}) async-start(), calls=%async_computation.8 | async-start | bytes 2949120 | tf_op jit(solution)/shard_map/all_gather | solution.py:349
  9.9 165.4 %all-gather.21.cloned.1.call-start = ((), (), s32[]{:S(2)}) async-start(), calls=%async_computation.9 | async-start | bytes 1966080 | tf_op jit(solution)/shard_map/all_gather | solution.py:154
  10.6 208.2 %all-gather.35.cloned.1.call-start = ((), (), s32[]{:S(2)}) async-start(), calls=%async_computation.23 | async-start | bytes 3031040 | tf_op jit(solution)/shard_map/all_gather | solution.py:154
  46.2 256.0 %copy-start.85 = (f32[1,512]{1,0:T(1,128)}, f32[1,512]{1,0:T(1,128)S(1)}, u32[]{:S(2)}) copy-start(f32[1,512]{1,0:T(1,128)S(1)} %get-tuple-element.559) | copy-start | bytes 6148
  46.2 258.1 %copy-start.82 = (f32[1,512]{1,0:T(1,128)}, f32[1,512]{1,0:T(1,128)S(1)}, u32[]{:S(2)}) copy-start(f32[1,512]{1,0:T(1,128)S(1)} %get-tuple-element.557) | copy-start | bytes 6148
  46.2 258.1 %copy-start.94 = (f32[1,512]{1,0:T(1,128)}, f32[1,512]{1,0:T(1,128)S(1)}, u32[]{:S(2)}) copy-start(f32[1,512]{1,0:T(1,128)S(1)} %get-tuple-element.556) | copy-start | bytes 6148
  46.2 371.3 %copy-start.87 = (f32[1,512]{1,0:T(1,128)}, f32[1,512]{1,0:T(1,128)S(1)}, u32[]{:S(2)}) copy-start(f32[1,512]{1,0:T(1,128)S(1)} %get-tuple-element.555) | copy-start | bytes 6148
  108.6 13.6 %copy-start.51 = (bf16[1,128,4,128]{1,3,2,0:T(8,128)(2,1)S(1)}, bf16[1,128,4,128]{1,3,2,0:T(8,128)(2,1)}, u32[]{:S(2)}) copy-start(bf16[1,128,4,128]{1,3,2,0:T(8,128)(2,1)} %copy.289) | copy-start | bytes 393220
  171.1 7.7 copy-start.12
  174.0 13.8 %collective-permute-start = (f32[12,512]{1,0:T(8,128)S(1)}, f32[12,512]{1,0:T(8,128)S(1)}, u32[]{:S(2)}, u32[]{:S(2)}) collective-permute-start(f32[12,512]{1,0:T(8,128)S(1)} %slice.178), channel_id=1, source_target_pairs={{0,1},{1,2},{2,3},{4,5},{5,6},{6,7},{8,9},{9,10},{10,11},{12,13},{... | collective-permute-start | bytes 73736
  181.0 25.6 %copy-start.53 = (bf16[1,128,4,128]{1,3,2,0:T(8,128)(2,1)}, bf16[1,128,4,128]{1,3,2,0:T(8,128)(2,1)S(1)}, u32[]{:S(2)}) copy-start(bf16[1,128,4,128]{1,3,2,0:T(8,128)(2,1)S(1)} %copy.297) | copy-start | bytes 393220
  194.6 110.9 %reduce-scatter.21.cloned.1.call-start = ((), (), s32[]{:S(2)}) async-start(), calls=%async_computation.10 | async-start | bytes 3932160 | tf_op jit(solution)/shard_map/reduce_scatter | solution.py:160
  210.2 11.5 %copy-start.62 = (bf16[4,2,128,128]{3,1,2,0:T(2,128)(2,1)S(1)}, bf16[4,2,128,128]{3,1,2,0:T(2,128)(2,1)}, u32[]{:S(2)}) copy-start(bf16[4,2,128,128]{3,1,2,0:T(2,128)(2,1)} %copy.291) | copy-start | bytes 786436
  210.2 123.7 %all-gather.37.cloned.1.call-start = ((), (), s32[]{:S(2)}) async-start(), calls=%async_computation.24 | async-start | bytes 3031040 | tf_op jit(solution)/shard_map/all_gather | solution.py:154
  221.7 9.4 copy-start.64
  296.4 2.1 collective-permute-start.1
  303.9 380.9 %copy-start.1 = (f32[588,512]{1,0:T(8,128)}, f32[588,512]{1,0:T(8,128)S(1)}, u32[]{:S(2)}) copy-start(f32[588,512]{1,0:T(8,128)S(1)} %get-tuple-element.505) | copy-start | bytes 3612676
  304.0 380.9 %copy-start.74 = (f32[588]{0:T(1024)}, f32[588]{0:T(1024)S(1)}, u32[]{:S(2)}) copy-start(f32[588]{0:T(1024)S(1)} %broadcast_multiply_fusion.4) | copy-start | bytes 7060
  304.3 380.6 %copy-start.76 = (f32[588]{0:T(1024)}, f32[588]{0:T(1024)S(1)}, u32[]{:S(2)}) copy-start(f32[588]{0:T(1024)S(1)} %add_rsqrt_fusion) | copy-start | bytes 7060
  305.4 50.4 %all-gather.23.cloned.1.call-start = ((), (), s32[]{:S(2)}) async-start(), calls=%async_computation.11 | async-start | bytes 1966080 | tf_op jit(solution)/shard_map/all_gather | solution.py:154
  306.8 110.7 %copy-start.79 = (f32[384]{0:T(512)}, f32[384]{0:T(512)S(1)}, u32[]{:S(2)}) copy-start(f32[384]{0:T(512)S(1)} %broadcast_multiply_fusion.14) | copy-start | bytes 4612
  307.1 110.4 %copy-start.89 = (f32[384]{0:T(512)}, f32[384]{0:T(512)S(1)}, u32[]{:S(2)}) copy-start(f32[384]{0:T(512)S(1)} %add_rsqrt_fusion.4) | copy-start | bytes 4612
  308.6 108.9 %reduce-scatter.23.cloned.1.call-start = ((), (), s32[]{:S(2)}) async-start(), calls=%async_computation.12 | async-start | bytes 3932160 | tf_op jit(solution)/shard_map/reduce_scatter | solution.py:160
  310.7 26.2 %copy-start.66 = (bf16[4,2,128,128]{3,1,2,0:T(2,128)(2,1)S(1)}, bf16[4,2,128,128]{3,1,2,0:T(2,128)(2,1)}, u32[]{:S(2)}) copy-start(bf16[4,2,128,128]{3,1,2,0:T(2,128)(2,1)} %copy.298) | copy-start | bytes 786436
  360.1 16.0 %copy-start.55 = (bf16[1,128,4,128]{1,3,2,0:T(8,128)(2,1)S(1)}, bf16[1,128,4,128]{1,3,2,0:T(8,128)(2,1)}, u32[]{:S(2)}) copy-start(bf16[1,128,4,128]{1,3,2,0:T(8,128)(2,1)} %copy.302) | copy-start | bytes 393220
  379.4 40.7 %copy-start.96 = (f32[1,512]{1,0:T(1,128)S(1)}, f32[1,512]{1,0:T(1,128)}, u32[]{:S(2)}) copy-start(f32[1,512]{1,0:T(1,128)} %get-tuple-element.552) | copy-start | bytes 6148
  379.4 43.6 %copy-start.58 = (bf16[8,128,128]{2,1,0:T(8,128)(2,1)S(1)}, bf16[8,128,128]{2,1,0:T(8,128)(2,1)}, u32[]{:S(2)}) copy-start(bf16[8,128,128]{2,1,0:T(8,128)(2,1)} %get-tuple-element.539) | copy-start | bytes 786436
  379.4 61.5 %all-gather.25.cloned.1.call-start = ((), (), s32[]{:S(2)}) async-start(), calls=%async_computation.13 | async-start | bytes 1966080 | tf_op jit(solution)/shard_map/all_gather | solution.py:154
  421.1 67.6 %reduce-scatter.25.cloned.1.call-start = ((), (), s32[]{:S(2)}) async-start(), calls=%async_computation.14 | async-start | bytes 3932160 | tf_op jit(solution)/shard_map/reduce_scatter | solution.py:160
  440.9 7.5 copy-start.61
  450.6 40.0 %copy-start.31 = (bf16[384,512]{1,0:T(8,128)(2,1)S(1)}, bf16[384,512]{1,0:T(8,128)(2,1)}, u32[]{:S(2)}) copy-start(bf16[384,512]{1,0:T(8,128)(2,1)} %param.28) | copy-start | bytes 1179652
  450.7 62.0 %all-gather.27.cloned.1.call-start = ((), (), s32[]{:S(2)}) async-start(), calls=%async_computation.15 | async-start | bytes 1966080 | tf_op jit(solution)/shard_map/all_gather | solution.py:164
  492.8 64.5 %reduce-scatter.27.cloned.1.call-start = ((), (), s32[]{:S(2)}) async-start(), calls=%async_computation.16 | async-start | bytes 3932160 | tf_op jit(solution)/shard_map/reduce_scatter | solution.py:168
  519.2 38.1 %copy-start.98 = (f32[1,512]{1,0:T(1,128)S(1)}, f32[1,512]{1,0:T(1,128)}, u32[]{:S(2)}) copy-start(f32[1,512]{1,0:T(1,128)} %get-tuple-element.551) | copy-start | bytes 6148
  519.2 63.0 %all-gather.29.cloned.1.call-start = ((), (), s32[]{:S(2)}) async-start(), calls=%async_computation.17 | async-start | bytes 1966080 | tf_op jit(solution)/shard_map/all_gather | solution.py:164
  561.0 21.1 %copy-start.56 = (bf16[1,128,4,128]{1,3,2,0:T(8,128)(2,1)S(1)}, bf16[1,128,4,128]{1,3,2,0:T(8,128)(2,1)}, u32[]{:S(2)}) copy-start(bf16[1,128,4,128]{1,3,2,0:T(8,128)(2,1)} %copy.302) | copy-start | bytes 393220
  562.4 152.9 %all-gather.39.cloned.1.call-start = ((), (), s32[]{:S(2)}) async-start(), calls=%async_computation.25 | async-start | bytes 3031040 | tf_op jit(solution)/shard_map/all_gather | solution.py:164
  675.2 7.5 copy-start.83
  676.0 2.1 collective-permute-start.2
  686.5 112.7 %reduce-scatter.29.cloned.1.call-start = ((), (), s32[]{:S(2)}) async-start(), calls=%async_computation.18 | async-start | bytes 3932160 | tf_op jit(solution)/shard_map/reduce_scatter | solution.py:168
  689.8 28.5 %copy-start.65 = (bf16[2,4,128,128]{3,1,2,0:T(4,128)(2,1)S(1)}, bf16[2,4,128,128]{3,1,2,0:T(4,128)(2,1)}, u32[]{:S(2)}) copy-start(bf16[2,4,128,128]{3,1,2,0:T(4,128)(2,1)} %copy.292) | copy-start | bytes 786436
  689.8 142.8 %all-gather.41.cloned.1.call-start = ((), (), s32[]{:S(2)}) async-start(), calls=%async_computation.26 | async-start | bytes 3031040 | tf_op jit(solution)/shard_map/all_gather | solution.py:164
  789.2 2.1 collective-permute-start.3
  799.1 50.0 %all-gather.31.cloned.1.call-start = ((), (), s32[]{:S(2)}) async-start(), calls=%async_computation.19 | async-start | bytes 1966080 | tf_op jit(solution)/shard_map/all_gather | solution.py:164
  802.2 151.6 %reduce-scatter.35.cloned.1.call-start = ((), (), s32[]{:S(2)}) async-start(), calls=%async_computation.27 | async-start | bytes 294912
  811.7 6.9 copy-start.16
  832.3 184.2 %reduce-scatter.31.cloned.1.call-start = ((), (), s32[]{:S(2)}) async-start(), calls=%async_computation.20 | async-start | bytes 3932160 | tf_op jit(solution)/shard_map/reduce_scatter | solution.py:168
  834.5 14.6 %copy-start.54 = (bf16[1,128,4,128]{1,3,2,0:T(8,128)(2,1)S(1)}, bf16[1,128,4,128]{1,3,2,0:T(8,128)(2,1)}, u32[]{:S(2)}) copy-start(bf16[1,128,4,128]{1,3,2,0:T(8,128)(2,1)} %copy-done.53) | copy-start | bytes 393220
  836.1 15.1 %copy-start.106 = (s32[3]{0:T(128)S(1)}, s32[3]{0:T(128)}, u32[]{:S(2)}) copy-start(s32[3]{0:T(128)} %param.29) | copy-start | bytes 40
  851.2 20.3 %copy-start.49 = (bf16[4,3,128,128]{2,0,3,1:T(4,128)(2,1)S(1)}, bf16[4,3,128,128]{2,0,3,1:T(4,128)(2,1)}, u32[]{:S(2)}) copy-start(bf16[4,3,128,128]{2,0,3,1:T(4,128)(2,1)} %copy.293) | copy-start | bytes 1179652
  874.3 186.7 %reduce-scatter.33.cloned.1.call-start = ((), (), s32[]{:S(2)}) async-start(), calls=%async_computation.21 | async-start | bytes 5898240 | tf_op jit(solution)/shard_map/reduce_scatter | solution.py:440
  918.2 6.3 copy-start.44
  952.7 7.9 copy-start.47
  960.6 51.8 %copy-start.93 = (f32[10,64]{1,0:T(8,128)}, f32[10,64]{1,0:T(8,128)S(1)}, u32[]{:S(2)}) copy-start(f32[10,64]{1,0:T(8,128)S(1)} %psum.7) | copy-start | bytes 7684
  965.7 46.7 %copy-start.92 = (f32[10,64]{1,0:T(8,128)S(1)}, f32[10,64]{1,0:T(8,128)}, u32[]{:S(2)}) copy-start(f32[10,64]{1,0:T(8,128)} %param.36) | copy-start | bytes 7684
  965.7 46.7 %copy-start.103 = (f32[10,64]{1,0:T(8,128)S(1)}, f32[10,64]{1,0:T(8,128)}, u32[]{:S(2)}) copy-start(f32[10,64]{1,0:T(8,128)} %param.37) | copy-start | bytes 7684
  1011.1 2.1 collective-permute-start.4
  1016.5 44.6 %copy-start.69 = (f32[1,10,128,128]{3,2,1,0:T(8,128)S(1)}, f32[1,10,128,128]{3,2,1,0:T(8,128)}, u32[]{:S(2)}) copy-start(f32[1,10,128,128]{3,2,1,0:T(8,128)} %param.34) | copy-start | bytes 1966084
  1016.5 46.5 %copy-start.40 = (f32[1,10,128,128]{3,2,1,0:T(8,128)S(1)}, f32[1,10,128,128]{3,2,1,0:T(8,128)}, u32[]{:S(2)}) copy-start(f32[1,10,128,128]{3,2,1,0:T(8,128)} %param.31) | copy-start | bytes 1966084
  1018.8 46.0 %copy-start.70 = (f32[1,10,128,128]{3,2,1,0:T(8,128)S(1)}, f32[1,10,128,128]{3,2,1,0:T(8,128)}, u32[]{:S(2)}) copy-start(f32[1,10,128,128]{3,2,1,0:T(8,128)} %param.33) | copy-start | bytes 1966084
  (71 other events, 188.1 us)
Sparse Core Ops, SparseCore 0:
  9.6 27.1 all-gather.32
  39.5 54.6 all-gather.18
  95.8 18.2 all-gather.20
  194.7 24.0 all-gather.34
  221.2 54.7 reduce-scatter.20
  305.5 28.3 all-gather.36
  336.1 19.6 all-gather.22
  379.5 37.9 reduce-scatter.22
  421.2 19.6 all-gather.24
  450.8 37.9 reduce-scatter.24
  492.9 19.6 all-gather.26
  519.3 37.9 reduce-scatter.26
  562.5 19.6 all-gather.28
  686.7 28.5 all-gather.38
  717.7 54.9 reduce-scatter.28
  799.3 28.6 all-gather.40
  829.4 19.6 all-gather.30
  853.2 61.2 reduce-scatter.34
  917.2 36.9 reduce-scatter.30
  958.3 102.7 reduce-scatter.32
where the time goes:
time: 1090 us; the launch traced here: 1080 us
  waiting for transfers between devices  343 us (31%)
  blocking collectives  300 us (28%)
  local copies, waits for them, and re-layouts  179 us (16%)
  matrix products  159 us (15%)
  other arithmetic  68.8 us (6%)
  between operations  16.8 us (2%)
    unnamed x5, blocking collectives  262 us
    all_gather x5, waiting for transfers between devices, gather_deltas(): return lax.all_gather(operand, 'tensor', axis=0, tiled=True)  77.4 us
    reduce_scatter x3, waiting for transfers between devices, spread_rows(): return lax.psum_scatter(operand, 'tensor', scatter_dimension=0, tiled=True)  75.4 us
    all_gather x6, waiting for transfers between devices, gather_rows(): lax.all_gather(for_sending(operand), 'tensor', axis=0, tiled=True)  61.6 us
    unnamed x244, local copies, waits for them, and re-layouts  48.3 us
    all_gather x1, waiting for transfers between devices, local(): lax.all_gather(master_blocks.astype(jnp.bfloat16), 'dp', axis=1, tiled=True)  43.7 us
    reduce_scatter x1, waiting for transfers between devices, local(): lax.psum_scatter(outgoing, 'dp', scatter_dimension=1, tiled=True)  42.3 us
    dot_general x11, matrix products, matmul(): return jnp.dot(former, latter, preferred_element_type=jnp.float32)  41.6 us
  transfers between devices with their start and end apart: 25, of which 17 were waited for; matrix products, arithmetic and copies ran while one was open for 46% of the time, Pallas kernels for 0%

commit v1 on v0

v1 whole, which is shorter than its diff:
```python
import jax
import jax.numpy as jnp
from jax import lax
from jax.experimental import pallas as pl
from jax.experimental.pallas import tpu as pltpu
from jax.sharding import PartitionSpec as P

D = 512
HEADS = 8
HEAD_DIM = 64
FF = 1024
TILE = 128
CHUNK = 16
CHUNKS = 5

NORM_EPSILON = 1e-05
MATRIX_RATE = 0.5
VECTOR_RATE = 0.2
STAT_DECAY = 0.5
MASKED_SCORE = -1e30

F32 = jnp.float32
BF16 = jnp.bfloat16
ANY = pl.BlockSpec(memory_space=pl.ANY)
VM = pl.BlockSpec(memory_space=pltpu.VMEM)


def core_pairs():
    return [(i, i ^ 1) for i in range(4)]


def chip_pairs():
    return [(i, i ^ 2) for i in range(4)]


def y_pairs():
    return [(i, i ^ 1) for i in range(8)]


def z_shift(step):
    return [(2 * z + y, 2 * ((z + step) % 4) + y) for z in range(4) for y in range(2)]


def relative_rank(position, size):
    me = lax.axis_index("dp")
    if size != 8:
        return jnp.int32(position)
    swapped, step = divmod(position, 4)
    return 2 * lax.rem(me // 2 - step + 4, 4) + lax.rem(me + swapped, 2)


def target_rank(position, size):
    me = lax.axis_index("dp")
    if size != 8:
        return jnp.int32(position)
    swapped, step = divmod(position, 4)
    return 2 * lax.rem(me // 2 + step, 4) + lax.rem(me + swapped, 2)


def gather_pieces(piece, size):
    if size != 8:
        return list(lax.all_gather(piece, "dp", axis=0, tiled=False))
    column = [piece] + [lax.ppermute(piece, "dp", z_shift(step)) for step in (1, 2, 3)]
    return column + [lax.ppermute(part, "dp", y_pairs()) for part in column]


def sum_pieces(pieces, size):
    if size != 8:
        whole = lax.psum_scatter(
            jnp.stack(pieces).astype(F32), "dp", scatter_dimension=0, tiled=False
        )
        return whole
    column = []
    for step in (1, 2, 3, 0):
        other = lax.ppermute(pieces[4 + step], "dp", y_pairs())
        both = pieces[step].astype(F32) + other.astype(F32)
        if step:
            column.append(lax.ppermute(both.astype(BF16), "dp", z_shift(step)).astype(F32))
        else:
            column.append(both)
    return (column[0] + column[1]) + (column[2] + column[3])


def gather_group(part):
    far = lax.ppermute(part, "tensor", chip_pairs())
    near = lax.ppermute(part, "tensor", core_pairs())
    far_near = lax.ppermute(far, "tensor", core_pairs())
    return (part, near, far, far_near)


def sum_group(parts):
    near = lax.ppermute(parts[1], "tensor", core_pairs())
    far_near = lax.ppermute(parts[3], "tensor", core_pairs())
    far = (parts[2].astype(F32) + far_near.astype(F32)).astype(BF16)
    far = lax.ppermute(far, "tensor", chip_pairs())
    return (parts[0].astype(F32) + near.astype(F32) + far.astype(F32)).astype(BF16)


def sum_over_group(value):
    value = value + lax.ppermute(value, "tensor", core_pairs())
    return value + lax.ppermute(value, "tensor", chip_pairs())


def pull_rows(rows, length):
    shards = lax.axis_size("tensor")
    later = lax.ppermute(rows, "tensor", [(i + 1, i) for i in range(shards - 1)])
    start = lax.axis_index("tensor") * (length - rows.shape[0])
    return lax.dynamic_slice_in_dim(jnp.concatenate([rows, later], axis=0), start, length, axis=0)


def push_rows(item, count):
    shards = lax.axis_size("tensor")
    length = item.shape[0]
    earlier = lax.ppermute(
        item[length - count :], "tensor", [(i, i + 1) for i in range(shards - 1)]
    )
    start = count - lax.axis_index("tensor") * (length - count)
    return lax.dynamic_slice_in_dim(
        jnp.concatenate([earlier, item[:count]], axis=0), start, count, axis=0
    )


def order_tiles(pieces, block_ids, slots):
    total = CHUNK * CHUNKS

    def kernel(ids, *refs):
        sources, out, sem = refs[:-2], refs[-2], refs[-1]

        def copy(p, j, b):
            return pltpu.make_async_copy(
                sources[p].at[pl.ds(j * TILE, TILE)], out.at[pl.ds(b * TILE, TILE)], sem
            )

        for p in range(len(sources)):
            for j in range(slots):
                block = ids[p * slots + j]

                @pl.when(block < total)
                def _():
                    copy(p, j, block).start()

        pltpu.make_async_copy(out, out, sem).wait()

    return pl.pallas_call(
        kernel,
        out_shape=jax.ShapeDtypeStruct((total * TILE, TILE), BF16),
        grid_spec=pltpu.PrefetchScalarGridSpec(
            num_scalar_prefetch=1,
            grid=(1,),
            in_specs=[ANY] * len(pieces),
            out_specs=ANY,
            scratch_shapes=[pltpu.SemaphoreType.DMA],
        ),
        name="order_tiles",
    )(block_ids, *pieces)


def deal_tiles(chunks, vector_rows, slot_of_block, positions, slots):
    count = len(positions)
    rows = slots * TILE + vector_rows.shape[1]

    def kernel(where, *refs):
        sources, extra, out, sem = refs[:CHUNKS], refs[CHUNKS], refs[CHUNKS + 1], refs[CHUNKS + 2]
        for c in range(CHUNKS):
            for k in range(CHUNK):
                pltpu.make_async_copy(
                    sources[c].at[pl.ds(k * TILE, TILE)],
                    out.at[pl.ds(pl.multiple_of(where[c * CHUNK + k], 16), TILE)],
                    sem,
                ).start()
        for p in range(count):
            pltpu.make_async_copy(
                extra.at[p], out.at[pl.ds(p * rows + slots * TILE, rows - slots * TILE)], sem
            ).start()
        for c in range(CHUNKS):
            pltpu.make_async_copy(sources[c], sources[c], sem).wait()
        pltpu.make_async_copy(extra, extra, sem).wait()

    owner = slot_of_block // slots
    place = jnp.zeros_like(owner)
    for p, rank in enumerate(positions):
        place = jnp.where(owner == rank, p, place)
    where = place * rows + lax.rem(slot_of_block, slots) * TILE
    out = pl.pallas_call(
        kernel,
        out_shape=jax.ShapeDtypeStruct((count * rows, TILE), BF16),
        grid_spec=pltpu.PrefetchScalarGridSpec(
            num_scalar_prefetch=1,
            grid=(1,),
            in_specs=[ANY] * (CHUNKS + 1),
            out_specs=ANY,
            scratch_shapes=[pltpu.SemaphoreType.DMA],
        ),
        name="deal_tiles",
    )(where, *chunks, vector_rows)
    return [out[p * rows : (p + 1) * rows] for p in range(count)]


def matmul(former, latter):
    return jnp.dot(former, latter, preferred_element_type=F32)


def times_transpose(former, latter):
    return lax.dot_general(former, latter, (((1,), (1,)), ((), ())), preferred_element_type=F32)


def transpose_times(former, latter):
    return lax.dot_general(former, latter, (((0,), (0,)), ((), ())), preferred_element_type=F32)


def smooth_gate(values):
    return jax.nn.gelu(values, approximate=False)


def gate_backward(preact, incoming):
    result, pullback = jax.vjp(smooth_gate, preact)
    return pullback(incoming)[0]


def norm_forward(residual, norm_gain, norm_shift):
    row_mean = jnp.mean(residual, axis=-1, keepdims=True)
    centered = residual - row_mean
    inverse_scale = lax.rsqrt(jnp.mean(centered * centered, axis=-1, keepdims=True) + NORM_EPSILON)
    normed = centered * inverse_scale
    return (normed * norm_gain + norm_shift, (normed, inverse_scale))


def norm_backward(gradient, stored, norm_gain):
    normed, inverse_scale = stored
    scaled = gradient * norm_gain
    adjusted = (
        scaled
        - jnp.mean(scaled, axis=-1, keepdims=True)
        - normed * jnp.mean(scaled * normed, axis=-1, keepdims=True)
    )
    return (inverse_scale * adjusted, jnp.sum(gradient * normed, axis=0), jnp.sum(gradient, axis=0))


def causal_allowed(item_length, live_count):
    row_index = lax.broadcasted_iota(jnp.int32, (item_length, item_length), 0)
    column_index = lax.broadcasted_iota(jnp.int32, (item_length, item_length), 1)
    return (column_index <= row_index) & (column_index < live_count)


def split_heads(matrix):
    return matrix.reshape(matrix.shape[0], matrix.shape[1] // HEAD_DIM, HEAD_DIM)


def head_scores(queries, key_rows, allowed):
    scores = jnp.einsum(
        "qhd,khd->hqk", split_heads(queries), split_heads(key_rows), preferred_element_type=F32
    ) * HEAD_DIM ** (-0.5)
    if allowed is None:
        return scores
    return jnp.where(allowed[None], scores, MASKED_SCORE)


def attend(queries, key_rows, value_rows, allowed):
    scores = head_scores(queries, key_rows, allowed)
    row_max = jnp.max(scores, axis=-1, keepdims=True)
    log_total = row_max + jnp.log(jnp.sum(jnp.exp(scores - row_max), axis=-1, keepdims=True))
    attention = jnp.exp(scores - log_total).astype(BF16)
    mixed = jnp.einsum("hqk,khd->qhd", attention, split_heads(value_rows), preferred_element_type=F32)
    return (mixed.reshape(queries.shape).astype(BF16), log_total)


def attend_back(queries, key_rows, value_rows, allowed, log_total, delta_mixed):
    scores = head_scores(queries, key_rows, allowed)
    attention = jnp.exp(scores - log_total)
    delta_heads = split_heads(delta_mixed)
    delta_attention = jnp.einsum(
        "qhd,khd->hqk", delta_heads, split_heads(value_rows), preferred_element_type=F32
    )
    delta_values = jnp.einsum(
        "hqk,qhd->khd", attention.astype(BF16), delta_heads, preferred_element_type=F32
    )
    delta_scores = attention * (
        delta_attention - jnp.sum(attention * delta_attention, axis=-1, keepdims=True)
    )
    delta_scores = delta_scores.astype(BF16)
    delta_queries = jnp.einsum(
        "hqk,khd->qhd", delta_scores, split_heads(key_rows), preferred_element_type=F32
    ) * HEAD_DIM ** (-0.5)
    delta_keys = jnp.einsum(
        "hqk,qhd->khd", delta_scores, split_heads(queries), preferred_element_type=F32
    ) * HEAD_DIM ** (-0.5)
    return (
        delta_queries.reshape(queries.shape).astype(BF16),
        delta_keys.reshape(key_rows.shape).astype(BF16),
        delta_values.reshape(value_rows.shape).astype(BF16),
    )


def tall(parts, first, count):
    picked = jnp.stack([p.reshape(CHUNK, TILE, TILE)[first : first + 4 * count] for p in parts])
    picked = picked.reshape(4, 4, count, TILE, TILE)
    return [picked[:, :, c].transpose(1, 2, 0, 3).reshape(D, 4 * TILE) for c in range(count)]


def wide(parts, first, count):
    picked = jnp.stack([p.reshape(CHUNK, TILE, TILE)[first : first + 4 * count] for p in parts])
    picked = picked.reshape(4, count, 4, TILE, TILE)
    return [picked[:, c].transpose(0, 2, 1, 3).reshape(4 * TILE, D) for c in range(count)]


def untall(matrices):
    stacked = jnp.stack([m.astype(BF16).reshape(4, TILE, 4, TILE) for m in matrices])
    stacked = stacked.transpose(3, 1, 0, 2, 4)
    return stacked.reshape(4, -1, TILE, TILE)


def unwide(matrices):
    stacked = jnp.stack([m.astype(BF16).reshape(4, TILE, 4, TILE) for m in matrices])
    stacked = stacked.transpose(1, 0, 3, 2, 4)
    return stacked.reshape(4, -1, TILE, TILE)


def as_parts(*tiles):
    whole = jnp.concatenate(tiles, axis=1).reshape(4, CHUNK * TILE, TILE)
    return [whole[r] for r in range(4)]


def compute(x, y, xc, yc, live, weights, vectors, alive):
    g = [vectors[i : i + 1] for i in range(10)]
    wq, wk, wv = tall(weights[0], 0, 3)
    (wo,) = wide(weights[0], 12, 1)
    w1 = jnp.concatenate(tall(weights[1], 0, 2), axis=1)
    w2 = jnp.concatenate(wide(weights[1], 8, 2), axis=0)
    sq, sk, sv = tall(weights[2], 0, 3)
    (so,) = wide(weights[2], 12, 1)
    (cq,) = tall(weights[3], 0, 1)
    ck, cv = tall(weights[3], 4, 2)
    (co,) = wide(weights[3], 12, 1)
    v1 = jnp.concatenate(tall(weights[4], 0, 2), axis=1)
    v2 = jnp.concatenate(wide(weights[4], 8, 2), axis=0)
    low = lambda a: a.astype(BF16)
    q, k, v = low(matmul(x, wq)), low(matmul(x, wk)), low(matmul(x, wv))
    o, lse = attend(q, k, v, None)
    first, n0 = norm_forward(x.astype(F32) + matmul(o, wo), g[0], g[1])
    pre = matmul(low(first), w1)
    hid = low(smooth_gate(pre))
    enc, n1 = norm_forward(first + matmul(hid, w2), g[2], g[3])
    encl = low(enc)
    allowed = causal_allowed(y.shape[0], live)
    q2, k2, v2_ = low(matmul(y, sq)), low(matmul(y, sk)), low(matmul(y, sv))
    o2, lse2 = attend(q2, k2, v2_, allowed)
    second, n2 = norm_forward(y.astype(F32) + matmul(o2, so), g[4], g[5])
    q3, k3, v3 = low(matmul(low(second), cq)), low(matmul(encl, ck)), low(matmul(encl, cv))
    o3, lse3 = attend(q3, k3, v3, None)
    third, n3 = norm_forward(second + matmul(o3, co), g[6], g[7])
    pre2 = matmul(low(third), v1)
    hid2 = low(smooth_gate(pre2))
    dec, n4 = norm_forward(third + matmul(hid2, v2), g[8], g[9])
    vg = [None] * 10
    rows = lax.broadcasted_iota(jnp.int32, (y.shape[0], 1), 0)
    b = jnp.where((rows < live) & alive, yc.astype(F32), 0.0)
    b, vg[8], vg[9] = norm_backward(b, n4, g[8])
    bl = low(b)
    dh = low(gate_backward(pre2, times_transpose(bl, v2)))
    gv2, gv1 = transpose_times(hid2, bl), transpose_times(low(third), dh)
    b = b + times_transpose(dh, v1)
    b, vg[6], vg[7] = norm_backward(b, n3, g[6])
    bl = low(b)
    do = low(times_transpose(bl, co))
    gco = transpose_times(o3, bl)
    dq, dk, dv = attend_back(q3, k3, v3, None, lse3, do)
    gcq, gck, gcv = transpose_times(low(second), dq), transpose_times(encl, dk), transpose_times(encl, dv)
    denc = times_transpose(dk, ck) + times_transpose(dv, cv)
    b = b + times_transpose(dq, cq)
    b, vg[4], vg[5] = norm_backward(b, n2, g[4])
    bl = low(b)
    do = low(times_transpose(bl, so))
    gso = transpose_times(o2, bl)
    dq, dk, dv = attend_back(q2, k2, v2_, allowed, lse2, do)
    gs = [transpose_times(y, d) for d in (dq, dk, dv)]
    dy = b + times_transpose(dq, sq) + times_transpose(dk, sk) + times_transpose(dv, sv)
    b = jnp.where(alive, xc.astype(F32), 0.0) + denc
    b, vg[2], vg[3] = norm_backward(b, n1, g[2])
    bl = low(b)
    dh = low(gate_backward(pre, times_transpose(bl, w2)))
    gw2, gw1 = transpose_times(hid, bl), transpose_times(low(first), dh)
    b = b + times_transpose(dh, w1)
    b, vg[0], vg[1] = norm_backward(b, n0, g[0])
    bl = low(b)
    do = low(times_transpose(bl, wo))
    gwo = transpose_times(o, bl)
    dq, dk, dv = attend_back(q, k, v, None, lse, do)
    ge = [transpose_times(x, d) for d in (dq, dk, dv)]
    dx = b + times_transpose(dq, wq) + times_transpose(dk, wk) + times_transpose(dv, wv)
    parts = [
        as_parts(untall(ge), unwide([gwo])),
        as_parts(untall([gw1[:, :D], gw1[:, D:]]), unwide([gw2[:D], gw2[D:]])),
        as_parts(untall(gs), unwide([gso])),
        as_parts(untall([gcq]), untall([gck, gcv]), unwide([gco])),
        as_parts(untall([gv1[:, :D], gv1[:, D:]]), unwide([gv2[:D], gv2[D:]])),
    ]
    return encl, low(dec), dx, dy, parts, jnp.stack(vg)


def one_hot(index, count, dtype):
    return (index[:, None] == lax.broadcasted_iota(jnp.int32, (1, count), 1)).astype(dtype)


def local(
    image_tokens,
    tag_tokens,
    image_cotangent,
    tag_cotangent,
    tag_lengths,
    slot_blocks,
    master_blocks,
    left_factor,
    right_factor,
    left_root,
    right_root,
    vector_master,
    vector_moment,
):
    dp = lax.axis_size("dp")
    shards = lax.axis_size("tensor")
    me = lax.axis_index("tensor")
    slots = master_blocks.shape[1]
    items = tag_lengths.shape[0]
    image_length = image_tokens.shape[0] * shards // items
    item_length = tag_tokens.shape[0] * shards // items
    lanes = vector_master.shape[1]
    total = CHUNK * CHUNKS

    def rows_of(value):
        return jnp.pad(value, ((0, 16 - value.shape[0]), (0, TILE - value.shape[1])))

    own = jnp.concatenate(
        [
            master_blocks.astype(BF16).reshape(slots * TILE, TILE),
            rows_of(vector_master.astype(BF16)),
        ],
        axis=0,
    )
    pieces = gather_pieces(own, dp)
    ranks = jnp.stack([relative_rank(p, dp) for p in range(dp)])
    by_rank = jnp.dot(
        one_hot(ranks, dp, F32),
        slot_blocks.reshape(dp, slots).astype(F32),
        precision=lax.Precision.HIGHEST,
    )
    tiles = order_tiles(pieces, by_rank.astype(jnp.int32).reshape(-1), slots)
    vector_list = jnp.stack([p[slots * TILE : slots * TILE + 10, :lanes] for p in pieces])
    vectors = jnp.einsum(
        "pr,pvl->vrl", one_hot(ranks, dp, BF16), vector_list, preferred_element_type=F32
    ).reshape(10, dp * lanes)
    weights = [
        gather_group(tiles[c * CHUNK * TILE : (c + 1) * CHUNK * TILE]) for c in range(CHUNKS)
    ]
    x = pull_rows(image_tokens, image_length)
    y = pull_rows(tag_tokens, item_length)
    xc = pull_rows(image_cotangent, image_length)
    yc = pull_rows(tag_cotangent, item_length)
    alive = me < items
    live = jnp.sum(jnp.where(lax.broadcasted_iota(jnp.int32, (items,), 0) == me, tag_lengths, 0))
    live = jnp.where(alive, live, 1)
    encoded, decoded, dx, dy, parts, vector_grads = compute(
        x, y, xc, yc, live, weights, vectors, alive
    )
    sums = [sum_group(p) for p in parts]
    vector_grads = sum_over_group(vector_grads).reshape(10, dp, lanes)
    targets = jnp.stack([target_rank(p, dp) for p in range(dp)])
    vector_rows = jnp.einsum(
        "pr,vrl->pvl",
        one_hot(targets, dp, F32),
        vector_grads,
        precision=lax.Precision.HIGHEST,
    )
    vector_rows = jnp.pad(vector_rows, ((0, 0), (0, 6), (0, TILE - lanes))).astype(BF16)
    slot_of_block = jnp.sum(
        jnp.where(
            slot_blocks[None, :] == lax.broadcasted_iota(jnp.int32, (total, 1), 0),
            lax.broadcasted_iota(jnp.int32, (1, dp * slots), 1),
            0,
        ),
        axis=1,
    )
    outgoing = deal_tiles(
        sums, vector_rows, slot_of_block, [target_rank(p, dp) for p in range(dp)], slots
    )
    summed = sum_pieces(outgoing, dp)
    dealt = summed[: slots * TILE].reshape(slots, TILE, TILE)
    own_blocks = lax.dynamic_slice_in_dim(slot_blocks, lax.axis_index("dp") * slots, slots)
    dealt = jnp.where((own_blocks < total)[:, None, None], dealt, 0.0)[None]
    vector_gradient = summed[slots * TILE : slots * TILE + 10, :lanes]
    highest = lax.Precision.HIGHEST
    left_updated = STAT_DECAY * left_factor + (1.0 - STAT_DECAY) * jnp.einsum(
        "asij,askj->asik", dealt, dealt, precision=highest
    )
    right_updated = STAT_DECAY * right_factor + (1.0 - STAT_DECAY) * jnp.einsum(
        "asji,asjk->asik", dealt, dealt, precision=highest
    )
    rotated = jnp.einsum("asij,asjk->asik", left_root, dealt, precision=highest)
    master_updated = master_blocks - MATRIX_RATE * jnp.einsum(
        "asij,asjk->asik", rotated, right_root, precision=highest
    )
    moment_updated = (
        STAT_DECAY * vector_moment + (1.0 - STAT_DECAY) * vector_gradient * vector_gradient
    )
    vector_updated = vector_master - VECTOR_RATE * vector_gradient / (
        jnp.sqrt(moment_updated) + 1e-08
    )
    return (
        push_rows(encoded, image_tokens.shape[0]),
        push_rows(decoded, tag_tokens.shape[0]),
        push_rows(dx.astype(BF16), image_tokens.shape[0]).astype(F32),
        push_rows(dy.astype(BF16), tag_tokens.shape[0]).astype(F32),
        dealt,
        left_updated,
        right_updated,
        master_updated,
        master_updated.astype(BF16),
        vector_gradient,
        moment_updated,
        vector_updated,
    )

def solution(mesh):
    in_specs = (
        P(("dp", "tensor"), None),
        P(("dp", "tensor"), None),
        P(("dp", "tensor"), None),
        P(("dp", "tensor"), None),
        P("dp"),
        P(),
        P("tensor", "dp", None, None),
        P("tensor", "dp", None, None),
        P("tensor", "dp", None, None),
        P("tensor", "dp", None, None),
        P("tensor", "dp", None, None),
        P(None, "dp"),
        P(None, "dp"),
    )
    out_specs = (
        P(("dp", "tensor"), None),
        P(("dp", "tensor"), None),
        P(("dp", "tensor"), None),
        P(("dp", "tensor"), None),
        P("tensor", "dp", None, None),
        P("tensor", "dp", None, None),
        P("tensor", "dp", None, None),
        P("tensor", "dp", None, None),
        P("tensor", "dp", None, None),
        P(None, "dp"),
        P(None, "dp"),
        P(None, "dp"),
    )
    return jax.shard_map(local, mesh=mesh, in_specs=in_specs, out_specs=out_specs, check_vma=False)
```

time: 1090 us -> 808 us (0.74)
  blocking collectives: 300 us -> 0 us
  waiting for transfers between devices: 343 us -> 132 us
  Pallas kernels: 0 us -> 163 us
  starting transfers between devices: 8.43 us -> 48.9 us
  other arithmetic: 68.8 us -> 108 us
  matrix products: 159 us -> 173 us
  between operations: 16.8 us -> 4.11 us
  local copies, waits for them, and re-layouts: 179 us -> 168 us
    unnamed x5 -> x0, blocking collectives: 262 us -> none
    all_gather x12 -> x0, waiting for transfers between devices: 183 us -> none  [the longest x5 77.4 us: gather_deltas(): return lax.all_gather(operand, 'tensor', axis=0, tiled=True)]
    pallas_call x0 -> x2, Pallas kernels: none -> 163 us  [the longest x1 82.2 us: deal_tiles(): pl.pallas_call(kernel, out_shape=jax.ShapeDtypeStruct((count * rows, TILE...]
    reduce_scatter x7 -> x0, waiting for transfers between devices: 156 us -> none  [the longest x3 75.4 us: spread_rows(): return lax.psum_scatter(operand, 'tensor', scatter_dimension=0, tiled=True)]
    ppermute x0 -> x54, waiting for transfers between devices: none -> 132 us  [the longest x5 46.2 us: sum_group(): far = lax.ppermute(far, 'tensor', chip_pairs())]
    another operation x6 -> x67, local copies, waits for them, and re-layouts: 3.06 us -> 73.8 us  [the longest x14 24.6 us: untall(): jnp.stack([m.astype(BF16).reshape(4, TILE, 4, TILE) for m in matrices])]
    ppermute x0 -> x54, starting transfers between devices: none -> 48.9 us  [the longest x4 8.72 us: push_rows(): lax.ppermute(item[length - count:], 'tensor', [(i, i + 1) for i in range(...]
    slice x21 -> x47, local copies, waits for them, and re-layouts: 3.34 us -> 37.3 us  [the longest x17 7.49 us: wide(): p.reshape(CHUNK, TILE, TILE)[first:first + 4 * count]]
  transfers between devices with their start and end apart: 25 -> 54, of which waited for: 17 -> 20; matrix products, arithmetic and copies ran while one was open for 46% -> 40% of each run, Pallas kernels for 0% -> 10%
where the time goes in v1:
time: 808 us; the launch traced here: 797 us
  matrix products  173 us (21%)
  local copies, waits for them, and re-layouts  168 us (21%)
  Pallas kernels  163 us (20%)
  waiting for transfers between devices  132 us (16%)
  other arithmetic  108 us (13%)
  starting transfers between devices  48.9 us (6%)
    pallas_call x1, Pallas kernels, deal_tiles(): pl.pallas_call(kernel, out_shape=jax.ShapeDtypeStruct((count * rows, TILE...  82.2 us
    pallas_call x1, Pallas kernels, order_tiles(): pl.pallas_call(kernel, out_shape=jax.ShapeDtypeStruct((total * TILE, TILE...  81.2 us
    ppermute x5, waiting for transfers between devices, sum_group(): far = lax.ppermute(far, 'tensor', chip_pairs())  46.2 us
    dot_general x16, matrix products, matmul(): return jnp.dot(former, latter, preferred_element_type=F32)  34.5 us
    unnamed x330, local copies, waits for them, and re-layouts  31.7 us
    dot_general x16, matrix products, transpose_times(): lax.dot_general(former, latter, (((0,), (0,)), ((), ())), preferred_eleme...  26 us
    convert_element_type x3, other arithmetic, attend_back(): delta_scores = delta_scores.astype(BF16)  24.7 us
    another operation x14, local copies, waits for them, and re-layouts, untall(): jnp.stack([m.astype(BF16).reshape(4, TILE, 4, TILE) for m in matrices])  24.6 us
  transfers between devices with their start and end apart: 54, of which 20 were waited for; matrix products, arithmetic and copies ran while one was open for 40% of the time, Pallas kernels for 10%

profile of v1, /device:TPU:0, one launch (start us, length us, event | category | flops | bytes accessed | tf_op | source)
XLA Modules:
  0.0 797.3 jit_solution(12440471722835402846)
XLA Ops:
  2.7 3.0 collective-permute-start.4
  5.7 3.6 collective-permute-start.3
  20.1 17.3 %collective-permute-done.2.refs_2_ = bf16[1296,128]{1,0:T(8,128)(2,1)} collective-permute-done((bf16[1296,128]{1,0:T(8,128)(2,1)S(1)}, bf16[1296,128]{1,0:T(8,128)(2,1)}, u32[]{:S(2)}, u32[]{:S(2)}) %collective-permute-start.2) | collective-permute-done | bytes 331808 | tf_op jit(solution)/shard_map/ppermute | solution.py:63
  43.5 2.4 fusion.61
  45.9 2.5 collective-permute-done.7.refs_7_
  49.1 6.4 collective-permute-done.6.refs_6_
  56.2 4.1 collective-permute-done.5.refs_5_
  60.3 81.2 %order_tiles.1 = bf16[10240,128]{1,0:T(8,128)(2,1)} custom-call(s32[80]{0:T(128)} %reshape.699.ids, bf16[1296,128]{1,0:T(8,128)(2,1)} %copy-done.83, bf16[1296,128]{1,0:T(8,128)(2,1)} %collective-permute-done.1.refs_1_, bf16[1296,128]{1,0:T(8,128)(2,1)} %collective-permute-done.2.refs_2_, bf16[1296,128]{1,0:T(8,128)(2,1)} %collective-permute-done.3.refs_3_, ...), custom_call_target="tpu_custom_call" | custom-call | tf_op jit(solution)/shard_map/order_tiles/pallas_call | solution.py:144
  168.1 5.7 collective-permute-done.23
  177.8 7.2 collective-permute-done.12
  185.2 8.8 %collective-permute-done.20 = bf16[2048,128]{1,0:T(8,128)(2,1)S(1)} collective-permute-done((bf16[2048,128]{1,0:T(8,128)(2,1)S(1)}, bf16[2048,128]{1,0:T(8,128)(2,1)S(1)}, u32[]{:S(2)}, u32[]{:S(2)}) %collective-permute-start.20) | collective-permute-done | bytes 524320 | tf_op jit(solution)/shard_map/ppermute | solution.py:85
  219.9 2.4 pad_maximum_fusion.5
  223.5 4.1 pad_maximum_fusion.2
  234.6 2.4 pad_maximum_fusion.3
  239.0 2.4 pad_maximum_fusion.4
  245.6 3.9 pad_maximum_fusion.1
  256.2 3.1 convolution_convert_fusion.8
  261.5 2.6 convolution_convert_fusion.10
  267.2 2.4 fusion.220
  275.2 2.4 convolution_convert_fusion.22
  279.5 3.1 multiply_reduce_fusion.1
  282.6 4.5 exponential_reduce_fusion
  287.2 3.2 copy-done.1
  290.4 11.5 %fusion.20 = bf16[8,64,784]{2,1,0:T(8,128)(2,1)S(1)} fusion(bf16[784,8,64]{0,2,1:T(8,128)(2,1)S(1)} %bitcast.541, f32[8,784,784]{1,2,0:T(8,128)} %copy-done.1, f32[8,784]{1,0:T(8,128)S(1)} %log_add_fusion), kind=kOutput, calls=%fused_computation.109 | convolution fusion | flops 644560896 | bytes 21299712 | tf_op jit(solution)/shard_map/hqk,khd->qhd/dot_general | solution.py:263
  305.8 9.6 %multiply_convert_fusion.3 = (bf16[784,1024]{1,0:T(8,128)(2,1)S(1)}, f32[784,1024]{1,0:T(8,128)}, f32[784,1024]{1,0:T(8,128)}) fusion(bf16[512,1024]{1,0:T(8,128)(2,1)S(1)} %bitcast_dynamic-update-slice_fusion.6, f32[784,512]{1,0:T(8,128)S(1)} %get-tuple-element.197, f32[512]{0:T(512)S(1)} %copy-done.140, f32[512]{0:T(512)S(1)} %mul.452, ...), kind=kOutput, calls=%fused_computation.22 | convolution fusion | flops 876273664 | bytes 10692736 | tf_op jit(solution)/shard_map/dot_general | solution.py:200
  321.9 2.8 convolution_convert_fusion.7
  326.9 2.5 pad_maximum_fusion.12
  334.3 2.8 convolution_convert_fusion.20
  339.6 5.1 multiply_convert_fusion.4
  345.9 2.6 multiply_reduce_fusion.13
  355.7 2.5 convolution_convert_fusion.4
  361.0 6.5 multiply_reduce_fusion.2
  367.4 7.1 multiply_convert_fusion.1
  387.7 3.2 multiply_reduce_fusion.5
  392.3 2.3 convolution_convert_fusion
  399.6 2.5 convolution_convert_fusion.1
  405.7 3.1 convolution_convert_fusion.19
  408.8 2.9 multiply_reduce_fusion.4
  411.8 2.7 multiply_convert_fusion.2
  419.6 2.4 copy.307
  422.0 12.6 %fusion.23 = bf16[8,64,784]{2,1,0:T(8,128)(2,1)} fusion(bf16[784,8,64]{0,2,1:T(8,128)(2,1)} %bitcast.543, f32[8,784,784]{1,2,0:T(8,128)} %copy-done.1, f32[8,784]{1,0:T(8,128)S(1)} %log_add_fusion), kind=kOutput, calls=%fused_computation.110 | convolution fusion | flops 644560896 | bytes 21299712 | tf_op jit(solution)/shard_map/hqk,qhd->khd/dot_general | solution.py:274
  434.6 14.5 %multiply_reduce_fusion = (f32[8,784]{1,0:T(8,128)S(1)}, f32[8,784,784]{1,2,0:T(8,128)}) fusion(f32[8,784,784]{1,2,0:T(8,128)} %copy-done.1, f32[8,784]{1,0:T(8,128)S(1)} %log_add_fusion, bf16[784,8,64]{0,2,1:T(8,128)(2,1)} %bitcast.544, bf16[784,8,64]{0,2,1:T(8,128)(2,1)S(1)} %bitcast.542), kind=kOutput, calls=%fused_computation.1 | convolution fusion | flops 649070464 | bytes 40993792 | tf_op jit(solution)/shard_map/qhd,khd->hqk/dot_general | solution.py:271
  449.1 15.0 %multiply_convert_fusion = bf16[8,784,784]{1,2,0:T(8,128)(2,1)S(1)} fusion(f32[8,784,784]{1,2,0:T(8,128)} %get-tuple-element.218, f32[8,784,784]{1,2,0:T(8,128)} %copy-done.1, f32[8,784]{1,0:T(8,128)S(1)} %get-tuple-element.217, f32[8,784]{1,0:T(8,128)S(1)} %log_add_fusion), kind=kLoop, calls=%fused_computation | loop fusion | flops 24586240 | bytes 49222656 | tf_op jit(solution)/shard_map/convert_element_type | solution.py:280
  464.1 4.6 multiply_convert_fusion.5
  468.7 3.4 multiply_convert_fusion.6
  479.0 3.2 collective-permute-start.14
  548.6 3.0 fusion.84
  560.2 2.7 maximum_bitcast_fusion.1
  569.4 2.7 add_convert_fusion.2
  588.5 12.2 %collective-permute-done.44 = bf16[2048,128]{1,0:T(8,128)(2,1)S(1)} collective-permute-done((bf16[2048,128]{1,0:T(8,128)(2,1)S(1)}, bf16[2048,128]{1,0:T(8,128)(2,1)S(1)}, u32[]{:S(2)}, u32[]{:S(2)}) %collective-permute-start.44) | collective-permute-done | bytes 524320 | tf_op jit(solution)/shard_map/ppermute | solution.py:95
  603.4 8.5 %collective-permute-done.35 = bf16[2048,128]{1,0:T(8,128)(2,1)S(1)} collective-permute-done((bf16[2048,128]{1,0:T(8,128)(2,1)S(1)}, bf16[2048,128]{1,0:T(8,128)(2,1)S(1)}, u32[]{:S(2)}, u32[]{:S(2)}) %collective-permute-start.35) | collective-permute-done | bytes 524320 | tf_op jit(solution)/shard_map/ppermute | solution.py:95
  614.6 8.5 %collective-permute-done.41 = bf16[2048,128]{1,0:T(8,128)(2,1)S(1)} collective-permute-done((bf16[2048,128]{1,0:T(8,128)(2,1)S(1)}, bf16[2048,128]{1,0:T(8,128)(2,1)S(1)}, u32[]{:S(2)}, u32[]{:S(2)}) %collective-permute-start.41) | collective-permute-done | bytes 524320 | tf_op jit(solution)/shard_map/ppermute | solution.py:95
  626.8 7.6 collective-permute-done.38
  635.4 9.4 %collective-permute-done.32 = bf16[2048,128]{1,0:T(8,128)(2,1)S(1)} collective-permute-done((bf16[2048,128]{1,0:T(8,128)(2,1)S(1)}, bf16[2048,128]{1,0:T(8,128)(2,1)S(1)}, u32[]{:S(2)}, u32[]{:S(2)}) %collective-permute-start.32) | collective-permute-done | bytes 524320 | tf_op jit(solution)/shard_map/ppermute | solution.py:95
  645.8 82.2 %deal_tiles.1 = bf16[10368,128]{1,0:T(8,128)(2,1)} custom-call(s32[80]{0:T(128)} %fusion.183.where, bf16[2048,128]{1,0:T(8,128)(2,1)} %fusion.51.refs_0_, bf16[2048,128]{1,0:T(8,128)(2,1)} %fusion.48.refs_1_, bf16[2048,128]{1,0:T(8,128)(2,1)} %fusion.45.refs_2_, bf16[2048,128]{1,0:T(8,128)(2,1)} %fusion.42.refs_3_, bf16[2048,128]{1,0:T(8,128)(2,1)} %fusion.39.refs_4_, ...), custom_call_target="tpu_custom_call" | custom-call | tf_op jit(solution)/shard_map/deal_tiles/pallas_call | solution.py:184
  735.2 5.8 collective-permute-done.47
  743.1 5.0 collective-permute-done.51
  748.6 6.6 collective-permute-done.49
  757.1 3.2 collective-permute-start.52
  763.1 2.3 copy.336
  765.4 2.7 fusion.68
  768.1 2.7 fusion.67
  772.0 12.8 %collective-permute-done.50 = bf16[1296,128]{1,0:T(8,128)(2,1)} collective-permute-done((bf16[1296,128]{1,0:T(8,128)(2,1)}, bf16[1296,128]{1,0:T(8,128)(2,1)}, u32[]{:S(2)}, u32[]{:S(2)}) %collective-permute-start.50) | collective-permute-done | bytes 331808 | tf_op jit(solution)/shard_map/ppermute | solution.py:78
  787.2 3.5 fusion.35
  (689 shorter events, 308.1 us)
Async XLA Ops:
  0.6 794.7 %copy-start = (f32[1,10,128,128]{3,2,1,0:T(8,128)S(1)}, f32[1,10,128,128]{3,2,1,0:T(8,128)}, u32[]{:S(2)}) copy-start(f32[1,10,128,128]{3,2,1,0:T(8,128)} %param.23) | copy-start | bytes 1966084
  2.7 43.2 %copy-start.83 = (bf16[1296,128]{1,0:T(8,128)(2,1)}, bf16[1296,128]{1,0:T(8,128)(2,1)S(1)}, u32[]{:S(2)}) copy-start(bf16[1296,128]{1,0:T(8,128)(2,1)S(1)} %fusion.156.refs_0_) | copy-start | bytes 995332
  2.7 38.8 %collective-permute-start.4 = (bf16[1296,128]{1,0:T(8,128)(2,1)S(1)}, bf16[1296,128]{1,0:T(8,128)(2,1)}, u32[]{:S(2)}, u32[]{:S(2)}) collective-permute-start(bf16[1296,128]{1,0:T(8,128)(2,1)S(1)} %fusion.156.refs_0_), channel_id=1, source_target_pairs={{0,4},{4,0},{8,12},{12,8},{16,20},{20,16},{24,28},{28,24},{1,5},{5... | collective-permute-start | bytes 995336 | tf_op jit(solution)/shard_map/ppermute | solution.py:64
  5.7 13.0 %collective-permute-start.3 = (bf16[1296,128]{1,0:T(8,128)(2,1)S(1)}, bf16[1296,128]{1,0:T(8,128)(2,1)}, u32[]{:S(2)}, u32[]{:S(2)}) collective-permute-start(bf16[1296,128]{1,0:T(8,128)(2,1)S(1)} %fusion.156.refs_0_), channel_id=1, source_target_pairs={{0,24},{4,28},{8,0},{12,4},{16,8},{20,12},{24,16},{28,20},{1,25},{... | collective-permute-start | bytes 995336 | tf_op jit(solution)/shard_map/ppermute | solution.py:63
  9.3 28.1 %collective-permute-start.2 = (bf16[1296,128]{1,0:T(8,128)(2,1)S(1)}, bf16[1296,128]{1,0:T(8,128)(2,1)}, u32[]{:S(2)}, u32[]{:S(2)}) collective-permute-start(bf16[1296,128]{1,0:T(8,128)(2,1)S(1)} %fusion.156.refs_0_), channel_id=1, source_target_pairs={{0,16},{4,20},{8,24},{12,28},{16,0},{20,4},{24,8},{28,12},{1,17},{... | collective-permute-start | bytes 995336 | tf_op jit(solution)/shard_map/ppermute | solution.py:63
  9.3 28.6 %collective-permute-start.1 = (bf16[1296,128]{1,0:T(8,128)(2,1)S(1)}, bf16[1296,128]{1,0:T(8,128)(2,1)}, u32[]{:S(2)}, u32[]{:S(2)}) collective-permute-start(bf16[1296,128]{1,0:T(8,128)(2,1)S(1)} %fusion.156.refs_0_), channel_id=1, source_target_pairs={{0,8},{4,12},{8,16},{12,20},{16,24},{20,28},{24,0},{28,4},{1,9},{5... | collective-permute-start | bytes 995336 | tf_op jit(solution)/shard_map/ppermute | solution.py:63
  11.6 31.8 %collective-permute-start.15 = (bf16[384,512]{0,1:T(8,128)(2,1)S(1)}, bf16[384,512]{0,1:T(8,128)(2,1)S(1)}, u32[]{:S(2)}, u32[]{:S(2)}) collective-permute-start(bf16[384,512]{0,1:T(8,128)(2,1)S(1)} %copy.271), channel_id=1, source_target_pairs={{1,0},{2,1},{3,2},{5,4},{6,5},{7,6},{9,8},{10,9},{11,10},{13,12},{... | collective-permute-start | bytes 1179656 | tf_op jit(solution)/shard_map/ppermute | solution.py:106
  18.8 255.0 %copy-start.16 = (pred[512,512]{0,1:T(8,128)(4,1)}, pred[512,512]{0,1:T(8,128)(4,1)S(1)}, u32[]{:S(2)}) copy-start(pred[512,512]{0,1:T(8,128)(4,1)S(1)} %fusion.55) | copy-start | bytes 786436
  18.8 24.7 %collective-permute-start = (bf16[588,512]{1,0:T(8,128)(2,1)S(1)}, bf16[588,512]{1,0:T(8,128)(2,1)S(1)}, u32[]{:S(2)}, u32[]{:S(2)}) collective-permute-start(bf16[588,512]{1,0:T(8,128)(2,1)S(1)} %copy-done.93), channel_id=1, source_target_pairs={{1,0},{2,1},{3,2},{5,4},{6,5},{7,6},{9,8},{10,9},{11,10},{13,12},{... | collective-permute-start | bytes 1806344 | tf_op jit(solution)/shard_map/ppermute | solution.py:106
  37.4 10.9 %collective-permute-start.7 = (bf16[1296,128]{1,0:T(8,128)(2,1)}, bf16[1296,128]{1,0:T(8,128)(2,1)S(1)}, u32[]{:S(2)}, u32[]{:S(2)}) collective-permute-start(bf16[1296,128]{1,0:T(8,128)(2,1)} %collective-permute-done.3.refs_3_), channel_id=1, source_target_pairs={{0,4},{4,0},{8,12},{12,8},{16,20},{20,16},{24,28},{28,24},{1,5},{5... | collective-permute-start | bytes 995336 | tf_op jit(solution)/shard_map/ppermute | solution.py:64
  38.0 17.5 %collective-permute-start.6 = (bf16[1296,128]{1,0:T(8,128)(2,1)}, bf16[1296,128]{1,0:T(8,128)(2,1)S(1)}, u32[]{:S(2)}, u32[]{:S(2)}) collective-permute-start(bf16[1296,128]{1,0:T(8,128)(2,1)} %collective-permute-done.2.refs_2_), channel_id=1, source_target_pairs={{0,4},{4,0},{8,12},{12,8},{16,20},{20,16},{24,28},{28,24},{1,5},{5... | collective-permute-start | bytes 995336 | tf_op jit(solution)/shard_map/ppermute | solution.py:64
  41.5 18.8 %collective-permute-start.5 = (bf16[1296,128]{1,0:T(8,128)(2,1)}, bf16[1296,128]{1,0:T(8,128)(2,1)}, u32[]{:S(2)}, u32[]{:S(2)}) collective-permute-start(bf16[1296,128]{1,0:T(8,128)(2,1)} %collective-permute-done.1.refs_1_), channel_id=1, source_target_pairs={{0,4},{4,0},{8,12},{12,8},{16,20},{20,16},{24,28},{28,24},{1,5},{5... | collective-permute-start | bytes 995336 | tf_op jit(solution)/shard_map/ppermute | solution.py:64
  43.5 234.6 %copy-start.4 = (bf16[512,512]{0,1:T(8,128)(2,1)}, bf16[512,512]{0,1:T(8,128)(2,1)S(1)}, u32[]{:S(2)}) copy-start(bf16[512,512]{0,1:T(8,128)(2,1)S(1)} %fusion.73) | copy-start | bytes 1572868
  148.5 47.0 %collective-permute-start.17 = (bf16[2048,128]{1,0:T(8,128)(2,1)}, bf16[2048,128]{1,0:T(8,128)(2,1)}, u32[]{:S(2)}, u32[]{:S(2)}) collective-permute-start(bf16[2048,128]{1,0:T(8,128)(2,1)} %get-tuple-element.108), channel_id=1, source_target_pairs={{0,2},{1,3},{2,0},{3,1},{4,6},{5,7},{6,4},{7,5},{8,10},{9,11},{10,... | collective-permute-start | bytes 1572872 | tf_op jit(solution)/shard_map/ppermute | solution.py:85
  150.0 49.6 %collective-permute-start.16 = (bf16[2048,128]{1,0:T(8,128)(2,1)}, bf16[2048,128]{1,0:T(8,128)(2,1)}, u32[]{:S(2)}, u32[]{:S(2)}) collective-permute-start(bf16[2048,128]{1,0:T(8,128)(2,1)} %get-tuple-element.108), channel_id=1, source_target_pairs={{0,1},{1,0},{2,3},{3,2},{4,5},{5,4},{6,7},{7,6},{8,9},{9,8},{10,11... | collective-permute-start | bytes 1572872 | tf_op jit(solution)/shard_map/ppermute | solution.py:86
  150.0 23.8 %collective-permute-start.23 = (bf16[2048,128]{1,0:T(8,128)(2,1)}, bf16[2048,128]{1,0:T(8,128)(2,1)}, u32[]{:S(2)}, u32[]{:S(2)}) collective-permute-start(bf16[2048,128]{1,0:T(8,128)(2,1)} %get-tuple-element.109), channel_id=1, source_target_pairs={{0,2},{1,3},{2,0},{3,1},{4,6},{5,7},{6,4},{7,5},{8,10},{9,11},{10,... | collective-permute-start | bytes 1572872 | tf_op jit(solution)/shard_map/ppermute | solution.py:85
  150.6 24.3 %collective-permute-start.22 = (bf16[2048,128]{1,0:T(8,128)(2,1)}, bf16[2048,128]{1,0:T(8,128)(2,1)}, u32[]{:S(2)}, u32[]{:S(2)}) collective-permute-start(bf16[2048,128]{1,0:T(8,128)(2,1)} %get-tuple-element.109), channel_id=1, source_target_pairs={{0,1},{1,0},{2,3},{3,2},{4,5},{5,4},{6,7},{7,6},{8,9},{9,8},{10,11... | collective-permute-start | bytes 1572872 | tf_op jit(solution)/shard_map/ppermute | solution.py:86
  166.3 18.6 %collective-permute-start.12 = (bf16[2048,128]{1,0:T(8,128)(2,1)S(1)}, bf16[2048,128]{1,0:T(8,128)(2,1)S(1)}, u32[]{:S(2)}, u32[]{:S(2)}) collective-permute-start(bf16[2048,128]{1,0:T(8,128)(2,1)S(1)} %copy-done.98), channel_id=1, source_target_pairs={{0,2},{1,3},{2,0},{3,1},{4,6},{5,7},{6,4},{7,5},{8,10},{9,11},{10,... | collective-permute-start | bytes 1572872 | tf_op jit(solution)/shard_map/ppermute | solution.py:85
  168.1 25.9 %copy-start.96 = (bf16[2048,128]{1,0:T(8,128)(2,1)S(1)}, bf16[2048,128]{1,0:T(8,128)(2,1)}, u32[]{:S(2)}) copy-start(bf16[2048,128]{1,0:T(8,128)(2,1)} %get-tuple-element.112) | copy-start | bytes 1572868
  173.8 21.7 %collective-permute-start.11 = (bf16[2048,128]{1,0:T(8,128)(2,1)S(1)}, bf16[2048,128]{1,0:T(8,128)(2,1)S(1)}, u32[]{:S(2)}, u32[]{:S(2)}) collective-permute-start(bf16[2048,128]{1,0:T(8,128)(2,1)S(1)} %copy-done.98), channel_id=1, source_target_pairs={{0,1},{1,0},{2,3},{3,2},{4,5},{5,4},{6,7},{7,6},{8,9},{9,8},{10,11... | collective-permute-start | bytes 1572872 | tf_op jit(solution)/shard_map/ppermute | solution.py:86
  174.9 19.1 %collective-permute-start.20 = (bf16[2048,128]{1,0:T(8,128)(2,1)S(1)}, bf16[2048,128]{1,0:T(8,128)(2,1)S(1)}, u32[]{:S(2)}, u32[]{:S(2)}) collective-permute-start(bf16[2048,128]{1,0:T(8,128)(2,1)S(1)} %copy-done.97), channel_id=1, source_target_pairs={{0,2},{1,3},{2,0},{3,1},{4,6},{5,7},{6,4},{7,5},{8,10},{9,11},{10,... | collective-permute-start | bytes 1572872 | tf_op jit(solution)/shard_map/ppermute | solution.py:85
  185.0 11.2 %collective-permute-start.19 = (bf16[2048,128]{1,0:T(8,128)(2,1)S(1)}, bf16[2048,128]{1,0:T(8,128)(2,1)S(1)}, u32[]{:S(2)}, u32[]{:S(2)}) collective-permute-start(bf16[2048,128]{1,0:T(8,128)(2,1)S(1)} %copy-done.97), channel_id=1, source_target_pairs={{0,1},{1,0},{2,3},{3,2},{4,5},{5,4},{6,7},{7,6},{8,9},{9,8},{10,11... | collective-permute-start | bytes 1572872 | tf_op jit(solution)/shard_map/ppermute | solution.py:86
  194.0 16.6 %collective-permute-start.9 = (bf16[2048,128]{1,0:T(8,128)(2,1)S(1)}, bf16[2048,128]{1,0:T(8,128)(2,1)S(1)}, u32[]{:S(2)}, u32[]{:S(2)}) collective-permute-start(bf16[2048,128]{1,0:T(8,128)(2,1)S(1)} %copy-done.96), channel_id=1, source_target_pairs={{0,2},{1,3},{2,0},{3,1},{4,6},{5,7},{6,4},{7,5},{8,10},{9,11},{10,... | collective-permute-start | bytes 1572872 | tf_op jit(solution)/shard_map/ppermute | solution.py:85
  195.5 17.9 %collective-permute-start.8 = (bf16[2048,128]{1,0:T(8,128)(2,1)S(1)}, bf16[2048,128]{1,0:T(8,128)(2,1)S(1)}, u32[]{:S(2)}, u32[]{:S(2)}) collective-permute-start(bf16[2048,128]{1,0:T(8,128)(2,1)S(1)} %copy-done.96), channel_id=1, source_target_pairs={{0,1},{1,0},{2,3},{3,2},{4,5},{5,4},{6,7},{7,6},{8,9},{9,8},{10,11... | collective-permute-start | bytes 1572872 | tf_op jit(solution)/shard_map/ppermute | solution.py:86
  195.6 23.4 %collective-permute-start.24 = (bf16[2048,128]{1,0:T(8,128)(2,1)}, bf16[2048,128]{1,0:T(8,128)(2,1)S(1)}, u32[]{:S(2)}, u32[]{:S(2)}) collective-permute-start(bf16[2048,128]{1,0:T(8,128)(2,1)} %collective-permute-done.23), channel_id=1, source_target_pairs={{0,1},{1,0},{2,3},{3,2},{4,5},{5,4},{6,7},{7,6},{8,9},{9,8},{10,11... | collective-permute-start | bytes 1572872 | tf_op jit(solution)/shard_map/ppermute | solution.py:87
  196.2 21.1 %collective-permute-start.18 = (bf16[2048,128]{1,0:T(8,128)(2,1)}, bf16[2048,128]{1,0:T(8,128)(2,1)S(1)}, u32[]{:S(2)}, u32[]{:S(2)}) collective-permute-start(bf16[2048,128]{1,0:T(8,128)(2,1)} %collective-permute-done.17), channel_id=1, source_target_pairs={{0,1},{1,0},{2,3},{3,2},{4,5},{5,4},{6,7},{7,6},{8,9},{9,8},{10,11... | collective-permute-start | bytes 1572872 | tf_op jit(solution)/shard_map/ppermute | solution.py:87
  199.7 146.2 %collective-permute-start.27 = (bf16[384,512]{0,1:T(8,128)(2,1)}, bf16[384,512]{0,1:T(8,128)(2,1)}, u32[]{:S(2)}, u32[]{:S(2)}) collective-permute-start(bf16[384,512]{0,1:T(8,128)(2,1)} %copy.305), channel_id=1, source_target_pairs={{1,0},{2,1},{3,2},{5,4},{6,5},{7,6},{9,8},{10,9},{11,10},{13,12},{... | collective-permute-start | bytes 1179656 | tf_op jit(solution)/shard_map/ppermute | solution.py:106
  210.6 177.1 %collective-permute-start.26 = (bf16[588,512]{1,0:T(8,128)(2,1)}, bf16[588,512]{1,0:T(8,128)(2,1)}, u32[]{:S(2)}, u32[]{:S(2)}) collective-permute-start(bf16[588,512]{1,0:T(8,128)(2,1)} %param.15), channel_id=1, source_target_pairs={{1,0},{2,1},{3,2},{5,4},{6,5},{7,6},{9,8},{10,9},{11,10},{13,12},{... | collective-permute-start | bytes 1806344 | tf_op jit(solution)/shard_map/ppermute | solution.py:106
  214.9 14.2 %collective-permute-start.21 = (bf16[2048,128]{1,0:T(8,128)(2,1)S(1)}, bf16[2048,128]{1,0:T(8,128)(2,1)S(1)}, u32[]{:S(2)}, u32[]{:S(2)}) collective-permute-start(bf16[2048,128]{1,0:T(8,128)(2,1)S(1)} %collective-permute-done.20), channel_id=1, source_target_pairs={{0,1},{1,0},{2,3},{3,2},{4,5},{5,4},{6,7},{7,6},{8,9},{9,8},{10,11... | collective-permute-start | bytes 1572872 | tf_op jit(solution)/shard_map/ppermute | solution.py:87
  217.2 16.8 %collective-permute-start.13 = (bf16[2048,128]{1,0:T(8,128)(2,1)S(1)}, bf16[2048,128]{1,0:T(8,128)(2,1)S(1)}, u32[]{:S(2)}, u32[]{:S(2)}) collective-permute-start(bf16[2048,128]{1,0:T(8,128)(2,1)S(1)} %collective-permute-done.12), channel_id=1, source_target_pairs={{0,1},{1,0},{2,3},{3,2},{4,5},{5,4},{6,7},{7,6},{8,9},{9,8},{10,11... | collective-permute-start | bytes 1572872 | tf_op jit(solution)/shard_map/ppermute | solution.py:87
  219.0 25.1 %collective-permute-start.10 = (bf16[2048,128]{1,0:T(8,128)(2,1)S(1)}, bf16[2048,128]{1,0:T(8,128)(2,1)S(1)}, u32[]{:S(2)}, u32[]{:S(2)}) collective-permute-start(bf16[2048,128]{1,0:T(8,128)(2,1)S(1)} %collective-permute-done.9), channel_id=1, source_target_pairs={{0,1},{1,0},{2,3},{3,2},{4,5},{5,4},{6,7},{7,6},{8,9},{9,8},{10,11... | collective-permute-start | bytes 1572872 | tf_op jit(solution)/shard_map/ppermute | solution.py:87
  256.2 22.7 %copy-start.6 = (bf16[784,512]{0,1:T(8,128)(2,1)}, bf16[784,512]{0,1:T(8,128)(2,1)S(1)}, u32[]{:S(2)}) copy-start(bf16[784,512]{0,1:T(8,128)(2,1)S(1)} %copy.254) | copy-start | bytes 2408452
  479.0 281.3 %collective-permute-start.14 = (bf16[588,512]{1,0:T(8,128)(2,1)}, bf16[588,512]{1,0:T(8,128)(2,1)}, u32[]{:S(2)}, u32[]{:S(2)}) collective-permute-start(bf16[588,512]{1,0:T(8,128)(2,1)} %get-tuple-element.161), channel_id=1, source_target_pairs={{0,1},{1,2},{2,3},{4,5},{5,6},{6,7},{8,9},{9,10},{10,11},{12,13},{... | collective-permute-start | bytes 1806344 | tf_op jit(solution)/shard_map/ppermute | solution.py:114
  504.2 84.1 %collective-permute-start.42 = (bf16[2048,128]{1,0:T(8,128)(2,1)}, bf16[2048,128]{1,0:T(8,128)(2,1)}, u32[]{:S(2)}, u32[]{:S(2)}) collective-permute-start(bf16[2048,128]{1,0:T(8,128)(2,1)} %bitcast.186), channel_id=1, source_target_pairs={{0,1},{1,0},{2,3},{3,2},{4,5},{5,4},{6,7},{7,6},{8,9},{9,8},{10,11... | collective-permute-start | bytes 1572872 | tf_op jit(solution)/shard_map/ppermute | solution.py:92
  506.2 75.8 %collective-permute-start.43 = (bf16[2048,128]{1,0:T(8,128)(2,1)}, bf16[2048,128]{1,0:T(8,128)(2,1)}, u32[]{:S(2)}, u32[]{:S(2)}) collective-permute-start(bf16[2048,128]{1,0:T(8,128)(2,1)} %bitcast.188), channel_id=1, source_target_pairs={{0,1},{1,0},{2,3},{3,2},{4,5},{5,4},{6,7},{7,6},{8,9},{9,8},{10,11... | collective-permute-start | bytes 1572872 | tf_op jit(solution)/shard_map/ppermute | solution.py:93
  534.3 42.7 %collective-permute-start.45 = (f32[10,512]{1,0:T(8,128)S(1)}, f32[10,512]{1,0:T(8,128)S(1)}, u32[]{:S(2)}, u32[]{:S(2)}) collective-permute-start(f32[10,512]{1,0:T(8,128)S(1)} %stack.381), channel_id=1, source_target_pairs={{0,1},{1,0},{2,3},{3,2},{4,5},{5,4},{6,7},{7,6},{8,9},{9,8},{10,11... | collective-permute-start | bytes 61448 | tf_op jit(solution)/shard_map/ppermute | solution.py:100
  551.5 51.8 %collective-permute-start.33 = (bf16[2048,128]{1,0:T(8,128)(2,1)}, bf16[2048,128]{1,0:T(8,128)(2,1)}, u32[]{:S(2)}, u32[]{:S(2)}) collective-permute-start(bf16[2048,128]{1,0:T(8,128)(2,1)} %bitcast.152), channel_id=1, source_target_pairs={{0,1},{1,0},{2,3},{3,2},{4,5},{5,4},{6,7},{7,6},{8,9},{9,8},{10,11... | collective-permute-start | bytes 1572872 | tf_op jit(solution)/shard_map/ppermute | solution.py:92
  577.1 4.0 collective-permute-start.46
  581.0 2.6 collective-permute-start.34
  582.0 3.0 collective-permute-start.40
  583.7 2.2 collective-permute-start.37
  585.0 2.1 collective-permute-start.31
  585.9 14.8 %collective-permute-start.44 = (bf16[2048,128]{1,0:T(8,128)(2,1)S(1)}, bf16[2048,128]{1,0:T(8,128)(2,1)S(1)}, u32[]{:S(2)}, u32[]{:S(2)}) collective-permute-start(bf16[2048,128]{1,0:T(8,128)(2,1)S(1)} %fusion.37), channel_id=1, source_target_pairs={{0,2},{1,3},{2,0},{3,1},{4,6},{5,7},{6,4},{7,5},{8,10},{9,11},{10,... | collective-permute-start | bytes 1572872 | tf_op jit(solution)/shard_map/ppermute | solution.py:95
  586.7 25.8 %copy-start.76 = (bf16[1,16,128,128]{3,2,1,0:T(8,128)(2,1)S(1)}, bf16[1,16,128,128]{3,2,1,0:T(8,128)(2,1)}, u32[]{:S(2)}) copy-start(bf16[1,16,128,128]{3,2,1,0:T(8,128)(2,1)} %get-tuple-element.125) | copy-start | bytes 1572868
  587.1 24.8 %collective-permute-start.35 = (bf16[2048,128]{1,0:T(8,128)(2,1)S(1)}, bf16[2048,128]{1,0:T(8,128)(2,1)S(1)}, u32[]{:S(2)}, u32[]{:S(2)}) collective-permute-start(bf16[2048,128]{1,0:T(8,128)(2,1)S(1)} %fusion.46), channel_id=1, source_target_pairs={{0,2},{1,3},{2,0},{3,1},{4,6},{5,7},{6,4},{7,5},{8,10},{9,11},{10,... | collective-permute-start | bytes 1572872 | tf_op jit(solution)/shard_map/ppermute | solution.py:95
  588.4 26.2 %collective-permute-start.39 = (bf16[2048,128]{1,0:T(8,128)(2,1)S(1)}, bf16[2048,128]{1,0:T(8,128)(2,1)S(1)}, u32[]{:S(2)}, u32[]{:S(2)}) collective-permute-start(bf16[2048,128]{1,0:T(8,128)(2,1)S(1)} %bitcast.671), channel_id=1, source_target_pairs={{0,1},{1,0},{2,3},{3,2},{4,5},{5,4},{6,7},{7,6},{8,9},{9,8},{10,11... | collective-permute-start | bytes 1572872 | tf_op jit(solution)/shard_map/ppermute | solution.py:92
  600.7 22.5 %collective-permute-start.41 = (bf16[2048,128]{1,0:T(8,128)(2,1)S(1)}, bf16[2048,128]{1,0:T(8,128)(2,1)S(1)}, u32[]{:S(2)}, u32[]{:S(2)}) collective-permute-start(bf16[2048,128]{1,0:T(8,128)(2,1)S(1)} %fusion.40), channel_id=1, source_target_pairs={{0,2},{1,3},{2,0},{3,1},{4,6},{5,7},{6,4},{7,5},{8,10},{9,11},{10,... | collective-permute-start | bytes 1572872 | tf_op jit(solution)/shard_map/ppermute | solution.py:95
  601.2 22.5 %copy-start.74 = (bf16[1,16,128,128]{3,2,1,0:T(8,128)(2,1)S(1)}, bf16[1,16,128,128]{3,2,1,0:T(8,128)(2,1)}, u32[]{:S(2)}) copy-start(bf16[1,16,128,128]{3,2,1,0:T(8,128)(2,1)} %get-tuple-element.117) | copy-start | bytes 1572868
  603.4 21.3 %collective-permute-start.36 = (bf16[2048,128]{1,0:T(8,128)(2,1)S(1)}, bf16[2048,128]{1,0:T(8,128)(2,1)S(1)}, u32[]{:S(2)}, u32[]{:S(2)}) collective-permute-start(bf16[2048,128]{1,0:T(8,128)(2,1)S(1)} %bitcast.673), channel_id=1, source_target_pairs={{0,1},{1,0},{2,3},{3,2},{4,5},{5,4},{6,7},{7,6},{8,9},{9,8},{10,11... | collective-permute-start | bytes 1572872 | tf_op jit(solution)/shard_map/ppermute | solution.py:92
  611.9 22.5 %collective-permute-start.38 = (bf16[2048,128]{1,0:T(8,128)(2,1)S(1)}, bf16[2048,128]{1,0:T(8,128)(2,1)S(1)}, u32[]{:S(2)}, u32[]{:S(2)}) collective-permute-start(bf16[2048,128]{1,0:T(8,128)(2,1)S(1)} %fusion.43), channel_id=1, source_target_pairs={{0,2},{1,3},{2,0},{3,1},{4,6},{5,7},{6,4},{7,5},{8,10},{9,11},{10,... | collective-permute-start | bytes 1572872 | tf_op jit(solution)/shard_map/ppermute | solution.py:95
  612.5 21.9 %copy-start.77 = (bf16[1,16,128,128]{3,2,1,0:T(8,128)(2,1)S(1)}, bf16[1,16,128,128]{3,2,1,0:T(8,128)(2,1)}, u32[]{:S(2)}) copy-start(bf16[1,16,128,128]{3,2,1,0:T(8,128)(2,1)} %get-tuple-element.121) | copy-start | bytes 1572868
  614.6 20.8 %collective-permute-start.30 = (bf16[2048,128]{1,0:T(8,128)(2,1)S(1)}, bf16[2048,128]{1,0:T(8,128)(2,1)S(1)}, u32[]{:S(2)}, u32[]{:S(2)}) collective-permute-start(bf16[2048,128]{1,0:T(8,128)(2,1)S(1)} %bitcast.674), channel_id=1, source_target_pairs={{0,1},{1,0},{2,3},{3,2},{4,5},{5,4},{6,7},{7,6},{8,9},{9,8},{10,11... | collective-permute-start | bytes 1572872 | tf_op jit(solution)/shard_map/ppermute | solution.py:92
  623.1 21.7 %collective-permute-start.32 = (bf16[2048,128]{1,0:T(8,128)(2,1)S(1)}, bf16[2048,128]{1,0:T(8,128)(2,1)S(1)}, u32[]{:S(2)}, u32[]{:S(2)}) collective-permute-start(bf16[2048,128]{1,0:T(8,128)(2,1)S(1)} %fusion.49), channel_id=1, source_target_pairs={{0,2},{1,3},{2,0},{3,1},{4,6},{5,7},{6,4},{7,5},{8,10},{9,11},{10,... | collective-permute-start | bytes 1572872 | tf_op jit(solution)/shard_map/ppermute | solution.py:95
  624.7 108.1 %collective-permute-start.29 = (bf16[384,512]{0,1:T(8,128)(2,1)}, bf16[384,512]{0,1:T(8,128)(2,1)}, u32[]{:S(2)}, u32[]{:S(2)}) collective-permute-start(bf16[384,512]{0,1:T(8,128)(2,1)} %get-tuple-element.163), channel_id=1, source_target_pairs={{0,1},{1,2},{2,3},{4,5},{5,6},{6,7},{8,9},{9,10},{10,11},{12,13},{... | collective-permute-start | bytes 1179656 | tf_op jit(solution)/shard_map/ppermute | solution.py:114
  730.2 25.0 %copy-start.11 = (bf16[10368,128]{1,0:T(8,128)(2,1)S(1)}, bf16[10368,128]{1,0:T(8,128)(2,1)}, u32[]{:S(2)}) copy-start(bf16[10368,128]{1,0:T(8,128)(2,1)} %deal_tiles.1) | copy-start | bytes 7962628
  730.2 10.7 %collective-permute-start.47 = (bf16[1296,128]{1,0:T(8,128)(2,1)S(1)}, bf16[1296,128]{1,0:T(8,128)(2,1)S(1)}, u32[]{:S(2)}, u32[]{:S(2)}) collective-permute-start(bf16[1296,128]{1,0:T(8,128)(2,1)S(1)} %get-tuple-element.93), channel_id=1, source_target_pairs={{0,4},{4,0},{8,12},{12,8},{16,20},{20,16},{24,28},{28,24},{1,5},{5... | collective-permute-start | bytes 995336 | tf_op jit(solution)/shard_map/ppermute | solution.py:75
  730.7 17.3 %collective-permute-start.51 = (bf16[1296,128]{1,0:T(8,128)(2,1)S(1)}, bf16[1296,128]{1,0:T(8,128)(2,1)S(1)}, u32[]{:S(2)}, u32[]{:S(2)}) collective-permute-start(bf16[1296,128]{1,0:T(8,128)(2,1)S(1)} %get-tuple-element.95), channel_id=1, source_target_pairs={{0,4},{4,0},{8,12},{12,8},{16,20},{20,16},{24,28},{28,24},{1,5},{5... | collective-permute-start | bytes 995336 | tf_op jit(solution)/shard_map/ppermute | solution.py:75
  732.2 22.9 %collective-permute-start.49 = (bf16[1296,128]{1,0:T(8,128)(2,1)S(1)}, bf16[1296,128]{1,0:T(8,128)(2,1)S(1)}, u32[]{:S(2)}, u32[]{:S(2)}) collective-permute-start(bf16[1296,128]{1,0:T(8,128)(2,1)S(1)} %get-tuple-element.96), channel_id=1, source_target_pairs={{0,4},{4,0},{8,12},{12,8},{16,20},{20,16},{24,28},{28,24},{1,5},{5... | collective-permute-start | bytes 995336 | tf_op jit(solution)/shard_map/ppermute | solution.py:75
  732.8 24.3 %collective-permute-start.25 = (bf16[384,512]{0,1:T(8,128)(2,1)S(1)}, bf16[384,512]{0,1:T(8,128)(2,1)S(1)}, u32[]{:S(2)}, u32[]{:S(2)}) collective-permute-start(bf16[384,512]{0,1:T(8,128)(2,1)S(1)} %get-tuple-element.165), channel_id=1, source_target_pairs={{0,1},{1,2},{2,3},{4,5},{5,6},{6,7},{8,9},{9,10},{10,11},{12,13},{... | collective-permute-start | bytes 1179656 | tf_op jit(solution)/shard_map/ppermute | solution.py:114
  740.9 27.2 %collective-permute-start.28 = (bf16[588,512]{1,0:T(8,128)(2,1)}, bf16[588,512]{1,0:T(8,128)(2,1)}, u32[]{:S(2)}, u32[]{:S(2)}) collective-permute-start(bf16[588,512]{1,0:T(8,128)(2,1)} %get-tuple-element.159), channel_id=1, source_target_pairs={{0,1},{1,2},{2,3},{4,5},{5,6},{6,7},{8,9},{9,10},{10,11},{12,13},{... | collective-permute-start | bytes 1806344 | tf_op jit(solution)/shard_map/ppermute | solution.py:114
  748.1 22.8 %collective-permute-start.53 = (bf16[1296,128]{1,0:T(8,128)(2,1)}, bf16[1296,128]{1,0:T(8,128)(2,1)}, u32[]{:S(2)}, u32[]{:S(2)}) collective-permute-start(bf16[1296,128]{1,0:T(8,128)(2,1)} %get-tuple-element.94), channel_id=1, source_target_pairs={{0,4},{4,0},{8,12},{12,8},{16,20},{20,16},{24,28},{28,24},{1,5},{5... | collective-permute-start | bytes 995336 | tf_op jit(solution)/shard_map/ppermute | solution.py:75
  756.3 14.6 %collective-permute-start.48 = (bf16[1296,128]{1,0:T(8,128)(2,1)}, bf16[1296,128]{1,0:T(8,128)(2,1)}, u32[]{:S(2)}, u32[]{:S(2)}) collective-permute-start(bf16[1296,128]{1,0:T(8,128)(2,1)} %get-tuple-element.90), channel_id=1, source_target_pairs={{0,8},{4,12},{8,16},{12,20},{16,24},{20,28},{24,0},{28,4},{1,9},{5... | collective-permute-start | bytes 995336 | tf_op jit(solution)/shard_map/ppermute | solution.py:78
  757.1 14.9 %collective-permute-start.52 = (bf16[1296,128]{1,0:T(8,128)(2,1)}, bf16[1296,128]{1,0:T(8,128)(2,1)}, u32[]{:S(2)}, u32[]{:S(2)}) collective-permute-start(bf16[1296,128]{1,0:T(8,128)(2,1)} %get-tuple-element.91), channel_id=1, source_target_pairs={{0,24},{4,28},{8,0},{12,4},{16,8},{20,12},{24,16},{28,20},{1,25},{... | collective-permute-start | bytes 995336 | tf_op jit(solution)/shard_map/ppermute | solution.py:78
  760.3 24.5 %collective-permute-start.50 = (bf16[1296,128]{1,0:T(8,128)(2,1)}, bf16[1296,128]{1,0:T(8,128)(2,1)}, u32[]{:S(2)}, u32[]{:S(2)}) collective-permute-start(bf16[1296,128]{1,0:T(8,128)(2,1)} %get-tuple-element.92), channel_id=1, source_target_pairs={{0,16},{4,20},{8,24},{12,28},{16,0},{20,4},{24,8},{28,12},{1,17},{... | collective-permute-start | bytes 995336 | tf_op jit(solution)/shard_map/ppermute | solution.py:78
  (145 other events, 648.6 us)

commit v2 on v1

v2 whole, which is shorter than its diff:
```python
import jax
import jax.numpy as jnp
from jax import lax
from jax.experimental import pallas as pl
from jax.experimental.pallas import tpu as pltpu
from jax.sharding import PartitionSpec as P

D = 512
HEADS = 8
HEAD_DIM = 64
FF = 1024
TILE = 128
CHUNK = 16
CHUNKS = 5

NORM_EPSILON = 1e-05
MATRIX_RATE = 0.5
VECTOR_RATE = 0.2
STAT_DECAY = 0.5
MASKED_SCORE = -1e30

F32 = jnp.float32
BF16 = jnp.bfloat16
ANY = pl.BlockSpec(memory_space=pl.ANY)
VM = pl.BlockSpec(memory_space=pltpu.VMEM)
SM = pl.BlockSpec(memory_space=pltpu.SMEM)


def core_pairs():
    return [(i, i ^ 1) for i in range(4)]


def chip_pairs():
    return [(i, i ^ 2) for i in range(4)]


def y_pairs():
    return [(i, i ^ 1) for i in range(8)]


def z_shift(step):
    return [(2 * z + y, 2 * ((z + step) % 4) + y) for z in range(4) for y in range(2)]


def relative_rank(position, size):
    me = lax.axis_index("dp")
    if size != 8:
        return jnp.int32(position)
    swapped, step = divmod(position, 4)
    return 2 * lax.rem(me // 2 - step + 4, 4) + lax.rem(me + swapped, 2)


def target_rank(position, size):
    me = lax.axis_index("dp")
    if size != 8:
        return jnp.int32(position)
    swapped, step = divmod(position, 4)
    return 2 * lax.rem(me // 2 + step, 4) + lax.rem(me + swapped, 2)


def gather_pieces(piece, size):
    if size != 8:
        return list(lax.all_gather(piece, "dp", axis=0, tiled=False))
    column = [piece] + [lax.ppermute(piece, "dp", z_shift(step)) for step in (1, 2, 3)]
    return column + [lax.ppermute(part, "dp", y_pairs()) for part in column]


def sum_pieces(pieces, size):
    if size != 8:
        whole = lax.psum_scatter(
            jnp.stack(pieces).astype(F32), "dp", scatter_dimension=0, tiled=False
        )
        return whole
    column = []
    for step in (1, 2, 3, 0):
        other = lax.ppermute(pieces[4 + step], "dp", y_pairs())
        both = pieces[step].astype(F32) + other.astype(F32)
        if step:
            column.append(lax.ppermute(both.astype(BF16), "dp", z_shift(step)).astype(F32))
        else:
            column.append(both)
    return (column[0] + column[1]) + (column[2] + column[3])


def gather_group(part):
    far = lax.ppermute(part, "tensor", chip_pairs())
    near = lax.ppermute(part, "tensor", core_pairs())
    far_near = lax.ppermute(far, "tensor", core_pairs())
    return (part, near, far, far_near)


def sum_group(parts):
    near = lax.ppermute(parts[1], "tensor", core_pairs())
    far_near = lax.ppermute(parts[3], "tensor", core_pairs())
    far = (parts[2].astype(F32) + far_near.astype(F32)).astype(BF16)
    far = lax.ppermute(far, "tensor", chip_pairs())
    return (parts[0].astype(F32) + near.astype(F32) + far.astype(F32)).astype(BF16)


def sum_over_group(value):
    value = value + lax.ppermute(value, "tensor", core_pairs())
    return value + lax.ppermute(value, "tensor", chip_pairs())


def pull_rows(rows, length):
    shards = lax.axis_size("tensor")
    later = lax.ppermute(rows, "tensor", [(i + 1, i) for i in range(shards - 1)])
    start = lax.axis_index("tensor") * (length - rows.shape[0])
    return lax.dynamic_slice_in_dim(jnp.concatenate([rows, later], axis=0), start, length, axis=0)


def push_rows(item, count):
    shards = lax.axis_size("tensor")
    length = item.shape[0]
    earlier = lax.ppermute(
        item[length - count :], "tensor", [(i, i + 1) for i in range(shards - 1)]
    )
    start = count - lax.axis_index("tensor") * (length - count)
    return lax.dynamic_slice_in_dim(
        jnp.concatenate([earlier, item[:count]], axis=0), start, count, axis=0
    )


def order_tiles(pieces, block_ids, slots):
    total = CHUNK * CHUNKS

    def kernel(ids, *refs):
        sources, out = refs[:-1], refs[-1]
        for p, source in enumerate(sources):
            for j in range(slots):
                block = ids[0, p * slots + j]

                @pl.when(block < total)
                def _(source=source, j=j, block=block):
                    out[pl.ds(pl.multiple_of(block * TILE, TILE), TILE), :] = source[
                        j * TILE : (j + 1) * TILE, :
                    ]

    return pl.pallas_call(
        kernel,
        out_shape=jax.ShapeDtypeStruct((total * TILE, TILE), BF16),
        in_specs=[SM] + [VM] * len(pieces),
        out_specs=VM,
        compiler_params=pltpu.CompilerParams(vmem_limit_bytes=40 * 2**20),
        name="order_tiles",
    )(block_ids, *pieces)


def deal_tiles(chunks, vector_rows, block_ids, slots):
    count = vector_rows.shape[0]
    extra = vector_rows.shape[1]
    total = CHUNK * CHUNKS
    rows = slots * TILE + extra

    def kernel(ids, *refs):
        sources, more = refs[:CHUNKS], refs[CHUNKS]
        outs, held = refs[CHUNKS + 1 : -1], refs[-1]
        for c, source in enumerate(sources):
            held[c * CHUNK * TILE : (c + 1) * CHUNK * TILE, :] = source[...]
        held[total * TILE :, :] = jnp.zeros((TILE, TILE), BF16)
        for p, out in enumerate(outs):
            for j in range(slots):
                block = jnp.minimum(ids[0, p * slots + j], total)
                out[j * TILE : (j + 1) * TILE, :] = held[
                    pl.ds(pl.multiple_of(block * TILE, TILE), TILE), :
                ]
            out[slots * TILE :, :] = more[p]

    return pl.pallas_call(
        kernel,
        out_shape=[jax.ShapeDtypeStruct((rows, TILE), BF16)] * count,
        in_specs=[SM] + [VM] * (CHUNKS + 1),
        out_specs=[VM] * count,
        scratch_shapes=[pltpu.VMEM(((total + 1) * TILE, TILE), BF16)],
        compiler_params=pltpu.CompilerParams(vmem_limit_bytes=40 * 2**20),
        name="deal_tiles",
    )(block_ids, *chunks, vector_rows)


LOG2E = 1.4426950408889634
SCORE_SCALE = HEAD_DIM ** (-0.5)
SCORE_LOG2 = SCORE_SCALE * LOG2E
PAIRS = HEADS // 2


def matmul(former, latter):
    return jnp.dot(former, latter, preferred_element_type=F32)


def times_transpose(former, latter):
    return lax.dot_general(former, latter, (((1,), (1,)), ((), ())), preferred_element_type=F32)


def transpose_times(former, latter):
    return lax.dot_general(former, latter, (((0,), (0,)), ((), ())), preferred_element_type=F32)


def low(value):
    return value.astype(BF16)


def tile_at(part, index):
    return part[index * TILE : (index + 1) * TILE, :]


def column_matrix(parts, first, count, column):
    return jnp.concatenate(
        [
            jnp.concatenate([tile_at(p, first + a * count + column) for p in parts], axis=1)
            for a in range(4)
        ],
        axis=0,
    )


def row_matrix(parts, first, group):
    return jnp.concatenate(
        [
            jnp.concatenate([tile_at(p, first + 4 * group + b) for b in range(4)], axis=1)
            for p in parts
        ],
        axis=0,
    )


def store_columns(parts, gradient, first, count, column):
    for r, part in enumerate(parts):
        for a in range(4):
            at = (first + a * count + column) * TILE
            part[at : at + TILE, :] = low(
                gradient[a * TILE : (a + 1) * TILE, r * TILE : (r + 1) * TILE]
            )


def store_rows(parts, gradient, first, group):
    for r, part in enumerate(parts):
        for b in range(4):
            at = (first + 4 * group + b) * TILE
            part[at : at + TILE, :] = low(
                gradient[r * TILE : (r + 1) * TILE, b * TILE : (b + 1) * TILE]
            )


def spans(count):
    half = (count // 2 + 15) // 16 * 16
    return [(0, half), (half, count)]


def norm_rows(value):
    mean = jnp.mean(value, axis=-1, keepdims=True)
    centered = value - mean
    scale = lax.rsqrt(jnp.mean(centered * centered, axis=-1, keepdims=True) + NORM_EPSILON)
    return centered * scale, scale


def norm_back(gradient, normed, scale, gain):
    scaled = gradient * gain
    return scale * (
        scaled
        - jnp.mean(scaled, axis=-1, keepdims=True)
        - normed * jnp.mean(scaled * normed, axis=-1, keepdims=True)
    )


def gate_both(value):
    size = jnp.abs(value) * (0.5**0.5)
    turn = 1.0 / (1.0 + 0.3275911 * size)
    bell = jnp.exp2(value * value * (-0.5 * LOG2E))
    series = turn * (
        0.254829592
        + turn * (-0.284496736 + turn * (1.421413741 + turn * (-1.453152027 + turn * 1.061405429)))
    )
    tail = 0.5 * series * bell
    phi = jnp.where(value < 0, tail, 1.0 - tail)
    return value * phi, phi + value * bell * 0.3989422804014327


def half_mask(which):
    lane = lax.broadcasted_iota(jnp.int32, (1, TILE), 1)
    return (lane < HEAD_DIM) if which == 0 else (lane >= HEAD_DIM)


def attend_pairs(q_ref, k_ref, v_ref, o_ref, stat_ref, bias):
    count = q_ref.shape[0]
    keys = k_ref.shape[0]
    ones = jnp.ones((keys, TILE), BF16)
    lane = lax.broadcasted_iota(jnp.int32, (count, TILE), 1)
    stats = jnp.zeros((count, TILE), F32)
    for pair in range(PAIRS):
        cut = slice(pair * TILE, (pair + 1) * TILE)
        queries, key_rows = q_ref[:, cut], k_ref[:, cut]
        values = jnp.concatenate([v_ref[:, cut], ones], axis=1)
        mixed = []
        for which in range(2):
            masked = jnp.where(half_mask(which), queries, jnp.zeros_like(queries))
            scores = times_transpose(masked, key_rows) * SCORE_LOG2
            if bias is not None:
                scores = scores + bias
            top = jnp.max(scores, axis=1, keepdims=True)
            weights = low(jnp.exp2(scores - top))
            both = matmul(weights, values)
            total = both[:, TILE:]
            mixed.append(both[:, :TILE] / total)
            stats = jnp.where(lane == 2 * pair + which, top + jnp.log2(total), stats)
        o_ref[:, cut] = low(jnp.where(half_mask(0), mixed[0], mixed[1]))
    stat_ref[...] = stats.T


def attend_pairs_back(q_ref, k_ref, v_ref, stat_ref, do_ref, delta, dq_ref, dk_ref, dv_ref, kt_ref, dqt_ref, bias):
    kt_ref[...] = k_ref[...].T
    for pair in range(PAIRS):
        cut = slice(pair * TILE, (pair + 1) * TILE)
        queries, key_rows, value_rows, incoming = q_ref[:, cut], k_ref[:, cut], v_ref[:, cut], do_ref[:, cut]
        dk = dv = None
        for which in range(2):
            head = 2 * pair + which
            mask = half_mask(which)
            q_one = jnp.where(mask, queries, jnp.zeros_like(queries))
            do_one = jnp.where(mask, incoming, jnp.zeros_like(incoming))
            scores = times_transpose(key_rows, q_one) * SCORE_LOG2
            if bias is not None:
                scores = scores + bias
            weights = jnp.exp2(scores - stat_ref[head : head + 1, :])
            d_weights = times_transpose(value_rows, do_one)
            d_scores = low(weights * (d_weights - delta[head : head + 1, :]))
            dv_one = matmul(low(weights), do_one)
            dk_one = matmul(d_scores, q_one)
            dv = dv_one if dv is None else dv + dv_one
            dk = dk_one if dk is None else dk + dk_one
            rows = slice(head * HEAD_DIM, (head + 1) * HEAD_DIM)
            dqt_ref[rows, :] = low(matmul(kt_ref[rows, :], d_scores) * SCORE_SCALE)
        dk_ref[:, cut] = low(dk * SCORE_SCALE)
        dv_ref[:, cut] = low(dv)
    dq_ref[...] = dqt_ref[...].T


def row_products(incoming, mixed):
    product = incoming * mixed
    first = low(product)
    rest = low(product - first.astype(F32))
    lane = lax.broadcasted_iota(jnp.int32, (TILE, D), 1) // HEAD_DIM
    row = lax.broadcasted_iota(jnp.int32, (TILE, D), 0)
    pick = (lane == row).astype(BF16)
    return times_transpose(pick, first) + times_transpose(pick, rest)


def struct(shape, dtype):
    return jax.ShapeDtypeStruct(shape, dtype)


def call(kernel, name, outs, scratch, *args, flops=0):
    return pl.pallas_call(
        kernel,
        out_shape=outs,
        in_specs=[pl.BlockSpec(memory_space=pltpu.SMEM) if a.dtype == jnp.int32 else VM for a in args],
        out_specs=[VM] * len(outs),
        scratch_shapes=scratch,
        compiler_params=pltpu.CompilerParams(vmem_limit_bytes=60 * 2**20),
        cost_estimate=pl.CostEstimate(flops=flops, bytes_accessed=4000000, transcendentals=0),
        name=name,
    )(*args)


def part_outs():
    return [struct((CHUNK * TILE, TILE), BF16)] * 4


def causal_bias(count, live, queries_on_rows):
    a = lax.broadcasted_iota(jnp.int32, (count, count), 0)
    b = lax.broadcasted_iota(jnp.int32, (count, count), 1)
    query, key = (a, b) if queries_on_rows else (b, a)
    return jnp.where((key <= query) & (key < live), 0.0, MASKED_SCORE)


def self_forward(x, parts, vectors, norm, live=None):
    rows = x.shape[0]

    def kernel(*refs):
        if live is not None:
            live_ref, *refs = refs
        x_ref, p0, p1, p2, p3, g_ref, first_ref, hat_ref, scale_ref, q_ref, k_ref, v_ref, o_ref, stat_ref = refs
        ps = (p0, p1, p2, p3)
        tokens = x_ref[...]
        for column, ref in enumerate((q_ref, k_ref, v_ref)):
            ref[...] = low(matmul(tokens, column_matrix(ps, 0, 3, column)))
        bias = None if live is None else causal_bias(rows, live_ref[0, 0], True)
        attend_pairs(q_ref, k_ref, v_ref, o_ref, stat_ref, bias)
        hat, scale = norm_rows(
            tokens.astype(F32) + matmul(o_ref[...], row_matrix(ps, 12, 0))
        )
        first_ref[...] = hat * g_ref[2 * norm : 2 * norm + 1, :] + g_ref[2 * norm + 1 : 2 * norm + 2, :]
        hat_ref[...] = low(hat)
        scale_ref[...] = scale

    outs = [struct((rows, D), F32), struct((rows, D), BF16), struct((rows, 1), F32)]
    outs += [struct((rows, D), BF16)] * 4 + [struct((TILE, rows), F32)]
    args = ([] if live is None else [live]) + [x, *parts, vectors]
    return call(kernel, f"self_forward_{norm}", outs, [], *args, flops=10**10)


def ffn_rows(rows_in, w1, w2):
    hid, slope, out = [], [], []
    for a, b in spans(rows_in.shape[0]):
        value, derivative = gate_both(matmul(rows_in[a:b], w1))
        value = low(value)
        hid.append(value)
        slope.append(low(derivative))
        out.append(matmul(value, w2))
    return hid, slope, out


def ffn_weights(ps):
    w1 = jnp.concatenate([column_matrix(ps, 0, 2, c) for c in range(2)], axis=1)
    w2 = jnp.concatenate([row_matrix(ps, 8, c) for c in range(2)], axis=0)
    return w1, w2


def unpack_hidden():
    pass


def ffn_forward(first, parts, vectors, norm):
    rows = first.shape[0]

    def kernel(f_ref, p0, p1, p2, p3, g_ref, enc_ref, hat_ref, scale_ref, hid_ref, slope_ref):
        w1, w2 = ffn_weights((p0, p1, p2, p3))
        for a, b in spans(rows):
            first_rows = f_ref[a:b, :]
            value, slope = gate_both(matmul(low(first_rows), w1))
            value = low(value)
            hid_ref[a:b, :] = value
            slope_ref[a:b, :] = low(slope)
            hat, scale = norm_rows(first_rows + matmul(value, w2))
            enc_ref[a:b, :] = low(hat * g_ref[2 * norm : 2 * norm + 1, :] + g_ref[2 * norm + 1 : 2 * norm + 2, :])
            hat_ref[a:b, :] = low(hat)
            scale_ref[a:b, :] = scale

    outs = [struct((rows, D), BF16), struct((rows, D), BF16), struct((rows, 1), F32)]
    outs += [struct((rows, FF), BF16)] * 2
    return call(kernel, f"ffn_forward_{norm}", outs, [], first, *parts, vectors, flops=3 * 10**9)


def cross_forward(second, encoded, parts, vectors):
    rows, keys = second.shape[0], encoded.shape[0]

    def kernel(s_ref, e_ref, p0, p1, p2, p3, g_ref, third_ref, hat_ref, scale_ref, q_ref, k_ref, v_ref, o_ref, stat_ref):
        ps = (p0, p1, p2, p3)
        q_ref[...] = low(matmul(low(s_ref[...]), column_matrix(ps, 0, 1, 0)))
        k_ref[...] = low(matmul(e_ref[...], column_matrix(ps, 4, 2, 0)))
        v_ref[...] = low(matmul(e_ref[...], column_matrix(ps, 4, 2, 1)))
        attend_pairs(q_ref, k_ref, v_ref, o_ref, stat_ref, None)
        hat, scale = norm_rows(s_ref[...] + matmul(o_ref[...], row_matrix(ps, 12, 0)))
        third_ref[...] = hat * g_ref[6:7, :] + g_ref[7:8, :]
        hat_ref[...] = low(hat)
        scale_ref[...] = scale

    outs = [struct((rows, D), F32), struct((rows, D), BF16), struct((rows, 1), F32)]
    outs += [struct((rows, D), BF16), struct((keys, D), BF16), struct((keys, D), BF16)]
    outs += [struct((rows, D), BF16), struct((TILE, rows), F32)]
    return call(kernel, "cross_forward", outs, [], second, encoded, *parts, vectors, flops=5 * 10**9)


def store_norm(ref, gradient, hat):
    ref[0:1, :] = jnp.sum(gradient * hat, axis=0, keepdims=True)
    ref[1:2, :] = jnp.sum(gradient, axis=0, keepdims=True)


def ffn_both(third, cotangent, live, parts, vectors):
    rows = third.shape[0]

    def kernel(live_ref, t_ref, c_ref, p0, p1, p2, p3, g_ref, dec_ref, back_ref, n_ref, d0, d1, d2, d3, hid_ref, dh_ref, db_ref):
        w1, w2 = ffn_weights((p0, p1, p2, p3))
        grads = (d0, d1, d2, d3)
        gain = g_ref[8:9, :]
        for part, (a, b) in enumerate(spans(rows)):
            third_rows = t_ref[a:b, :]
            value, slope = gate_both(matmul(low(third_rows), w1))
            value = low(value)
            hid_ref[a:b, :] = value
            hat, scale = norm_rows(third_rows + matmul(value, w2))
            dec_ref[a:b, :] = low(hat * gain + g_ref[9:10, :])
            row = lax.broadcasted_iota(jnp.int32, (b - a, 1), 0) + a
            incoming = jnp.where(row < live_ref[0, 0], c_ref[a:b, :].astype(F32), 0.0)
            if part == 0:
                n_ref[...] = jnp.zeros_like(n_ref)
            n_ref[0:1, :] += jnp.sum(incoming * hat, axis=0, keepdims=True)
            n_ref[1:2, :] += jnp.sum(incoming, axis=0, keepdims=True)
            back = norm_back(incoming, hat, scale, gain)
            back_low = low(back)
            db_ref[a:b, :] = back_low
            dh = low(slope * times_transpose(back_low, w2))
            dh_ref[a:b, :] = dh
            back_ref[a:b, :] = back + times_transpose(dh, w1)
        third_low = low(t_ref[...])
        for c in range(2):
            store_columns(grads, transpose_times(third_low, dh_ref[:, c * D : (c + 1) * D]), 0, 2, c)
            store_rows(grads, transpose_times(hid_ref[:, c * D : (c + 1) * D], db_ref[...]), 8, c)

    outs = [struct((rows, D), BF16), struct((rows, D), F32), struct((8, D), F32)] + part_outs()
    scratch = [pltpu.VMEM((rows, FF), BF16), pltpu.VMEM((rows, FF), BF16), pltpu.VMEM((rows, D), BF16)]
    return call(kernel, "ffn_both", outs, scratch, live, third, cotangent, *parts, vectors, flops=10**10)


def ffn_backward(cotangent, more, hat, scale, first, hid, slope, parts, vectors, norm):
    rows = first.shape[0]

    def kernel(c_ref, m_ref, h_ref, s_ref, f_ref, hid_ref, slope_ref, p0, p1, p2, p3, g_ref, back_ref, n_ref, d0, d1, d2, d3, dh_ref, db_ref):
        w1, w2 = ffn_weights((p0, p1, p2, p3))
        grads = (d0, d1, d2, d3)
        n_ref[...] = jnp.zeros_like(n_ref)
        for a, b in spans(rows):
            incoming = c_ref[a:b, :].astype(F32) + m_ref[a:b, :]
            hat_rows = h_ref[a:b, :].astype(F32)
            n_ref[0:1, :] += jnp.sum(incoming * hat_rows, axis=0, keepdims=True)
            n_ref[1:2, :] += jnp.sum(incoming, axis=0, keepdims=True)
            back = norm_back(incoming, hat_rows, s_ref[a:b, :], g_ref[2 * norm : 2 * norm + 1, :])
            back_low = low(back)
            db_ref[a:b, :] = back_low
            dh = low(slope_ref[a:b, :].astype(F32) * times_transpose(back_low, w2))
            dh_ref[a:b, :] = dh
            back_ref[a:b, :] = back + times_transpose(dh, w1)
        first_low = low(f_ref[...])
        for c in range(2):
            store_columns(grads, transpose_times(first_low, dh_ref[:, c * D : (c + 1) * D]), 0, 2, c)
            store_rows(grads, transpose_times(hid_ref[:, c * D : (c + 1) * D], db_ref[...]), 8, c)

    outs = [struct((rows, D), F32), struct((8, D), F32)] + part_outs()
    scratch = [pltpu.VMEM((rows, FF), BF16), pltpu.VMEM((rows, D), BF16)]
    return call(kernel, f"ffn_backward_{norm}", outs, scratch, cotangent, more, hat, scale, first, hid, slope, *parts, vectors, flops=10**10)


def self_backward(back, hat, scale, x, q, k, v, o, stats, parts, vectors, norm, live=None):
    rows = x.shape[0]

    def kernel(*refs):
        if live is not None:
            live_ref, *refs = refs
        (b_ref, h_ref, s_ref, x_ref, q_ref, k_ref, v_ref, o_ref, stat_ref, p0, p1, p2, p3, g_ref,
         dx_ref, n_ref, d0, d1, d2, d3, do_ref, dq_ref, dk_ref, dv_ref, kt_ref, dqt_ref) = refs
        ps, grads = (p0, p1, p2, p3), (d0, d1, d2, d3)
        incoming = b_ref[...]
        hat_rows = h_ref[...].astype(F32)
        n_ref[...] = jnp.zeros_like(n_ref)
        store_norm(n_ref, incoming, hat_rows)
        branch = norm_back(incoming, hat_rows, s_ref[...], g_ref[2 * norm : 2 * norm + 1, :])
        branch_low = low(branch)
        dx_ref[...] = branch
        do = low(times_transpose(branch_low, row_matrix(ps, 12, 0)))
        do_ref[...] = do
        store_rows(grads, transpose_times(o_ref[...], branch_low), 12, 0)
        delta = row_products(do.astype(F32), o_ref[...].astype(F32))
        bias = None if live is None else causal_bias(rows, live_ref[0, 0], False)
        attend_pairs_back(q_ref, k_ref, v_ref, stat_ref, do_ref, delta, dq_ref, dk_ref, dv_ref, kt_ref, dqt_ref, bias)
        xt = x_ref[...].T
        total = dx_ref[...]
        for column, ref in enumerate((dq_ref, dk_ref, dv_ref)):
            total = total + times_transpose(ref[...], column_matrix(ps, 0, 3, column))
            store_columns(grads, matmul(xt, ref[...]), 0, 3, column)
        dx_ref[...] = total

    outs = [struct((rows, D), F32), struct((8, D), F32)] + part_outs()
    scratch = [pltpu.VMEM((rows, D), BF16)] * 4 + [pltpu.VMEM((D, rows), BF16)] * 2
    args = ([] if live is None else [live]) + [back, hat, scale, x, q, k, v, o, stats, *parts, vectors]
    return call(kernel, f"self_backward_{norm}", outs, scratch, *args, flops=2 * 10**10)


def cross_backward(back, hat, scale, second, encoded, q, k, v, o, stats, parts, vectors):
    rows, keys = second.shape[0], encoded.shape[0]

    def kernel(b_ref, h_ref, s_ref, x_ref, e_ref, q_ref, k_ref, v_ref, o_ref, stat_ref, p0, p1, p2, p3, g_ref,
               dx_ref, de_ref, n_ref, d0, d1, d2, d3, do_ref, dq_ref, dk_ref, dv_ref, kt_ref, dqt_ref):
        ps, grads = (p0, p1, p2, p3), (d0, d1, d2, d3)
        incoming = b_ref[...]
        hat_rows = h_ref[...].astype(F32)
        n_ref[...] = jnp.zeros_like(n_ref)
        store_norm(n_ref, incoming, hat_rows)
        branch = norm_back(incoming, hat_rows, s_ref[...], g_ref[6:7, :])
        branch_low = low(branch)
        do = low(times_transpose(branch_low, row_matrix(ps, 12, 0)))
        do_ref[...] = do
        store_rows(grads, transpose_times(o_ref[...], branch_low), 12, 0)
        delta = row_products(do.astype(F32), o_ref[...].astype(F32))
        attend_pairs_back(q_ref, k_ref, v_ref, stat_ref, do_ref, delta, dq_ref, dk_ref, dv_ref, kt_ref, dqt_ref, None)
        dx_ref[...] = branch + times_transpose(dq_ref[...], column_matrix(ps, 0, 1, 0))
        de_ref[...] = times_transpose(dk_ref[...], column_matrix(ps, 4, 2, 0)) + times_transpose(
            dv_ref[...], column_matrix(ps, 4, 2, 1)
        )
        store_columns(grads, transpose_times(low(x_ref[...]), dq_ref[...]), 0, 1, 0)
        et = e_ref[...].T
        store_columns(grads, matmul(et, dk_ref[...]), 4, 2, 0)
        store_columns(grads, matmul(et, dv_ref[...]), 4, 2, 1)

    outs = [struct((rows, D), F32), struct((keys, D), F32), struct((8, D), F32)] + part_outs()
    scratch = [pltpu.VMEM((rows, D), BF16)] * 2 + [pltpu.VMEM((keys, D), BF16)] * 2
    scratch += [pltpu.VMEM((D, keys), BF16), pltpu.VMEM((D, rows), BF16)]
    return call(kernel, "cross_backward", outs, scratch, back, hat, scale, second, encoded, q, k, v, o, stats, *parts, vectors, flops=2 * 10**10)


def compute(x, y, xc, yc, live, weights, vectors, alive):
    xc = jnp.where(alive, xc, jnp.zeros_like(xc))
    live_tags = jnp.where(alive, live, 0).reshape(1, 1)
    live = live.reshape(1, 1)
    first, hat0, scale0, q, k, v, o, stat = self_forward(x, weights[0], vectors, 0)
    encoded, hat1, scale1, hid, slope = ffn_forward(first, weights[1], vectors, 1)
    second, hat2, scale2, q2, k2, v2, o2, stat2 = self_forward(y, weights[2], vectors, 2, live)
    third, hat3, scale3, q3, k3, v3, o3, stat3 = cross_forward(second, encoded, weights[3], vectors)
    decoded, back, n4, *parts4 = ffn_both(third, yc, live_tags, weights[4], vectors)
    back, d_encoded, n3, *parts3 = cross_backward(
        back, hat3, scale3, second, encoded, q3, k3, v3, o3, stat3, weights[3], vectors
    )
    dy, n2, *parts2 = self_backward(back, hat2, scale2, y, q2, k2, v2, o2, stat2, weights[2], vectors, 2, live)
    back, n1, *parts1 = ffn_backward(xc, d_encoded, hat1, scale1, first, hid, slope, weights[1], vectors, 1)
    dx, n0, *parts0 = self_backward(back, hat0, scale0, x, q, k, v, o, stat, weights[0], vectors, 0)
    grads = jnp.concatenate([n[:2] for n in (n0, n1, n2, n3, n4)], axis=0)
    return encoded, decoded, dx, dy, [parts0, parts1, parts2, parts3, parts4], grads


def one_hot(index, count, dtype):
    return (index[:, None] == lax.broadcasted_iota(jnp.int32, (1, count), 1)).astype(dtype)


def local(
    image_tokens,
    tag_tokens,
    image_cotangent,
    tag_cotangent,
    tag_lengths,
    slot_blocks,
    master_blocks,
    left_factor,
    right_factor,
    left_root,
    right_root,
    vector_master,
    vector_moment,
):
    dp = lax.axis_size("dp")
    shards = lax.axis_size("tensor")
    me = lax.axis_index("tensor")
    slots = master_blocks.shape[1]
    items = tag_lengths.shape[0]
    image_length = image_tokens.shape[0] * shards // items
    item_length = tag_tokens.shape[0] * shards // items
    lanes = vector_master.shape[1]
    def rows_of(value):
        return jnp.pad(value, ((0, 16 - value.shape[0]), (0, TILE - value.shape[1])))

    own = jnp.concatenate(
        [
            master_blocks.astype(BF16).reshape(slots * TILE, TILE),
            rows_of(vector_master.astype(BF16)),
        ],
        axis=0,
    )
    pieces = gather_pieces(own, dp)
    ranks = jnp.stack([relative_rank(p, dp) for p in range(dp)])

    def blocks_of(those):
        picked = one_hot(those, dp, jnp.int32)[:, :, None] * slot_blocks.reshape(1, dp, slots)
        return jnp.sum(picked, axis=1).reshape(1, dp * slots)

    tiles = order_tiles(pieces, blocks_of(ranks), slots)
    vector_list = jnp.stack([p[slots * TILE : slots * TILE + 10, :lanes] for p in pieces])
    vectors = jnp.einsum(
        "pr,pvl->vrl", one_hot(ranks, dp, BF16), vector_list, preferred_element_type=F32
    ).reshape(10, dp * lanes)
    weights = [
        gather_group(tiles[c * CHUNK * TILE : (c + 1) * CHUNK * TILE]) for c in range(CHUNKS)
    ]
    x = pull_rows(image_tokens, image_length)
    y = pull_rows(tag_tokens, item_length)
    xc = pull_rows(image_cotangent, image_length)
    yc = pull_rows(tag_cotangent, item_length)
    alive = me < items
    live = jnp.sum(jnp.where(lax.broadcasted_iota(jnp.int32, (items,), 0) == me, tag_lengths, 0))
    live = jnp.where(alive, live, 1)
    encoded, decoded, dx, dy, parts, vector_grads = compute(
        x, y, xc, yc, live, weights, vectors, alive
    )
    sums = [sum_group(p) for p in parts]
    vector_grads = sum_over_group(vector_grads).reshape(10, dp, lanes)
    targets = jnp.stack([target_rank(p, dp) for p in range(dp)])
    vector_rows = jnp.einsum(
        "pr,vrl->pvl",
        one_hot(targets, dp, F32),
        vector_grads,
        precision=lax.Precision.HIGHEST,
    )
    vector_rows = jnp.pad(vector_rows, ((0, 0), (0, 6), (0, TILE - lanes))).astype(BF16)
    outgoing = deal_tiles(sums, vector_rows, blocks_of(targets), slots)
    summed = sum_pieces(outgoing, dp)
    dealt = summed[: slots * TILE].reshape(slots, TILE, TILE)
    dealt = dealt[None]
    vector_gradient = summed[slots * TILE : slots * TILE + 10, :lanes]
    highest = lax.Precision.HIGHEST
    left_updated = STAT_DECAY * left_factor + (1.0 - STAT_DECAY) * jnp.einsum(
        "asij,askj->asik", dealt, dealt, precision=highest
    )
    right_updated = STAT_DECAY * right_factor + (1.0 - STAT_DECAY) * jnp.einsum(
        "asji,asjk->asik", dealt, dealt, precision=highest
    )
    rotated = jnp.einsum("asij,asjk->asik", left_root, dealt, precision=highest)
    master_updated = master_blocks - MATRIX_RATE * jnp.einsum(
        "asij,asjk->asik", rotated, right_root, precision=highest
    )
    moment_updated = (
        STAT_DECAY * vector_moment + (1.0 - STAT_DECAY) * vector_gradient * vector_gradient
    )
    vector_updated = vector_master - VECTOR_RATE * vector_gradient / (
        jnp.sqrt(moment_updated) + 1e-08
    )
    return (
        push_rows(encoded, image_tokens.shape[0]),
        push_rows(decoded, tag_tokens.shape[0]),
        push_rows(dx.astype(BF16), image_tokens.shape[0]).astype(F32),
        push_rows(dy.astype(BF16), tag_tokens.shape[0]).astype(F32),
        dealt,
        left_updated,
        right_updated,
        master_updated,
        master_updated.astype(BF16),
        vector_gradient,
        moment_updated,
        vector_updated,
    )

def solution(mesh):
    in_specs = (
        P(("dp", "tensor"), None),
        P(("dp", "tensor"), None),
        P(("dp", "tensor"), None),
        P(("dp", "tensor"), None),
        P("dp"),
        P(),
        P("tensor", "dp", None, None),
        P("tensor", "dp", None, None),
        P("tensor", "dp", None, None),
        P("tensor", "dp", None, None),
        P("tensor", "dp", None, None),
        P(None, "dp"),
        P(None, "dp"),
    )
    out_specs = (
        P(("dp", "tensor"), None),
        P(("dp", "tensor"), None),
        P(("dp", "tensor"), None),
        P(("dp", "tensor"), None),
        P("tensor", "dp", None, None),
        P("tensor", "dp", None, None),
        P("tensor", "dp", None, None),
        P("tensor", "dp", None, None),
        P("tensor", "dp", None, None),
        P(None, "dp"),
        P(None, "dp"),
        P(None, "dp"),
    )
    return jax.shard_map(local, mesh=mesh, in_specs=in_specs, out_specs=out_specs, check_vma=False)
```

time: 808 us -> 362 us (0.45)
  the two profiles are of different devices: /device:TPU:0 before, /device:TPU:15 now
where the time goes in v2:
time: 362 us; the launch traced here: 359 us
  Pallas kernels  120 us (33%)
  waiting for transfers between devices  107 us (30%)
  starting transfers between devices  79.4 us (22%)
  other arithmetic  28.1 us (8%)
  local copies, waits for them, and re-layouts  15.4 us (4%)
  matrix products  7.27 us (2%)
    pallas_call x9, Pallas kernels, call(): pl.pallas_call(kernel, out_shape=outs, in_specs=[pl.BlockSpec(memory_spac...  117 us
    ppermute x5, waiting for transfers between devices, sum_group(): far = lax.ppermute(far, 'tensor', chip_pairs())  49.2 us
    ppermute x4, starting transfers between devices, pull_rows(): lax.ppermute(rows, 'tensor', [(i + 1, i) for i in range(shards - 1)])  26.5 us
    ppermute x3, waiting for transfers between devices, sum_pieces(): lax.ppermute(both.astype(BF16), 'dp', z_shift(step)).astype(F32)  22.1 us
    ppermute x4, waiting for transfers between devices, sum_pieces(): other = lax.ppermute(pieces[4 + step], 'dp', y_pairs())  17.6 us
    ppermute x5, starting transfers between devices, gather_group(): far_near = lax.ppermute(far, 'tensor', core_pairs())  12.7 us
    ppermute x5, starting transfers between devices, gather_group(): near = lax.ppermute(part, 'tensor', core_pairs())  9.68 us
    ppermute x4, waiting for transfers between devices, gather_pieces(): return column + [lax.ppermute(part, 'dp', y_pairs()) for part in column]  7.75 us
  transfers between devices with their start and end apart: 54, of which 20 were waited for; matrix products, arithmetic and copies ran while one was open for 9% of the time, Pallas kernels for 12%

profile of v2, /device:TPU:15, one launch (start us, length us, event | category | flops | bytes accessed | tf_op | source)
XLA Modules:
  0.0 358.8 jit_solution(18138839994479880312)
XLA Ops:
  0.7 1.4 constant_dynamic-update-slice_fusion.7
  3.3 1.3 collective-permute-start.1
  5.7 1.4 collective-permute-start.3
  7.3 4.4 %collective-permute-start.15 = (bf16[384,512]{1,0:T(8,128)(2,1)}, bf16[384,512]{1,0:T(8,128)(2,1)}, u32[]{:S(2)}, u32[]{:S(2)}) collective-permute-start(bf16[384,512]{1,0:T(8,128)(2,1)} %param.14), channel_id=1, source_target_pairs={{1,0},{2,1},{3,2},{5,4},{6,5},{7,6},{9,8},{10,9},{11,10},{13,12},{... | collective-permute-start | bytes 1179656 | tf_op jit(solution)/shard_map/ppermute | solution.py:107
  12.3 1.3 fusion.32
  14.4 15.5 %collective-permute-start = (bf16[588,512]{1,0:T(8,128)(2,1)S(1)}, bf16[588,512]{1,0:T(8,128)(2,1)S(1)}, u32[]{:S(2)}, u32[]{:S(2)}) collective-permute-start(bf16[588,512]{1,0:T(8,128)(2,1)S(1)} %copy-done.11), channel_id=1, source_target_pairs={{1,0},{2,1},{3,2},{5,4},{6,5},{7,6},{9,8},{10,9},{11,10},{13,12},{... | collective-permute-start | bytes 1806344 | tf_op jit(solution)/shard_map/ppermute | solution.py:107
  30.5 1.9 collective-permute-done.2.refs_2_
  33.2 2.0 collective-permute-done.3.refs_3_
  36.1 1.2 collective-permute-start.7
  37.9 3.0 collective-permute-start.22
  40.9 2.1 fusion.17.refs_1_.refs_4_
  43.0 3.6 collective-permute-start.27
  47.3 7.1 %collective-permute-done.7.refs_7_ = bf16[1296,128]{1,0:T(8,128)(2,1)S(1)} collective-permute-done((bf16[1296,128]{1,0:T(8,128)(2,1)S(1)}, bf16[1296,128]{1,0:T(8,128)(2,1)S(1)}, u32[]{:S(2)}, u32[]{:S(2)}) %collective-permute-start.7) | collective-permute-done | bytes 331808 | tf_op jit(solution)/shard_map/ppermute | solution.py:65
  54.4 1.7 order_tiles.1
  57.5 1.4 fusion.16.c_ref
  58.9 2.4 fusion.8.refs_0_.refs_3_
  61.3 2.6 fusion.7.c_ref
  65.1 3.0 collective-permute-start.16
  68.3 6.4 %collective-permute-start.10 = (bf16[2048,128]{1,0:T(8,128)(2,1)}, bf16[2048,128]{1,0:T(8,128)(2,1)}, u32[]{:S(2)}, u32[]{:S(2)}) collective-permute-start(bf16[2048,128]{1,0:T(8,128)(2,1)} %collective-permute-done.9.refs_3_.refs_11_), channel_id=1, source_target_pairs={{0,1},{1,0},{2,3},{3,2},{4,5},{5,4},{6,7},{7,6},{8,9},{9,8},{10,11... | collective-permute-start | bytes 1572872 | tf_op jit(solution)/shard_map/ppermute | solution.py:88
  75.8 3.8 %collective-permute-done.17.refs_4_.refs_12_ = bf16[2048,128]{1,0:T(8,128)(2,1)} collective-permute-done((bf16[2048,128]{1,0:T(8,128)(2,1)S(1)}, bf16[2048,128]{1,0:T(8,128)(2,1)}, u32[]{:S(2)}, u32[]{:S(2)}) %collective-permute-start.17) | collective-permute-done | bytes 524320 | tf_op jit(solution)/shard_map/ppermute | solution.py:86
  79.6 6.4 %collective-permute-start.11 = (bf16[2048,128]{1,0:T(8,128)(2,1)S(1)}, bf16[2048,128]{1,0:T(8,128)(2,1)}, u32[]{:S(2)}, u32[]{:S(2)}) collective-permute-start(bf16[2048,128]{1,0:T(8,128)(2,1)S(1)} %get-tuple-element.160.p0), channel_id=1, source_target_pairs={{0,1},{1,0},{2,3},{3,2},{4,5},{5,4},{6,7},{7,6},{8,9},{9,8},{10,11... | collective-permute-start | bytes 1572872 | tf_op jit(solution)/shard_map/ppermute | solution.py:87
  86.7 14.1 %self_forward_0.1 = (f32[784,512]{1,0:T(8,128)}, bf16[784,512]{1,0:T(8,128)(2,1)}, f32[784,1]{1,0:T(8,128)}, bf16[784,512]{1,0:T(8,128)(2,1)}, bf16[784,512]{1,0...) custom-call(bf16[784,512]{1,0:T(8,128)(2,1)} %fusion.8.refs_0_.refs_3_, ...), custom_call_target="tpu_custom_call" | custom-call | flops 10000000000 | bytes 4000000 | tf_op jit(solution)/shard_map/self_forward_0/pallas_call | solution.py:352
  102.2 4.4 %collective-permute-start.13 = (bf16[2048,128]{1,0:T(8,128)(2,1)}, bf16[2048,128]{1,0:T(8,128)(2,1)S(1)}, u32[]{:S(2)}, u32[]{:S(2)}) collective-permute-start(bf16[2048,128]{1,0:T(8,128)(2,1)} %collective-permute-done.12.p2), channel_id=1, source_target_pairs={{0,1},{1,0},{2,3},{3,2},{4,5},{5,4},{6,7},{7,6},{8,9},{9,8},{10,11... | collective-permute-start | bytes 1572872 | tf_op jit(solution)/shard_map/ppermute | solution.py:88
  107.4 7.3 %self_forward_2.1 = (f32[512,512]{1,0:T(8,128)}, bf16[512,512]{1,0:T(8,128)(2,1)}, f32[512,1]{1,0:T(8,128)}, bf16[512,512]{1,0:T(8,128)(2,1)}, bf16[512,512]{1,0...) custom-call(s32[1,1]{1,0:T(1,128)} %bitcast.20.refs_0_, ...), custom_call_target="tpu_custom_call" | custom-call | flops 10000000000 | bytes 4000000 | tf_op jit(solution)/shard_map/self_forward_2/pallas_call | solution.py:352
  115.1 1.6 collective-permute-start.25
  117.5 8.1 %ffn_forward_1.1 = (bf16[784,512]{1,0:T(8,128)(2,1)}, bf16[784,512]{1,0:T(8,128)(2,1)}, f32[784,1]{1,0:T(8,128)}, bf16[784,1024]{1,0:T(8,128)(2,1)}, bf16[784,1024]{1,0:T(8,128)(2,1)}) custom-call(f32[784,512]{1,0:T(8,128)} %get-tuple-element.81.f_ref, bf16[2048,128]{1,0:T(8,128)(2,1)} %copy-done.13, bf16[2048,128]{1,0:T(8,128)(2,1)} %collective-permute-done.11.p1, ...), custom_call_target="tpu_custom_call" | custom-call | flops 3000000000 | bytes 4000000 | tf_op jit(solution)/shard_map/ffn_forward_1/pallas_call | solution.py:352
  126.3 11.3 %cross_forward.1 = (f32[512,512]{1,0:T(8,128)}, bf16[512,512]{1,0:T(8,128)(2,1)}, f32[512,1]{1,0:T(8,128)}, bf16[512,512]{1,0:T(8,128)(2,1)}, bf16[784,512]{1,0:...) custom-call(f32[512,512]{1,0:T(8,128)} %get-tuple-element.83.s_ref.x_ref, ...), custom_call_target="tpu_custom_call" | custom-call | flops 5000000000 | bytes 4000000 | tf_op jit(solution)/shard_map/cross_forward/pallas_call | solution.py:352
  138.6 9.2 %ffn_both.1 = (bf16[512,512]{1,0:T(8,128)(2,1)}, f32[512,512]{1,0:T(8,128)}, f32[8,512]{1,0:T(8,128)}, bf16[2048,128]{1,0:T(8,128)(2,1)}, bf16[2048,128]{1,0:T(8...) custom-call(s32[1,1]{1,0:T(1,128)} %bitcast.19.live_ref, f32[512,512]{1,0:T(8,128)} %get-tuple-element.84.t_ref, ...), custom_call_target="tpu_custom_call" | custom-call | flops 10000000000 | bytes 4000000 | tf_op jit(solution)/shard_map/ffn_both/pallas_call | solution.py:352
  147.8 17.0 %cross_backward.1 = (f32[512,512]{1,0:T(8,128)}, f32[784,512]{1,0:T(8,128)}, f32[8,512]{1,0:T(8,128)}, bf16[2048,128]{1,0:T(8,128)(2,1)}, bf16[2048,128]{1,0:T(8...) custom-call(f32[512,512]{1,0:T(8,128)} %get-tuple-element.86.b_ref, ...), custom_call_target="tpu_custom_call" | custom-call | flops 20000000000 | bytes 4000000 | tf_op jit(solution)/shard_map/cross_backward/pallas_call | solution.py:352
  164.8 13.3 %self_backward_2.1 = (f32[512,512]{1,0:T(8,128)}, f32[8,512]{1,0:T(8,128)}, bf16[2048,128]{1,0:T(8,128)(2,1)}, bf16[2048,128]{1,0:T(8,128)(2,1)}, bf16[2048,128]{1,0:T(8,128)(2,1)}, /*index=5*/bf16[2048,128]{1,0:T(8,128)(2,1)}) custom-call(s32[1,1]{1,0:T(1,128)} %bitcast.20.refs_0_, f32[512,512]{1,0:T(8,128)} %get-tuple-element.108.refs_1_, ...), custom_call_target="tpu_custom_call" | custom-call | flops 20000000000 | bytes 4000000 | tf_op jit(solution)/shard_map/self_backward_2/pallas_call | solution.py:352
  178.8 9.9 %ffn_backward_1.1 = (f32[784,512]{1,0:T(8,128)}, f32[8,512]{1,0:T(8,128)}, bf16[2048,128]{1,0:T(8,128)(2,1)}, bf16[2048,128]{1,0:T(8,128)(2,1)}, bf16[2048,128]{1,0:T(8,128)(2,1)}, /*index=5*/bf16[2048,128]{1,0:T(8,128)(2,1)}) custom-call(bf16[784,512]{1,0:T(8,128)(2,1)} %fusion.7.c_ref, f32[784,512]{1,0:T(8,128)} %get-tuple-element.94.m_ref, ...), custom_call_target="tpu_custom_call" | custom-call | flops 10000000000 | bytes 4000000 | tf_op jit(solution)/shard_map/ffn_backward_1/pallas_call | solution.py:352
  188.7 27.1 %self_backward_0.1 = (f32[784,512]{1,0:T(8,128)}, f32[8,512]{1,0:T(8,128)}, bf16[2048,128]{1,0:T(8,128)(2,1)}, bf16[2048,128]{1,0:T(8,128)(2,1)}, bf16[2048,128]{1,0:T(8,128)(2,1)}, /*index=5*/bf16[2048,128]{1,0:T(8,128)(2,1)}) custom-call(f32[784,512]{1,0:T(8,128)} %get-tuple-element.99.refs_0_, bf16[784,512]{1,0:T(8,128)(2,1)} %get-tuple-element.100.refs_1_, ...), custom_call_target="tpu_custom_call" | custom-call | flops 20000000000 | bytes 4000000 | tf_op jit(solution)/shard_map/self_backward_0/pallas_call | solution.py:352
  222.3 1.7 collective-permute-done.46
  224.0 1.6 collective-permute-start.37
  226.0 1.3 add_convert_fusion.1
  229.2 1.3 add_convert_fusion.5
  233.6 10.0 %collective-permute-done.44 = bf16[2048,128]{1,0:T(8,128)(2,1)S(1)} collective-permute-done((bf16[2048,128]{1,0:T(8,128)(2,1)S(1)}, bf16[2048,128]{1,0:T(8,128)(2,1)S(1)}, u32[]{:S(2)}, u32[]{:S(2)}) %collective-permute-start.44) | collective-permute-done | bytes 524320 | tf_op jit(solution)/shard_map/ppermute | solution.py:96
  243.9 1.2 add_convert_fusion.refs_4_
  245.2 2.6 collective-permute-start.30
  247.7 7.1 %collective-permute-done.41 = bf16[2048,128]{1,0:T(8,128)(2,1)S(1)} collective-permute-done((bf16[2048,128]{1,0:T(8,128)(2,1)S(1)}, bf16[2048,128]{1,0:T(8,128)(2,1)S(1)}, u32[]{:S(2)}, u32[]{:S(2)}) %collective-permute-start.41) | collective-permute-done | bytes 524320 | tf_op jit(solution)/shard_map/ppermute | solution.py:96
  255.1 1.2 add_convert_fusion.2.refs_3_
  256.4 1.4 collective-permute-start.29
  257.8 8.2 %collective-permute-done.38 = bf16[2048,128]{1,0:T(8,128)(2,1)S(1)} collective-permute-done((bf16[2048,128]{1,0:T(8,128)(2,1)S(1)}, bf16[2048,128]{1,0:T(8,128)(2,1)S(1)}, u32[]{:S(2)}, u32[]{:S(2)}) %collective-permute-start.38) | collective-permute-done | bytes 524320 | tf_op jit(solution)/shard_map/ppermute | solution.py:96
  266.6 1.4 collective-permute-start.28
  268.0 9.3 %collective-permute-done.35 = bf16[2048,128]{1,0:T(8,128)(2,1)S(1)} collective-permute-done((bf16[2048,128]{1,0:T(8,128)(2,1)S(1)}, bf16[2048,128]{1,0:T(8,128)(2,1)S(1)}, u32[]{:S(2)}, u32[]{:S(2)}) %collective-permute-start.35) | collective-permute-done | bytes 524320 | tf_op jit(solution)/shard_map/ppermute | solution.py:96
  277.3 1.3 collective-permute-start.26
  278.8 14.6 %collective-permute-done.32 = bf16[2048,128]{1,0:T(8,128)(2,1)S(1)} collective-permute-done((bf16[2048,128]{1,0:T(8,128)(2,1)S(1)}, bf16[2048,128]{1,0:T(8,128)(2,1)S(1)}, u32[]{:S(2)}, u32[]{:S(2)}) %collective-permute-start.32) | collective-permute-done | bytes 524320 | tf_op jit(solution)/shard_map/ppermute | solution.py:96
  295.0 1.3 collective-permute-start.14
  296.3 1.4 fusion.19
  297.7 1.2 collective-permute-start.49
  298.9 3.6 collective-permute-done.47
  302.6 7.0 %collective-permute-done.49 = bf16[1296,128]{1,0:T(8,128)(2,1)S(1)} collective-permute-done((bf16[1296,128]{1,0:T(8,128)(2,1)S(1)}, bf16[1296,128]{1,0:T(8,128)(2,1)S(1)}, u32[]{:S(2)}, u32[]{:S(2)}) %collective-permute-start.49) | collective-permute-done | bytes 331808 | tf_op jit(solution)/shard_map/ppermute | solution.py:76
  309.7 7.0 %collective-permute-done.51 = bf16[1296,128]{1,0:T(8,128)(2,1)S(1)} collective-permute-done((bf16[1296,128]{1,0:T(8,128)(2,1)S(1)}, bf16[1296,128]{1,0:T(8,128)(2,1)S(1)}, u32[]{:S(2)}, u32[]{:S(2)}) %collective-permute-start.51) | collective-permute-done | bytes 331808 | tf_op jit(solution)/shard_map/ppermute | solution.py:76
  316.7 2.0 collective-permute-start.48
  320.0 1.6 collective-permute-start.52
  321.6 1.3 fusion.20
  322.9 2.2 fusion.15
  325.1 2.2 fusion.14
  327.4 12.7 %collective-permute-done.48 = bf16[1296,128]{1,0:T(8,128)(2,1)S(1)} collective-permute-done((bf16[1296,128]{1,0:T(8,128)(2,1)S(1)}, bf16[1296,128]{1,0:T(8,128)(2,1)S(1)}, u32[]{:S(2)}, u32[]{:S(2)}) %collective-permute-start.48) | collective-permute-done | bytes 331808 | tf_op jit(solution)/shard_map/ppermute | solution.py:79
  340.1 7.3 %collective-permute-done.50 = bf16[1296,128]{1,0:T(8,128)(2,1)S(1)} collective-permute-done((bf16[1296,128]{1,0:T(8,128)(2,1)S(1)}, bf16[1296,128]{1,0:T(8,128)(2,1)S(1)}, u32[]{:S(2)}, u32[]{:S(2)}) %collective-permute-start.50) | collective-permute-done | bytes 331808 | tf_op jit(solution)/shard_map/ppermute | solution.py:79
  347.3 2.1 collective-permute-done.52
  351.8 2.3 fusion.2
  354.2 2.1 fusion.4
  356.9 1.8 fusion.39
  (212 shorter events, 36.0 us)
Async XLA Ops:
  0.6 356.2 %copy-start = (f32[1,10,128,128]{3,2,1,0:T(8,128)S(1)}, f32[1,10,128,128]{3,2,1,0:T(8,128)}, u32[]{:S(2)}) copy-start(f32[1,10,128,128]{3,2,1,0:T(8,128)} %param.23) | copy-start | bytes 1966084
  3.2 39.8 %copy-start.10 = (bf16[588,512]{1,0:T(8,128)(2,1)S(1)}, bf16[588,512]{1,0:T(8,128)(2,1)}, u32[]{:S(2)}) copy-start(bf16[588,512]{1,0:T(8,128)(2,1)} %param.15) | copy-start | bytes 1806340
  3.3 11.1 %collective-permute-start.1 = (bf16[1296,128]{1,0:T(8,128)(2,1)S(1)}, bf16[1296,128]{1,0:T(8,128)(2,1)S(1)}, u32[]{:S(2)}, u32[]{:S(2)}) collective-permute-start(bf16[1296,128]{1,0:T(8,128)(2,1)S(1)} %fusion.21.refs_0_), channel_id=1, source_target_pairs={{0,8},{4,12},{8,16},{12,20},{16,24},{20,28},{24,0},{28,4},{1,9},{5... | collective-permute-start | bytes 995336 | tf_op jit(solution)/shard_map/ppermute | solution.py:64
  4.6 27.8 %collective-permute-start.2 = (bf16[1296,128]{1,0:T(8,128)(2,1)S(1)}, bf16[1296,128]{1,0:T(8,128)(2,1)S(1)}, u32[]{:S(2)}, u32[]{:S(2)}) collective-permute-start(bf16[1296,128]{1,0:T(8,128)(2,1)S(1)} %fusion.21.refs_0_), channel_id=1, source_target_pairs={{0,16},{4,20},{8,24},{12,28},{16,0},{20,4},{24,8},{28,12},{1,17},{... | collective-permute-start | bytes 995336 | tf_op jit(solution)/shard_map/ppermute | solution.py:64
  5.7 29.6 %collective-permute-start.3 = (bf16[1296,128]{1,0:T(8,128)(2,1)S(1)}, bf16[1296,128]{1,0:T(8,128)(2,1)S(1)}, u32[]{:S(2)}, u32[]{:S(2)}) collective-permute-start(bf16[1296,128]{1,0:T(8,128)(2,1)S(1)} %fusion.21.refs_0_), channel_id=1, source_target_pairs={{0,24},{4,28},{8,0},{12,4},{16,8},{20,12},{24,16},{28,20},{1,25},{... | collective-permute-start | bytes 995336 | tf_op jit(solution)/shard_map/ppermute | solution.py:64
  7.1 29.0 %collective-permute-start.4 = (bf16[1296,128]{1,0:T(8,128)(2,1)S(1)}, bf16[1296,128]{1,0:T(8,128)(2,1)S(1)}, u32[]{:S(2)}, u32[]{:S(2)}) collective-permute-start(bf16[1296,128]{1,0:T(8,128)(2,1)S(1)} %fusion.21.refs_0_), channel_id=1, source_target_pairs={{0,4},{4,0},{8,12},{12,8},{16,20},{20,16},{24,28},{28,24},{1,5},{5... | collective-permute-start | bytes 995336 | tf_op jit(solution)/shard_map/ppermute | solution.py:65
  7.3 30.6 %collective-permute-start.15 = (bf16[384,512]{1,0:T(8,128)(2,1)}, bf16[384,512]{1,0:T(8,128)(2,1)}, u32[]{:S(2)}, u32[]{:S(2)}) collective-permute-start(bf16[384,512]{1,0:T(8,128)(2,1)} %param.14), channel_id=1, source_target_pairs={{1,0},{2,1},{3,2},{5,4},{6,5},{7,6},{9,8},{10,9},{11,10},{13,12},{... | collective-permute-start | bytes 1179656 | tf_op jit(solution)/shard_map/ppermute | solution.py:107
  14.4 44.6 %collective-permute-start = (bf16[588,512]{1,0:T(8,128)(2,1)S(1)}, bf16[588,512]{1,0:T(8,128)(2,1)S(1)}, u32[]{:S(2)}, u32[]{:S(2)}) collective-permute-start(bf16[588,512]{1,0:T(8,128)(2,1)S(1)} %copy-done.11), channel_id=1, source_target_pairs={{1,0},{2,1},{3,2},{5,4},{6,5},{7,6},{9,8},{10,9},{11,10},{13,12},{... | collective-permute-start | bytes 1806344 | tf_op jit(solution)/shard_map/ppermute | solution.py:107
  32.4 10.6 %collective-permute-start.5 = (bf16[1296,128]{1,0:T(8,128)(2,1)S(1)}, bf16[1296,128]{1,0:T(8,128)(2,1)S(1)}, u32[]{:S(2)}, u32[]{:S(2)}) collective-permute-start(bf16[1296,128]{1,0:T(8,128)(2,1)S(1)} %collective-permute-done.1.refs_1_), channel_id=1, source_target_pairs={{0,4},{4,0},{8,12},{12,8},{16,20},{20,16},{24,28},{28,24},{1,5},{5... | collective-permute-start | bytes 995336 | tf_op jit(solution)/shard_map/ppermute | solution.py:65
  35.3 12.0 %collective-permute-start.6 = (bf16[1296,128]{1,0:T(8,128)(2,1)S(1)}, bf16[1296,128]{1,0:T(8,128)(2,1)S(1)}, u32[]{:S(2)}, u32[]{:S(2)}) collective-permute-start(bf16[1296,128]{1,0:T(8,128)(2,1)S(1)} %collective-permute-done.2.refs_2_), channel_id=1, source_target_pairs={{0,4},{4,0},{8,12},{12,8},{16,20},{20,16},{24,28},{28,24},{1,5},{5... | collective-permute-start | bytes 995336 | tf_op jit(solution)/shard_map/ppermute | solution.py:65
  36.1 18.3 %collective-permute-start.7 = (bf16[1296,128]{1,0:T(8,128)(2,1)S(1)}, bf16[1296,128]{1,0:T(8,128)(2,1)S(1)}, u32[]{:S(2)}, u32[]{:S(2)}) collective-permute-start(bf16[1296,128]{1,0:T(8,128)(2,1)S(1)} %collective-permute-done.3.refs_3_), channel_id=1, source_target_pairs={{0,4},{4,0},{8,12},{12,8},{16,20},{20,16},{24,28},{28,24},{1,5},{5... | collective-permute-start | bytes 995336 | tf_op jit(solution)/shard_map/ppermute | solution.py:65
  37.9 19.6 %collective-permute-start.22 = (bf16[384,512]{1,0:T(8,128)(2,1)}, bf16[384,512]{1,0:T(8,128)(2,1)S(1)}, u32[]{:S(2)}, u32[]{:S(2)}) collective-permute-start(bf16[384,512]{1,0:T(8,128)(2,1)} %param.16), channel_id=1, source_target_pairs={{1,0},{2,1},{3,2},{5,4},{6,5},{7,6},{9,8},{10,9},{11,10},{13,12},{... | collective-permute-start | bytes 1179656 | tf_op jit(solution)/shard_map/ppermute | solution.py:107
  43.0 18.3 %collective-permute-start.27 = (bf16[588,512]{1,0:T(8,128)(2,1)S(1)}, bf16[588,512]{1,0:T(8,128)(2,1)S(1)}, u32[]{:S(2)}, u32[]{:S(2)}) collective-permute-start(bf16[588,512]{1,0:T(8,128)(2,1)S(1)} %copy-done.10), channel_id=1, source_target_pairs={{1,0},{2,1},{3,2},{5,4},{6,5},{7,6},{9,8},{10,9},{11,10},{13,12},{... | collective-permute-start | bytes 1806344 | tf_op jit(solution)/shard_map/ppermute | solution.py:107
  57.3 22.3 %copy-start.13 = (bf16[2048,128]{1,0:T(8,128)(2,1)}, bf16[2048,128]{1,0:T(8,128)(2,1)S(1)}, u32[]{:S(2)}) copy-start(bf16[2048,128]{1,0:T(8,128)(2,1)S(1)} %get-tuple-element.160.p0) | copy-start | bytes 1572868
  57.3 11.1 %collective-permute-start.9 = (bf16[2048,128]{1,0:T(8,128)(2,1)S(1)}, bf16[2048,128]{1,0:T(8,128)(2,1)}, u32[]{:S(2)}, u32[]{:S(2)}) collective-permute-start(bf16[2048,128]{1,0:T(8,128)(2,1)S(1)} %get-tuple-element.161.refs_1_.refs_9_), channel_id=1, source_target_pairs={{0,2},{1,3},{2,0},{3,1},{4,6},{5,7},{6,4},{7,5},{8,10},{9,11},{10,... | collective-permute-start | bytes 1572872 | tf_op jit(solution)/shard_map/ppermute | solution.py:86
  61.3 24.6 %copy-start.15 = (bf16[2048,128]{1,0:T(8,128)(2,1)S(1)}, bf16[2048,128]{1,0:T(8,128)(2,1)}, u32[]{:S(2)}) copy-start(bf16[2048,128]{1,0:T(8,128)(2,1)} %get-tuple-element.158.p0) | copy-start | bytes 1572868
  63.9 15.7 %collective-permute-start.17 = (bf16[2048,128]{1,0:T(8,128)(2,1)S(1)}, bf16[2048,128]{1,0:T(8,128)(2,1)}, u32[]{:S(2)}, u32[]{:S(2)}) collective-permute-start(bf16[2048,128]{1,0:T(8,128)(2,1)S(1)} %get-tuple-element.159.refs_2_.refs_10_), channel_id=1, source_target_pairs={{0,2},{1,3},{2,0},{3,1},{4,6},{5,7},{6,4},{7,5},{8,10},{9,11},{10,... | collective-permute-start | bytes 1572872 | tf_op jit(solution)/shard_map/ppermute | solution.py:86
  65.1 35.7 %collective-permute-start.16 = (bf16[2048,128]{1,0:T(8,128)(2,1)S(1)}, bf16[2048,128]{1,0:T(8,128)(2,1)}, u32[]{:S(2)}, u32[]{:S(2)}) collective-permute-start(bf16[2048,128]{1,0:T(8,128)(2,1)S(1)} %get-tuple-element.159.refs_2_.refs_10_), channel_id=1, source_target_pairs={{0,1},{1,0},{2,3},{3,2},{4,5},{5,4},{6,7},{7,6},{8,9},{9,8},{10,11... | collective-permute-start | bytes 1572872 | tf_op jit(solution)/shard_map/ppermute | solution.py:87
  68.1 17.8 %collective-permute-start.8 = (bf16[2048,128]{1,0:T(8,128)(2,1)S(1)}, bf16[2048,128]{1,0:T(8,128)(2,1)S(1)}, u32[]{:S(2)}, u32[]{:S(2)}) collective-permute-start(bf16[2048,128]{1,0:T(8,128)(2,1)S(1)} %get-tuple-element.161.refs_1_.refs_9_), channel_id=1, source_target_pairs={{0,1},{1,0},{2,3},{3,2},{4,5},{5,4},{6,7},{7,6},{8,9},{9,8},{10,11... | collective-permute-start | bytes 1572872 | tf_op jit(solution)/shard_map/ppermute | solution.py:87
  68.3 18.0 %collective-permute-start.10 = (bf16[2048,128]{1,0:T(8,128)(2,1)}, bf16[2048,128]{1,0:T(8,128)(2,1)}, u32[]{:S(2)}, u32[]{:S(2)}) collective-permute-start(bf16[2048,128]{1,0:T(8,128)(2,1)} %collective-permute-done.9.refs_3_.refs_11_), channel_id=1, source_target_pairs={{0,1},{1,0},{2,3},{3,2},{4,5},{5,4},{6,7},{7,6},{8,9},{9,8},{10,11... | collective-permute-start | bytes 1572872 | tf_op jit(solution)/shard_map/ppermute | solution.py:88
  75.5 25.4 %collective-permute-start.12 = (bf16[2048,128]{1,0:T(8,128)(2,1)S(1)}, bf16[2048,128]{1,0:T(8,128)(2,1)}, u32[]{:S(2)}, u32[]{:S(2)}) collective-permute-start(bf16[2048,128]{1,0:T(8,128)(2,1)S(1)} %get-tuple-element.160.p0), channel_id=1, source_target_pairs={{0,2},{1,3},{2,0},{3,1},{4,6},{5,7},{6,4},{7,5},{8,10},{9,11},{10,... | collective-permute-start | bytes 1572872 | tf_op jit(solution)/shard_map/ppermute | solution.py:86
  79.6 35.2 %collective-permute-start.11 = (bf16[2048,128]{1,0:T(8,128)(2,1)S(1)}, bf16[2048,128]{1,0:T(8,128)(2,1)}, u32[]{:S(2)}, u32[]{:S(2)}) collective-permute-start(bf16[2048,128]{1,0:T(8,128)(2,1)S(1)} %get-tuple-element.160.p0), channel_id=1, source_target_pairs={{0,1},{1,0},{2,3},{3,2},{4,5},{5,4},{6,7},{7,6},{8,9},{9,8},{10,11... | collective-permute-start | bytes 1572872 | tf_op jit(solution)/shard_map/ppermute | solution.py:87
  86.0 16.2 %collective-permute-start.20 = (bf16[2048,128]{1,0:T(8,128)(2,1)S(1)}, bf16[2048,128]{1,0:T(8,128)(2,1)}, u32[]{:S(2)}, u32[]{:S(2)}) collective-permute-start(bf16[2048,128]{1,0:T(8,128)(2,1)S(1)} %copy-done.15), channel_id=1, source_target_pairs={{0,2},{1,3},{2,0},{3,1},{4,6},{5,7},{6,4},{7,5},{8,10},{9,11},{10,... | collective-permute-start | bytes 1572872 | tf_op jit(solution)/shard_map/ppermute | solution.py:86
  86.3 20.3 %collective-permute-start.18 = (bf16[2048,128]{1,0:T(8,128)(2,1)}, bf16[2048,128]{1,0:T(8,128)(2,1)S(1)}, u32[]{:S(2)}, u32[]{:S(2)}) collective-permute-start(bf16[2048,128]{1,0:T(8,128)(2,1)} %collective-permute-done.17.refs_4_.refs_12_), channel_id=1, source_target_pairs={{0,1},{1,0},{2,3},{3,2},{4,5},{5,4},{6,7},{7,6},{8,9},{9,8},{10,11... | collective-permute-start | bytes 1572872 | tf_op jit(solution)/shard_map/ppermute | solution.py:88
  100.8 24.7 %collective-permute-start.19 = (bf16[2048,128]{1,0:T(8,128)(2,1)S(1)}, bf16[2048,128]{1,0:T(8,128)(2,1)S(1)}, u32[]{:S(2)}, u32[]{:S(2)}) collective-permute-start(bf16[2048,128]{1,0:T(8,128)(2,1)S(1)} %copy-done.15), channel_id=1, source_target_pairs={{0,1},{1,0},{2,3},{3,2},{4,5},{5,4},{6,7},{7,6},{8,9},{9,8},{10,11... | collective-permute-start | bytes 1572872 | tf_op jit(solution)/shard_map/ppermute | solution.py:87
  100.9 14.2 %collective-permute-start.24 = (bf16[2048,128]{1,0:T(8,128)(2,1)S(1)}, bf16[2048,128]{1,0:T(8,128)(2,1)}, u32[]{:S(2)}, u32[]{:S(2)}) collective-permute-start(bf16[2048,128]{1,0:T(8,128)(2,1)S(1)} %copy-done.17), channel_id=1, source_target_pairs={{0,2},{1,3},{2,0},{3,1},{4,6},{5,7},{6,4},{7,5},{8,10},{9,11},{10,... | collective-permute-start | bytes 1572872 | tf_op jit(solution)/shard_map/ppermute | solution.py:86
  102.2 14.5 %collective-permute-start.13 = (bf16[2048,128]{1,0:T(8,128)(2,1)}, bf16[2048,128]{1,0:T(8,128)(2,1)S(1)}, u32[]{:S(2)}, u32[]{:S(2)}) collective-permute-start(bf16[2048,128]{1,0:T(8,128)(2,1)} %collective-permute-done.12.p2), channel_id=1, source_target_pairs={{0,1},{1,0},{2,3},{3,2},{4,5},{5,4},{6,7},{7,6},{8,9},{9,8},{10,11... | collective-permute-start | bytes 1572872 | tf_op jit(solution)/shard_map/ppermute | solution.py:88
  106.6 19.0 %collective-permute-start.21 = (bf16[2048,128]{1,0:T(8,128)(2,1)}, bf16[2048,128]{1,0:T(8,128)(2,1)}, u32[]{:S(2)}, u32[]{:S(2)}) collective-permute-start(bf16[2048,128]{1,0:T(8,128)(2,1)} %collective-permute-done.20.p2), channel_id=1, source_target_pairs={{0,1},{1,0},{2,3},{3,2},{4,5},{5,4},{6,7},{7,6},{8,9},{9,8},{10,11... | collective-permute-start | bytes 1572872 | tf_op jit(solution)/shard_map/ppermute | solution.py:88
  114.7 22.9 %collective-permute-start.23 = (bf16[2048,128]{1,0:T(8,128)(2,1)S(1)}, bf16[2048,128]{1,0:T(8,128)(2,1)S(1)}, u32[]{:S(2)}, u32[]{:S(2)}) collective-permute-start(bf16[2048,128]{1,0:T(8,128)(2,1)S(1)} %copy-done.17), channel_id=1, source_target_pairs={{0,1},{1,0},{2,3},{3,2},{4,5},{5,4},{6,7},{7,6},{8,9},{9,8},{10,11... | collective-permute-start | bytes 1572872 | tf_op jit(solution)/shard_map/ppermute | solution.py:87
  115.1 22.5 %collective-permute-start.25 = (bf16[2048,128]{1,0:T(8,128)(2,1)}, bf16[2048,128]{1,0:T(8,128)(2,1)S(1)}, u32[]{:S(2)}, u32[]{:S(2)}) collective-permute-start(bf16[2048,128]{1,0:T(8,128)(2,1)} %collective-permute-done.24.p2), channel_id=1, source_target_pairs={{0,1},{1,0},{2,3},{3,2},{4,5},{5,4},{6,7},{7,6},{8,9},{9,8},{10,11... | collective-permute-start | bytes 1572872 | tf_op jit(solution)/shard_map/ppermute | solution.py:88
  188.7 31.3 %copy-start.6 = (f32[512,512]{1,0:T(8,128)S(1)}, f32[512,512]{1,0:T(8,128)}, u32[]{:S(2)}) copy-start(f32[512,512]{1,0:T(8,128)} %get-tuple-element.116) | copy-start | bytes 3145732
  218.8 2.3 collective-permute-start.45
  218.9 7.0 %collective-permute-start.43 = (bf16[2048,128]{1,0:T(8,128)(2,1)}, bf16[2048,128]{1,0:T(8,128)(2,1)}, u32[]{:S(2)}, u32[]{:S(2)}) collective-permute-start(bf16[2048,128]{1,0:T(8,128)(2,1)} %get-tuple-element.136), channel_id=1, source_target_pairs={{0,1},{1,0},{2,3},{3,2},{4,5},{5,4},{6,7},{7,6},{8,9},{9,8},{10,11... | collective-permute-start | bytes 1572872 | tf_op jit(solution)/shard_map/ppermute | solution.py:94
  219.4 13.1 %collective-permute-start.42 = (bf16[2048,128]{1,0:T(8,128)(2,1)}, bf16[2048,128]{1,0:T(8,128)(2,1)}, u32[]{:S(2)}, u32[]{:S(2)}) collective-permute-start(bf16[2048,128]{1,0:T(8,128)(2,1)} %get-tuple-element.134), channel_id=1, source_target_pairs={{0,1},{1,0},{2,3},{3,2},{4,5},{5,4},{6,7},{7,6},{8,9},{9,8},{10,11... | collective-permute-start | bytes 1572872 | tf_op jit(solution)/shard_map/ppermute | solution.py:93
  219.5 7.8 %collective-permute-start.40 = (bf16[2048,128]{1,0:T(8,128)(2,1)}, bf16[2048,128]{1,0:T(8,128)(2,1)}, u32[]{:S(2)}, u32[]{:S(2)}) collective-permute-start(bf16[2048,128]{1,0:T(8,128)(2,1)} %get-tuple-element.132), channel_id=1, source_target_pairs={{0,1},{1,0},{2,3},{3,2},{4,5},{5,4},{6,7},{7,6},{8,9},{9,8},{10,11... | collective-permute-start | bytes 1572872 | tf_op jit(solution)/shard_map/ppermute | solution.py:94
  219.9 25.2 %collective-permute-start.39 = (bf16[2048,128]{1,0:T(8,128)(2,1)}, bf16[2048,128]{1,0:T(8,128)(2,1)}, u32[]{:S(2)}, u32[]{:S(2)}) collective-permute-start(bf16[2048,128]{1,0:T(8,128)(2,1)} %get-tuple-element.130), channel_id=1, source_target_pairs={{0,1},{1,0},{2,3},{3,2},{4,5},{5,4},{6,7},{7,6},{8,9},{9,8},{10,11... | collective-permute-start | bytes 1572872 | tf_op jit(solution)/shard_map/ppermute | solution.py:93
  221.2 2.8 collective-permute-start.46
  224.0 5.1 %collective-permute-start.37 = (bf16[2048,128]{1,0:T(8,128)(2,1)}, bf16[2048,128]{1,0:T(8,128)(2,1)}, u32[]{:S(2)}, u32[]{:S(2)}) collective-permute-start(bf16[2048,128]{1,0:T(8,128)(2,1)} %get-tuple-element.128), channel_id=1, source_target_pairs={{0,1},{1,0},{2,3},{3,2},{4,5},{5,4},{6,7},{7,6},{8,9},{9,8},{10,11... | collective-permute-start | bytes 1572872 | tf_op jit(solution)/shard_map/ppermute | solution.py:94
  225.9 30.4 %collective-permute-start.36 = (bf16[2048,128]{1,0:T(8,128)(2,1)}, bf16[2048,128]{1,0:T(8,128)(2,1)S(1)}, u32[]{:S(2)}, u32[]{:S(2)}) collective-permute-start(bf16[2048,128]{1,0:T(8,128)(2,1)} %get-tuple-element.126), channel_id=1, source_target_pairs={{0,1},{1,0},{2,3},{3,2},{4,5},{5,4},{6,7},{7,6},{8,9},{9,8},{10,11... | collective-permute-start | bytes 1572872 | tf_op jit(solution)/shard_map/ppermute | solution.py:93
  227.3 3.2 collective-permute-start.34
  229.1 2.0 collective-permute-start.31
  230.5 13.1 %collective-permute-start.44 = (bf16[2048,128]{1,0:T(8,128)(2,1)S(1)}, bf16[2048,128]{1,0:T(8,128)(2,1)S(1)}, u32[]{:S(2)}, u32[]{:S(2)}) collective-permute-start(bf16[2048,128]{1,0:T(8,128)(2,1)S(1)} %add_convert_fusion.1), channel_id=1, source_target_pairs={{0,2},{1,3},{2,0},{3,1},{4,6},{5,7},{6,4},{7,5},{8,10},{9,11},{10,... | collective-permute-start | bytes 1572872 | tf_op jit(solution)/shard_map/ppermute | solution.py:96
  231.1 23.7 %collective-permute-start.41 = (bf16[2048,128]{1,0:T(8,128)(2,1)S(1)}, bf16[2048,128]{1,0:T(8,128)(2,1)S(1)}, u32[]{:S(2)}, u32[]{:S(2)}) collective-permute-start(bf16[2048,128]{1,0:T(8,128)(2,1)S(1)} %add_convert_fusion.3), channel_id=1, source_target_pairs={{0,2},{1,3},{2,0},{3,1},{4,6},{5,7},{6,4},{7,5},{8,10},{9,11},{10,... | collective-permute-start | bytes 1572872 | tf_op jit(solution)/shard_map/ppermute | solution.py:96
  232.4 22.7 %copy-start.22 = (bf16[2048,128]{1,0:T(8,128)(2,1)S(1)}, bf16[2048,128]{1,0:T(8,128)(2,1)}, u32[]{:S(2)}) copy-start(bf16[2048,128]{1,0:T(8,128)(2,1)} %get-tuple-element.129) | copy-start | bytes 1572868
  232.5 34.1 %collective-permute-start.33 = (bf16[2048,128]{1,0:T(8,128)(2,1)S(1)}, bf16[2048,128]{1,0:T(8,128)(2,1)S(1)}, u32[]{:S(2)}, u32[]{:S(2)}) collective-permute-start(bf16[2048,128]{1,0:T(8,128)(2,1)S(1)} %copy-done.35), channel_id=1, source_target_pairs={{0,1},{1,0},{2,3},{3,2},{4,5},{5,4},{6,7},{7,6},{8,9},{9,8},{10,11... | collective-permute-start | bytes 1572872 | tf_op jit(solution)/shard_map/ppermute | solution.py:93
  243.6 22.5 %collective-permute-start.38 = (bf16[2048,128]{1,0:T(8,128)(2,1)S(1)}, bf16[2048,128]{1,0:T(8,128)(2,1)S(1)}, u32[]{:S(2)}, u32[]{:S(2)}) collective-permute-start(bf16[2048,128]{1,0:T(8,128)(2,1)S(1)} %add_convert_fusion.5), channel_id=1, source_target_pairs={{0,2},{1,3},{2,0},{3,1},{4,6},{5,7},{6,4},{7,5},{8,10},{9,11},{10,... | collective-permute-start | bytes 1572872 | tf_op jit(solution)/shard_map/ppermute | solution.py:96
  245.1 21.2 %copy-start.23 = (bf16[2048,128]{1,0:T(8,128)(2,1)S(1)}, bf16[2048,128]{1,0:T(8,128)(2,1)}, u32[]{:S(2)}) copy-start(bf16[2048,128]{1,0:T(8,128)(2,1)} %get-tuple-element.125) | copy-start | bytes 1572868
  245.2 33.7 %collective-permute-start.30 = (bf16[2048,128]{1,0:T(8,128)(2,1)S(1)}, bf16[2048,128]{1,0:T(8,128)(2,1)S(1)}, u32[]{:S(2)}, u32[]{:S(2)}) collective-permute-start(bf16[2048,128]{1,0:T(8,128)(2,1)S(1)} %copy-done.34), channel_id=1, source_target_pairs={{0,1},{1,0},{2,3},{3,2},{4,5},{5,4},{6,7},{7,6},{8,9},{9,8},{10,11... | collective-permute-start | bytes 1572872 | tf_op jit(solution)/shard_map/ppermute | solution.py:93
  254.8 22.5 %collective-permute-start.35 = (bf16[2048,128]{1,0:T(8,128)(2,1)S(1)}, bf16[2048,128]{1,0:T(8,128)(2,1)S(1)}, u32[]{:S(2)}, u32[]{:S(2)}) collective-permute-start(bf16[2048,128]{1,0:T(8,128)(2,1)S(1)} %add_convert_fusion.7), channel_id=1, source_target_pairs={{0,2},{1,3},{2,0},{3,1},{4,6},{5,7},{6,4},{7,5},{8,10},{9,11},{10,... | collective-permute-start | bytes 1572872 | tf_op jit(solution)/shard_map/ppermute | solution.py:96
  256.4 21.0 %copy-start.28 = (bf16[384,512]{1,0:T(8,128)(2,1)S(1)}, bf16[384,512]{1,0:T(8,128)(2,1)}, u32[]{:S(2)}) copy-start(bf16[384,512]{1,0:T(8,128)(2,1)} %get-tuple-element.169) | copy-start | bytes 1179652
  256.4 22.2 %copy-start.24 = (bf16[2048,128]{1,0:T(8,128)(2,1)S(1)}, bf16[2048,128]{1,0:T(8,128)(2,1)}, u32[]{:S(2)}) copy-start(bf16[2048,128]{1,0:T(8,128)(2,1)} %get-tuple-element.121) | copy-start | bytes 1572868
  256.4 39.9 %collective-permute-start.29 = (bf16[384,512]{1,0:T(8,128)(2,1)S(1)}, bf16[384,512]{1,0:T(8,128)(2,1)S(1)}, u32[]{:S(2)}, u32[]{:S(2)}) collective-permute-start(bf16[384,512]{1,0:T(8,128)(2,1)S(1)} %copy-done.29), channel_id=1, source_target_pairs={{0,1},{1,2},{2,3},{4,5},{5,6},{6,7},{8,9},{9,10},{10,11},{12,13},{... | collective-permute-start | bytes 1179656 | tf_op jit(solution)/shard_map/ppermute | solution.py:115
  266.1 27.3 %collective-permute-start.32 = (bf16[2048,128]{1,0:T(8,128)(2,1)S(1)}, bf16[2048,128]{1,0:T(8,128)(2,1)S(1)}, u32[]{:S(2)}, u32[]{:S(2)}) collective-permute-start(bf16[2048,128]{1,0:T(8,128)(2,1)S(1)} %add_convert_fusion.9), channel_id=1, source_target_pairs={{0,2},{1,3},{2,0},{3,1},{4,6},{5,7},{6,4},{7,5},{8,10},{9,11},{10,... | collective-permute-start | bytes 1572872 | tf_op jit(solution)/shard_map/ppermute | solution.py:96
  266.5 26.8 %copy-start.26 = (bf16[2048,128]{1,0:T(8,128)(2,1)S(1)}, bf16[2048,128]{1,0:T(8,128)(2,1)}, u32[]{:S(2)}) copy-start(bf16[2048,128]{1,0:T(8,128)(2,1)} %get-tuple-element.117) | copy-start | bytes 1572868
  266.6 58.5 %collective-permute-start.28 = (bf16[588,512]{1,0:T(8,128)(2,1)S(1)}, bf16[588,512]{1,0:T(8,128)(2,1)S(1)}, u32[]{:S(2)}, u32[]{:S(2)}) collective-permute-start(bf16[588,512]{1,0:T(8,128)(2,1)S(1)} %get-tuple-element.163), channel_id=1, source_target_pairs={{0,1},{1,2},{2,3},{4,5},{5,6},{6,7},{8,9},{9,10},{10,11},{12,13},{... | collective-permute-start | bytes 1806344 | tf_op jit(solution)/shard_map/ppermute | solution.py:115
  277.3 41.5 %collective-permute-start.26 = (bf16[384,512]{1,0:T(8,128)(2,1)S(1)}, bf16[384,512]{1,0:T(8,128)(2,1)S(1)}, u32[]{:S(2)}, u32[]{:S(2)}) collective-permute-start(bf16[384,512]{1,0:T(8,128)(2,1)S(1)} %copy-done.28), channel_id=1, source_target_pairs={{0,1},{1,2},{2,3},{4,5},{5,6},{6,7},{8,9},{9,10},{10,11},{12,13},{... | collective-permute-start | bytes 1179656 | tf_op jit(solution)/shard_map/ppermute | solution.py:115
  294.5 8.0 %collective-permute-start.47 = (bf16[1296,128]{1,0:T(8,128)(2,1)S(1)}, bf16[1296,128]{1,0:T(8,128)(2,1)S(1)}, u32[]{:S(2)}, u32[]{:S(2)}) collective-permute-start(bf16[1296,128]{1,0:T(8,128)(2,1)S(1)} %get-tuple-element.143), channel_id=1, source_target_pairs={{0,4},{4,0},{8,12},{12,8},{16,20},{20,16},{24,28},{28,24},{1,5},{5... | collective-permute-start | bytes 995336 | tf_op jit(solution)/shard_map/ppermute | solution.py:76
  295.0 25.0 %collective-permute-start.14 = (bf16[588,512]{1,0:T(8,128)(2,1)S(1)}, bf16[588,512]{1,0:T(8,128)(2,1)S(1)}, u32[]{:S(2)}, u32[]{:S(2)}) collective-permute-start(bf16[588,512]{1,0:T(8,128)(2,1)S(1)} %get-tuple-element.165), channel_id=1, source_target_pairs={{0,1},{1,2},{2,3},{4,5},{5,6},{6,7},{8,9},{9,10},{10,11},{12,13},{... | collective-permute-start | bytes 1806344 | tf_op jit(solution)/shard_map/ppermute | solution.py:115
  297.7 11.9 %collective-permute-start.49 = (bf16[1296,128]{1,0:T(8,128)(2,1)S(1)}, bf16[1296,128]{1,0:T(8,128)(2,1)S(1)}, u32[]{:S(2)}, u32[]{:S(2)}) collective-permute-start(bf16[1296,128]{1,0:T(8,128)(2,1)S(1)} %get-tuple-element.145), channel_id=1, source_target_pairs={{0,4},{4,0},{8,12},{12,8},{16,20},{20,16},{24,28},{28,24},{1,5},{5... | collective-permute-start | bytes 995336 | tf_op jit(solution)/shard_map/ppermute | solution.py:76
  302.5 14.2 %collective-permute-start.51 = (bf16[1296,128]{1,0:T(8,128)(2,1)S(1)}, bf16[1296,128]{1,0:T(8,128)(2,1)S(1)}, u32[]{:S(2)}, u32[]{:S(2)}) collective-permute-start(bf16[1296,128]{1,0:T(8,128)(2,1)S(1)} %get-tuple-element.147), channel_id=1, source_target_pairs={{0,4},{4,0},{8,12},{12,8},{16,20},{20,16},{24,28},{28,24},{1,5},{5... | collective-permute-start | bytes 995336 | tf_op jit(solution)/shard_map/ppermute | solution.py:76
  309.6 17.8 %collective-permute-start.53 = (bf16[1296,128]{1,0:T(8,128)(2,1)S(1)}, bf16[1296,128]{1,0:T(8,128)(2,1)S(1)}, u32[]{:S(2)}, u32[]{:S(2)}) collective-permute-start(bf16[1296,128]{1,0:T(8,128)(2,1)S(1)} %get-tuple-element.149), channel_id=1, source_target_pairs={{0,4},{4,0},{8,12},{12,8},{16,20},{20,16},{24,28},{28,24},{1,5},{5... | collective-permute-start | bytes 995336 | tf_op jit(solution)/shard_map/ppermute | solution.py:76
  316.7 23.4 %collective-permute-start.48 = (bf16[1296,128]{1,0:T(8,128)(2,1)S(1)}, bf16[1296,128]{1,0:T(8,128)(2,1)S(1)}, u32[]{:S(2)}, u32[]{:S(2)}) collective-permute-start(bf16[1296,128]{1,0:T(8,128)(2,1)S(1)} %add_convert_fusion.12), channel_id=1, source_target_pairs={{0,8},{4,12},{8,16},{12,20},{16,24},{20,28},{24,0},{28,4},{1,9},{5... | collective-permute-start | bytes 995336 | tf_op jit(solution)/shard_map/ppermute | solution.py:79
  318.8 28.5 %collective-permute-start.50 = (bf16[1296,128]{1,0:T(8,128)(2,1)S(1)}, bf16[1296,128]{1,0:T(8,128)(2,1)S(1)}, u32[]{:S(2)}, u32[]{:S(2)}) collective-permute-start(bf16[1296,128]{1,0:T(8,128)(2,1)S(1)} %add_convert_fusion.11), channel_id=1, source_target_pairs={{0,16},{4,20},{8,24},{12,28},{16,0},{20,4},{24,8},{28,12},{1,17},{... | collective-permute-start | bytes 995336 | tf_op jit(solution)/shard_map/ppermute | solution.py:79
  320.0 29.5 %collective-permute-start.52 = (bf16[1296,128]{1,0:T(8,128)(2,1)S(1)}, bf16[1296,128]{1,0:T(8,128)(2,1)S(1)}, u32[]{:S(2)}, u32[]{:S(2)}) collective-permute-start(bf16[1296,128]{1,0:T(8,128)(2,1)S(1)} %add_convert_fusion.10), channel_id=1, source_target_pairs={{0,24},{4,28},{8,0},{12,4},{16,8},{20,12},{24,16},{28,20},{1,25},{... | collective-permute-start | bytes 995336 | tf_op jit(solution)/shard_map/ppermute | solution.py:79
  (34 other events, 155.5 us)

commit v3 on v2

v3 whole, which is shorter than its diff:
```python
import jax
import jax.numpy as jnp
from jax import lax
from jax.experimental import pallas as pl
from jax.experimental.pallas import tpu as pltpu
from jax.sharding import PartitionSpec as P

D = 512
HEADS = 8
HEAD_DIM = 64
FF = 1024
TILE = 128
CHUNK = 16
CHUNKS = 5

NORM_EPSILON = 1e-05
MATRIX_RATE = 0.5
VECTOR_RATE = 0.2
STAT_DECAY = 0.5
MASKED_SCORE = -1e30

F32 = jnp.float32
BF16 = jnp.bfloat16
ANY = pl.BlockSpec(memory_space=pl.ANY)
VM = pl.BlockSpec(memory_space=pltpu.VMEM)
SM = pl.BlockSpec(memory_space=pltpu.SMEM)
HB = pl.BlockSpec(memory_space=pltpu.HBM)


def core_pairs():
    return [(i, i ^ 1) for i in range(4)]


def chip_pairs():
    return [(i, i ^ 2) for i in range(4)]


def y_pairs():
    return [(i, i ^ 1) for i in range(8)]


def z_shift(step):
    return [(2 * z + y, 2 * ((z + step) % 4) + y) for z in range(4) for y in range(2)]


def relative_rank(position, size):
    me = lax.axis_index("dp")
    if size != 8:
        return jnp.int32(position)
    swapped, step = divmod(position, 4)
    return 2 * lax.rem(me // 2 - step + 4, 4) + lax.rem(me + swapped, 2)


def target_rank(position, size):
    me = lax.axis_index("dp")
    if size != 8:
        return jnp.int32(position)
    swapped, step = divmod(position, 4)
    return 2 * lax.rem(me // 2 + step, 4) + lax.rem(me + swapped, 2)


def gather_pieces(piece, size):
    if size != 8:
        return list(lax.all_gather(piece, "dp", axis=0, tiled=False))
    z = {step: lax.ppermute(piece, "dp", z_shift(step)) for step in (1, 2, 3)}
    other = lax.ppermute(piece, "dp", y_pairs())
    y3 = lax.ppermute(lax.optimization_barrier((z[3], other))[0], "dp", y_pairs())
    y1 = lax.ppermute(lax.optimization_barrier((z[1], other))[0], "dp", y_pairs())
    y2 = lax.ppermute(lax.optimization_barrier((z[2], y3))[0], "dp", y_pairs())
    return [piece, z[1], z[2], z[3], other, y1, y2, y3]


def sum_pieces(pieces, size):
    if size != 8:
        whole = lax.psum_scatter(
            jnp.stack(pieces).astype(F32), "dp", scatter_dimension=0, tiled=False
        )
        return [whole.astype(BF16)], pieces[0]
    column, ready, mark = [pieces[0]], [], None
    for at, step in enumerate((2, 1, 3, 0)):
        piece = pieces[4 + step]
        if at > 1:
            piece = lax.optimization_barrier((piece, ready[at - 2]))[0]
        other = lax.ppermute(piece, "dp", y_pairs())
        if step == 0:
            column.append(other)
            continue
        both = (pieces[step].astype(F32) + other.astype(F32)).astype(BF16)
        ready.append(both)
        column.append(lax.ppermute(both, "dp", z_shift(step)))
    return column, pieces[0]


def send_near(part):
    return lax.ppermute(part[1], "tensor", core_pairs())


def sum_far(part, near):
    rows = CHUNK * TILE
    return (part[2].astype(F32) + near[rows : rows + part[2].shape[0]].astype(F32)).astype(BF16)


def send_far(value):
    return lax.ppermute(value, "tensor", chip_pairs())


def pull_rows(arrays, lengths, me, keep):
    shards = lax.axis_size("tensor")
    later = lax.ppermute(
        jnp.concatenate(arrays, axis=0), "tensor", [(i + 1, i) for i in range(shards - 1)]
    )
    n = len(arrays)

    def kernel(me_ref, *refs):
        owns, more, outs = refs[:n], refs[n], refs[n + 1 :]
        for t in range(shards):

            @pl.when(me_ref[0, 0] == t)
            def _(t=t):
                first = 0
                for own, out, length in zip(owns, outs, lengths):
                    rows = own.shape[0]
                    first += rows
                    if t == shards - 1:
                        if keep:
                            both = jnp.concatenate([own[...].astype(F32), own[...].astype(F32)[: length - rows, :]], axis=0)
                        else:
                            both = jnp.zeros(out.shape, F32)
                    else:
                        start = (length - rows) * t
                        both = jnp.concatenate(
                            [
                                own[...].astype(F32)[start:, :],
                                more[...].astype(F32)[first - rows : first - rows + length - rows + start, :],
                            ],
                            axis=0,
                        )
                    out[...] = both.astype(BF16)

    return pl.pallas_call(
        kernel,
        out_shape=[jax.ShapeDtypeStruct((length, D), BF16) for length in lengths],
        in_specs=[SM] + [VM] * (n + 1),
        out_specs=[VM] * n,
        compiler_params=pltpu.CompilerParams(vmem_limit_bytes=24 * 2**20),
        name="pull_rows",
    )(me, *arrays, later)


def push_rows(items, tails, counts, dtypes, me):
    shards = lax.axis_size("tensor")
    earlier = [
        lax.ppermute(a, "tensor", [(i, i + 1) for i in range(shards - 1)]) for a in tails
    ]
    n = len(items)

    def kernel(me_ref, *refs):
        owns, befores, outs = refs[:n], refs[n : 2 * n], refs[2 * n :]
        for t in range(shards):

            @pl.when(me_ref[0, 0] == t)
            def _(t=t):
                for own, before, out in zip(owns, befores, outs):
                    count, length = out.shape[0], own.shape[0]
                    mine = count - (length - count) * t
                    rows = own[...].astype(F32)[:mine, :]
                    if t:
                        skip = before.shape[0] - count + mine
                        rows = jnp.concatenate([before[...].astype(F32)[skip:, :], rows], axis=0) if mine else before[...].astype(F32)[skip:, :]
                    out[...] = rows.astype(out.dtype)

    return pl.pallas_call(
        kernel,
        out_shape=[jax.ShapeDtypeStruct((c, D), d) for c, d in zip(counts, dtypes)],
        in_specs=[SM] + [VM] * (2 * n),
        out_specs=[VM] * n,
        compiler_params=pltpu.CompilerParams(vmem_limit_bytes=24 * 2**20),
        name="push_rows",
    )(me, *items, *earlier)


def order_tiles(pieces, block_ids, slots):
    total = CHUNK * CHUNKS

    def kernel(ids, *refs):
        sources, out = refs[:-1], refs[-1]
        for p, source in enumerate(sources):
            for j in range(slots):
                block = ids[0, p * slots + j]

                @pl.when(block < total)
                def _(source=source, j=j, block=block):
                    out[pl.ds(pl.multiple_of(block * TILE, TILE), TILE), :] = source[
                        j * TILE : (j + 1) * TILE, :
                    ]

    return pl.pallas_call(
        kernel,
        out_shape=jax.ShapeDtypeStruct((total * TILE, TILE), BF16),
        in_specs=[SM] + [VM] * len(pieces),
        out_specs=VM,
        compiler_params=pltpu.CompilerParams(vmem_limit_bytes=16 * 2**20),
        name="order_tiles",
    )(block_ids, *pieces)


def sum_chunks(sums, after):
    part = CHUNK * TILE
    count = len(sums)

    def kernel(*refs):
        sources, out = refs[: 3 * count], refs[3 * count + 1]
        for c in range(count):
            own, near, far = sources[3 * c : 3 * c + 3]
            out[c * part : (c + 1) * part, :] = (
                own[...].astype(F32) + near[...].astype(F32) + far[...].astype(F32)
            ).astype(BF16)

    flat = [(own, near, far) for own, near, far in sums]
    return call(
        kernel,
        "sum_chunks",
        [Held(struct((count * part, TILE), BF16))],
        [],
        *[Part((a, 0, part)) for chunk in flat for a in chunk],
        Part((after, 0, TILE)),
    )[0]


def deal_tiles(chunk, early, extra, block_ids, ranks, slots, lanes):
    count = ranks.shape[1]
    total = CHUNK * CHUNKS
    part = CHUNK * TILE
    rows = slots * TILE + 16

    def kernel(ids, to, own, near, near_extra, far, v_ref, rest, *refs):
        outs, held = refs[:-1], refs[-1]
        held[:part, :] = (
            own[...].astype(F32) + near[...].astype(F32) + far[:part, :].astype(F32)
        ).astype(BF16)
        held[part : total * TILE, :] = rest[...]
        held[total * TILE :, :] = jnp.zeros((TILE, TILE), BF16)
        summed = (
            v_ref[...].astype(F32) + near_extra[...].astype(F32) + far[part:, :].astype(F32)
        ).astype(BF16)
        summed = jnp.concatenate([summed[16 * j : 16 * (j + 1)] for j in range(4)], axis=1)
        feature = lax.broadcasted_iota(jnp.int32, (D, TILE), 0)
        lane = lax.broadcasted_iota(jnp.int32, (D, TILE), 1)
        for p, out in enumerate(outs):
            for j in range(slots):
                block = jnp.minimum(ids[0, p * slots + j], total)
                out[j * TILE : (j + 1) * TILE, :] = held[
                    pl.ds(pl.multiple_of(block * TILE, TILE), TILE), :
                ]
            pick = ((feature == to[0, p] * lanes + lane) & (lane < lanes)).astype(BF16)
            out[slots * TILE :, :] = matmul(summed, pick).astype(BF16)

    own, near, far = chunk
    return call(
        kernel,
        "deal_tiles",
        [struct((rows, TILE), BF16)] * count,
        [pltpu.VMEM(((total + 1) * TILE, TILE), BF16)],
        block_ids,
        ranks,
        Part((own, 0, part)),
        Part((near, 0, part)),
        Part((near, 2 * part, VECTOR_ROWS)),
        Part((far, 0, part + VECTOR_ROWS)),
        Held(extra),
        Held(early),
    )


def shampoo(terms, master, left, right, left_root, right_root, vector_master, vector_moment):
    slots = master.shape[1]
    lanes = vector_master.shape[1]

    def exact(a, b, dims):
        return lax.dot_general(
            a, b, (dims, ((), ())), precision=lax.Precision.HIGHEST, preferred_element_type=F32
        )

    def kernel(*refs):
        parts, refs = refs[: len(terms)], refs[len(terms) :]
        m_ref, l_ref, r_ref, lr_ref, rr_ref, vm_ref, vn_ref = refs[:7]
        g_out, l_out, r_out, m_out, c_out, vg_out, vn_out, vm_out = refs[7:]

        def rows_at(a, b):
            total = parts[0][a:b, :].astype(F32)
            for part in parts[1:]:
                total = total + part[a:b, :].astype(F32)
            return total

        for s in range(slots):
            g = rows_at(s * TILE, (s + 1) * TILE)
            g_out[0, s] = g
            l_out[0, s] = STAT_DECAY * l_ref[0, s] + (1.0 - STAT_DECAY) * exact(g, g, ((1,), (1,)))
            r_out[0, s] = STAT_DECAY * r_ref[0, s] + (1.0 - STAT_DECAY) * exact(g, g, ((0,), (0,)))
            rotated = exact(lr_ref[0, s], g, ((1,), (0,)))
            updated = m_ref[0, s] - MATRIX_RATE * exact(rotated, rr_ref[0, s], ((1,), (0,)))
            m_out[0, s] = updated
            c_out[0, s] = updated.astype(BF16)
        g = rows_at(slots * TILE, slots * TILE + 16)[:10, :lanes]
        moment = STAT_DECAY * vn_ref[...] + (1.0 - STAT_DECAY) * g * g
        vg_out[...] = g
        vn_out[...] = moment
        vm_out[...] = vm_ref[...] - VECTOR_RATE * g / (jnp.sqrt(moment) + 1e-08)

    whole = jax.ShapeDtypeStruct(master.shape, F32)
    row = jax.ShapeDtypeStruct(vector_master.shape, F32)
    outs = [whole] * 4 + [jax.ShapeDtypeStruct(master.shape, BF16)] + [row] * 3
    return pl.pallas_call(
        kernel,
        out_shape=outs,
        in_specs=[VM] * (len(terms) + 7),
        out_specs=[VM] * len(outs),
        compiler_params=pltpu.CompilerParams(vmem_limit_bytes=24 * 2**20),
        name="shampoo",
    )(*terms, master, left, right, left_root, right_root, vector_master, vector_moment)


LOG2E = 1.4426950408889634
SCORE_SCALE = HEAD_DIM ** (-0.5)
SCORE_LOG2 = SCORE_SCALE * LOG2E
PAIRS = HEADS // 2


def matmul(former, latter):
    return jnp.dot(former, latter, preferred_element_type=F32)


def times_transpose(former, latter):
    return lax.dot_general(former, latter, (((1,), (1,)), ((), ())), preferred_element_type=F32)


def transpose_times(former, latter):
    return lax.dot_general(former, latter, (((0,), (0,)), ((), ())), preferred_element_type=F32)


def low(value):
    return value.astype(BF16)


def tile_at(part, index):
    return part[index * TILE : (index + 1) * TILE, :]


def column_matrix(parts, first, count, column):
    return jnp.concatenate(
        [
            jnp.concatenate([tile_at(p, first + a * count + column) for p in parts], axis=1)
            for a in range(4)
        ],
        axis=0,
    )


def row_matrix(parts, first, group):
    return jnp.concatenate(
        [
            jnp.concatenate([tile_at(p, first + 4 * group + b) for b in range(4)], axis=1)
            for p in parts
        ],
        axis=0,
    )


def store_columns(parts, gradient, first, count, column):
    for r, part in enumerate(parts):
        for a in range(4):
            at = (first + a * count + column) * TILE
            part[at : at + TILE, :] = low(
                gradient[a * TILE : (a + 1) * TILE, r * TILE : (r + 1) * TILE]
            )


def store_rows(parts, gradient, first, group):
    for r, part in enumerate(parts):
        for b in range(4):
            at = (first + 4 * group + b) * TILE
            part[at : at + TILE, :] = low(
                gradient[r * TILE : (r + 1) * TILE, b * TILE : (b + 1) * TILE]
            )


def spans(count):
    half = (count // 2 + 15) // 16 * 16
    return [(0, half), (half, count)]


def norm_rows(value):
    mean = jnp.mean(value, axis=-1, keepdims=True)
    centered = value - mean
    scale = lax.rsqrt(jnp.mean(centered * centered, axis=-1, keepdims=True) + NORM_EPSILON)
    return centered * scale, scale


def norm_back(gradient, normed, scale, gain):
    scaled = gradient * gain
    return scale * (
        scaled
        - jnp.mean(scaled, axis=-1, keepdims=True)
        - normed * jnp.mean(scaled * normed, axis=-1, keepdims=True)
    )


def gate_both(value):
    size = jnp.abs(value) * (0.5**0.5)
    turn = 1.0 / (1.0 + 0.3275911 * size)
    bell = jnp.exp2(value * value * (-0.5 * LOG2E))
    series = turn * (
        0.254829592
        + turn * (-0.284496736 + turn * (1.421413741 + turn * (-1.453152027 + turn * 1.061405429)))
    )
    tail = 0.5 * series * bell
    phi = jnp.where(value < 0, tail, 1.0 - tail)
    return value * phi, phi + value * bell * 0.3989422804014327


STATS = 16


def store_stats(stat_ref, stats, scale):
    lane = lax.broadcasted_iota(jnp.int32, stats.shape, 1)
    stat_ref[...] = jnp.where(lane == HEADS, scale, stats).T[:STATS, :]


def norm_scale(stat_ref):
    return jnp.concatenate([stat_ref[...]] * (TILE // STATS), axis=0).T[:, HEADS : HEADS + 1]


def half_mask(which):
    lane = lax.broadcasted_iota(jnp.int32, (1, TILE), 1)
    return (lane < HEAD_DIM) if which == 0 else (lane >= HEAD_DIM)


def attend_pairs(q_ref, k_ref, v_ref, o_ref, bias):
    count = q_ref.shape[0]
    keys = k_ref.shape[0]
    ones = jnp.ones((keys, TILE), BF16)
    lane = lax.broadcasted_iota(jnp.int32, (count, TILE), 1)
    stats = jnp.zeros((count, TILE), F32)
    for pair in range(PAIRS):
        cut = slice(pair * TILE, (pair + 1) * TILE)
        queries, key_rows = q_ref[:, cut], k_ref[:, cut]
        values = jnp.concatenate([v_ref[:, cut], ones], axis=1)
        mixed = []
        for which in range(2):
            masked = jnp.where(half_mask(which), queries, jnp.zeros_like(queries))
            scores = times_transpose(masked, key_rows) * SCORE_LOG2
            if bias is not None:
                scores = scores + bias
            top = jnp.max(scores, axis=1, keepdims=True)
            weights = low(jnp.exp2(scores - top))
            both = matmul(weights, values)
            total = both[:, TILE:]
            mixed.append(both[:, :TILE] / total)
            stats = jnp.where(lane == 2 * pair + which, top + jnp.log2(total), stats)
        o_ref[:, cut] = low(jnp.where(half_mask(0), mixed[0], mixed[1]))
    return stats


def pair_back(queries, key_rows, value_rows, incoming, stats, deltas, bias):
    key_columns = key_rows.T
    dk = dv = None
    dq = []
    for which in range(2):
        mask = half_mask(which)
        q_one = jnp.where(mask, queries, jnp.zeros_like(queries))
        do_one = jnp.where(mask, incoming, jnp.zeros_like(incoming))
        scores = times_transpose(key_rows, q_one) * SCORE_LOG2
        if bias is not None:
            scores = scores + bias
        weights = jnp.exp2(scores - stats[which])
        d_weights = times_transpose(value_rows, do_one)
        d_scores = low(weights * (d_weights - deltas[which]))
        dv_one = matmul(low(weights), do_one)
        dk_one = matmul(d_scores, q_one)
        dv = dv_one if dv is None else dv + dv_one
        dk = dk_one if dk is None else dk + dk_one
        rows = slice(which * HEAD_DIM, (which + 1) * HEAD_DIM)
        dq.append(low(matmul(key_columns[rows, :], d_scores) * SCORE_SCALE))
    return jnp.concatenate(dq, axis=0).T, low(dk * SCORE_SCALE), low(dv)


def pair_columns(pair):
    return slice(pair * TILE, (pair + 1) * TILE)


def pair_rows(ref, pair):
    return [ref[h : h + 1, :] for h in (2 * pair, 2 * pair + 1)]


def row_products(incoming, mixed):
    product = incoming * mixed
    first = low(product)
    rest = low(product - first.astype(F32))
    lane = lax.broadcasted_iota(jnp.int32, (TILE, D), 1) // HEAD_DIM
    row = lax.broadcasted_iota(jnp.int32, (TILE, D), 0)
    pick = (lane == row).astype(BF16)
    return times_transpose(pick, first) + times_transpose(pick, rest)


def struct(shape, dtype):
    return jax.ShapeDtypeStruct(shape, dtype)


class Inward:
    def __init__(self, source, held, sem):
        self.shape = held.shape
        self.copy, self.held, self.waiting = pltpu.make_async_copy(source, held, sem), held, True
        self.copy.start()

    def wait(self):
        if self.waiting:
            self.copy.wait()
            self.waiting = False

    def __getitem__(self, index):
        self.wait()
        return self.held[index]


class Outward:
    def __init__(self, held, target, sem):
        self.held, self.target, self.sem, self.copies = held, target, sem, []
        self.shape, self.dtype = held.shape, held.dtype

    @property
    def at(self):
        return self.held.at

    def __getitem__(self, index):
        return self.held[index]

    def __setitem__(self, index, value):
        self.held[index] = value

    def send(self, *spans_of):
        for a, b in spans_of or ((0, self.shape[0]),):
            rows = pl.ds(a, b - a)
            copy = pltpu.make_async_copy(
                self.held.at[rows], self.target.at[rows], self.sem.at[len(self.copies)]
            )
            copy.start()
            self.copies.append(copy)

    def finish(self):
        if not self.copies:
            self.send()


SENDS = 4


class Part(tuple):
    pass


class Held:
    def __init__(self, array):
        self.array = array


def call(kernel, name, outs, scratch, *args, flops=0, limit=56):
    plain, held, takes = [], [], []
    for arg in args:
        part = None
        if isinstance(arg, Held):
            plain.append(pltpu.with_memory_space_constraint(arg.array, pltpu.VMEM))
            takes.append(None)
            continue
        free = isinstance(arg, Part)
        if isinstance(arg, tuple):
            arg, *part = arg
        if arg.dtype == jnp.int32:
            plain.append(arg)
            takes.append(None)
            continue
        plain.append(arg if free else pltpu.with_memory_space_constraint(arg, pltpu.HBM))
        if part is None:
            part = (0, arg.shape[0])
        columns = part[2] if len(part) > 2 else slice(0, arg.shape[1])
        takes.append((part[0], part[1], columns, free))
        held.append(pltpu.VMEM((part[1], columns.stop - columns.start), arg.dtype))
    n, m = len(plain), len(outs)
    sent = [o for o in outs if not isinstance(o, Held)]

    def body(*refs):
        sources, targets, rest = refs[:n], refs[n : n + m], refs[n + m :]
        in_held, rest = list(rest[: len(held)]), rest[len(held) :]
        out_held, rest = list(rest[: len(sent)]), rest[len(sent) :]
        in_sem, out_sem, rest = rest[0], rest[1], rest[2:]
        ins = []
        for source, take in zip(sources, takes):
            if take is None:
                ins.append(source)
                continue
            first, rows, columns, _ = take
            source = source.at[pl.ds(first, rows), pl.ds(columns.start, columns.stop - columns.start)]
            at = len(held) - len(in_held)
            ins.append(Inward(source, in_held.pop(0), in_sem.at[at]))
        finished = []
        for out, target in zip(outs, targets):
            if not isinstance(out, Held):
                at = len(sent) - len(out_held)
                target = Outward(out_held.pop(0), target, out_sem.at[at])
            finished.append(target)
        kernel(*ins, *finished, *rest)
        for value in ins:
            if isinstance(value, Inward):
                value.wait()
        finished = [f for f in finished if isinstance(f, Outward)]
        for out in finished:
            out.finish()
        for out in finished:
            for copy in out.copies:
                copy.wait()

    shapes = [pltpu.VMEM(o.array.shape, o.array.dtype) if isinstance(o, Held) else pltpu.HBM(o.shape, o.dtype) for o in outs]
    return pl.pallas_call(
        body,
        out_shape=shapes,
        in_specs=[
            SM if a.dtype == jnp.int32 else VM if take is None else ANY if take[3] else HB for a, take in zip(plain, takes)
        ],
        out_specs=[VM if isinstance(o, Held) else HB for o in outs],
        scratch_shapes=[
            *held,
            *[pltpu.VMEM(o.shape, o.dtype) for o in sent],
            pltpu.SemaphoreType.DMA((max(1, len(held)),)),
            pltpu.SemaphoreType.DMA((max(1, len(sent)), SENDS)),
            *scratch,
        ],
        compiler_params=pltpu.CompilerParams(vmem_limit_bytes=limit * 2**20),
        cost_estimate=pl.CostEstimate(flops=flops, bytes_accessed=4000000, transcendentals=0),
        name=name,
    )(*plain)


def part_outs():
    rows = CHUNK * TILE
    return [struct((rows, TILE), BF16), struct((2 * rows, TILE), BF16), struct((rows, TILE), BF16)]


def four_parts(own, near, far):
    rows = CHUNK * TILE
    return (own, near.at[pl.ds(0, rows)], far, near.at[pl.ds(rows, rows)])


def rows_of(chunk, first=0, count=CHUNK):
    own, near, far, far_near, at = chunk
    start = (at * CHUNK + first) * TILE
    size = count * TILE
    return [
        Part((own, start, size)),
        Part((near, start, size)),
        Part((far, first * TILE, size)),
        Part((far_near, first * TILE, size)),
    ]


def causal_bias(count, live, queries_on_rows):
    a = lax.broadcasted_iota(jnp.int32, (count, count), 0)
    b = lax.broadcasted_iota(jnp.int32, (count, count), 1)
    query, key = (a, b) if queries_on_rows else (b, a)
    return jnp.where((key <= query) & (key < live), 0.0, MASKED_SCORE)


def self_forward(x, parts, vectors, norm, live=None):
    rows = x.shape[0]

    def kernel(*refs):
        if live is not None:
            live_ref, *refs = refs
        x_ref, p0, p1, p2, p3, g_ref, first_ref, low_ref, hat_ref, q_ref, k_ref, v_ref, o_ref, stat_ref = refs
        ps = (p0, p1, p2, p3)
        tokens = x_ref[...]
        for column, ref in enumerate((q_ref, k_ref, v_ref)):
            ref[...] = low(matmul(tokens, column_matrix(ps, 0, 3, column)))
            ref.send()
        bias = None if live is None else causal_bias(rows, live_ref[0, 0], True)
        stats = attend_pairs(q_ref, k_ref, v_ref, o_ref, bias)
        o_ref.send()
        wo = row_matrix(ps, 12, 0)
        scales = []
        for a, b in spans(rows):
            hat, scale = norm_rows(tokens[a:b].astype(F32) + matmul(o_ref[a:b, :], wo))
            first = hat * g_ref[2 * norm : 2 * norm + 1, :] + g_ref[2 * norm + 1 : 2 * norm + 2, :]
            first_ref[a:b, :] = first
            low_ref[a:b, :] = low(first)
            hat_ref[a:b, :] = low(hat)
            for out in (hat_ref, low_ref):
                out.send((a, b))
            scales.append(scale)
        store_stats(stat_ref, stats, jnp.concatenate(scales, axis=0))

    outs = [Held(struct((rows, D), F32))] + [struct((rows, D), BF16)] * 6 + [struct((STATS, rows), F32)]
    args = ([] if live is None else [live]) + [x, *rows_of(parts), vectors]
    return call(kernel, f"self_forward_{norm}", outs, [], *args, flops=10**10)


def ffn_weights(ps):
    w1 = jnp.concatenate([column_matrix(ps, 0, 2, c) for c in range(2)], axis=1)
    w2 = jnp.concatenate([row_matrix(ps, 8, c) for c in range(2)], axis=0)
    return w1, w2


def tail_rows(length, count):
    return (length - count) // 16 * 16


def column_as_row(column):
    return jnp.broadcast_to(column, (column.shape[0], TILE)).T[:8, :]


def row_as_column(ref):
    return jnp.concatenate([ref[...]] * STATS, axis=0).T[:, :1]


def ffn_forward(first, parts, vectors, norm, tail):
    rows = first.shape[0]

    def kernel(f_ref, p0, p1, p2, p3, g_ref, enc_ref, hat_ref, scale_ref, hid_ref, slope_ref, tail_ref):
        w1, w2 = ffn_weights((p0, p1, p2, p3))
        scales = []
        for a, b in spans(rows):
            first_rows = f_ref[a:b, :]
            value, slope = gate_both(matmul(low(first_rows), w1))
            value = low(value)
            hid_ref[a:b, :] = value
            hid_ref.send((a, b))
            slope_ref[a:b, :] = low(slope)
            slope_ref.send((a, b))
            hat, scale = norm_rows(first_rows + matmul(value, w2))
            enc_ref[a:b, :] = low(hat * g_ref[2 * norm : 2 * norm + 1, :] + g_ref[2 * norm + 1 : 2 * norm + 2, :])
            hat_ref[a:b, :] = low(hat)
            for out in (hat_ref, enc_ref):
                out.send((a, b))
            scales.append(scale)
        tail_ref[...] = enc_ref[tail:, :]
        scale_ref[...] = column_as_row(jnp.concatenate(scales, axis=0))

    outs = [struct((rows, D), BF16), struct((rows, D), BF16), struct((8, rows), F32)]
    outs += [struct((rows, FF), BF16)] * 2 + [struct((rows - tail, D), BF16)]
    return call(kernel, f"ffn_forward_{norm}", outs, [], Held(first), *rows_of(parts), vectors, flops=3 * 10**9)


def cross_forward(second, encoded, parts, vectors):
    rows, keys = second.shape[0], encoded.shape[0]

    def kernel(s_ref, p0, p1, p2, p3, e_ref, g_ref, third_ref, hat_ref, q_ref, k_ref, v_ref, o_ref, stat_ref):
        ps = (p0, p1, p2, p3)
        q_ref[...] = low(matmul(low(s_ref[...]), column_matrix(ps, 0, 1, 0)))
        k_ref[...] = low(matmul(e_ref[...], column_matrix(ps, 4, 2, 0)))
        v_ref[...] = low(matmul(e_ref[...], column_matrix(ps, 4, 2, 1)))
        for ref in (q_ref, k_ref, v_ref):
            ref.send()
        stats = attend_pairs(q_ref, k_ref, v_ref, o_ref, None)
        o_ref.send()
        hat, scale = norm_rows(s_ref[...] + matmul(o_ref[...], row_matrix(ps, 12, 0)))
        third_ref[...] = hat * g_ref[6:7, :] + g_ref[7:8, :]
        hat_ref[...] = low(hat)
        hat_ref.send()
        store_stats(stat_ref, stats, scale)

    outs = [Held(struct((rows, D), F32)), struct((rows, D), BF16)]
    outs += [struct((rows, D), BF16), struct((keys, D), BF16), struct((keys, D), BF16)]
    outs += [struct((rows, D), BF16), struct((STATS, rows), F32)]
    return call(kernel, "cross_forward", outs, [], Held(second), *rows_of(parts), encoded, vectors, flops=5 * 10**9)


def store_norm(ref, gradient, hat):
    ref[0:1, :] = jnp.sum(gradient * hat, axis=0, keepdims=True)
    ref[1:2, :] = jnp.sum(gradient, axis=0, keepdims=True)


def send_parts(outs, first, count):
    a, b, rows = first * TILE, (first + count) * TILE, CHUNK * TILE
    own, near, far = outs
    near.send((a, b), (rows + a, rows + b))
    far.send((a, b))
    own.send((a, b))


def ffn_weight_gradients(inputs, hid_ref, dh_ref, db_ref, grads, outs):
    for c in range(2):
        store_columns(grads, transpose_times(inputs, dh_ref[:, c * D : (c + 1) * D]), 0, 2, c)
    send_parts(outs, 0, 8)
    for c in range(2):
        store_rows(grads, transpose_times(hid_ref[:, c * D : (c + 1) * D], db_ref[...]), 8, c)
    send_parts(outs, 8, 8)


def ffn_both(third, cotangent, live, parts, vectors, tail):
    rows = third.shape[0]

    def kernel(live_ref, t_ref, p0, p1, p2, p3, g_ref, c_ref, dec_ref, tail_ref, back_ref, n_ref, d0, d1, d2, hid_ref, dh_ref, db_ref):
        w1, w2 = ffn_weights((p0, p1, p2, p3))
        grads = four_parts(d0, d1, d2)
        gain = g_ref[8:9, :]
        for part, (a, b) in enumerate(spans(rows)):
            third_rows = t_ref[a:b, :]
            value, slope = gate_both(matmul(low(third_rows), w1))
            value = low(value)
            hid_ref[a:b, :] = value
            hat, scale = norm_rows(third_rows + matmul(value, w2))
            dec_ref[a:b, :] = low(hat * gain + g_ref[9:10, :])
            row = lax.broadcasted_iota(jnp.int32, (b - a, 1), 0) + a
            incoming = jnp.where(row < live_ref[0, 0], c_ref[a:b, :].astype(F32), 0.0)
            if part == 0:
                n_ref[...] = jnp.zeros_like(n_ref)
            n_ref[0:1, :] += jnp.sum(incoming * hat, axis=0, keepdims=True)
            n_ref[1:2, :] += jnp.sum(incoming, axis=0, keepdims=True)
            back = norm_back(incoming, hat, scale, gain)
            back_low = low(back)
            db_ref[a:b, :] = back_low
            dh = low(slope * times_transpose(back_low, w2))
            dh_ref[a:b, :] = dh
            back_ref[a:b, :] = back + times_transpose(dh, w1)
            dec_ref.send((a, b))
        tail_ref[...] = dec_ref[tail:, :]
        tail_ref.send()
        ffn_weight_gradients(low(t_ref[...]), hid_ref, dh_ref, db_ref, grads, (d0, d1, d2))

    outs = [struct((rows, D), BF16), struct((rows - tail, D), BF16), Held(struct((rows, D), F32))]
    outs += [struct((8, D), F32)] + part_outs()
    scratch = [pltpu.VMEM((rows, FF), BF16), pltpu.VMEM((rows, FF), BF16), pltpu.VMEM((rows, D), BF16)]
    return call(kernel, "ffn_both", outs, scratch, live, Held(third), *rows_of(parts), vectors, cotangent, flops=10**10)


def ffn_backward(cotangent, more, hat, scale, first, hid, slope, parts, vectors, norm):
    rows = first.shape[0]

    def kernel(m_ref, c_ref, h_ref, s_ref, g_ref, p0, p1, p2, p3, slope_ref, f_ref, hid_ref, back_ref, n_ref, d0, d1, d2, dh_ref, db_ref):
        grads = four_parts(d0, d1, d2)
        n_ref[...] = jnp.zeros_like(n_ref)
        scale = row_as_column(s_ref)
        for a, b in spans(rows):
            incoming = c_ref[a:b, :].astype(F32) + m_ref[a:b, :]
            hat_rows = h_ref[a:b, :].astype(F32)
            n_ref[0:1, :] += jnp.sum(incoming * hat_rows, axis=0, keepdims=True)
            n_ref[1:2, :] += jnp.sum(incoming, axis=0, keepdims=True)
            back = norm_back(incoming, hat_rows, scale[a:b], g_ref[2 * norm : 2 * norm + 1, :])
            back_low = low(back)
            db_ref[a:b, :] = back_low
            if not a:
                w1, w2 = ffn_weights((p0, p1, p2, p3))
            dh = low(slope_ref[a:b, :].astype(F32) * times_transpose(back_low, w2))
            dh_ref[a:b, :] = dh
            back_ref[a:b, :] = back + times_transpose(dh, w1)
        ffn_weight_gradients(f_ref[...], hid_ref, dh_ref, db_ref, grads, (d0, d1, d2))

    outs = [Held(struct((rows, D), F32)), struct((8, D), F32)] + part_outs()
    scratch = [pltpu.VMEM((rows, FF), BF16), pltpu.VMEM((rows, D), BF16)]
    return call(kernel, f"ffn_backward_{norm}", outs, scratch, Held(more), cotangent, hat, scale, vectors, *rows_of(parts), slope, first, hid, flops=10**10)


def before_heads(b_ref, h_ref, stat_ref, gain, wo, n_ref):
    incoming = b_ref[...]
    hat_rows = h_ref[...].astype(F32)
    n_ref[...] = jnp.zeros_like(n_ref)
    store_norm(n_ref, incoming, hat_rows)
    branch = norm_back(incoming, hat_rows, norm_scale(stat_ref), gain)
    branch_low = low(branch)
    return branch, branch_low, low(times_transpose(branch_low, wo()))


def self_backward(back, hat, x, q, k, v, o, stats, parts, vectors, norm, live, tail):
    rows = x.shape[0]

    def kernel(live_ref, b_ref, h_ref, stat_ref, g_ref, w0, w1, w2, w3, o_ref, q_ref, k_ref, v_ref, x_ref, p0, p1, p2, p3,
               dx_ref, tail_ref, n_ref, d0, d1, d2, do_ref, dq_ref, dk_ref, dv_ref):
        ps, grads = (p0, p1, p2, p3), four_parts(d0, d1, d2)
        branch, branch_low, do = before_heads(
            b_ref, h_ref, stat_ref, g_ref[2 * norm : 2 * norm + 1, :], lambda: row_matrix((w0, w1, w2, w3), 0, 0), n_ref
        )
        do_ref[...] = do
        store_rows(grads, transpose_times(o_ref[...], branch_low), 12, 0)
        send_parts((d0, d1, d2), 12, 4)
        delta = row_products(do.astype(F32), o_ref[...].astype(F32))
        bias = causal_bias(rows, live_ref[0, 0], False)
        for pair in range(PAIRS):
            cut = pair_columns(pair)
            dq_ref[:, cut], dk_ref[:, cut], dv_ref[:, cut] = pair_back(
                q_ref[:, cut], k_ref[:, cut], v_ref[:, cut], do_ref[:, cut],
                pair_rows(stat_ref, pair), pair_rows(delta, pair), bias,
            )
        xt = x_ref[...].T
        for column, ref in enumerate((dq_ref, dk_ref, dv_ref)):
            store_columns(grads, matmul(xt, ref[...]), 0, 3, column)
        send_parts((d0, d1, d2), 0, 12)
        total = branch
        for column, ref in enumerate((dq_ref, dk_ref, dv_ref)):
            total = total + times_transpose(ref[...], column_matrix(ps, 0, 3, column))
        dx_ref[...] = low(total)
        dx_ref.send()
        tail_ref[...] = dx_ref[tail:, :]

    outs = [struct((rows, D), BF16), struct((rows - tail, D), BF16), struct((8, D), F32)] + part_outs()
    scratch = [pltpu.VMEM((rows, D), BF16)] * 4
    args = [live, Held(back), hat, stats, vectors, *rows_of(parts, 12, 4), o, q, k, v, x, *rows_of(parts, 0, 12)]
    return call(kernel, f"self_backward_{norm}", outs, scratch, *args, flops=2 * 10**10)


def cross_backward(back, hat, second, encoded, q, k, v, o, stats, parts, vectors):
    rows, keys = second.shape[0], encoded.shape[0]

    def kernel(b_ref, h_ref, stat_ref, g_ref, w0, w1, w2, w3, o_ref, q_ref, k_ref, v_ref, x_ref, e_ref, p0, p1, p2, p3,
               dx_ref, de_ref, n_ref, d0, d1, d2, do_ref, dq_ref, dk_ref, dv_ref):
        ps, grads = (p0, p1, p2, p3), four_parts(d0, d1, d2)
        branch, branch_low, do = before_heads(
            b_ref, h_ref, stat_ref, g_ref[6:7, :], lambda: row_matrix((w0, w1, w2, w3), 0, 0), n_ref
        )
        do_ref[...] = do
        store_rows(grads, transpose_times(o_ref[...], branch_low), 12, 0)
        send_parts((d0, d1, d2), 12, 4)
        delta = row_products(do.astype(F32), o_ref[...].astype(F32))
        for pair in range(PAIRS):
            cut = pair_columns(pair)
            dq_ref[:, cut], dk_ref[:, cut], dv_ref[:, cut] = pair_back(
                q_ref[:, cut], k_ref[:, cut], v_ref[:, cut], do_ref[:, cut],
                pair_rows(stat_ref, pair), pair_rows(delta, pair), None,
            )
        store_columns(grads, transpose_times(x_ref[...], dq_ref[...]), 0, 1, 0)
        et = e_ref[...].T
        store_columns(grads, matmul(et, dk_ref[...]), 4, 2, 0)
        store_columns(grads, matmul(et, dv_ref[...]), 4, 2, 1)
        send_parts((d0, d1, d2), 0, 12)
        dx_ref[...] = branch + times_transpose(dq_ref[...], column_matrix(ps, 0, 1, 0))
        de_ref[...] = times_transpose(dk_ref[...], column_matrix(ps, 4, 2, 0)) + times_transpose(
            dv_ref[...], column_matrix(ps, 4, 2, 1)
        )

    outs = [Held(struct((rows, D), F32)), Held(struct((keys, D), F32)), struct((8, D), F32)] + part_outs()
    scratch = [pltpu.VMEM((rows, D), BF16)] * 2 + [pltpu.VMEM((keys, D), BF16)] * 2
    return call(kernel, "cross_backward", outs, scratch, Held(back), hat, stats, vectors, *rows_of(parts, 12, 4),
                o, q, k, v, second, encoded, *rows_of(parts, 0, 12), flops=2 * 10**10)


def column_tiles(out, gradient, column):
    for a in range(4):
        at = (a * 3 + column) * TILE
        out[at : at + TILE, :] = low(gradient[a * TILE : (a + 1) * TILE, :])


VECTOR_ROWS = 64


def first_backward(back, hat, x, q, k, v, o, stats, parts, vectors, norms):
    rows = x.shape[0]
    size = CHUNK * TILE

    def kernel(b_ref, h_ref, stat_ref, g_ref, w0, w1, w2, w3, o_ref, q_ref, k_ref, v_ref, x_ref, n1, n2, n3, n4,
               branch_ref, do_ref, delta_ref, v_out, near_ref, out0_ref, out2_ref, xt_ref, dq_ref, dk_ref, dv_ref, n_ref):
        branch, branch_low, do = before_heads(
            b_ref, h_ref, stat_ref, g_ref[0:1, :], lambda: row_matrix((w0, w1, w2, w3), 0, 0), n_ref
        )
        branch_ref[...] = branch
        branch_ref.send()
        do_ref[...] = do
        do_ref.send()
        norms_low = low(jnp.concatenate([n[:2, :] for n in (n_ref, n1, n2, n3, n4)] + [jnp.zeros((6, D), F32)], axis=0))
        for j in range(4):
            v_out[16 * j : 16 * (j + 1), :] = norms_low[:, j * TILE : (j + 1) * TILE]
        near_ref[2 * size :, :] = v_out[...]
        near_ref.send((2 * size, 2 * size + VECTOR_ROWS))
        wo = low(transpose_times(o_ref[...], branch_low))
        for r, (ref, at) in enumerate(
            ((out0_ref, 0), (near_ref, 12 * TILE), (out2_ref, 0), (near_ref, size + 12 * TILE))
        ):
            for b in range(4):
                ref[at + b * TILE : at + (b + 1) * TILE, :] = wo[
                    r * TILE : (r + 1) * TILE, b * TILE : (b + 1) * TILE
                ]
        delta_ref[...] = row_products(do.astype(F32), o_ref[...].astype(F32))[:STATS, :]
        xt = x_ref[...].T
        xt_ref[...] = xt
        for out in (xt_ref, out0_ref, out2_ref, delta_ref):
            out.send()
        for at, pair in enumerate((1, 3)):
            cut = pair_columns(pair)
            grads = pair_back(
                q_ref[:, cut], k_ref[:, cut], v_ref[:, cut], do_ref[:, cut],
                pair_rows(stat_ref, pair), pair_rows(delta_ref, pair), None,
            )
            for column, (ref, value) in enumerate(zip((dq_ref, dk_ref, dv_ref), grads)):
                ref[:, at * TILE : (at + 1) * TILE] = value
                column_tiles(near_ref.at[pl.ds(at * size, size)], matmul(xt, value), column)
            near_ref.send((at * size, (at + 1) * size))

    outs = [struct((rows, D), F32), struct((rows, D), BF16), struct((STATS, rows), F32)]
    outs += [struct((VECTOR_ROWS, TILE), BF16), struct((2 * size + VECTOR_ROWS, TILE), BF16)]
    outs += [struct((4 * TILE, TILE), BF16)] * 2 + [struct((D, rows), BF16)]
    outs += [struct((rows, 2 * TILE), BF16)] * 3
    return call(kernel, "first_backward", outs, [pltpu.VMEM((8, D), F32)], Held(back), hat, stats, vectors,
                *rows_of(parts, 12, 4), o, q, k, v, x, *norms, flops=2 * 10**10)


def pair_arguments(pair, rows, *arrays):
    return [(a, 0, rows, pair_columns(pair)) for a in arrays]


def pair_backward(pair, xt, q, k, v, do, stats, delta, wo_part, extra):
    rows = q.shape[0]

    def kernel(q_ref, k_ref, do_ref, v_ref, stat_ref, delta_ref, xt_ref, wo_ref, v_ref2, out_ref, dq_ref, dk_ref, dv_ref):
        grads = pair_back(
            q_ref[...], k_ref[...], v_ref[...], do_ref[...],
            pair_rows(stat_ref, pair), pair_rows(delta_ref, pair), None,
        )
        for column, (ref, value) in enumerate(zip((dq_ref, dk_ref, dv_ref), grads)):
            ref[...] = value
            column_tiles(out_ref, matmul(xt_ref[...], value), column)
        out_ref[12 * TILE : CHUNK * TILE, :] = wo_ref[...]
        out_ref[CHUNK * TILE :, :] = v_ref2[...]

    outs = [struct((CHUNK * TILE + VECTOR_ROWS, TILE), BF16)] + [struct((rows, TILE), BF16)] * 3
    return call(kernel, f"pair_backward_{pair}", outs, [], *pair_arguments(pair, rows, q, k, do, v), stats, delta,
                xt, wo_part, extra, flops=5 * 10**9)


def last_backward(xt, q, k, v, do, stats, delta, wo_part, branch, odd, two, parts, tail):
    rows = branch.shape[0]

    def kernel(q_ref, k_ref, do_ref, v_ref, stat_ref, delta_ref, xt_ref, wo_ref, b_ref, *refs):
        refs, ps, (out_ref, dx_ref, tail_ref) = refs[:6], refs[6:10], refs[10:]
        grads = pair_back(
            q_ref[...], k_ref[...], v_ref[...], do_ref[...],
            pair_rows(stat_ref, 0), pair_rows(delta_ref, 0), None,
        )
        for column, value in enumerate(grads):
            column_tiles(out_ref, matmul(xt_ref[...], value), column)
        out_ref[12 * TILE :, :] = wo_ref[...]
        out_ref.send()
        total = b_ref[...]
        for column, zero in enumerate(grads):
            pairs, single = refs[column], refs[3 + column]
            rows_in = jnp.concatenate([zero, pairs[:, :TILE], single[...], pairs[:, TILE:]], axis=1)
            total = total + times_transpose(rows_in, column_matrix(ps, 0, 3, column))
        dx_ref[...] = low(total)
        dx_ref.send()
        tail_ref[...] = dx_ref[tail:, :]

    outs = [struct((CHUNK * TILE, TILE), BF16), struct((rows, D), BF16), struct((rows - tail, D), BF16)]
    return call(kernel, "last_backward", outs, [], *pair_arguments(0, rows, q, k, do, v), stats, delta, xt, wo_part,
                branch, *odd, *two, *rows_of(parts, 0, 12), flops=10**10)


def tie(value, *others):
    return lax.optimization_barrier((value, *others))[0]


def compute(x, y, xc, yc, live, tiles, near, vectors, alive, image_rows, tag_rows):
    live_tags = jnp.where(alive, live, 0).reshape(1, 1)
    live = live.reshape(1, 1)
    image_tail = tail_rows(x.shape[0], image_rows)
    tag_tail = tail_rows(y.shape[0], tag_rows)

    def far_part(c, *others):
        part = tiles[c * CHUNK * TILE : (c + 1) * CHUNK * TILE]
        return lax.ppermute(tie(part, *others) if others else part, "tensor", chip_pairs())

    def chunk(c, far, *others):
        return (tiles, near, far, lax.ppermute(tie(far, *others) if others else far, "tensor", core_pairs()), c)

    fars = [far_part(0)]
    chunk0 = chunk(0, fars[0])
    fars += [far_part(1), far_part(2)]
    first, first_low, hat0, q, k, v, o, stat = self_forward(x, chunk0, vectors, 0)
    fars += [far_part(3, first), far_part(4, first)]
    chunk1 = chunk(1, fars[1], first)
    encoded, hat1, scale1, hid, slope, encoded_tail = ffn_forward(
        first, chunk1, vectors, 1, image_tail
    )
    chunk2 = chunk(2, fars[2], encoded)
    second, second_low, hat2, q2, k2, v2, o2, stat2 = self_forward(y, chunk2, vectors, 2, live)
    chunk3 = chunk(3, fars[3], second)
    third, hat3, q3, k3, v3, o3, stat3 = cross_forward(second, encoded, chunk3, vectors)
    chunk4 = chunk(4, fars[4], third)
    decoded, decoded_tail, back, n4, *part4 = ffn_both(third, yc, live_tags, chunk4, vectors, tag_tail)
    near4 = send_near(part4)
    back, d_encoded, n3, *part3 = cross_backward(
        back, hat3, second_low, encoded, q3, k3, v3, o3, stat3, chunk3, vectors
    )
    far4 = send_far(sum_far(part4, tie(near4, back)))
    near3 = send_near(part3)
    d_first, n1, *part1 = ffn_backward(
        xc, d_encoded, hat1, scale1, first_low, hid, slope, chunk1, vectors, 1
    )
    far3 = send_far(sum_far(part3, tie(near3, d_first)))
    near1 = send_near(part1)
    back = tie(back, d_first, far4)
    dy, dy_tail, n2, *part2 = self_backward(
        back, hat2, y, q2, k2, v2, o2, stat2, chunk2, vectors, 2, live, tag_tail
    )
    near2 = send_near(part2)
    far_sum1 = sum_far(part1, tie(near1, dy))
    far1 = send_far(far_sum1)
    d_first = tie(d_first, dy, far3, far_sum1)
    branch, do, delta, extra, near_part0, out0, out2, xt, *odd = first_backward(
        d_first, hat0, x, q, k, v, o, stat, chunk0, vectors, (n1, n2, n3, n4)
    )
    near0 = send_near([None, near_part0])
    far_sum2 = sum_far(part2, tie(near2, branch))
    far2 = send_far(far_sum2)
    far_part0, *two = pair_backward(
        2, tie(xt, near_part0, far_sum2), q, k, v, do, stat, delta, out2, extra
    )
    far_sum0 = sum_far([None, None, far_part0], tie(near0, far_part0))
    far0 = send_far(far_sum0)
    own_part0, dx, dx_tail = last_backward(
        tie(xt, far_sum0), q, k, v, do, stat, delta, out0, branch, odd, two, chunk0, image_tail
    )
    owns = [own_part0, part1[0], part2[0], part3[0], part4[0]]
    nears, fars = [near0, near1, near2, near3, near4], [far0, far1, far2, far3, far4]
    items = [encoded, decoded, dx, dy]
    tails = [encoded_tail, decoded_tail, dx_tail, dy_tail]
    return items, tails, list(zip(owns, nears, fars)), extra, dx


def one_hot(index, count, dtype):
    return (index[:, None] == lax.broadcasted_iota(jnp.int32, (1, count), 1)).astype(dtype)


def local(
    image_tokens,
    tag_tokens,
    image_cotangent,
    tag_cotangent,
    tag_lengths,
    slot_blocks,
    master_blocks,
    left_factor,
    right_factor,
    left_root,
    right_root,
    vector_master,
    vector_moment,
):
    dp = lax.axis_size("dp")
    shards = lax.axis_size("tensor")
    me = lax.axis_index("tensor")
    slots = master_blocks.shape[1]
    items = tag_lengths.shape[0]
    image_length = image_tokens.shape[0] * shards // items
    item_length = tag_tokens.shape[0] * shards // items
    lanes = vector_master.shape[1]
    def rows_of(value):
        return jnp.pad(value, ((0, 16 - value.shape[0]), (0, TILE - value.shape[1])))

    own = jnp.concatenate(
        [
            master_blocks.astype(BF16).reshape(slots * TILE, TILE),
            rows_of(vector_master.astype(BF16)),
        ],
        axis=0,
    )
    pieces = gather_pieces(own, dp)
    alive = me < items
    rank = me.reshape(1, 1)
    tokens = lax.optimization_barrier((image_tokens, tag_tokens, pieces[3]))[:2]
    x, y = pull_rows(tokens, (image_length, item_length), rank, True)
    cotangents = lax.optimization_barrier((image_cotangent, tag_cotangent, pieces[1]))[:2]
    xc, yc = pull_rows(cotangents, (image_length, item_length), rank, False)
    x, y, xc, yc, *pieces = lax.optimization_barrier((x, y, xc, yc, *pieces))
    ranks = jnp.stack([relative_rank(p, dp) for p in range(dp)])

    def blocks_of(those):
        picked = one_hot(those, dp, jnp.int32)[:, :, None] * slot_blocks.reshape(1, dp, slots)
        return jnp.sum(picked, axis=1).reshape(1, dp * slots)

    tiles = order_tiles(pieces, blocks_of(ranks), slots)
    vector_list = jnp.stack([p[slots * TILE : slots * TILE + 10, :lanes] for p in pieces])
    vectors = jnp.einsum(
        "pr,pvl->vrl", one_hot(ranks, dp, BF16), vector_list, preferred_element_type=F32
    ).reshape(10, dp * lanes)
    near = lax.ppermute(tiles, "tensor", core_pairs())
    live = jnp.sum(jnp.where(lax.broadcasted_iota(jnp.int32, (items,), 0) == me, tag_lengths, 0))
    live = jnp.where(alive, live, 1)
    wholes, tails, sums, extra, dx = compute(
        x,
        y,
        xc,
        yc,
        live,
        tiles,
        near,
        vectors,
        alive,
        image_tokens.shape[0],
        tag_tokens.shape[0],
    )
    targets = jnp.stack([target_rank(p, dp) for p in range(dp)])
    early = sum_chunks(sums[1:], sums[0][0])
    outgoing = deal_tiles(sums[0], early, extra, blocks_of(targets), targets.reshape(1, dp), slots, lanes)
    terms, mark = sum_pieces(outgoing, dp)
    tails = [lax.optimization_barrier((tail, mark))[0] for tail in tails]
    images, tags = image_tokens.shape[0], tag_tokens.shape[0]
    rows = push_rows(wholes, tails, (images, tags, images, tags), (BF16, BF16, F32, F32), rank)
    updates = shampoo(
        terms,
        master_blocks,
        left_factor,
        right_factor,
        left_root,
        right_root,
        vector_master,
        vector_moment,
    )
    return (*rows, *updates)


def solution(mesh):
    in_specs = (
        P(("dp", "tensor"), None),
        P(("dp", "tensor"), None),
        P(("dp", "tensor"), None),
        P(("dp", "tensor"), None),
        P("dp"),
        P(),
        P("tensor", "dp", None, None),
        P("tensor", "dp", None, None),
        P("tensor", "dp", None, None),
        P("tensor", "dp", None, None),
        P("tensor", "dp", None, None),
        P(None, "dp"),
        P(None, "dp"),
    )
    out_specs = (
        P(("dp", "tensor"), None),
        P(("dp", "tensor"), None),
        P(("dp", "tensor"), None),
        P(("dp", "tensor"), None),
        P("tensor", "dp", None, None),
        P("tensor", "dp", None, None),
        P("tensor", "dp", None, None),
        P("tensor", "dp", None, None),
        P("tensor", "dp", None, None),
        P(None, "dp"),
        P(None, "dp"),
        P(None, "dp"),
    )
    return jax.shard_map(local, mesh=mesh, in_specs=in_specs, out_specs=out_specs, check_vma=False)
```

time: 362 us -> 319 us (0.88)
  the two profiles are of different devices: /device:TPU:15 before, /device:TPU:0 now
where the time goes in v3:
time: 319 us; the launch traced here: 314 us
  Pallas kernels  142 us (45%)
  waiting for transfers between devices  99.3 us (31%)
  starting transfers between devices  43.2 us (14%)
  local copies, waits for them, and re-layouts  16.6 us (5%)
  other arithmetic  10.3 us (3%)
    pallas_call x13, Pallas kernels, call(): pl.pallas_call(body, out_shape=shapes, in_specs=[SM if a.dtype == jnp.int...  129 us
    ppermute x3, waiting for transfers between devices, gather_pieces(): z = {step: lax.ppermute(piece, 'dp', z_shift(step)) for step in (1, 2, 3)}  27 us
    ppermute x5, waiting for transfers between devices, far_part(): lax.ppermute(tie(part, *others) if others else part, 'tensor', chip_pairs())  18.4 us
    ppermute x3, waiting for transfers between devices, sum_pieces(): column.append(lax.ppermute(both, 'dp', z_shift(step)))  17.7 us
    ppermute x5, waiting for transfers between devices, send_far(): return lax.ppermute(value, 'tensor', chip_pairs())  14.8 us
    unnamed x127, local copies, waits for them, and re-layouts  12.7 us
    ppermute x4, waiting for transfers between devices, sum_pieces(): other = lax.ppermute(piece, 'dp', y_pairs())  11.6 us
    ppermute x4, starting transfers between devices, push_rows(): lax.ppermute(a, 'tensor', [(i, i + 1) for i in range(shards - 1)])  7.65 us
  transfers between devices with their start and end apart: 41, of which 20 were waited for; matrix products, arithmetic and copies ran while one was open for 5% of the time, Pallas kernels for 38%

profile of v3, /device:TPU:0, one launch (start us, length us, event | category | flops | bytes accessed | tf_op | source)
XLA Modules:
  0.0 314.0 jit_solution(7551064103075220947)
XLA Ops:
  1.5 1.2 convert_element_type.95
  2.7 3.1 collective-permute-start.2
  5.8 2.1 collective-permute-start
  7.9 1.7 collective-permute-start.5
  9.6 6.9 %collective-permute-done.2.refs_1_ = bf16[1296,128]{1,0:T(8,128)(2,1)S(1)} collective-permute-done((bf16[1296,128]{1,0:T(8,128)(2,1)S(1)}, bf16[1296,128]{1,0:T(8,128)(2,1)S(1)}, u32[]{:S(2)}, u32[]{:S(2)}) %collective-permute-start.2) | collective-permute-done | bytes 331808 | tf_op jit(solution)/shard_map/ppermute | solution.py:65
  16.5 5.7 %collective-permute-done.refs_3_ = bf16[1296,128]{1,0:T(8,128)(2,1)S(1)} collective-permute-done((bf16[1296,128]{1,0:T(8,128)(2,1)S(1)}, bf16[1296,128]{1,0:T(8,128)(2,1)S(1)}, u32[]{:S(2)}, u32[]{:S(2)}) %collective-permute-start) | collective-permute-done | bytes 331808 | tf_op jit(solution)/shard_map/ppermute | solution.py:65
  22.2 1.1 pad_maximum_fusion.1
  23.3 1.3 collective-permute-start.3
  24.6 1.1 pad_maximum_fusion
  25.6 1.3 collective-permute-start.1
  26.9 1.4 collective-permute-start.4
  28.3 1.5 collective-permute-start.7
  30.7 14.4 %collective-permute-done.4.refs_2_ = bf16[1296,128]{1,0:T(8,128)(2,1)} collective-permute-done((bf16[1296,128]{1,0:T(8,128)(2,1)S(1)}, bf16[1296,128]{1,0:T(8,128)(2,1)}, u32[]{:S(2)}, u32[]{:S(2)}) %collective-permute-start.4) | collective-permute-done | bytes 331808 | tf_op jit(solution)/shard_map/ppermute | solution.py:65
  45.1 1.5 collective-permute-start.8
  46.9 1.4 pull_rows.3
  49.2 1.5 pull_rows.2
  50.8 4.8 %collective-permute-done.8.refs_6_ = bf16[1296,128]{1,0:T(8,128)(2,1)} collective-permute-done((bf16[1296,128]{1,0:T(8,128)(2,1)}, bf16[1296,128]{1,0:T(8,128)(2,1)}, u32[]{:S(2)}, u32[]{:S(2)}) %collective-permute-start.8) | collective-permute-done | bytes 331808 | tf_op jit(solution)/shard_map/ppermute | solution.py:69
  57.6 2.5 order_tiles.1.refs_1_.refs_2_.refs_4_.refs_14_.refs_5_.refs_15_
  60.2 1.6 fusion.9
  62.3 3.5 %collective-permute-start.10 = (bf16[2048,128]{1,0:T(8,128)(2,1)S(1)}, bf16[2048,128]{1,0:T(8,128)(2,1)}, u32[]{:S(2)}, u32[]{:S(2)}) collective-permute-start(bf16[2048,128]{1,0:T(8,128)(2,1)S(1)} %get-tuple-element.288), channel_id=1, source_target_pairs={{0,2},{1,3},{2,0},{3,1},{4,6},{5,7},{6,4},{7,5},{8,10},{9,11},{10,... | collective-permute-start | bytes 1572872 | tf_op jit(solution)/shard_map/ppermute | solution.py:1063
  68.6 9.2 %collective-permute-done.10.refs_3_.refs_6_.refs_17_ = bf16[2048,128]{1,0:T(8,128)(2,1)} collective-permute-done((bf16[2048,128]{1,0:T(8,128)(2,1)S(1)}, bf16[2048,128]{1,0:T(8,128)(2,1)}, u32[]{:S(2)}, u32[]{:S(2)}) %collective-permute-start.10) | collective-permute-done | bytes 524320 | tf_op jit(solution)/shard_map/ppermute | solution.py:1063
  80.0 1.7 collective-permute-start.12
  82.6 14.0 %self_forward_0.1 = (f32[784,512]{1,0:T(8,128)S(1)}, bf16[784,512]{1,0:T(8,128)(2,1)}, bf16[784,512]{1,0:T(8,128)(2,1)}, bf16[784,512]{1,0:T(8,128)(2,1)}, bf16[...) custom-call(bf16[784,512]{1,0:T(8,128)(2,1)} %copy-done.22, ...), custom_call_target="tpu_custom_call" | custom-call | flops 10000000000 | bytes 4000000 | tf_op jit(solution)/shard_map/self_forward_0/pallas_call | solution.py:622
  97.1 1.4 collective-permute-done.13.refs_4_.refs_8_
  99.3 8.0 %ffn_forward_1.1 = (bf16[784,512]{1,0:T(8,128)(2,1)}, bf16[784,512]{1,0:T(8,128)(2,1)}, f32[8,784]{1,0:T(8,128)}, bf16[784,1024]{1,0:T(8,128)(2,1)}, bf16[784,10...) custom-call(f32[784,512]{1,0:T(8,128)S(1)} %get-tuple-element.167.refs_0_, bf16[10240,128]{1,0:T(8,128)(2,1)} %copy-done, ...), custom_call_target="tpu_custom_call" | custom-call | flops 3000000000 | bytes 4000000 | tf_op jit(solution)/shard_map/ffn_forward_1/pallas_call | solution.py:622
  107.3 3.7 %collective-permute-done.14.refs_4_.refs_7_.refs_16_ = bf16[2048,128]{1,0:T(8,128)(2,1)S(1)} collective-permute-done((bf16[2048,128]{1,0:T(8,128)(2,1)S(1)}, bf16[2048,128]{1,0:T(8,128)(2,1)S(1)}, u32[]{:S(2)}, u32[]{:S(2)}) %collective-permute-start.14) | collective-permute-done | bytes 524320 | tf_op jit(solution)/shard_map/ppermute | solution.py:1063
  113.7 7.7 %self_forward_2.1 = (f32[512,512]{1,0:T(8,128)S(1)}, bf16[512,512]{1,0:T(8,128)(2,1)}, bf16[512,512]{1,0:T(8,128)(2,1)}, bf16[512,512]{1,0:T(8,128)(2,1)}, bf16[...) custom-call(s32[1,1]{1,0:T(1,128)} %bitcast.21.refs_0_, ...), custom_call_target="tpu_custom_call" | custom-call | flops 10000000000 | bytes 4000000 | tf_op jit(solution)/shard_map/self_forward_2/pallas_call | solution.py:622
  121.4 5.3 %collective-permute-done.16.refs_3_.refs_6_.refs_16_ = bf16[2048,128]{1,0:T(8,128)(2,1)S(1)} collective-permute-done((bf16[2048,128]{1,0:T(8,128)(2,1)S(1)}, bf16[2048,128]{1,0:T(8,128)(2,1)S(1)}, u32[]{:S(2)}, u32[]{:S(2)}) %collective-permute-start.16) | collective-permute-done | bytes 524320 | tf_op jit(solution)/shard_map/ppermute | solution.py:1063
  127.0 1.6 collective-permute-done.17.refs_4_.refs_7_.refs_17_
  129.4 11.5 %cross_forward.1 = (f32[512,512]{1,0:T(8,128)S(1)}, bf16[512,512]{1,0:T(8,128)(2,1)}, bf16[512,512]{1,0:T(8,128)(2,1)}, bf16[784,512]{1,0:T(8,128)(2,1)}, bf16[7...) custom-call(f32[512,512]{1,0:T(8,128)S(1)} %get-tuple-element.172.refs_0_, ...), custom_call_target="tpu_custom_call" | custom-call | flops 5000000000 | bytes 4000000 | tf_op jit(solution)/shard_map/cross_forward/pallas_call | solution.py:622
  141.1 1.9 collective-permute-done.19.refs_5_
  143.7 8.6 %ffn_both.1 = (bf16[512,512]{1,0:T(8,128)(2,1)}, bf16[384,512]{1,0:T(8,128)(2,1)}, f32[512,512]{1,0:T(8,128)S(1)}, f32[8,512]{1,0:T(8,128)}, bf16[2048,128]{1,0:...) custom-call(s32[1,1]{1,0:T(1,128)} %bitcast.20.refs_0_, f32[512,512]{1,0:T(8,128)S(1)} %get-tuple-element.175.refs_1_, ...), custom_call_target="tpu_custom_call" | custom-call | flops 10000000000 | bytes 4000000 | tf_op jit(solution)/shard_map/ffn_both/pallas_call | solution.py:622
  152.5 15.5 %cross_backward.1 = (f32[512,512]{1,0:T(8,128)S(1)}, f32[784,512]{1,0:T(8,128)S(1)}, f32[8,512]{1,0:T(8,128)}, bf16[2048,128]{1,0:T(8,128)(2,1)}, bf16[4096,128]{1,0:T(8,128)(2,1)}, /*index=5*/bf16[2048,128]{1,0:T(8,128)(2,1)}) custom-call(f32[512,512]{1,0:T(8,128)S(1)} %get-tuple-element.182.refs_0_, bf16[512,512]{1,0:T(8,128)(2,1)} %get-tuple-element.183.refs_1_, ...), custom_call_target="tpu_custom_call" | custom-call | flops 20000000000 | bytes 4000000 | tf_op jit(solution)/shard_map/cross_backward/pallas_call | solution.py:622
  169.0 8.6 %ffn_backward_1.1 = (f32[784,512]{1,0:T(8,128)S(1)}, f32[8,512]{1,0:T(8,128)}, bf16[2048,128]{1,0:T(8,128)(2,1)}, bf16[4096,128]{1,0:T(8,128)(2,1)}, bf16[2048,128]{1,0:T(8,128)(2,1)}) custom-call(f32[784,512]{1,0:T(8,128)S(1)} %get-tuple-element.190.refs_0_, bf16[784,512]{1,0:T(8,128)(2,1)} %copy-done.23, bf16[784,512]{1,0:T(8,128)(2,1)} %get-tuple-element.192.refs_2_, ...), custom_call_target="tpu_custom_call" | custom-call | flops 10000000000 | bytes 4000000 | tf_op jit(solution)/shard_map/ffn_backward_1/pallas_call | solution.py:622
  177.9 1.8 collective-permute-start.23
  179.7 3.8 %collective-permute-done.21.refs_11_ = bf16[2048,128]{1,0:T(8,128)(2,1)S(1)} collective-permute-done((bf16[2048,128]{1,0:T(8,128)(2,1)S(1)}, bf16[2048,128]{1,0:T(8,128)(2,1)S(1)}, u32[]{:S(2)}, u32[]{:S(2)}) %collective-permute-start.21) | collective-permute-done | bytes 524320 | tf_op jit(solution)/shard_map/ppermute | solution.py:104
  183.5 12.8 %self_backward_2.1 = (bf16[512,512]{1,0:T(8,128)(2,1)}, bf16[384,512]{1,0:T(8,128)(2,1)}, f32[8,512]{1,0:T(8,128)}, bf16[2048,128]{1,0:T(8,128)(2,1)}, bf16[4096...) custom-call(s32[1,1]{1,0:T(1,128)} %bitcast.21.refs_0_, f32[512,512]{1,0:T(8,128)S(1)} %get-tuple-element.202.refs_1_, ...), custom_call_target="tpu_custom_call" | custom-call | flops 20000000000 | bytes 4000000 | tf_op jit(solution)/shard_map/self_backward_2/pallas_call | solution.py:622
  196.6 16.9 %first_backward.1 = (f32[784,512]{1,0:T(8,128)}, bf16[784,512]{1,0:T(8,128)(2,1)}, f32[16,784]{1,0:T(8,128)}, bf16[64,128]{1,0:T(8,128)(2,1)}, bf16[4160,128]{1,...) custom-call(f32[784,512]{1,0:T(8,128)S(1)} %get-tuple-element.216.re, ...), custom_call_target="tpu_custom_call" | custom-call | flops 20000000000 | bytes 4000000 | tf_op jit(solution)/shard_map/first_backward/pallas_call | solution.py:622
  214.6 2.1 collective-permute-start.29
  216.7 8.2 %pair_backward_2.1 = (bf16[2112,128]{1,0:T(8,128)(2,1)}, bf16[784,128]{1,0:T(8,128)(2,1)}, bf16[784,128]{1,0:T(8,128)(2,1)}, bf16[784,128]{1,0:T(8,128)(2,1)}) custom-call(bf16[784,512]{1,0:T(8,128)(2,1)} %get-tuple-element.180.refs_9_.refs_0_, bf16[784,512]{1,0:T(8,128)(2,1)} %get-tuple-element.181.refs_10_.refs_1_, ...), custom_call_target="tpu_custom_call" | custom-call | flops 5000000000 | bytes 4000000 | tf_op jit(solution)/shard_map/pair_backward_2/pallas_call | solution.py:622
  224.9 1.6 add_convert_fusion
  226.7 9.7 %last_backward.1 = (bf16[2048,128]{1,0:T(8,128)(2,1)}, bf16[784,512]{1,0:T(8,128)(2,1)}, bf16[592,512]{1,0:T(8,128)(2,1)}) custom-call(bf16[784,512]{1,0:T(8,128)(2,1)} %get-tuple-element.180.refs_9_.refs_0_, bf16[784,512]{1,0:T(8,128)(2,1)} %get-tuple-element.181.refs_10_.refs_1_, bf16[784,512]{1,0:T(8,128)(2,1)} %get-tuple-element.225.refs_2_, ...), custom_call_target="tpu_custom_call" | custom-call | flops 10000000000 | bytes 4000000 | tf_op jit(solution)/shard_map/last_backward/pallas_call | solution.py:622
  236.5 3.9 %collective-permute-done.29.refs_5_ = bf16[2048,128]{1,0:T(8,128)(2,1)S(1)} collective-permute-done((bf16[2048,128]{1,0:T(8,128)(2,1)S(1)}, bf16[2048,128]{1,0:T(8,128)(2,1)S(1)}, u32[]{:S(2)}, u32[]{:S(2)}) %collective-permute-start.29) | collective-permute-done | bytes 524320 | tf_op jit(solution)/shard_map/ppermute | solution.py:104
  241.2 3.0 sum_chunks.1.refs_7_
  244.2 7.1 %collective-permute-done.27.refs_5_ = bf16[2112,128]{1,0:T(8,128)(2,1)S(1)} collective-permute-done((bf16[2112,128]{1,0:T(8,128)(2,1)S(1)}, bf16[2112,128]{1,0:T(8,128)(2,1)S(1)}, u32[]{:S(2)}, u32[]{:S(2)}) %collective-permute-start.27) | collective-permute-done | bytes 540704 | tf_op jit(solution)/shard_map/ppermute | solution.py:104
  252.2 4.4 %deal_tiles.1 = (bf16[1296,128]{1,0:T(8,128)(2,1)}, bf16[1296,128]{1,0:T(8,128)(2,1)}, bf16[1296,128]{1,0:T(8,128)(2,1)}, bf16[1296,128]{1,0:T(8,128)(2,1)}, bf1...) custom-call(s32[1,80]{1,0:T(1,128)} %reshape.101.refs_0_, ...), custom_call_target="tpu_custom_call" | custom-call | bytes 4000000 | tf_op jit(solution)/shard_map/deal_tiles/pallas_call | solution.py:622
  256.6 1.6 collective-permute-start.34
  258.7 1.3 collective-permute-start.31
  260.0 3.1 collective-permute-start.33
  263.2 1.9 collective-permute-start.30
  265.1 2.5 collective-permute-done.34
  267.6 1.3 collective-permute-start.32
  269.0 1.1 add_convert_fusion.7
  270.0 3.1 %collective-permute-done.36 = bf16[1296,128]{1,0:T(8,128)(2,1)S(1)} collective-permute-done((bf16[1296,128]{1,0:T(8,128)(2,1)}, bf16[1296,128]{1,0:T(8,128)(2,1)S(1)}, u32[]{:S(2)}, u32[]{:S(2)}) %collective-permute-start.36) | collective-permute-done | bytes 331808 | tf_op jit(solution)/shard_map/ppermute | solution.py:84
  273.2 1.5 collective-permute-start.38
  274.7 1.1 add_convert_fusion.6
  275.8 5.9 %collective-permute-done.38 = bf16[1296,128]{1,0:T(8,128)(2,1)S(1)} collective-permute-done((bf16[1296,128]{1,0:T(8,128)(2,1)}, bf16[1296,128]{1,0:T(8,128)(2,1)S(1)}, u32[]{:S(2)}, u32[]{:S(2)}) %collective-permute-start.38) | collective-permute-done | bytes 331808 | tf_op jit(solution)/shard_map/ppermute | solution.py:84
  281.6 1.1 add_convert_fusion.5
  282.7 2.9 collective-permute-start.37
  285.7 1.5 collective-permute-start.40
  288.2 1.8 push_rows.1
  290.1 13.8 %collective-permute-done.35.refs_1_ = bf16[1296,128]{1,0:T(8,128)(2,1)S(1)} collective-permute-done((bf16[1296,128]{1,0:T(8,128)(2,1)S(1)}, bf16[1296,128]{1,0:T(8,128)(2,1)S(1)}, u32[]{:S(2)}, u32[]{:S(2)}) %collective-permute-start.35) | collective-permute-done | bytes 331808 | tf_op jit(solution)/shard_map/ppermute | solution.py:90
  303.9 3.9 %collective-permute-done.39.refs_3_ = bf16[1296,128]{1,0:T(8,128)(2,1)S(1)} collective-permute-done((bf16[1296,128]{1,0:T(8,128)(2,1)S(1)}, bf16[1296,128]{1,0:T(8,128)(2,1)S(1)}, u32[]{:S(2)}, u32[]{:S(2)}) %collective-permute-start.39) | collective-permute-done | bytes 331808 | tf_op jit(solution)/shard_map/ppermute | solution.py:90
  307.8 5.9 %shampoo.1 = (f32[1,10,128,128]{3,2,1,0:T(8,128)}, f32[1,10,128,128]{3,2,1,0:T(8,128)}, f32[1,10,128,128]{3,2,1,0:T(8,128)}, f32[1,10,128,128]{3,2,1,0:T(8,128)}...) custom-call(bf16[1296,128]{1,0:T(8,128)(2,1)S(1)} %copy-done.18, ...), custom_call_target="tpu_custom_call" | custom-call | tf_op jit(solution)/shard_map/shampoo/pallas_call | solution.py:313
  (190 shorter events, 22.9 us)
Async XLA Ops:
  0.6 21.5 %copy-start.4 = (bf16[384,512]{1,0:T(8,128)(2,1)S(1)}, bf16[384,512]{1,0:T(8,128)(2,1)}, u32[]{:S(2)}) copy-start(bf16[384,512]{1,0:T(8,128)(2,1)} %refs_1_.1) | copy-start | bytes 1179652
  0.7 21.5 %copy-start.2 = (bf16[588,512]{1,0:T(8,128)(2,1)S(1)}, bf16[588,512]{1,0:T(8,128)(2,1)}, u32[]{:S(2)}) copy-start(bf16[588,512]{1,0:T(8,128)(2,1)} %refs_0_.1) | copy-start | bytes 1806340
  1.4 23.1 %copy-start.3 = (bf16[588,512]{1,0:T(8,128)(2,1)S(1)}, bf16[588,512]{1,0:T(8,128)(2,1)}, u32[]{:S(2)}) copy-start(bf16[588,512]{1,0:T(8,128)(2,1)} %refs_0_) | copy-start | bytes 1806340
  1.4 23.1 %copy-start.5 = (bf16[384,512]{1,0:T(8,128)(2,1)S(1)}, bf16[384,512]{1,0:T(8,128)(2,1)}, u32[]{:S(2)}) copy-start(bf16[384,512]{1,0:T(8,128)(2,1)} %refs_1_) | copy-start | bytes 1179652
  2.7 27.1 %copy-start.44 = (s32[80]{0:T(128)S(1)}, s32[80]{0:T(128)}, u32[]{:S(2)}) copy-start(s32[80]{0:T(128)} %param.18) | copy-start | bytes 964
  2.7 13.8 %collective-permute-start.2 = (bf16[1296,128]{1,0:T(8,128)(2,1)S(1)}, bf16[1296,128]{1,0:T(8,128)(2,1)S(1)}, u32[]{:S(2)}, u32[]{:S(2)}) collective-permute-start(bf16[1296,128]{1,0:T(8,128)(2,1)S(1)} %fusion.1.refs_0_), channel_id=1, source_target_pairs={{0,8},{4,12},{8,16},{12,20},{16,24},{20,28},{24,0},{28,4},{1,9},{5... | collective-permute-start | bytes 995336 | tf_op jit(solution)/shard_map/ppermute | solution.py:65
  5.8 16.4 %collective-permute-start = (bf16[1296,128]{1,0:T(8,128)(2,1)S(1)}, bf16[1296,128]{1,0:T(8,128)(2,1)S(1)}, u32[]{:S(2)}, u32[]{:S(2)}) collective-permute-start(bf16[1296,128]{1,0:T(8,128)(2,1)S(1)} %fusion.1.refs_0_), channel_id=1, source_target_pairs={{0,24},{4,28},{8,0},{12,4},{16,8},{20,12},{24,16},{28,20},{1,25},{... | collective-permute-start | bytes 995336 | tf_op jit(solution)/shard_map/ppermute | solution.py:65
  7.9 20.4 %collective-permute-start.5 = (bf16[1296,128]{1,0:T(8,128)(2,1)S(1)}, bf16[1296,128]{1,0:T(8,128)(2,1)S(1)}, u32[]{:S(2)}, u32[]{:S(2)}) collective-permute-start(bf16[1296,128]{1,0:T(8,128)(2,1)S(1)} %fusion.1.refs_0_), channel_id=1, source_target_pairs={{0,4},{4,0},{8,12},{12,8},{16,20},{20,16},{24,28},{28,24},{1,5},{5... | collective-permute-start | bytes 995336 | tf_op jit(solution)/shard_map/ppermute | solution.py:66
  16.5 39.1 %copy-start.16 = (bf16[1296,128]{1,0:T(8,128)(2,1)}, bf16[1296,128]{1,0:T(8,128)(2,1)S(1)}, u32[]{:S(2)}) copy-start(bf16[1296,128]{1,0:T(8,128)(2,1)S(1)} %collective-permute-done.2.refs_1_) | copy-start | bytes 995332
  23.3 23.7 %collective-permute-start.3 = (bf16[972,512]{1,0:T(8,128)(2,1)}, bf16[972,512]{1,0:T(8,128)(2,1)}, u32[]{:S(2)}, u32[]{:S(2)}) collective-permute-start(bf16[972,512]{1,0:T(8,128)(2,1)} %pad_maximum_fusion.1), channel_id=1, source_target_pairs={{1,0},{2,1},{3,2},{5,4},{6,5},{7,6},{9,8},{10,9},{11,10},{13,12},{... | collective-permute-start | bytes 2985992 | tf_op jit(solution)/shard_map/ppermute | solution.py:109
  25.6 23.6 %collective-permute-start.1 = (bf16[972,512]{1,0:T(8,128)(2,1)}, bf16[972,512]{1,0:T(8,128)(2,1)}, u32[]{:S(2)}, u32[]{:S(2)}) collective-permute-start(bf16[972,512]{1,0:T(8,128)(2,1)} %pad_maximum_fusion), channel_id=1, source_target_pairs={{1,0},{2,1},{3,2},{5,4},{6,5},{7,6},{9,8},{10,9},{11,10},{13,12},{... | collective-permute-start | bytes 2985992 | tf_op jit(solution)/shard_map/ppermute | solution.py:109
  26.9 18.2 %collective-permute-start.4 = (bf16[1296,128]{1,0:T(8,128)(2,1)S(1)}, bf16[1296,128]{1,0:T(8,128)(2,1)}, u32[]{:S(2)}, u32[]{:S(2)}) collective-permute-start(bf16[1296,128]{1,0:T(8,128)(2,1)S(1)} %fusion.1.refs_0_), channel_id=1, source_target_pairs={{0,16},{4,20},{8,24},{12,28},{16,0},{20,4},{24,8},{28,12},{1,17},{... | collective-permute-start | bytes 995336 | tf_op jit(solution)/shard_map/ppermute | solution.py:65
  28.3 22.5 %copy-start.14 = (bf16[1296,128]{1,0:T(8,128)(2,1)}, bf16[1296,128]{1,0:T(8,128)(2,1)S(1)}, u32[]{:S(2)}) copy-start(bf16[1296,128]{1,0:T(8,128)(2,1)S(1)} %collective-permute-done.5.refs_4_) | copy-start | bytes 995332
  28.3 16.8 %collective-permute-start.7 = (bf16[1296,128]{1,0:T(8,128)(2,1)S(1)}, bf16[1296,128]{1,0:T(8,128)(2,1)}, u32[]{:S(2)}, u32[]{:S(2)}) collective-permute-start(bf16[1296,128]{1,0:T(8,128)(2,1)S(1)} %collective-permute-done.refs_3_), channel_id=1, source_target_pairs={{0,4},{4,0},{8,12},{12,8},{16,20},{20,16},{24,28},{28,24},{1,5},{5... | collective-permute-start | bytes 995336 | tf_op jit(solution)/shard_map/ppermute | solution.py:67
  30.1 20.6 %copy-start.43 = (s32[8]{0:T(128)}, s32[8]{0:T(128)S(1)}, u32[]{:S(2)}) copy-start(s32[8]{0:T(128)S(1)} %stack.89) | copy-start | bytes 100
  30.1 20.6 %collective-permute-start.6 = (bf16[1296,128]{1,0:T(8,128)(2,1)S(1)}, bf16[1296,128]{1,0:T(8,128)(2,1)}, u32[]{:S(2)}, u32[]{:S(2)}) collective-permute-start(bf16[1296,128]{1,0:T(8,128)(2,1)S(1)} %collective-permute-done.2.refs_1_), channel_id=1, source_target_pairs={{0,4},{4,0},{8,12},{12,8},{16,20},{20,16},{24,28},{28,24},{1,5},{5... | collective-permute-start | bytes 995336 | tf_op jit(solution)/shard_map/ppermute | solution.py:68
  45.1 10.5 %collective-permute-start.8 = (bf16[1296,128]{1,0:T(8,128)(2,1)}, bf16[1296,128]{1,0:T(8,128)(2,1)}, u32[]{:S(2)}, u32[]{:S(2)}) collective-permute-start(bf16[1296,128]{1,0:T(8,128)(2,1)} %collective-permute-done.4.refs_2_), channel_id=1, source_target_pairs={{0,4},{4,0},{8,12},{12,8},{16,20},{20,16},{24,28},{28,24},{1,5},{5... | collective-permute-start | bytes 995336 | tf_op jit(solution)/shard_map/ppermute | solution.py:69
  60.1 21.7 %collective-permute-start.9 = (bf16[10240,128]{1,0:T(8,128)(2,1)S(1)}, bf16[10240,128]{1,0:T(8,128)(2,1)}, u32[]{:S(2)}, u32[]{:S(2)}) collective-permute-start(bf16[10240,128]{1,0:T(8,128)(2,1)S(1)} %order_tiles.1.refs_1_.refs_2_.refs_4_.refs_14_.refs_5_.refs_15_), channel_id=1, source_target_pairs={{0,1},{1,0},{2,3},{3,2},{4,5},{5,4},{6,7},{7,6},{8,9},{9,8},{10,11... | collective-permute-start | bytes 7864328 | tf_op jit(solution)/shard_map/ppermute | solution.py:1179
  62.3 15.5 %collective-permute-start.10 = (bf16[2048,128]{1,0:T(8,128)(2,1)S(1)}, bf16[2048,128]{1,0:T(8,128)(2,1)}, u32[]{:S(2)}, u32[]{:S(2)}) collective-permute-start(bf16[2048,128]{1,0:T(8,128)(2,1)S(1)} %get-tuple-element.288), channel_id=1, source_target_pairs={{0,2},{1,3},{2,0},{3,1},{4,6},{5,7},{6,4},{7,5},{8,10},{9,11},{10,... | collective-permute-start | bytes 1572872 | tf_op jit(solution)/shard_map/ppermute | solution.py:1063
  77.8 3.9 %collective-permute-start.11 = (bf16[2048,128]{1,0:T(8,128)(2,1)}, bf16[2048,128]{1,0:T(8,128)(2,1)S(1)}, u32[]{:S(2)}, u32[]{:S(2)}) collective-permute-start(bf16[2048,128]{1,0:T(8,128)(2,1)} %collective-permute-done.10.refs_3_.refs_6_.refs_17_), channel_id=1, source_target_pairs={{0,1},{1,0},{2,3},{3,2},{4,5},{5,4},{6,7},{7,6},{8,9},{9,8},{10,11... | collective-permute-start | bytes 1572872 | tf_op jit(solution)/shard_map/ppermute | solution.py:1066
  80.0 16.5 %collective-permute-start.12 = (bf16[2048,128]{1,0:T(8,128)(2,1)}, bf16[2048,128]{1,0:T(8,128)(2,1)S(1)}, u32[]{:S(2)}, u32[]{:S(2)}) collective-permute-start(bf16[2048,128]{1,0:T(8,128)(2,1)} %get-tuple-element.287), channel_id=1, source_target_pairs={{0,2},{1,3},{2,0},{3,1},{4,6},{5,7},{6,4},{7,5},{8,10},{9,11},{10,... | collective-permute-start | bytes 1572872 | tf_op jit(solution)/shard_map/ppermute | solution.py:1063
  96.6 2.0 collective-permute-start.13
  96.9 14.1 %collective-permute-start.14 = (bf16[2048,128]{1,0:T(8,128)(2,1)S(1)}, bf16[2048,128]{1,0:T(8,128)(2,1)S(1)}, u32[]{:S(2)}, u32[]{:S(2)}) collective-permute-start(bf16[2048,128]{1,0:T(8,128)(2,1)S(1)} %copy-done.34), channel_id=1, source_target_pairs={{0,2},{1,3},{2,0},{3,1},{4,6},{5,7},{6,4},{7,5},{8,10},{9,11},{10,... | collective-permute-start | bytes 1572872 | tf_op jit(solution)/shard_map/ppermute | solution.py:1063
  111.0 1.9 collective-permute-start.15
  112.3 14.4 %collective-permute-start.16 = (bf16[2048,128]{1,0:T(8,128)(2,1)S(1)}, bf16[2048,128]{1,0:T(8,128)(2,1)S(1)}, u32[]{:S(2)}, u32[]{:S(2)}) collective-permute-start(bf16[2048,128]{1,0:T(8,128)(2,1)S(1)} %copy-done.33), channel_id=1, source_target_pairs={{0,2},{1,3},{2,0},{3,1},{4,6},{5,7},{6,4},{7,5},{8,10},{9,11},{10,... | collective-permute-start | bytes 1572872 | tf_op jit(solution)/shard_map/ppermute | solution.py:1063
  126.7 1.9 collective-permute-start.17
  126.7 14.3 %collective-permute-start.18 = (bf16[2048,128]{1,0:T(8,128)(2,1)S(1)}, bf16[2048,128]{1,0:T(8,128)(2,1)S(1)}, u32[]{:S(2)}, u32[]{:S(2)}) collective-permute-start(bf16[2048,128]{1,0:T(8,128)(2,1)S(1)} %copy-done.32), channel_id=1, source_target_pairs={{0,2},{1,3},{2,0},{3,1},{4,6},{5,7},{6,4},{7,5},{8,10},{9,11},{10,... | collective-permute-start | bytes 1572872 | tf_op jit(solution)/shard_map/ppermute | solution.py:1063
  141.0 1.9 collective-permute-start.19
  152.3 16.2 %collective-permute-start.20 = (bf16[4096,128]{1,0:T(8,128)(2,1)}, bf16[4096,128]{1,0:T(8,128)(2,1)S(1)}, u32[]{:S(2)}, u32[]{:S(2)}) collective-permute-start(bf16[4096,128]{1,0:T(8,128)(2,1)} %get-tuple-element.200), channel_id=1, source_target_pairs={{0,1},{1,0},{2,3},{3,2},{4,5},{5,4},{6,7},{7,6},{8,9},{9,8},{10,11... | collective-permute-start | bytes 3145736 | tf_op jit(solution)/shard_map/ppermute | solution.py:95
  168.1 9.7 %collective-permute-start.22 = (bf16[4096,128]{1,0:T(8,128)(2,1)}, bf16[4096,128]{1,0:T(8,128)(2,1)S(1)}, u32[]{:S(2)}, u32[]{:S(2)}) collective-permute-start(bf16[4096,128]{1,0:T(8,128)(2,1)} %get-tuple-element.211), channel_id=1, source_target_pairs={{0,1},{1,0},{2,3},{3,2},{4,5},{5,4},{6,7},{7,6},{8,9},{9,8},{10,11... | collective-permute-start | bytes 3145736 | tf_op jit(solution)/shard_map/ppermute | solution.py:95
  168.6 14.8 %collective-permute-start.21 = (bf16[2048,128]{1,0:T(8,128)(2,1)S(1)}, bf16[2048,128]{1,0:T(8,128)(2,1)S(1)}, u32[]{:S(2)}, u32[]{:S(2)}) collective-permute-start(bf16[2048,128]{1,0:T(8,128)(2,1)S(1)} %add_convert_fusion.4), channel_id=1, source_target_pairs={{0,2},{1,3},{2,0},{3,1},{4,6},{5,7},{6,4},{7,5},{8,10},{9,11},{10,... | collective-permute-start | bytes 1572872 | tf_op jit(solution)/shard_map/ppermute | solution.py:104
  177.6 18.7 %collective-permute-start.24 = (bf16[4096,128]{1,0:T(8,128)(2,1)}, bf16[4096,128]{1,0:T(8,128)(2,1)S(1)}, u32[]{:S(2)}, u32[]{:S(2)}) collective-permute-start(bf16[4096,128]{1,0:T(8,128)(2,1)} %get-tuple-element.214), channel_id=1, source_target_pairs={{0,1},{1,0},{2,3},{3,2},{4,5},{5,4},{6,7},{7,6},{8,9},{9,8},{10,11... | collective-permute-start | bytes 3145736 | tf_op jit(solution)/shard_map/ppermute | solution.py:95
  177.7 18.6 %copy-start.28 = (bf16[4096,128]{1,0:T(8,128)(2,1)}, bf16[4096,128]{1,0:T(8,128)(2,1)S(1)}, u32[]{:S(2)}) copy-start(bf16[4096,128]{1,0:T(8,128)(2,1)S(1)} %collective-permute-done.22.refs_7_) | copy-start | bytes 3145732
  177.9 18.6 %collective-permute-start.23 = (bf16[2048,128]{1,0:T(8,128)(2,1)S(1)}, bf16[2048,128]{1,0:T(8,128)(2,1)S(1)}, u32[]{:S(2)}, u32[]{:S(2)}) collective-permute-start(bf16[2048,128]{1,0:T(8,128)(2,1)S(1)} %add_convert_fusion.3), channel_id=1, source_target_pairs={{0,2},{1,3},{2,0},{3,1},{4,6},{5,7},{6,4},{7,5},{8,10},{9,11},{10,... | collective-permute-start | bytes 1572872 | tf_op jit(solution)/shard_map/ppermute | solution.py:104
  196.5 17.9 %collective-permute-start.25 = (bf16[4096,128]{1,0:T(8,128)(2,1)}, bf16[4096,128]{1,0:T(8,128)(2,1)S(1)}, u32[]{:S(2)}, u32[]{:S(2)}) collective-permute-start(bf16[4096,128]{1,0:T(8,128)(2,1)} %get-tuple-element.230), channel_id=1, source_target_pairs={{0,1},{1,0},{2,3},{3,2},{4,5},{5,4},{6,7},{7,6},{8,9},{9,8},{10,11... | collective-permute-start | bytes 3145736 | tf_op jit(solution)/shard_map/ppermute | solution.py:95
  196.6 17.8 %copy-start.35 = (bf16[2048,128]{1,0:T(8,128)(2,1)S(1)}, bf16[2048,128]{1,0:T(8,128)(2,1)}, u32[]{:S(2)}) copy-start(bf16[2048,128]{1,0:T(8,128)(2,1)} %get-tuple-element.229) | copy-start | bytes 1572868
  213.5 11.4 %collective-permute-start.26 = (bf16[4160,128]{1,0:T(8,128)(2,1)}, bf16[4160,128]{1,0:T(8,128)(2,1)S(1)}, u32[]{:S(2)}, u32[]{:S(2)}) collective-permute-start(bf16[4160,128]{1,0:T(8,128)(2,1)} %get-tuple-element.228), channel_id=1, source_target_pairs={{0,1},{1,0},{2,3},{3,2},{4,5},{5,4},{6,7},{7,6},{8,9},{9,8},{10,11... | collective-permute-start | bytes 3194888 | tf_op jit(solution)/shard_map/ppermute | solution.py:95
  214.4 22.1 %collective-permute-start.28 = (bf16[2048,128]{1,0:T(8,128)(2,1)S(1)}, bf16[2048,128]{1,0:T(8,128)(2,1)S(1)}, u32[]{:S(2)}, u32[]{:S(2)}) collective-permute-start(bf16[2048,128]{1,0:T(8,128)(2,1)S(1)} %add_convert_fusion.2), channel_id=1, source_target_pairs={{0,2},{1,3},{2,0},{3,1},{4,6},{5,7},{6,4},{7,5},{8,10},{9,11},{10,... | collective-permute-start | bytes 1572872 | tf_op jit(solution)/shard_map/ppermute | solution.py:104
  214.6 25.8 %collective-permute-start.29 = (bf16[2048,128]{1,0:T(8,128)(2,1)S(1)}, bf16[2048,128]{1,0:T(8,128)(2,1)S(1)}, u32[]{:S(2)}, u32[]{:S(2)}) collective-permute-start(bf16[2048,128]{1,0:T(8,128)(2,1)S(1)} %add_convert_fusion.1), channel_id=1, source_target_pairs={{0,2},{1,3},{2,0},{3,1},{4,6},{5,7},{6,4},{7,5},{8,10},{9,11},{10,... | collective-permute-start | bytes 1572872 | tf_op jit(solution)/shard_map/ppermute | solution.py:104
  226.5 24.8 %collective-permute-start.27 = (bf16[2112,128]{1,0:T(8,128)(2,1)S(1)}, bf16[2112,128]{1,0:T(8,128)(2,1)S(1)}, u32[]{:S(2)}, u32[]{:S(2)}) collective-permute-start(bf16[2112,128]{1,0:T(8,128)(2,1)S(1)} %add_convert_fusion), channel_id=1, source_target_pairs={{0,2},{1,3},{2,0},{3,1},{4,6},{5,7},{6,4},{7,5},{8,10},{9,11},{10,... | collective-permute-start | bytes 1622024 | tf_op jit(solution)/shard_map/ppermute | solution.py:104
  256.6 29.1 %copy-start.58 = (bf16[1296,128]{1,0:T(8,128)(2,1)S(1)}, bf16[1296,128]{1,0:T(8,128)(2,1)}, u32[]{:S(2)}) copy-start(bf16[1296,128]{1,0:T(8,128)(2,1)} %get-tuple-element.273) | copy-start | bytes 995332
  256.6 31.5 %copy-start.6 = (bf16[784,512]{1,0:T(8,128)(2,1)S(1)}, bf16[784,512]{1,0:T(8,128)(2,1)}, u32[]{:S(2)}) copy-start(bf16[784,512]{1,0:T(8,128)(2,1)} %get-tuple-element.169.refs_5_.refs_13_.refs_0_) | copy-start | bytes 2408452
  256.6 31.5 %copy-start.7 = (bf16[784,512]{1,0:T(8,128)(2,1)S(1)}, bf16[784,512]{1,0:T(8,128)(2,1)}, u32[]{:S(2)}) copy-start(bf16[784,512]{1,0:T(8,128)(2,1)} %get-tuple-element.246.refs_2_) | copy-start | bytes 2408452
  256.6 31.5 %copy-start.12 = (bf16[512,512]{1,0:T(8,128)(2,1)S(1)}, bf16[512,512]{1,0:T(8,128)(2,1)}, u32[]{:S(2)}) copy-start(bf16[512,512]{1,0:T(8,128)(2,1)} %get-tuple-element.179.refs_1_) | copy-start | bytes 1572868
  256.6 31.5 %copy-start.13 = (bf16[512,512]{1,0:T(8,128)(2,1)S(1)}, bf16[512,512]{1,0:T(8,128)(2,1)}, u32[]{:S(2)}) copy-start(bf16[512,512]{1,0:T(8,128)(2,1)} %get-tuple-element.209.refs_3_) | copy-start | bytes 1572868
  256.6 11.0 %collective-permute-start.34 = (bf16[1296,128]{1,0:T(8,128)(2,1)}, bf16[1296,128]{1,0:T(8,128)(2,1)S(1)}, u32[]{:S(2)}, u32[]{:S(2)}) collective-permute-start(bf16[1296,128]{1,0:T(8,128)(2,1)} %get-tuple-element.266), channel_id=1, source_target_pairs={{0,4},{4,0},{8,12},{12,8},{16,20},{20,16},{24,28},{28,24},{1,5},{5... | collective-permute-start | bytes 995336 | tf_op jit(solution)/shard_map/ppermute | solution.py:84
  258.2 15.0 %collective-permute-start.36 = (bf16[1296,128]{1,0:T(8,128)(2,1)}, bf16[1296,128]{1,0:T(8,128)(2,1)S(1)}, u32[]{:S(2)}, u32[]{:S(2)}) collective-permute-start(bf16[1296,128]{1,0:T(8,128)(2,1)} %get-tuple-element.268), channel_id=1, source_target_pairs={{0,4},{4,0},{8,12},{12,8},{16,20},{20,16},{24,28},{28,24},{1,5},{5... | collective-permute-start | bytes 995336 | tf_op jit(solution)/shard_map/ppermute | solution.py:84
  258.7 24.0 %collective-permute-start.31 = (bf16[384,512]{1,0:T(8,128)(2,1)S(1)}, bf16[384,512]{1,0:T(8,128)(2,1)S(1)}, u32[]{:S(2)}, u32[]{:S(2)}) collective-permute-start(bf16[384,512]{1,0:T(8,128)(2,1)S(1)} %copy-done.56), channel_id=1, source_target_pairs={{0,1},{1,2},{2,3},{4,5},{5,6},{6,7},{8,9},{9,10},{10,11},{12,13},{... | collective-permute-start | bytes 1179656 | tf_op jit(solution)/shard_map/ppermute | solution.py:153
  260.0 25.6 %collective-permute-start.33 = (bf16[384,512]{1,0:T(8,128)(2,1)S(1)}, bf16[384,512]{1,0:T(8,128)(2,1)S(1)}, u32[]{:S(2)}, u32[]{:S(2)}) collective-permute-start(bf16[384,512]{1,0:T(8,128)(2,1)S(1)} %copy-done.57), channel_id=1, source_target_pairs={{0,1},{1,2},{2,3},{4,5},{5,6},{6,7},{8,9},{9,10},{10,11},{12,13},{... | collective-permute-start | bytes 1179656 | tf_op jit(solution)/shard_map/ppermute | solution.py:153
  263.2 24.0 %collective-permute-start.30 = (bf16[592,512]{1,0:T(8,128)(2,1)S(1)}, bf16[592,512]{1,0:T(8,128)(2,1)S(1)}, u32[]{:S(2)}, u32[]{:S(2)}) collective-permute-start(bf16[592,512]{1,0:T(8,128)(2,1)S(1)} %copy-done.45), channel_id=1, source_target_pairs={{0,1},{1,2},{2,3},{4,5},{5,6},{6,7},{8,9},{9,10},{10,11},{12,13},{... | collective-permute-start | bytes 1818632 | tf_op jit(solution)/shard_map/ppermute | solution.py:153
  267.6 20.5 %collective-permute-start.32 = (bf16[592,512]{1,0:T(8,128)(2,1)S(1)}, bf16[592,512]{1,0:T(8,128)(2,1)S(1)}, u32[]{:S(2)}, u32[]{:S(2)}) collective-permute-start(bf16[592,512]{1,0:T(8,128)(2,1)S(1)} %copy-done.46), channel_id=1, source_target_pairs={{0,1},{1,2},{2,3},{4,5},{5,6},{6,7},{8,9},{9,10},{10,11},{12,13},{... | collective-permute-start | bytes 1818632 | tf_op jit(solution)/shard_map/ppermute | solution.py:153
  273.2 8.5 %collective-permute-start.38 = (bf16[1296,128]{1,0:T(8,128)(2,1)}, bf16[1296,128]{1,0:T(8,128)(2,1)S(1)}, u32[]{:S(2)}, u32[]{:S(2)}) collective-permute-start(bf16[1296,128]{1,0:T(8,128)(2,1)} %get-tuple-element.271), channel_id=1, source_target_pairs={{0,4},{4,0},{8,12},{12,8},{16,20},{20,16},{24,28},{28,24},{1,5},{5... | collective-permute-start | bytes 995336 | tf_op jit(solution)/shard_map/ppermute | solution.py:84
  281.6 22.3 %collective-permute-start.35 = (bf16[1296,128]{1,0:T(8,128)(2,1)S(1)}, bf16[1296,128]{1,0:T(8,128)(2,1)S(1)}, u32[]{:S(2)}, u32[]{:S(2)}) collective-permute-start(bf16[1296,128]{1,0:T(8,128)(2,1)S(1)} %add_convert_fusion.7), channel_id=1, source_target_pairs={{0,16},{4,20},{8,24},{12,28},{16,0},{20,4},{24,8},{28,12},{1,17},{... | collective-permute-start | bytes 995336 | tf_op jit(solution)/shard_map/ppermute | solution.py:90
  282.7 21.2 %collective-permute-start.37 = (bf16[1296,128]{1,0:T(8,128)(2,1)S(1)}, bf16[1296,128]{1,0:T(8,128)(2,1)S(1)}, u32[]{:S(2)}, u32[]{:S(2)}) collective-permute-start(bf16[1296,128]{1,0:T(8,128)(2,1)S(1)} %add_convert_fusion.6), channel_id=1, source_target_pairs={{0,8},{4,12},{8,16},{12,20},{16,24},{20,28},{24,0},{28,4},{1,9},{5... | collective-permute-start | bytes 995336 | tf_op jit(solution)/shard_map/ppermute | solution.py:90
  285.7 18.2 %collective-permute-start.40 = (bf16[1296,128]{1,0:T(8,128)(2,1)S(1)}, bf16[1296,128]{1,0:T(8,128)(2,1)S(1)}, u32[]{:S(2)}, u32[]{:S(2)}) collective-permute-start(bf16[1296,128]{1,0:T(8,128)(2,1)S(1)} %copy-done.58), channel_id=1, source_target_pairs={{0,4},{4,0},{8,12},{12,8},{16,20},{20,16},{24,28},{28,24},{1,5},{5... | collective-permute-start | bytes 995336 | tf_op jit(solution)/shard_map/ppermute | solution.py:84
  287.2 20.6 %collective-permute-start.39 = (bf16[1296,128]{1,0:T(8,128)(2,1)S(1)}, bf16[1296,128]{1,0:T(8,128)(2,1)S(1)}, u32[]{:S(2)}, u32[]{:S(2)}) collective-permute-start(bf16[1296,128]{1,0:T(8,128)(2,1)S(1)} %add_convert_fusion.5), channel_id=1, source_target_pairs={{0,24},{4,28},{8,0},{12,4},{16,8},{20,12},{24,16},{28,20},{1,25},{... | collective-permute-start | bytes 995336 | tf_op jit(solution)/shard_map/ppermute | solution.py:90
  288.1 19.6 %copy-start.1 = (f32[1,10,128,128]{3,2,1,0:T(8,128)S(1)}, f32[1,10,128,128]{3,2,1,0:T(8,128)}, u32[]{:S(2)}) copy-start(f32[1,10,128,128]{3,2,1,0:T(8,128)} %refs_5_.1) | copy-start | bytes 1966084
  288.2 19.6 %copy-start.8 = (f32[1,10,128,128]{3,2,1,0:T(8,128)S(1)}, f32[1,10,128,128]{3,2,1,0:T(8,128)}, u32[]{:S(2)}) copy-start(f32[1,10,128,128]{3,2,1,0:T(8,128)} %refs_6_.1) | copy-start | bytes 1966084
  288.2 19.6 %copy-start.9 = (f32[1,10,128,128]{3,2,1,0:T(8,128)S(1)}, f32[1,10,128,128]{3,2,1,0:T(8,128)}, u32[]{:S(2)}) copy-start(f32[1,10,128,128]{3,2,1,0:T(8,128)} %refs_7_.1) | copy-start | bytes 1966084
  288.2 19.6 %copy-start.10 = (f32[1,10,128,128]{3,2,1,0:T(8,128)S(1)}, f32[1,10,128,128]{3,2,1,0:T(8,128)}, u32[]{:S(2)}) copy-start(f32[1,10,128,128]{3,2,1,0:T(8,128)} %refs_8_.1) | copy-start | bytes 1966084
  288.2 19.6 %copy-start.11 = (f32[1,10,128,128]{3,2,1,0:T(8,128)S(1)}, f32[1,10,128,128]{3,2,1,0:T(8,128)}, u32[]{:S(2)}) copy-start(f32[1,10,128,128]{3,2,1,0:T(8,128)} %refs_9_.1) | copy-start | bytes 1966084
  288.2 19.6 %copy-start.18 = (bf16[1296,128]{1,0:T(8,128)(2,1)S(1)}, bf16[1296,128]{1,0:T(8,128)(2,1)}, u32[]{:S(2)}) copy-start(bf16[1296,128]{1,0:T(8,128)(2,1)} %get-tuple-element.253.refs_0_) | copy-start | bytes 995332
  288.2 19.6 %copy-start.19 = (f32[10,64]{1,0:T(8,128)S(1)}, f32[10,64]{1,0:T(8,128)}, u32[]{:S(2)}) copy-start(f32[10,64]{1,0:T(8,128)} %refs_10_.1) | copy-start | bytes 7684
  288.2 19.6 %copy-start.21 = (f32[10,64]{1,0:T(8,128)S(1)}, f32[10,64]{1,0:T(8,128)}, u32[]{:S(2)}) copy-start(f32[10,64]{1,0:T(8,128)} %refs_11_.1) | copy-start | bytes 7684
  (37 other events, 278.9 us)

commit v4 on v3

v4 whole, which is shorter than its diff:
```python
import jax
import jax.numpy as jnp
from jax import lax
from jax.experimental import pallas as pl
from jax.experimental.pallas import tpu as pltpu
from jax.sharding import PartitionSpec as P

D = 512
HEADS = 8
HEAD_DIM = 64
FF = 1024
TILE = 128
CHUNK = 16
CHUNKS = 5

NORM_EPSILON = 1e-05
MATRIX_RATE = 0.5
VECTOR_RATE = 0.2
STAT_DECAY = 0.5
MASKED_SCORE = -1e30

F32 = jnp.float32
BF16 = jnp.bfloat16
ANY = pl.BlockSpec(memory_space=pl.ANY)
VM = pl.BlockSpec(memory_space=pltpu.VMEM)
SM = pl.BlockSpec(memory_space=pltpu.SMEM)
HB = pl.BlockSpec(memory_space=pltpu.HBM)


def core_pairs():
    return [(i, i ^ 1) for i in range(4)]


def chip_pairs():
    return [(i, i ^ 2) for i in range(4)]


def diagonal_pairs():
    return [(i, i ^ 3) for i in range(4)]


def y_pairs():
    return [(i, i ^ 1) for i in range(8)]


def z_shift(step):
    return [(2 * z + y, 2 * ((z + step) % 4) + y) for z in range(4) for y in range(2)]


def relative_rank(position, size):
    me = lax.axis_index("dp")
    if size != 8:
        return jnp.int32(position)
    swapped, step = divmod(position, 4)
    return 2 * lax.rem(me // 2 - step + 4, 4) + lax.rem(me + swapped, 2)


def target_rank(position, size):
    me = lax.axis_index("dp")
    if size != 8:
        return jnp.int32(position)
    swapped, step = divmod(position, 4)
    return 2 * lax.rem(me // 2 + step, 4) + lax.rem(me + swapped, 2)


def after(value, *others):
    return lax.optimization_barrier((value, *others))[0]


def together(*arrived):
    return lax.optimization_barrier(arrived)


def gather_rows(image, tags, cotangents, piece, size, meanwhile, ready):
    shards = lax.axis_size("tensor")
    split = tags.shape[0]

    def near(value):
        return lax.ppermute(value, "tensor", core_pairs())

    def far(value):
        return lax.ppermute(value, "tensor", chip_pairs())

    def later(value):
        return lax.ppermute(value, "tensor", [(i + 1, i) for i in range(shards - 1)])

    both = jnp.concatenate([tags, image], axis=0)
    if size != 8:
        pieces = list(lax.all_gather(piece, "dp", axis=0, tiled=False))
        near_both, far_image, far_tags = near(both), far(image), far(tags)
        last_image, last_tags, moved = near(far_image), near(far_tags), later(cotangents)
        images = meanwhile([(image, 0), (near_both, split), (far_image, 0), (last_image, 0)], ready[0])
    else:

        def column(part, step):
            return lax.ppermute(part, "dp", z_shift(step))

        def row(part):
            return lax.ppermute(part, "dp", y_pairs())

        one, three, other, far_image, near_both, *ready = together(
            column(piece, 1), column(piece, 3), row(piece), far(image), near(both), *ready
        )
        two, row_one, row_three, far_tags, last_image = together(
            column(after(piece, other), 2), row(one), row(three), far(after(tags, other)), near(far_image)
        )
        images = [(image, 0), (near_both, split), (far_image, 0), (last_image, 0)]
        images, row_two, last_tags, moved = together(
            meanwhile(images, ready[0]), row(two), near(far_tags), later(after(cotangents, two))
        )
        pieces = [piece, one, two, three, other, row_one, row_two, row_three]
    sequences = [(tags, 0), (near_both, 0), (far_tags, 0), (last_tags, 0)]
    return pieces, images, sequences, moved, ready


def sum_pieces(pieces, size):
    if size != 8:
        whole = lax.psum_scatter(
            jnp.stack(pieces).astype(F32), "dp", scatter_dimension=0, tiled=False
        )
        return [whole.astype(BF16)], pieces[0]
    column, ready, mark = [pieces[0]], [], None
    for at, step in enumerate((2, 1, 3, 0)):
        piece = pieces[4 + step]
        if at > 1:
            piece = lax.optimization_barrier((piece, ready[at - 2]))[0]
        other = lax.ppermute(piece, "dp", y_pairs())
        if step == 0:
            column.append(other)
            continue
        both = (pieces[step].astype(F32) + other.astype(F32)).astype(BF16)
        ready.append(both)
        column.append(lax.ppermute(both, "dp", z_shift(step)))
    return column, pieces[0]


GROUPS = ((12, 20), (44, 20), (64, 16))


def send_near(part):
    return lax.ppermute(part[1], "tensor", core_pairs())


def sum_far(part, near):
    rows = part[0].shape[0]
    return (part[2].astype(F32) + near[rows : rows + part[2].shape[0]].astype(F32)).astype(BF16)


def send_far(value):
    return lax.ppermute(value, "tensor", chip_pairs())


def spread(pieces):
    return [
        pieces[0],
        lax.ppermute(pieces[1], "tensor", core_pairs()),
        lax.ppermute(pieces[2], "tensor", chip_pairs()),
        lax.ppermute(pieces[3], "tensor", diagonal_pairs()),
    ]


def whole_group(parts, info, name):
    shards = len(parts)
    count = parts[0][0].shape[0]

    def kernel(info_ref, *refs):
        refs, out = refs[:-1], refs[-1]
        refs = [ref.at[pl.ds(first, count)] for ref, (_, first) in zip(refs, parts)]
        for t in range(shards):

            @pl.when(info_ref[0, 1] == t)
            def _(t=t):
                out[...] = jnp.concatenate([refs[r ^ t][...].astype(F32) for r in range(shards)], axis=0).astype(BF16)

    return pl.pallas_call(
        kernel,
        out_shape=jax.ShapeDtypeStruct((count * shards, D), BF16),
        in_specs=[SM] + [VM] * shards,
        out_specs=VM,
        compiler_params=pltpu.CompilerParams(vmem_limit_bytes=56 * 2**20),
        name=name,
    )(info, *[a for a, _ in parts])


def fill_item(info_ref, own, later, out):
    shards = 4
    own, later = own[...].astype(F32), later[...].astype(F32)
    rows, length = own.shape[0], out.shape[0]
    for t in range(shards):

        @pl.when(info_ref[0, 1] == t)
        def _(t=t):
            if t == shards - 1:
                both = jnp.zeros(out.shape, F32)
            else:
                start = (length - rows) * t
                both = jnp.concatenate([own[start:, :], later[: length - rows + start, :]], axis=0)
            out[...] = both.astype(BF16)


def push_tails(tails):
    shards = lax.axis_size("tensor")
    return lax.ppermute(tails, "tensor", [(i, i + 1) for i in range(shards - 1)])


def push_rows(items, pushed, counts, sums, info):
    shards = lax.axis_size("tensor")
    n = len(items)
    sizes = [item.shape[0] - tail_rows(item.shape[0], count) for item, count in zip(items, counts)]
    extra = [a for terms in sums if terms for a, _ in terms]

    def kernel(info_ref, *refs):
        owns, before, more, outs = refs[:n], refs[n], refs[n + 1 : -n], refs[-n:]
        for t in range(shards):

            @pl.when(info_ref[0, 1] == t)
            def _(t=t):
                used = end = 0
                for own, size, out, terms in zip(owns, sizes, outs, sums):
                    end += size
                    count, length = out.shape[0], own.shape[0]
                    mine = count - (length - count) * t
                    rows = [before[...].astype(F32)[end - count + mine : end, :]] if t else []
                    if mine:
                        rows.append(own[...].astype(F32)[:mine, :])
                    rows = jnp.concatenate(rows, axis=0) if len(rows) > 1 else rows[0]
                    if terms:
                        piece, whole = piece_size(count), count * shards
                        skip = count * t - min(count * t // 16 * 16, whole - piece)
                        added = None
                        for _, begin in terms:
                            term = more[used][begin : begin + piece, :].astype(F32)
                            added = term if added is None else added + term
                            used += 1
                        rows = rows + added[skip : skip + count, :]
                    out[...] = rows.astype(out.dtype)

    return pl.pallas_call(
        kernel,
        out_shape=[jax.ShapeDtypeStruct((c, D), F32 if terms else BF16) for c, terms in zip(counts, sums)],
        in_specs=[SM] + [VM] * (n + 1 + len(extra)),
        out_specs=[VM] * n,
        compiler_params=pltpu.CompilerParams(vmem_limit_bytes=32 * 2**20),
        name="push_gradients" if extra else "push_outputs",
    )(info, *items, pushed, *extra)


def order_tiles(pieces, block_ids, ranks, slots, lanes):
    total = CHUNK * CHUNKS

    def kernel(ids, to, *refs):
        sources, (out, *groups, vector_ref) = refs[: -2 - len(GROUPS)], refs[-2 - len(GROUPS) :]
        feature = lax.broadcasted_iota(jnp.int32, (TILE, D), 1)
        lane = lax.broadcasted_iota(jnp.int32, (TILE, D), 0)
        vectors = jnp.zeros((16, D), F32)
        for p, source in enumerate(sources):
            for j in range(slots):
                block = ids[p, j]
                tile = source[j * TILE : (j + 1) * TILE, :]

                @pl.when(block < total)
                def _(block=block, tile=tile):
                    out.held[pl.ds(pl.multiple_of(block * TILE, TILE), TILE), :] = tile

            pick = ((feature == to[p] * lanes + lane) & (lane < lanes)).astype(BF16)
            vectors = vectors + matmul(source[slots * TILE :, :], pick)
        vector_ref[...] = vectors
        out.send()
        for (first, number), ref in zip(GROUPS, groups):
            ref[...] = out[first * TILE : (first + number) * TILE, :]

    args = [Part((piece, 0, slots * TILE + 16)) for piece in pieces]
    outs = [struct((total * TILE, TILE), BF16)] + [Held(struct((number * TILE, TILE), BF16)) for _, number in GROUPS]
    outs.append(struct((16, D), F32))
    return call(kernel, "order_tiles", outs, [], block_ids, ranks, *args)


def deal_tiles(groups, finals, extra, block_ids, ranks, slots, lanes):
    count = ranks.shape[0]
    total = CHUNK * CHUNKS
    rows = slots * TILE + 16
    sizes = [number * TILE for _, number in GROUPS[: len(groups)]]
    order = tuple(reversed(range(len(groups))))

    def kernel(ids, to, *refs):
        done, refs = refs[: len(finals)], refs[len(finals) :]
        sources, refs = refs[: 3 * len(groups)], refs[3 * len(groups) :]
        near_extra, far_extra, v_ref, *outs, held = refs
        held[total * TILE :, :] = jnp.zeros((TILE, TILE), BF16)
        for (block, array), ref in zip(finals, done):
            held[block * TILE : block * TILE + array.shape[0], :] = ref[...]
        for place, at in enumerate(order):
            own, near, far = sources[3 * place : 3 * place + 3]
            first = GROUPS[at][0] * TILE
            held[first : first + sizes[at], :] = (
                own[...].astype(F32) + near[...].astype(F32) + far[...].astype(F32)
            ).astype(BF16)
        summed = (
            v_ref[...].astype(F32) + near_extra[...].astype(F32) + far_extra[...].astype(F32)
        ).astype(BF16)
        summed = jnp.concatenate([summed[16 * j : 16 * (j + 1)] for j in range(4)], axis=1)
        feature = lax.broadcasted_iota(jnp.int32, (D, TILE), 0)
        lane = lax.broadcasted_iota(jnp.int32, (D, TILE), 1)
        for p, out in enumerate(outs):
            for j in range(slots):
                block = jnp.minimum(ids[p, j], total)
                out[j * TILE : (j + 1) * TILE, :] = held[
                    pl.ds(pl.multiple_of(block * TILE, TILE), TILE), :
                ]
            pick = ((feature == to[p] * lanes + lane) & (lane < lanes)).astype(BF16)
            out[slots * TILE :, :] = matmul(summed, pick).astype(BF16)
            send(out)

    flat = [Part((a, 0, sizes[at])) for at in order for a in groups[at]]
    _, near, far = groups[0]
    return call(
        kernel,
        "deal_tiles",
        [Held(struct((rows, TILE), BF16)) if count == 8 else struct((rows, TILE), BF16)] * count,
        [pltpu.VMEM(((total + 1) * TILE, TILE), BF16)],
        block_ids,
        ranks,
        *[Part((a, 0, a.shape[0])) for _, a in finals],
        *flat,
        Part((near, 2 * sizes[0], VECTOR_ROWS)),
        Part((far, sizes[0], VECTOR_ROWS)),
        extra,
    )


def sum_group(own, near, far):
    size = own.shape[0]

    def kernel(own_ref, near_ref, far_ref, out):
        out[...] = (
            own_ref[...].astype(F32) + near_ref[...].astype(F32) + far_ref[...].astype(F32)
        ).astype(BF16)

    return call(kernel, "sum_group", [struct((size, TILE), BF16)], [], *[Part((a, 0, size)) for a in (own, near, far)])[0]


def shampoo(terms, master, left, right, left_root, right_root, vector_master, vector_moment):
    slots = master.shape[1]
    lanes = vector_master.shape[1]

    def split(a):
        high = a.astype(BF16)
        return high, (a - high.astype(F32)).astype(BF16)

    def exact(a, b, dims):
        def product(x, y):
            return lax.dot_general(x, y, (dims, ((), ())), preferred_element_type=F32)

        return product(a[0], b[0]) + (product(a[0], b[1]) + product(a[1], b[0]))

    def kernel(*refs):
        parts, refs = refs[: len(terms)], refs[len(terms) :]
        m_ref, l_ref, r_ref, lr_ref, rr_ref, vm_ref, vn_ref = refs[:7]
        targets, (vg_out, vn_out, vm_out) = refs[7:12], refs[12:15]
        held, sem = refs[15:20], refs[20]

        def rows_at(a, b):
            total = parts[0][a:b, :].astype(F32)
            for part in parts[1:]:
                total = total + part[a:b, :].astype(F32)
            return total

        copies = []
        for s in range(slots):
            g = rows_at(s * TILE, (s + 1) * TILE)
            gs = split(g)
            rotated = exact(split(lr_ref[0, s]), gs, ((1,), (0,)))
            updated = m_ref[0, s] - MATRIX_RATE * exact(split(rotated), split(rr_ref[0, s]), ((1,), (0,)))
            values = (
                g,
                STAT_DECAY * l_ref[0, s] + (1.0 - STAT_DECAY) * exact(gs, gs, ((1,), (1,))),
                STAT_DECAY * r_ref[0, s] + (1.0 - STAT_DECAY) * exact(gs, gs, ((0,), (0,))),
                updated,
                updated.astype(BF16),
            )
            for k, value in enumerate(values):
                held[k][0, s] = value
                copy = pltpu.make_async_copy(held[k].at[0, s], targets[k].at[0, s], sem.at[k, s])
                copy.start()
                copies.append(copy)
        g = rows_at(slots * TILE, slots * TILE + 16)[:10, :lanes]
        moment = STAT_DECAY * vn_ref[...] + (1.0 - STAT_DECAY) * g * g
        vg_out[...] = g
        vn_out[...] = moment
        vm_out[...] = vm_ref[...] - VECTOR_RATE * g / (jnp.sqrt(moment) + 1e-08)
        for copy in copies:
            copy.wait()

    whole = jax.ShapeDtypeStruct(master.shape, F32)
    row = jax.ShapeDtypeStruct(vector_master.shape, F32)
    outs = [whole] * 4 + [jax.ShapeDtypeStruct(master.shape, BF16)] + [row] * 3
    return pl.pallas_call(
        kernel,
        out_shape=outs,
        in_specs=[VM] * (len(terms) + 7),
        out_specs=[HB] * 5 + [VM] * 3,
        scratch_shapes=[
            *[pltpu.VMEM(o.shape, o.dtype) for o in outs[:5]],
            pltpu.SemaphoreType.DMA((5, slots)),
        ],
        compiler_params=pltpu.CompilerParams(vmem_limit_bytes=24 * 2**20),
        name="shampoo",
    )(*terms, master, left, right, left_root, right_root, vector_master, vector_moment)


LOG2E = 1.4426950408889634
SCORE_SCALE = HEAD_DIM ** (-0.5)
SCORE_LOG2 = SCORE_SCALE * LOG2E
PAIRS = HEADS // 2


def matmul(former, latter):
    return jnp.dot(former, latter, preferred_element_type=F32)


def times_transpose(former, latter):
    return lax.dot_general(former, latter, (((1,), (1,)), ((), ())), preferred_element_type=F32)


def transpose_times(former, latter):
    return lax.dot_general(former, latter, (((0,), (0,)), ((), ())), preferred_element_type=F32)


def low(value):
    return value.astype(BF16)


def tile_at(part, index):
    return part[index * TILE : (index + 1) * TILE, :]


def column_matrix(parts, first, count, column):
    return jnp.concatenate(
        [
            jnp.concatenate([tile_at(p, first + a * count + column) for p in parts], axis=1)
            for a in range(4)
        ],
        axis=0,
    )


def row_matrix(parts, first, group):
    return jnp.concatenate(
        [
            jnp.concatenate([tile_at(p, first + 4 * group + b) for b in range(4)], axis=1)
            for p in parts
        ],
        axis=0,
    )


def store_columns(parts, gradient, first, count, column):
    for r, part in enumerate(parts):
        for a in range(4):
            at = (first + a * count + column) * TILE
            part[at : at + TILE, :] = low(
                gradient[a * TILE : (a + 1) * TILE, r * TILE : (r + 1) * TILE]
            )


def store_rows(parts, gradient, first, group):
    for r, part in enumerate(parts):
        for b in range(4):
            at = (first + 4 * group + b) * TILE
            part[at : at + TILE, :] = low(
                gradient[r * TILE : (r + 1) * TILE, b * TILE : (b + 1) * TILE]
            )


def spans(count):
    half = (count // 2 + 15) // 16 * 16
    return [(0, half), (half, count)]


def norm_rows(value):
    mean = jnp.mean(value, axis=-1, keepdims=True)
    centered = value - mean
    scale = lax.rsqrt(jnp.mean(centered * centered, axis=-1, keepdims=True) + NORM_EPSILON)
    return centered * scale, scale


def norm_back(gradient, normed, scale, gain):
    scaled = gradient * gain
    return scale * (
        scaled
        - jnp.mean(scaled, axis=-1, keepdims=True)
        - normed * jnp.mean(scaled * normed, axis=-1, keepdims=True)
    )


def gate_both(value):
    size = jnp.abs(value) * (0.5**0.5)
    turn = 1.0 / (1.0 + 0.3275911 * size)
    bell = jnp.exp2(value * value * (-0.5 * LOG2E))
    series = turn * (
        0.254829592
        + turn * (-0.284496736 + turn * (1.421413741 + turn * (-1.453152027 + turn * 1.061405429)))
    )
    tail = 0.5 * series * bell
    phi = jnp.where(value < 0, tail, 1.0 - tail)
    return value * phi, phi + value * bell * 0.3989422804014327


STATS = 16


def store_stats(stat_ref, stats, *scales):
    if stats is None:
        stats = jnp.zeros((scales[0].shape[0], TILE), F32)
    lane = lax.broadcasted_iota(jnp.int32, stats.shape, 1)
    for at, scale in enumerate(scales):
        stats = jnp.where(lane == HEADS + at, scale, stats)
    stat_ref[...] = stats.T[:STATS, :]


def norm_scales(stat_ref, count):
    columns = jnp.concatenate([stat_ref[...]] * (TILE // STATS), axis=0).T
    return [columns[:, HEADS + at : HEADS + at + 1] for at in range(count)]


def half_mask(which):
    lane = lax.broadcasted_iota(jnp.int32, (1, TILE), 1)
    return (lane < HEAD_DIM) if which == 0 else (lane >= HEAD_DIM)


def attend_pair(queries, key_rows, value_rows, bias, first, stats):
    values = jnp.concatenate([value_rows, jnp.ones_like(value_rows)], axis=1)
    lane = lax.broadcasted_iota(jnp.int32, stats.shape, 1)
    mixed = []
    for which in range(2):
        masked = jnp.where(half_mask(which), queries, jnp.zeros_like(queries))
        scores = times_transpose(masked, key_rows) * SCORE_LOG2
        if bias is not None:
            scores = scores + bias
        top = jnp.max(scores, axis=1, keepdims=True)
        both = matmul(low(jnp.exp2(scores - top)), values)
        total = both[:, TILE:]
        mixed.append(both[:, :TILE] / total)
        stats = jnp.where(lane == first + which, top + jnp.log2(total), stats)
    return low(jnp.where(half_mask(0), mixed[0], mixed[1])), stats


def pair_back(queries, key_rows, value_rows, incoming, stats, deltas, bias):
    key_columns = key_rows.T
    dk = dv = None
    dq = []
    for which in range(2):
        mask = half_mask(which)
        q_one = jnp.where(mask, queries, jnp.zeros_like(queries))
        do_one = jnp.where(mask, incoming, jnp.zeros_like(incoming))
        scores = times_transpose(key_rows, q_one) * SCORE_LOG2
        if bias is not None:
            scores = scores + bias
        weights = jnp.exp2(scores - stats[which])
        d_weights = times_transpose(value_rows, do_one)
        d_scores = low(weights * (d_weights - deltas[which]))
        dv_one = matmul(low(weights), do_one)
        dk_one = matmul(d_scores, q_one)
        dv = dv_one if dv is None else dv + dv_one
        dk = dk_one if dk is None else dk + dk_one
        rows = slice(which * HEAD_DIM, (which + 1) * HEAD_DIM)
        dq.append(low(matmul(key_columns[rows, :], d_scores) * SCORE_SCALE))
    return jnp.concatenate(dq, axis=0).T, low(dk * SCORE_SCALE), low(dv)


def pair_columns(pair):
    return slice(pair * TILE, (pair + 1) * TILE)


def pair_rows(ref, pair):
    return [ref[h : h + 1, :] for h in (2 * pair, 2 * pair + 1)]


def row_products(incoming, mixed):
    product = incoming * mixed
    first = low(product)
    rest = low(product - first.astype(F32))
    lane = lax.broadcasted_iota(jnp.int32, (STATS, product.shape[1]), 1) // HEAD_DIM
    row = lax.broadcasted_iota(jnp.int32, (STATS, product.shape[1]), 0)
    pick = (lane == row).astype(BF16)
    return times_transpose(pick, first) + times_transpose(pick, rest)


def struct(shape, dtype):
    return jax.ShapeDtypeStruct(shape, dtype)


class Inward:
    def __init__(self, source, held, sem):
        self.shape = held.shape
        self.copy, self.held, self.waiting = pltpu.make_async_copy(source, held, sem), held, True
        self.copy.start()

    def wait(self):
        if self.waiting:
            self.copy.wait()
            self.waiting = False

    def __getitem__(self, index):
        self.wait()
        return self.held[index]


class Outward:
    def __init__(self, held, target, sem):
        self.held, self.target, self.sem, self.copies = held, target, sem, []
        self.shape, self.dtype = held.shape, held.dtype

    @property
    def at(self):
        return self.held.at

    def __getitem__(self, index):
        return self.held[index]

    def __setitem__(self, index, value):
        self.held[index] = value

    def send(self, *spans_of):
        for a, b in spans_of or ((0, self.shape[0]),):
            rows = pl.ds(a, b - a)
            copy = pltpu.make_async_copy(
                self.held.at[rows], self.target.at[rows], self.sem.at[len(self.copies)]
            )
            copy.start()
            self.copies.append(copy)

    def finish(self):
        if not self.copies:
            self.send()


def send(out, *spans_of):
    if isinstance(out, Outward):
        out.send(*spans_of)


SENDS = 4


class Part(tuple):
    pass


class Own(tuple):
    pass


class Held:
    def __init__(self, array):
        self.array = array


def call(kernel, name, outs, scratch, *args, flops=0, limit=52):
    plain, held, takes = [], [], []
    for arg in args:
        part = None
        if isinstance(arg, Held):
            plain.append(pltpu.with_memory_space_constraint(arg.array, pltpu.VMEM))
            takes.append(None)
            continue
        free = isinstance(arg, Part)
        if isinstance(arg, Own):
            array, rows = arg
            plain.append(pltpu.with_memory_space_constraint(array, pltpu.HBM))
            takes.append((None, rows, slice(0, array.shape[1]), False))
            held.append(pltpu.VMEM((rows, array.shape[1]), array.dtype))
            continue
        if isinstance(arg, tuple):
            arg, *part = arg
        if arg.dtype == jnp.int32:
            plain.append(arg)
            takes.append(None)
            continue
        plain.append(arg if free else pltpu.with_memory_space_constraint(arg, pltpu.HBM))
        if part is None:
            part = (0, arg.shape[0])
        columns = part[2] if len(part) > 2 else slice(0, arg.shape[1])
        takes.append((part[0], part[1], columns, free))
        held.append(pltpu.VMEM((part[1], columns.stop - columns.start), arg.dtype))
    n, m = len(plain), len(outs)
    sent = [o for o in outs if not isinstance(o, Held)]

    def body(*refs):
        sources, targets, rest = refs[:n], refs[n : n + m], refs[n + m :]
        in_held, rest = list(rest[: len(held)]), rest[len(held) :]
        out_held, rest = list(rest[: len(sent)]), rest[len(sent) :]
        in_sem, out_sem, rest = rest[0], rest[1], rest[2:]
        ins = []
        for source, take in zip(sources, takes):
            if take is None:
                ins.append(source)
                continue
            first, rows, columns, _ = take
            if first is None:
                first = pl.multiple_of(sources[0][0, 0] * rows, 16)
            source = source.at[pl.ds(first, rows), pl.ds(columns.start, columns.stop - columns.start)]
            at = len(held) - len(in_held)
            ins.append(Inward(source, in_held.pop(0), in_sem.at[at]))
        finished = []
        for out, target in zip(outs, targets):
            if not isinstance(out, Held):
                at = len(sent) - len(out_held)
                target = Outward(out_held.pop(0), target, out_sem.at[at])
            finished.append(target)
        kernel(*ins, *finished, *rest)
        for value in ins:
            if isinstance(value, Inward):
                value.wait()
        finished = [f for f in finished if isinstance(f, Outward)]
        for out in finished:
            out.finish()
        for out in finished:
            for copy in out.copies:
                copy.wait()

    shapes = [pltpu.VMEM(o.array.shape, o.array.dtype) if isinstance(o, Held) else pltpu.HBM(o.shape, o.dtype) for o in outs]
    return pl.pallas_call(
        body,
        out_shape=shapes,
        in_specs=[
            SM if a.dtype == jnp.int32 else VM if take is None else ANY if take[3] else HB for a, take in zip(plain, takes)
        ],
        out_specs=[VM if isinstance(o, Held) else HB for o in outs],
        scratch_shapes=[
            *held,
            *[pltpu.VMEM(o.shape, o.dtype) for o in sent],
            pltpu.SemaphoreType.DMA((max(1, len(held)),)),
            pltpu.SemaphoreType.DMA((max(1, len(sent)), SENDS)),
            *scratch,
        ],
        compiler_params=pltpu.CompilerParams(vmem_limit_bytes=limit * 2**20),
        cost_estimate=pl.CostEstimate(flops=flops, bytes_accessed=4000000, transcendentals=0),
        name=name,
    )(*plain)


VECTOR_ROWS = 64


def part_outs(count, extra=0):
    rows = count * TILE
    return [struct((rows, TILE), BF16), Held(struct((2 * rows + extra, TILE), BF16)), Held(struct((rows + extra, TILE), BF16))]


def four_parts(own, near, far):
    rows = own.shape[0]
    return (own, near.at[pl.ds(0, rows)], far, near.at[pl.ds(rows, rows)])


def send_parts(outs, first, count):
    own, near, far = outs
    a, b, rows = first * TILE, (first + count) * TILE, own.shape[0]
    send(near, (a, b), (rows + a, rows + b))
    send(far, (a, b))
    send(own, (a, b))


def rows_of(group, first=0, count=None):
    own, near, far, far_near, at = group
    begin, number = GROUPS[at]
    count = number - first if count is None else count
    start, size = (begin + first) * TILE, count * TILE
    first = first * TILE
    return [Part((own, start, size)), Part((near, start, size)), Part((far, first, size)), Part((far_near, first, size))]


def causal_bias(count, live, queries_on_rows):
    a = lax.broadcasted_iota(jnp.int32, (count, count), 0)
    b = lax.broadcasted_iota(jnp.int32, (count, count), 1)
    query, key = (a, b) if queries_on_rows else (b, a)
    return jnp.where((key <= query) & (key < live), 0.0, MASKED_SCORE)


def tail_rows(length, count):
    return (length - count) // 16 * 16


def column_as_row(column):
    return jnp.broadcast_to(column, (column.shape[0], TILE)).T[:8, :]


def row_as_column(ref):
    return jnp.concatenate([ref[...]] * STATS, axis=0).T[:, :1]


def store_norm(ref, gradient, hat):
    ref[0:1, :] = jnp.sum(gradient * hat, axis=0, keepdims=True)
    ref[1:2, :] = jnp.sum(gradient, axis=0, keepdims=True)


def ffn_weights(ps, first=0):
    w1 = jnp.concatenate([column_matrix(ps, first, 2, c) for c in range(2)], axis=1)
    w2 = jnp.concatenate([row_matrix(ps, first + 8, c) for c in range(2)], axis=0)
    return w1, w2


def heads_weights(part):
    return jnp.concatenate(
        [jnp.concatenate([tile_at(part, 3 * a + c) for c in range(3)], axis=1) for a in range(4)], axis=0
    )


def heads_forward(name, info, rows_all, tiles, first, causal):
    count = 3
    rows = rows_all.shape[0] // count

    def kernel(info_ref, w_ref, *refs):
        xs, (qkv_ref, o_ref, stat_ref, *pieces) = refs[:count], refs[count:]
        weights = heads_weights(w_ref)
        for j in range(count):
            span = slice(j * rows, (j + 1) * rows)
            packed = low(matmul(xs[j][...], weights))
            qkv_ref[span, :] = packed
            qkv_ref.send((span.start, span.stop))
            bias = causal_bias(rows, info_ref[0, 5 + j], True) if causal else None
            mixed, stats = attend_pair(
                packed[:, :TILE], packed[:, TILE : 2 * TILE], packed[:, 2 * TILE :], bias, 0, jnp.zeros((rows, TILE), F32)
            )
            o_ref[span, :] = mixed
            stat_ref[j * STATS : (j + 1) * STATS, :] = stats.T[:STATS, :]
        o_ref.send()
        for r, piece in enumerate(pieces):
            piece[...] = o_ref[pl.ds(pl.multiple_of(info_ref[0, 2 + r] * rows, 16), rows), :]

    outs = [struct((count * rows, 3 * TILE), BF16), struct((count * rows, TILE), BF16)]
    outs += [struct((count * STATS, rows), F32)] + [Held(struct((rows, TILE), BF16))] * 3
    return call(
        kernel, name, outs, [], info, Part((tiles, first * TILE, 12 * TILE)),
        *[(rows_all, j * rows, rows) for j in range(count)], flops=10**10,
    )


def piece_size(share):
    return share if share % 16 == 0 else (share + 15) // 16 * 16 + 16


def heads_backward(name, info, rows_all, tiles, first, qkv, mixed, stats, incoming, causal, piece_rows):
    count = 3
    rows = rows_all.shape[0] // count
    shards = 4
    share = count * rows // shards

    def kernel(info_ref, i0, i1, i2, i3, o_ref, stat_ref, *refs):
        qkvs, xs, (w_ref, own_ref, near_ref, far_ref, tile_ref, do_ref, dx_ref) = (
            refs[:count], refs[count : 2 * count], refs[2 * count :]
        )
        for r, ref in enumerate((i0, i1, i2, i3)):
            do_ref[r * rows : (r + 1) * rows, :] = ref[...]
        total = None
        weights = None
        for j in range(count):
            span = slice(j * rows, (j + 1) * rows)
            do = do_ref[pl.ds(pl.multiple_of(info_ref[0, 9 + j] * rows, 16), rows), :]
            delta = row_products(do.astype(F32), o_ref[span, :].astype(F32))
            packed = qkvs[j][...]
            bias = causal_bias(rows, info_ref[0, 5 + j], False) if causal else None
            at = j * STATS
            grads = pair_back(
                packed[:, :TILE], packed[:, TILE : 2 * TILE], packed[:, 2 * TILE :], do,
                [stat_ref[at : at + 1, :], stat_ref[at + 1 : at + 2, :]], [delta[0:1, :], delta[1:2, :]], bias,
            )
            grads = jnp.concatenate(grads, axis=1)
            gradient = transpose_times(xs[j][...], grads)
            total = gradient if total is None else total + gradient
            if weights is None:
                weights = heads_weights(w_ref)
            dx_ref[span, :] = low(times_transpose(grads, weights))
        for a in range(4):
            for c in range(3):
                at = (3 * a + c) * TILE
                tile_ref[at : at + TILE, :] = low(total[a * TILE : (a + 1) * TILE, c * TILE : (c + 1) * TILE])
        tile_ref.send()
        for r, (ref, at) in enumerate(((near_ref, 0), (near_ref, piece_rows), (far_ref, 0), (own_ref, 0))):
            rank = info_ref[0, 1] ^ (1, 3, 2, 0)[r]
            begin = jnp.minimum(rank * share // 16 * 16, count * rows - piece_rows)
            ref[at : at + piece_rows, :] = dx_ref[pl.ds(pl.multiple_of(begin, 16), piece_rows), :]

    outs = [struct((piece_rows, D), BF16), Held(struct((2 * piece_rows, D), BF16)), struct((piece_rows, D), BF16)]
    outs += [struct((12 * TILE, TILE), BF16)]
    scratch = [pltpu.VMEM((shards * rows, TILE), BF16), pltpu.VMEM((count * rows, D), BF16)]
    return call(
        kernel, name, outs, scratch, info, *incoming, mixed, stats,
        *[(qkv, j * rows, rows) for j in range(count)], *[(rows_all, j * rows, rows) for j in range(count)],
        Part((tiles, first * TILE, 12 * TILE)), flops=2 * 10**10,
    )


def join(refs):
    return jnp.concatenate([r[...] for r in refs], axis=1)


def ffn_forward(info, rows_all, mixed, group, vectors, tail):
    rows = mixed[1].shape[0]

    def kernel(info_ref, o0, o1, o2, o3, p0, p1, p2, p3, x_ref, g_ref,
               enc_ref, hat0_ref, hat_ref, stat_ref, low_ref, hid_ref, slope_ref, tail_ref):
        ps = (p0, p1, p2, p3)
        wo = row_matrix(ps, 0, 0)
        branch = matmul(join((o0, o1, o2, o3)), wo)
        w1, w2 = ffn_weights(ps, 4)
        scales0, scales = [], []
        for a, b in spans(rows):
            hat, scale = norm_rows(x_ref[a:b, :].astype(F32) + branch[a:b])
            scales0.append(scale)
            hat0_ref[a:b, :] = low(hat)
            first_rows = hat * g_ref[0:1, :] + g_ref[1:2, :]
            first_low = low(first_rows)
            low_ref[a:b, :] = first_low
            value, slope = gate_both(matmul(first_low, w1))
            value = low(value)
            hid_ref[a:b, :] = value
            slope_ref[a:b, :] = low(slope)
            for out in (hat0_ref, low_ref, hid_ref, slope_ref):
                out.send((a, b))
            hat, scale = norm_rows(first_rows + matmul(value, w2))
            enc_ref[a:b, :] = low(hat * g_ref[2:3, :] + g_ref[3:4, :])
            hat_ref[a:b, :] = low(hat)
            for out in (hat_ref, enc_ref):
                out.send((a, b))
            scales.append(scale)
        tail_ref[...] = enc_ref[tail:, :]
        store_stats(stat_ref, None, jnp.concatenate(scales0, axis=0), jnp.concatenate(scales, axis=0))

    outs = [struct((rows, D), BF16)] * 3 + [struct((STATS, rows), F32), struct((rows, D), BF16)]
    outs += [struct((rows, FF), BF16)] * 2 + [struct((rows - tail, D), BF16)]
    return call(kernel, "ffn_forward", outs, [], info, Own((mixed[0], rows)), *mixed[1:], *rows_of(group),
                Own((rows_all, rows)), vectors, flops=8 * 10**9)


def cross_forward(info, rows_all, mixed, encoded, group, vectors):
    rows, keys = mixed[1].shape[0], encoded.shape[0]

    def kernel(info_ref, o0, o1, o2, o3, p0, p1, p2, p3, y_ref, e_ref, g_ref,
               third_ref, hat2_ref, low_ref, hat_ref, q_ref, k_ref, v_ref, o_ref, stat_ref):
        ps = (p0, p1, p2, p3)
        hat, scale2 = norm_rows(y_ref[...].astype(F32) + matmul(join((o0, o1, o2, o3)), row_matrix(ps, 0, 0)))
        hat2_ref[...] = low(hat)
        second = hat * g_ref[4:5, :] + g_ref[5:6, :]
        second_low = low(second)
        low_ref[...] = second_low
        third_ref[...] = second
        q_ref[...] = low(matmul(second_low, column_matrix(ps, 4, 1, 0)))
        k_ref[...] = low(matmul(e_ref[...], column_matrix(ps, 8, 2, 0)))
        v_ref[...] = low(matmul(e_ref[...], column_matrix(ps, 8, 2, 1)))
        for ref in (hat2_ref, low_ref, q_ref, k_ref, v_ref):
            ref.send()
        stats = jnp.zeros((rows, TILE), F32)
        for pair in range(PAIRS):
            cut = pair_columns(pair)
            o_ref[:, cut], stats = attend_pair(q_ref[:, cut], k_ref[:, cut], v_ref[:, cut], None, 2 * pair, stats)
        o_ref.send()
        hat, scale = norm_rows(third_ref[...] + matmul(o_ref[...], row_matrix(ps, 16, 0)))
        third_ref[...] = hat * g_ref[6:7, :] + g_ref[7:8, :]
        hat_ref[...] = low(hat)
        hat_ref.send()
        store_stats(stat_ref, stats, scale, scale2)

    outs = [Held(struct((rows, D), F32))] + [struct((rows, D), BF16)] * 3
    outs += [struct((rows, D), BF16), struct((keys, D), BF16), struct((keys, D), BF16)]
    outs += [struct((rows, D), BF16), struct((STATS, rows), F32)]
    return call(kernel, "cross_forward", outs, [], info, Own((mixed[0], rows)), *mixed[1:], *rows_of(group),
                Own((rows_all, rows)), encoded, vectors, flops=8 * 10**9)


def ffn_weight_gradients(inputs, hid_ref, dh_ref, db_ref, grads, outs, first=0):
    for c in range(2):
        store_columns(grads, transpose_times(inputs, dh_ref[:, c * D : (c + 1) * D]), first, 2, c)
    send_parts(outs, first, 8)
    for c in range(2):
        store_rows(grads, transpose_times(hid_ref[:, c * D : (c + 1) * D], db_ref[...]), first + 8, c)
    send_parts(outs, first + 8, 8)


def ffn_both(info, third, cotangent, encoded_tail, group, vectors, tail):
    rows = third.shape[0]

    def kernel(info_ref, t_ref, p0, p1, p2, p3, g_ref, c_own, c_later, e_ref, dec_ref, tail_ref, back_ref, n_ref, d0, d1,
               d2, hid_ref, dh_ref, db_ref, c_ref):
        fill_item(info_ref, c_own, c_later, c_ref)
        w1, w2 = ffn_weights((p0, p1, p2, p3))
        grads = four_parts(d0, d1, d2)
        gain = g_ref[8:9, :]
        n_ref[...] = jnp.zeros_like(n_ref)
        for a, b in spans(rows):
            third_rows = t_ref[a:b, :]
            value, slope = gate_both(matmul(low(third_rows), w1))
            value = low(value)
            hid_ref[a:b, :] = value
            hat, scale = norm_rows(third_rows + matmul(value, w2))
            dec_ref[a:b, :] = low(hat * gain + g_ref[9:10, :])
            dec_ref.send((a, b))
            row = lax.broadcasted_iota(jnp.int32, (b - a, 1), 0) + a
            incoming = jnp.where(row < info_ref[0, 8], c_ref[a:b, :].astype(F32), 0.0)
            n_ref[0:1, :] += jnp.sum(incoming * hat, axis=0, keepdims=True)
            n_ref[1:2, :] += jnp.sum(incoming, axis=0, keepdims=True)
            back = norm_back(incoming, hat, scale, gain)
            back_low = low(back)
            db_ref[a:b, :] = back_low
            dh = low(slope * times_transpose(back_low, w2))
            dh_ref[a:b, :] = dh
            back_ref[a:b, :] = back + times_transpose(dh, w1)
        tail_ref[: encoded_tail.shape[0], :] = e_ref[...]
        tail_ref[encoded_tail.shape[0] :, :] = dec_ref[tail:, :]
        tail_ref.send()
        ffn_weight_gradients(low(t_ref[...]), hid_ref, dh_ref, db_ref, grads, (d0, d1, d2))

    outs = [struct((rows, D), BF16), struct((encoded_tail.shape[0] + rows - tail, D), BF16)]
    outs += [Held(struct((rows, D), F32))]
    outs += [struct((8, D), F32)] + part_outs(16)
    scratch = [pltpu.VMEM((rows, FF), BF16), pltpu.VMEM((rows, FF), BF16)] + [pltpu.VMEM((rows, D), BF16)] * 2
    return call(kernel, "ffn_both", outs, scratch, info, Held(third), *rows_of(group), vectors, *cotangent, encoded_tail,
                flops=10**10)


def norm_and_branch(incoming, hat_rows, scale, gain, n_ref):
    n_ref[...] = jnp.zeros_like(n_ref)
    store_norm(n_ref, incoming, hat_rows)
    branch = norm_back(incoming, hat_rows, scale, gain)
    return branch, low(branch)


def spread_heads(do, refs):
    for r, ref in enumerate(refs):
        ref[...] = do[:, r * TILE : (r + 1) * TILE]
        send(ref)


def cross_backward(info, back, hat, low_rows, encoded, q, k, v, o, stats, hat2, mixed, group, vectors, tail):
    rows, keys = low_rows.shape[0], encoded.shape[0]

    def kernel(info_ref, b_ref, h_ref, stat_ref, g_ref, w0, w1, w2, w3, o_ref, q_ref, k_ref, v_ref, x_ref, e_ref,
               p0, p1, p2, p3, h2_ref, m0, m1, m2, m3,
               de_ref, branch_ref, tail_ref, e0, e1, e2, e3, n_ref, n2_ref, d0, d1, d2, do_ref, dq_ref, dk_ref, dv_ref):
        ps, grads = (p0, p1, p2, p3), four_parts(d0, d1, d2)
        scale, scale2 = norm_scales(stat_ref, 2)
        branch, branch_low = norm_and_branch(b_ref[...], h_ref[...].astype(F32), scale, g_ref[6:7, :], n_ref)
        do = low(times_transpose(branch_low, row_matrix((w0, w1, w2, w3), 0, 0)))
        do_ref[...] = do
        store_rows(grads, transpose_times(o_ref[...], branch_low), 16, 0)
        delta = row_products(do.astype(F32), o_ref[...].astype(F32))
        for pair in range(PAIRS):
            cut = pair_columns(pair)
            dq_ref[:, cut], dk_ref[:, cut], dv_ref[:, cut] = pair_back(
                q_ref[:, cut], k_ref[:, cut], v_ref[:, cut], do_ref[:, cut],
                pair_rows(stat_ref, pair), pair_rows(delta, pair), None,
            )
        incoming = branch + times_transpose(dq_ref[...], column_matrix(ps, 4, 1, 0))
        branch, branch_low = norm_and_branch(incoming, h2_ref[...].astype(F32), scale2, g_ref[4:5, :], n2_ref)
        spread_heads(low(times_transpose(branch_low, row_matrix(ps, 0, 0))), (e0, e1, e2, e3))
        branch_ref[...] = branch_low
        branch_ref.send()
        tail_ref[...] = branch_ref[tail:, :]
        store_rows(grads, transpose_times(join((m0, m1, m2, m3)), branch_low), 0, 0)
        store_columns(grads, transpose_times(x_ref[...], dq_ref[...]), 4, 1, 0)
        et = e_ref[...].T
        store_columns(grads, matmul(et, dk_ref[...]), 8, 2, 0)
        store_columns(grads, matmul(et, dv_ref[...]), 8, 2, 1)
        send_parts((d0, d1, d2), 0, 20)
        de_ref[...] = times_transpose(dk_ref[...], column_matrix(ps, 8, 2, 0)) + times_transpose(
            dv_ref[...], column_matrix(ps, 8, 2, 1)
        )

    outs = [Held(struct((keys, D), F32)), struct((rows, D), BF16), struct((rows - tail, D), BF16)]
    outs += [struct((rows, TILE), BF16)] + [Held(struct((rows, TILE), BF16))] * 3 + [struct((8, D), F32)] * 2 + part_outs(20)
    scratch = [pltpu.VMEM((rows, D), BF16)] * 2 + [pltpu.VMEM((keys, D), BF16)] * 2
    return call(kernel, "cross_backward", outs, scratch, info, Held(back), hat, stats, vectors, *rows_of(group, 16, 4),
                o, q, k, v, low_rows, encoded, *rows_of(group, 0, 16), hat2, Own((mixed[0], rows)), *mixed[1:],
                flops=2 * 10**10)


def ffn_backward(info, cotangent, more, hat, stats, low_rows, hid, slope, hat0, mixed, norms, branch2_tail, group, vectors, tail):
    rows = low_rows.shape[0]

    def kernel(info_ref, m_ref, c_own, c_later, h_ref, stat_ref, g_ref, p0, p1, p2, p3, slope_ref, h0_ref, f_ref, hid_ref,
               m0, m1, m2, m3, n2, n3, n4, t2_ref,
               branch_ref, tail_ref, e0, e1, e2, e3, v_ref, d0, d1, d2, back_ref, dh_ref, db_ref, c_ref, n1_ref, n0_ref):
        fill_item(info_ref, c_own, c_later, c_ref)
        grads = four_parts(d0, d1, d2)
        n1_ref[...] = jnp.zeros_like(n1_ref)
        scale0, scale = norm_scales(stat_ref, 2)
        for a, b in spans(rows):
            incoming = c_ref[a:b, :].astype(F32) + m_ref[a:b, :]
            hat_rows = h_ref[a:b, :].astype(F32)
            n1_ref[0:1, :] += jnp.sum(incoming * hat_rows, axis=0, keepdims=True)
            n1_ref[1:2, :] += jnp.sum(incoming, axis=0, keepdims=True)
            back = norm_back(incoming, hat_rows, scale[a:b], g_ref[2:3, :])
            back_low = low(back)
            db_ref[a:b, :] = back_low
            if not a:
                w1, w2 = ffn_weights((p0, p1, p2, p3), 4)
            dh = low(slope_ref[a:b, :].astype(F32) * times_transpose(back_low, w2))
            dh_ref[a:b, :] = dh
            back_ref[a:b, :] = back + times_transpose(dh, w1)
        branch, branch_low = norm_and_branch(back_ref[...], h0_ref[...].astype(F32), scale0, g_ref[0:1, :], n0_ref)
        spread_heads(low(times_transpose(branch_low, row_matrix((p0, p1, p2, p3), 0, 0))), (e0, e1, e2, e3))
        branch_ref[...] = branch_low
        branch_ref.send()
        tail_ref[: rows - tail, :] = branch_ref[tail:, :]
        tail_ref[rows - tail :, :] = t2_ref[...]
        norms_low = low(jnp.concatenate([n[:2, :] for n in (n0_ref, n1_ref, n2, n3, n4)] + [jnp.zeros((6, D), F32)], axis=0))
        size = d0.shape[0]
        for j in range(4):
            v_ref[16 * j : 16 * (j + 1), :] = norms_low[:, j * TILE : (j + 1) * TILE]
        d1[2 * size :, :] = v_ref[...]
        d2[size:, :] = v_ref[...]
        send(d1, (2 * size, 2 * size + VECTOR_ROWS))
        send(d2, (size, size + VECTOR_ROWS))
        store_rows(grads, transpose_times(join((m0, m1, m2, m3)), branch_low), 0, 0)
        for c in range(2):
            store_columns(grads, transpose_times(f_ref[...], dh_ref[:, c * D : (c + 1) * D]), 4, 2, c)
        send_parts((d0, d1, d2), 0, 12)
        for c in range(2):
            store_rows(grads, transpose_times(hid_ref[:, c * D : (c + 1) * D], db_ref[...]), 12, c)
        send_parts((d0, d1, d2), 12, 8)

    outs = [struct((rows, D), BF16), struct((rows - tail + branch2_tail.shape[0], D), BF16)]
    outs += [struct((rows, TILE), BF16)] + [Held(struct((rows, TILE), BF16))] * 3
    outs += [struct((VECTOR_ROWS, TILE), BF16)] + part_outs(20, VECTOR_ROWS)
    scratch = [pltpu.VMEM((rows, D), F32), pltpu.VMEM((rows, FF), BF16)] + [pltpu.VMEM((rows, D), BF16)] * 2
    scratch += [pltpu.VMEM((8, D), F32)] * 2
    return call(kernel, "ffn_backward", outs, scratch, info, Held(more), *cotangent, hat, stats, vectors, *rows_of(group),
                slope, hat0, low_rows, hid, Own((mixed[0], rows)), *mixed[1:], *norms, branch2_tail, flops=12 * 10**9)


def beside(outs, *arrived):
    both = lax.optimization_barrier((*outs, *arrived))
    return list(both[: len(outs)]), list(both[len(outs) :])


def compute(info, x_all, y_all, image_cotangent, yc, tiles, group_tiles, near, vectors, image_rows, tag_rows):
    items = 3
    image_tail = tail_rows(x_all.shape[0] // items, image_rows)
    tag_tail = tail_rows(y_all.shape[0] // items, tag_rows)

    def far_part(g, *others):
        part = group_tiles[g]
        return lax.ppermute(after(part, *others) if others else part, "tensor", chip_pairs())

    def across(far):
        return lax.ppermute(far, "tensor", core_pairs())

    far_a = far_part(0)
    outs = heads_forward("heads_forward_0", info, x_all, tiles, 0, False)
    (qkv0, mixed0, stats0, *pieces0), (near, far_a, y_all) = beside(outs, near, far_a, y_all)
    mixed0 = spread([mixed0, *pieces0])
    last_a = across(far_a)
    outs = heads_forward("heads_forward_2", info, after(y_all, qkv0), tiles, 32, True)
    (qkv2, mixed2, stats2, *pieces2), (*mixed0, last_a) = beside(outs, *mixed0, last_a)
    mixed2 = spread([mixed2, *pieces2])
    far_b = far_part(1, qkv2)
    outs = ffn_forward(info, after(x_all, qkv2), mixed0, (tiles, near, far_a, last_a, 0), vectors, image_tail)
    (encoded, hat0, hat1, stats1, low1, hid, slope, encoded_tail), (*mixed2, far_b) = beside(outs, *mixed2, far_b)
    last_b = across(far_b)
    far_c = far_part(2, last_b)
    outs = cross_forward(info, after(y_all, last_b), mixed2, encoded, (tiles, near, far_b, last_b, 1), vectors)
    (third, hat2, low2, hat3, q3, k3, v3, o3, stats3), (far_c,) = beside(outs, far_c)
    last_c = across(far_c)
    moved = lax.ppermute(after(image_cotangent, third), "tensor", [(i + 1, i) for i in range(3)])
    outs = ffn_both(info, third, yc, encoded_tail, (tiles, near, far_c, last_c, 2), vectors, tag_tail)
    (decoded, output_tails, back, n4, *part_c), (moved,) = beside(outs, moved)
    near_c = send_near(part_c)
    pushed = push_tails(output_tails)
    outs = cross_backward(
        info, back, hat3, low2, encoded, q3, k3, v3, o3, stats3, hat2, mixed2, (tiles, near, far_b, last_b, 1), vectors,
        tag_tail,
    )
    (d_encoded, branch2, branch2_tail, *rest), (near_c, pushed) = beside(outs, near_c, pushed)
    d_mixed2, (n3, n2), part_b = rest[:4], rest[4:6], rest[6:]
    d_mixed2 = spread(d_mixed2)
    far_sum_c = sum_far(part_c, near_c)
    far_c_sum = send_far(far_sum_c)
    near_b = send_near(part_b)
    outs = ffn_backward(
        info, (after(image_cotangent, far_sum_c), moved), d_encoded, hat1, stats1, low1, hid, slope, hat0, mixed0, (n2, n3, n4), branch2_tail,
        (tiles, near, far_a, last_a, 0), vectors, image_tail,
    )
    (branch0, branch_tails, *rest), (*d_mixed2, near_b, far_c_sum) = beside(outs, *d_mixed2, near_b, far_c_sum)
    d_mixed0, extra, part_a = rest[:4], rest[4], rest[5:]
    d_mixed0 = spread(d_mixed0)
    near_a = send_near(part_a)
    far_sum_b = sum_far(part_b, near_b)
    outs = heads_backward(
        "heads_backward_2", info, after(y_all, far_sum_b), tiles, 32, qkv2, mixed2[0], stats2, d_mixed2, True, piece_size(tag_rows)
    )
    sum_c = sum_group(part_c[0], after(near_c, outs[-1]), far_c_sum)
    outs, (*d_mixed0, near_a, sum_c) = beside(outs, *d_mixed0, near_a, sum_c)
    *dy, tiles2 = outs
    far_sum_a = sum_far(part_a, near_a)
    far_a_sum, far_b_sum = send_far(far_sum_a), send_far(far_sum_b)
    came_y = lax.ppermute(dy[1], "tensor", core_pairs())
    branch_pushed = push_tails(after(branch_tails, tiles2))
    outs = heads_backward(
        "heads_backward_0", info, after(x_all, far_sum_a), tiles, 0, qkv0, mixed0[0], stats0, d_mixed0, False,
        piece_size(image_rows),
    )
    outs, (came_y, far_a, far_b, branch_pushed) = beside(outs, came_y, far_a_sum, far_b_sum, branch_pushed)
    *dx, tiles0 = outs
    dy = [dy[0], came_y, dy[2]]
    groups = [(part_a[0], near_a, far_a), (part_b[0], near_b, far_b)]
    finals = [(GROUPS[2][0], sum_c), (32, tiles2), (0, tiles0)]
    outputs = push_rows((encoded, decoded), pushed, (image_rows, tag_rows), (None, None), info)
    return outputs, (branch0, branch2), branch_pushed, (dx, dy), groups, finals, extra


def one_hot(index, count, dtype):
    return (index[:, None] == lax.broadcasted_iota(jnp.int32, (1, count), 1)).astype(dtype)


def local(
    image_tokens,
    tag_tokens,
    image_cotangent,
    tag_cotangent,
    tag_lengths,
    slot_blocks,
    master_blocks,
    left_factor,
    right_factor,
    left_root,
    right_root,
    vector_master,
    vector_moment,
):
    dp = lax.axis_size("dp")
    shards = lax.axis_size("tensor")
    me = lax.axis_index("tensor")
    slots = master_blocks.shape[1]
    items = tag_lengths.shape[0]
    image_length = image_tokens.shape[0] * shards // items
    item_length = tag_tokens.shape[0] * shards // items
    lanes = vector_master.shape[1]
    def rows_of(value):
        return jnp.pad(value, ((0, 16 - value.shape[0]), (0, TILE - value.shape[1])))

    own = jnp.concatenate(
        [
            master_blocks.astype(BF16).reshape(slots * TILE, TILE),
            rows_of(vector_master.astype(BF16)),
        ],
        axis=0,
    )
    at = lax.broadcasted_iota(jnp.int32, (items,), 0)
    live = jnp.sum(jnp.where(at == me, tag_lengths, 0))
    info = jnp.concatenate(
        [
            jnp.stack([jnp.minimum(me, items - 1), me] + [jnp.minimum(me ^ r, items - 1) for r in (1, 2, 3)]),
            tag_lengths,
            live[None],
            me ^ at,
            jnp.zeros((4,), jnp.int32),
        ]
    ).reshape(1, 16)
    ranks = jnp.stack([relative_rank(p, dp) for p in range(dp)])

    def blocks_of(those):
        picked = one_hot(those, dp, jnp.int32)[:, :, None] * slot_blocks.reshape(1, dp, slots)
        return jnp.sum(picked, axis=1)

    targets = jnp.stack([target_rank(p, dp) for p in range(dp)])
    ready = (info, blocks_of(ranks), blocks_of(targets), ranks, targets)
    pieces, x_all, sequences, moved, ready = gather_rows(
        image_tokens, tag_tokens, tag_cotangent, own, dp,
        lambda parts, info: whole_group(parts, info, "whole_images"), ready
    )
    info, source_blocks, target_blocks, ranks, targets = ready
    y_all = whole_group(sequences, info, "whole_sequences")
    tiles, *group_tiles, vectors = order_tiles(pieces, source_blocks, ranks, slots, lanes)
    near = lax.ppermute(tiles, "tensor", core_pairs())
    images, tags = image_tokens.shape[0], tag_tokens.shape[0]
    outputs, branches, pushed, (dx, dy), groups, finals, extra = compute(
        info, x_all, y_all, image_cotangent, (tag_cotangent, moved), tiles, group_tiles, near, vectors, images, tags
    )
    came_x = lax.ppermute(dx[1], "tensor", core_pairs())
    outgoing = deal_tiles(groups, finals, extra, target_blocks, targets, slots, lanes)
    outgoing, (came_x,) = beside(outgoing, came_x)
    terms, mark = sum_pieces(outgoing, dp)
    came = [came_x, dy[1]]
    far = [
        (part[2].astype(F32) + near_part[part[0].shape[0] :].astype(F32)).astype(BF16)
        for part, near_part in zip((dx, dy), came)
    ]
    far = lax.ppermute(after(jnp.concatenate(far, axis=0), mark), "tensor", chip_pairs())
    sums = [
        ((part[0], 0), (near_part, 0), (far, begin))
        for part, near_part, begin in zip((dx, dy), came, (0, dx[0].shape[0]))
    ]
    rows = push_rows(branches, pushed, (images, tags), sums, info)
    updates = shampoo(
        [*terms[:-1], after(terms[-1], *rows)] if dp == 8 else terms,
        master_blocks,
        left_factor,
        right_factor,
        left_root,
        right_root,
        vector_master,
        vector_moment,
    )
    return (*outputs, *rows, *updates)


def solution(mesh):
    in_specs = (
        P(("dp", "tensor"), None),
        P(("dp", "tensor"), None),
        P(("dp", "tensor"), None),
        P(("dp", "tensor"), None),
        P("dp"),
        P(),
        P("tensor", "dp", None, None),
        P("tensor", "dp", None, None),
        P("tensor", "dp", None, None),
        P("tensor", "dp", None, None),
        P("tensor", "dp", None, None),
        P(None, "dp"),
        P(None, "dp"),
    )
    out_specs = (
        P(("dp", "tensor"), None),
        P(("dp", "tensor"), None),
        P(("dp", "tensor"), None),
        P(("dp", "tensor"), None),
        P("tensor", "dp", None, None),
        P("tensor", "dp", None, None),
        P("tensor", "dp", None, None),
        P("tensor", "dp", None, None),
        P("tensor", "dp", None, None),
        P(None, "dp"),
        P(None, "dp"),
        P(None, "dp"),
    )
    return jax.shard_map(local, mesh=mesh, in_specs=in_specs, out_specs=out_specs, check_vma=False)
```

time: 319 us -> 294 us (0.922)
  local copies, waits for them, and re-layouts: 16.6 us -> 3.58 us
  waiting for transfers between devices: 99.3 us -> 89.7 us
  starting transfers between devices: 43.2 us -> 52.5 us
  Pallas kernels: 142 us -> 136 us
  other arithmetic: 10.3 us -> 4.86 us
    ppermute x5 -> x3, waiting for transfers between devices: 14.8 us -> 0.01 us  [send_far(): return lax.ppermute(value, 'tensor', chip_pairs())]
    ppermute x23 -> x37, starting transfers between devices: 28.7 us -> 39.8 us  [the longest x4 6.46 us: spread(): lax.ppermute(pieces[2], 'tensor', chip_pairs())]
    unnamed x127 -> x116, local copies, waits for them, and re-layouts: 12.7 us -> 2.05 us
    ppermute x23 -> x37, waiting for transfers between devices: 55.2 us -> 65 us  [the longest x3 25.6 us: column(): return lax.ppermute(part, 'dp', z_shift(step))]
    ppermute x3, waiting for transfers between devices: 17.7 us -> 9.26 us  [sum_pieces(): column.append(lax.ppermute(both, 'dp', z_shift(step)))]
    pallas_call x13 -> x12, Pallas kernels: 129 us -> 121 us  [call(): pl.pallas_call(body, out_shape=shapes, in_specs=[SM if a.dtype == jnp.int...]
    ppermute x4, waiting for transfers between devices: 11.6 us -> 15.5 us  [sum_pieces(): other = lax.ppermute(piece, 'dp', y_pairs())]
    pallas_call x4, Pallas kernels: 7.21 us -> 10.5 us  [the longest x2 6.65 us: whole_group(): pl.pallas_call(kernel, out_shape=jax.ShapeDtypeStruct((count * shards, D)...]
  transfers between devices with their start and end apart: 41 -> 51, of which waited for: 20 -> 19; matrix products, arithmetic and copies ran while one was open for 5% -> 1% of each run, Pallas kernels for 38% -> 44%
where the time goes in v4:
time: 294 us; the launch traced here: 289 us
  Pallas kernels  136 us (46%)
  waiting for transfers between devices  89.7 us (31%)
  starting transfers between devices  52.5 us (18%)
  other arithmetic  4.86 us (2%)
  local copies, waits for them, and re-layouts  3.58 us (1%)
    pallas_call x12, Pallas kernels, call(): pl.pallas_call(body, out_shape=shapes, in_specs=[SM if a.dtype == jnp.int...  121 us
    ppermute x3, waiting for transfers between devices, column(): return lax.ppermute(part, 'dp', z_shift(step))  25.6 us
    ppermute x4, waiting for transfers between devices, sum_pieces(): other = lax.ppermute(piece, 'dp', y_pairs())  15.5 us
    ppermute x3, waiting for transfers between devices, far_part(): lax.ppermute(after(part, *others) if others else part, 'tensor', chip_pai...  13 us
    ppermute x4, waiting for transfers between devices, spread(): lax.ppermute(pieces[2], 'tensor', chip_pairs())  9.7 us
    ppermute x3, waiting for transfers between devices, sum_pieces(): column.append(lax.ppermute(both, 'dp', z_shift(step)))  9.26 us
    ppermute x4, waiting for transfers between devices, row(): return lax.ppermute(part, 'dp', y_pairs())  7.49 us
    pallas_call x2, Pallas kernels, whole_group(): pl.pallas_call(kernel, out_shape=jax.ShapeDtypeStruct((count * shards, D)...  6.65 us
  transfers between devices with their start and end apart: 51, of which 19 were waited for; matrix products, arithmetic and copies ran while one was open for 1% of the time, Pallas kernels for 44%

profile of v4, /device:TPU:0, one launch (start us, length us, event | category | flops | bytes accessed | tf_op | source)
XLA Modules:
  0.0 289.0 jit_solution(13070854832006622896)
XLA Ops:
  0.7 2.3 pad_maximum_fusion.1
  3.4 2.6 collective-permute-start.3
  6.1 1.6 collective-permute-start.2
  7.7 3.6 %collective-permute-start.1 = (bf16[1296,128]{1,0:T(8,128)(2,1)S(1)}, bf16[1296,128]{1,0:T(8,128)(2,1)}, u32[]{:S(2)}, u32[]{:S(2)}) collective-permute-start(bf16[1296,128]{1,0:T(8,128)(2,1)S(1)} %fusion.1.refs_2_), channel_id=1, source_target_pairs={{0,24},{4,28},{8,0},{12,4},{16,8},{20,12},{24,16},{28,20},{1,25},{... | collective-permute-start | bytes 995336 | tf_op jit(solution)/shard_map/ppermute | solution.py:96
  12.2 1.3 concatenate.14
  13.6 0.7 multiply_reduce_fusion
  14.2 1.8 collective-permute-done.2.refs_6_
  16.0 3.5 %collective-permute-done.1.refs_5_ = bf16[1296,128]{1,0:T(8,128)(2,1)} collective-permute-done((bf16[1296,128]{1,0:T(8,128)(2,1)S(1)}, bf16[1296,128]{1,0:T(8,128)(2,1)}, u32[]{:S(2)}, u32[]{:S(2)}) %collective-permute-start.1) | collective-permute-done | bytes 331808 | tf_op jit(solution)/shard_map/ppermute | solution.py:96
  19.5 7.0 %collective-permute-done.refs_3_ = bf16[1296,128]{1,0:T(8,128)(2,1)} collective-permute-done((bf16[1296,128]{1,0:T(8,128)(2,1)S(1)}, bf16[1296,128]{1,0:T(8,128)(2,1)}, u32[]{:S(2)}, u32[]{:S(2)}) %collective-permute-start) | collective-permute-done | bytes 331808 | tf_op jit(solution)/shard_map/ppermute | solution.py:96
  27.2 0.7 collective-permute-start.5
  28.5 1.5 collective-permute-start.7
  30.0 15.1 %collective-permute-done.5.refs_4_ = bf16[1296,128]{1,0:T(8,128)(2,1)S(1)} collective-permute-done((bf16[1296,128]{1,0:T(8,128)(2,1)S(1)}, bf16[1296,128]{1,0:T(8,128)(2,1)S(1)}, u32[]{:S(2)}, u32[]{:S(2)}) %collective-permute-start.5) | collective-permute-done | bytes 331808 | tf_op jit(solution)/shard_map/ppermute | solution.py:96
  45.2 1.3 collective-permute-start.12
  46.5 1.2 collective-permute-start.11
  48.2 3.6 %whole_images.1.refs_2_.refs_3_.refs_4_.refs_9_.refs_10_.refs_11_.refs_12_ = bf16[2352,512]{1,0:T(8,128)(2,1)} custom-call(s32[1,16]{1,0:T(1,128)} %bitcast.18, bf16[588,512]{1,0:T(8,128)(2,1)} %refs_0_.2, bf16[972,512]{1,0:T(8,128)(2,1)} %copy-done.20, bf16[588,512]{1,0:T(8,128)(2,1)} %collective-permute-done.3.refs_2_, bf16[588,512]{1,0:T(8,128)(2,1)} %copy-done.28), custom_call_target="tpu_custom_call" | custom-call | tf_op jit(solution)/shard_map/whole_images/pallas_call | solution.py:175
  51.8 5.7 %collective-permute-done.10.refs_8_ = bf16[1296,128]{1,0:T(8,128)(2,1)S(1)} collective-permute-done((bf16[1296,128]{1,0:T(8,128)(2,1)S(1)}, bf16[1296,128]{1,0:T(8,128)(2,1)S(1)}, u32[]{:S(2)}, u32[]{:S(2)}) %collective-permute-start.10) | collective-permute-done | bytes 331808 | tf_op jit(solution)/shard_map/ppermute | solution.py:99
  57.5 0.7 copy-done.36
  58.2 4.2 %order_tiles.1 = (bf16[10240,128]{1,0:T(8,128)(2,1)}, bf16[2560,128]{1,0:T(8,128)(2,1)S(1)}, bf16[2560,128]{1,0:T(8,128)(2,1)S(1)}, bf16[2048,128]{1,0:T(8,128)(2,1)S(1)}, f32[16,512]{1,0:T(8,128)}) custom-call(s32[8,10]{1,0:T(8,128)S(1)} %get-tuple-element.249.refs_0_, s32[8]{0:T(128)S(1)} %stack.70.refs_1_, bf16[1296,128]{1,0:T(8,128)(2,1)} %copy-done.26, ...), custom_call_target="tpu_custom_call" | custom-call | bytes 4000000 | tf_op jit(solution)/shard_map/order_tiles/pallas_call | solution.py:723
  62.4 3.1 %whole_sequences.1.refs_2_.refs_3_.refs_4_.refs_9_.refs_10_.refs_11_.refs_12_ = bf16[1536,512]{1,0:T(8,128)(2,1)} custom-call(s32[1,16]{1,0:T(1,128)} %bitcast.19, bf16[384,512]{1,0:T(8,128)(2,1)} %refs_0_.3, bf16[972,512]{1,0:T(8,128)(2,1)} %copy-done.20, bf16[384,512]{1,0:T(8,128)(2,1)} %copy-done.30, bf16[384,512]{1,0:T(8,128)(2,1)} %copy-done.31), custom_call_target="tpu_custom_call" | custom-call | tf_op jit(solution)/shard_map/whole_sequences/pallas_call | solution.py:175
  65.5 1.5 collective-permute-start.14
  67.0 12.7 %heads_forward_0.1 = (bf16[2352,384]{1,0:T(8,128)(2,1)}, bf16[2352,128]{1,0:T(8,128)(2,1)}, f32[48,784]{1,0:T(8,128)}, bf16[784,128]{1,0:T(8,128)(2,1)S(1)}, bf1...) custom-call(s32[1,16]{1,0:T(1,128)S(1)} %bitcast.23, ...), custom_call_target="tpu_custom_call" | custom-call | flops 10000000000 | bytes 4000000 | tf_op jit(solution)/shard_map/heads_forward_0/pallas_call | solution.py:723
  79.7 2.9 collective-permute-done.14.refs_7_.refs_9_
  82.6 1.6 collective-permute-start.16
  84.9 7.3 %heads_forward_2.1 = (bf16[1536,384]{1,0:T(8,128)(2,1)}, bf16[1536,128]{1,0:T(8,128)(2,1)}, f32[48,512]{1,0:T(8,128)}, bf16[512,128]{1,0:T(8,128)(2,1)S(1)}, bf1...) custom-call(s32[1,16]{1,0:T(1,128)S(1)} %bitcast.24, ...), custom_call_target="tpu_custom_call" | custom-call | flops 10000000000 | bytes 4000000 | tf_op jit(solution)/shard_map/heads_forward_2/pallas_call | solution.py:723
  92.3 1.6 collective-permute-done.17.refs_4_.refs_18_
  94.2 1.5 collective-permute-start.20
  95.8 1.5 collective-permute-start.22
  97.3 9.2 %ffn_forward.1 = (bf16[784,512]{1,0:T(8,128)(2,1)}, bf16[784,512]{1,0:T(8,128)(2,1)}, bf16[784,512]{1,0:T(8,128)(2,1)}, f32[16,784]{1,0:T(8,128)}, bf16[784,512]...) custom-call(s32[1,16]{1,0:T(1,128)S(1)} %bitcast.25, ...), custom_call_target="tpu_custom_call" | custom-call | flops 8000000000 | bytes 4000000 | tf_op jit(solution)/shard_map/ffn_forward/pallas_call | solution.py:723
  106.6 10.1 %collective-permute-done.22.refs_7_.refs_17_ = bf16[2560,128]{1,0:T(8,128)(2,1)S(1)} collective-permute-done((bf16[2560,128]{1,0:T(8,128)(2,1)S(1)}, bf16[2560,128]{1,0:T(8,128)(2,1)S(1)}, u32[]{:S(2)}, u32[]{:S(2)}) %collective-permute-start.22) | collective-permute-done | bytes 655392 | tf_op jit(solution)/shard_map/ppermute | solution.py:1143
  116.7 2.1 collective-permute-done.23.refs_8_.refs_18_
  118.8 1.5 collective-permute-start.24
  120.3 12.8 %cross_forward.1 = (f32[512,512]{1,0:T(8,128)S(1)}, bf16[512,512]{1,0:T(8,128)(2,1)}, bf16[512,512]{1,0:T(8,128)(2,1)}, bf16[512,512]{1,0:T(8,128)(2,1)}, bf16[5...) custom-call(s32[1,16]{1,0:T(1,128)S(1)} %bitcast.26, ...), custom_call_target="tpu_custom_call" | custom-call | flops 8000000000 | bytes 4000000 | tf_op jit(solution)/shard_map/cross_forward/pallas_call | solution.py:723
  133.2 1.3 collective-permute-start.26
  135.1 0.8 copy-done.44
  135.9 9.2 %ffn_both.1 = (bf16[512,512]{1,0:T(8,128)(2,1)}, bf16[976,512]{1,0:T(8,128)(2,1)}, f32[512,512]{1,0:T(8,128)S(1)}, f32[8,512]{1,0:T(8,128)}, bf16[2048,128]{1,0:...) custom-call(s32[1,16]{1,0:T(1,128)} %bitcast.20, f32[512,512]{1,0:T(8,128)S(1)} %get-tuple-element.330.refs_1_, ...), custom_call_target="tpu_custom_call" | custom-call | flops 10000000000 | bytes 4000000 | tf_op jit(solution)/shard_map/ffn_both/pallas_call | solution.py:723
  145.2 2.9 %collective-permute-start.28 = (bf16[976,512]{1,0:T(8,128)(2,1)}, bf16[976,512]{1,0:T(8,128)(2,1)S(1)}, u32[]{:S(2)}, u32[]{:S(2)}) collective-permute-start(bf16[976,512]{1,0:T(8,128)(2,1)} %get-tuple-element.365), channel_id=1, source_target_pairs={{0,1},{1,2},{2,3},{4,5},{5,6},{6,7},{8,9},{9,10},{10,11},{12,13},{... | collective-permute-start | bytes 2998280 | tf_op jit(solution)/shard_map/ppermute | solution.py:203
  148.1 1.7 collective-permute-start.27
  149.9 17.3 %cross_backward.1 = (f32[784,512]{1,0:T(8,128)S(1)}, bf16[512,512]{1,0:T(8,128)(2,1)}, bf16[384,512]{1,0:T(8,128)(2,1)}, bf16[512,128]{1,0:T(8,128)(2,1)}, bf16[...) custom-call(s32[1,16]{1,0:T(1,128)} %bitcast.21, ...), custom_call_target="tpu_custom_call" | custom-call | flops 20000000000 | bytes 4000000 | tf_op jit(solution)/shard_map/cross_backward/pallas_call | solution.py:723
  168.3 1.7 collective-permute-start.30
  170.0 11.7 %ffn_backward.1 = (bf16[784,512]{1,0:T(8,128)(2,1)}, bf16[976,512]{1,0:T(8,128)(2,1)}, bf16[784,128]{1,0:T(8,128)(2,1)}, bf16[784,128]{1,0:T(8,128)(2,1)S(1)}, b...) custom-call(s32[1,16]{1,0:T(1,128)} %bitcast.22, ...), custom_call_target="tpu_custom_call" | custom-call | flops 12000000000 | bytes 4000000 | tf_op jit(solution)/shard_map/ffn_backward/pallas_call | solution.py:723
  181.7 3.4 %collective-permute-done.30.refs_3_ = bf16[512,128]{1,0:T(8,128)(2,1)S(1)} collective-permute-done((bf16[512,128]{1,0:T(8,128)(2,1)S(1)}, bf16[512,128]{1,0:T(8,128)(2,1)S(1)}, u32[]{:S(2)}, u32[]{:S(2)}) %collective-permute-start.30) | collective-permute-done | bytes 131104 | tf_op jit(solution)/shard_map/ppermute | solution.py:157
  185.1 1.9 collective-permute-done.31.refs_4_
  187.6 1.7 collective-permute-start.35
  189.8 10.8 %heads_backward_2.1 = (bf16[384,512]{1,0:T(8,128)(2,1)}, bf16[768,512]{1,0:T(8,128)(2,1)S(1)}, bf16[384,512]{1,0:T(8,128)(2,1)}, bf16[1536,128]{1,0:T(8,128)(2,1)}) custom-call(s32[1,16]{1,0:T(1,128)S(1)} %bitcast.27, bf16[512,128]{1,0:T(8,128)(2,1)} %get-tuple-element.401.refs_1_, bf16[512,128]{1,0:T(8,128)(2,1)} %copy-done.55, ...), custom_call_target="tpu_custom_call" | custom-call | flops 20000000000 | bytes 4000000 | tf_op jit(solution)/shard_map/heads_backward_2/pallas_call | solution.py:723
  200.6 2.2 sum_group.1.refs_2_
  202.8 6.3 %collective-permute-done.35.refs_3_ = bf16[784,128]{1,0:T(8,128)(2,1)S(1)} collective-permute-done((bf16[784,128]{1,0:T(8,128)(2,1)S(1)}, bf16[784,128]{1,0:T(8,128)(2,1)S(1)}, u32[]{:S(2)}, u32[]{:S(2)}) %collective-permute-start.35) | collective-permute-done | bytes 200736 | tf_op jit(solution)/shard_map/ppermute | solution.py:157
  209.2 3.0 %collective-permute-done.36.refs_4_ = bf16[784,128]{1,0:T(8,128)(2,1)S(1)} collective-permute-done((bf16[784,128]{1,0:T(8,128)(2,1)S(1)}, bf16[784,128]{1,0:T(8,128)(2,1)S(1)}, u32[]{:S(2)}, u32[]{:S(2)}) %collective-permute-start.36) | collective-permute-done | bytes 200736 | tf_op jit(solution)/shard_map/ppermute | solution.py:158
  213.0 2.3 collective-permute-start.41
  215.3 19.9 %heads_backward_0.1 = (bf16[608,512]{1,0:T(8,128)(2,1)}, bf16[1216,512]{1,0:T(8,128)(2,1)S(1)}, bf16[608,512]{1,0:T(8,128)(2,1)}, bf16[1536,128]{1,0:T(8,128)(2,1)}) custom-call(s32[1,16]{1,0:T(1,128)S(1)} %bitcast.28, bf16[784,128]{1,0:T(8,128)(2,1)} %get-tuple-element.421.refs_1_, bf16[784,128]{1,0:T(8,128)(2,1)} %copy-done.49, ...), custom_call_target="tpu_custom_call" | custom-call | flops 20000000000 | bytes 4000000 | tf_op jit(solution)/shard_map/heads_backward_0/pallas_call | solution.py:723
  235.3 3.3 %collective-permute-start.42 = (bf16[1216,512]{1,0:T(8,128)(2,1)S(1)}, bf16[1216,512]{1,0:T(8,128)(2,1)S(1)}, u32[]{:S(2)}, u32[]{:S(2)}) collective-permute-start(bf16[1216,512]{1,0:T(8,128)(2,1)S(1)} %get-tuple-element.456), channel_id=1, source_target_pairs={{0,1},{1,0},{2,3},{3,2},{4,5},{5,4},{6,7},{7,6},{8,9},{9,8},{10,11... | collective-permute-start | bytes 3735560 | tf_op jit(solution)/shard_map/ppermute | solution.py:1279
  238.6 3.9 %deal_tiles.1 = (bf16[1296,128]{1,0:T(8,128)(2,1)S(1)}, bf16[1296,128]{1,0:T(8,128)(2,1)S(1)}, bf16[1296,128]{1,0:T(8,128)(2,1)S(1)}, bf16[1296,128]{1,0:T(8,128...) custom-call(s32[8,10]{1,0:T(8,128)} %get-tuple-element.439.refs_0_, ...), custom_call_target="tpu_custom_call" | custom-call | bytes 4000000 | tf_op jit(solution)/shard_map/deal_tiles/pallas_call | solution.py:723
  243.9 1.2 collective-permute-start.46
  245.1 2.4 collective-permute-start.43
  247.5 5.9 %collective-permute-done.44 = bf16[1296,128]{1,0:T(8,128)(2,1)S(1)} collective-permute-done((bf16[1296,128]{1,0:T(8,128)(2,1)S(1)}, bf16[1296,128]{1,0:T(8,128)(2,1)S(1)}, u32[]{:S(2)}, u32[]{:S(2)}) %collective-permute-start.44) | collective-permute-done | bytes 331808 | tf_op jit(solution)/shard_map/ppermute | solution.py:127
  253.4 2.0 collective-permute-start.45
  256.0 4.5 %collective-permute-done.46 = bf16[1296,128]{1,0:T(8,128)(2,1)S(1)} collective-permute-done((bf16[1296,128]{1,0:T(8,128)(2,1)S(1)}, bf16[1296,128]{1,0:T(8,128)(2,1)S(1)}, u32[]{:S(2)}, u32[]{:S(2)}) %collective-permute-start.46) | collective-permute-done | bytes 331808 | tf_op jit(solution)/shard_map/ppermute | solution.py:127
  260.6 1.3 collective-permute-start.47
  262.4 5.1 %collective-permute-done.48 = bf16[1296,128]{1,0:T(8,128)(2,1)S(1)} collective-permute-done((bf16[1296,128]{1,0:T(8,128)(2,1)S(1)}, bf16[1296,128]{1,0:T(8,128)(2,1)S(1)}, u32[]{:S(2)}, u32[]{:S(2)}) %collective-permute-start.48) | collective-permute-done | bytes 331808 | tf_op jit(solution)/shard_map/ppermute | solution.py:127
  267.7 3.0 %collective-permute-start.49 = (bf16[1296,128]{1,0:T(8,128)(2,1)S(1)}, bf16[1296,128]{1,0:T(8,128)(2,1)S(1)}, u32[]{:S(2)}, u32[]{:S(2)}) collective-permute-start(bf16[1296,128]{1,0:T(8,128)(2,1)S(1)} %add_convert_fusion.5), channel_id=1, source_target_pairs={{0,24},{4,28},{8,0},{12,4},{16,8},{20,12},{24,16},{28,20},{1,25},{... | collective-permute-start | bytes 995336 | tf_op jit(solution)/shard_map/ppermute | solution.py:133
  270.7 1.6 push_outputs.1
  272.4 2.3 push_gradients.1
  274.7 3.1 %collective-permute-done.45.refs_1_ = bf16[1296,128]{1,0:T(8,128)(2,1)S(1)} collective-permute-done((bf16[1296,128]{1,0:T(8,128)(2,1)S(1)}, bf16[1296,128]{1,0:T(8,128)(2,1)S(1)}, u32[]{:S(2)}, u32[]{:S(2)}) %collective-permute-start.45) | collective-permute-done | bytes 331808 | tf_op jit(solution)/shard_map/ppermute | solution.py:133
  277.8 6.2 %collective-permute-done.49.refs_3_ = bf16[1296,128]{1,0:T(8,128)(2,1)S(1)} collective-permute-done((bf16[1296,128]{1,0:T(8,128)(2,1)S(1)}, bf16[1296,128]{1,0:T(8,128)(2,1)S(1)}, u32[]{:S(2)}, u32[]{:S(2)}) %collective-permute-start.49) | collective-permute-done | bytes 331808 | tf_op jit(solution)/shard_map/ppermute | solution.py:133
  284.0 4.5 %shampoo.1 = (f32[1,10,128,128]{3,2,1,0:T(8,128)}, f32[1,10,128,128]{3,2,1,0:T(8,128)}, f32[1,10,128,128]{3,2,1,0:T(8,128)}, f32[1,10,128,128]{3,2,1,0:T(8,128)}...) custom-call(bf16[1296,128]{1,0:T(8,128)(2,1)S(1)} %get-tuple-element.461.refs_0_, ...), custom_call_target="tpu_custom_call" | custom-call | tf_op jit(solution)/shard_map/shampoo/pallas_call | solution.py:397
  (192 shorter events, 10.8 us)
Async XLA Ops:
  3.0 23.6 %copy-start.25 = (bf16[384,512]{1,0:T(8,128)(2,1)S(1)}, bf16[384,512]{1,0:T(8,128)(2,1)}, u32[]{:S(2)}) copy-start(bf16[384,512]{1,0:T(8,128)(2,1)} %refs_0_.3) | copy-start | bytes 1179652
  3.0 23.6 %collective-permute-start.4 = (bf16[972,512]{1,0:T(8,128)(2,1)}, bf16[972,512]{1,0:T(8,128)(2,1)S(1)}, u32[]{:S(2)}, u32[]{:S(2)}) collective-permute-start(bf16[972,512]{1,0:T(8,128)(2,1)} %pad_maximum_fusion.1), channel_id=1, source_target_pairs={{0,1},{1,0},{2,3},{3,2},{4,5},{5,4},{6,7},{7,6},{8,9},{9,8},{10,11... | collective-permute-start | bytes 2985992 | tf_op jit(solution)/shard_map/ppermute | solution.py:79
  3.4 23.1 %collective-permute-start.3 = (bf16[588,512]{1,0:T(8,128)(2,1)S(1)}, bf16[588,512]{1,0:T(8,128)(2,1)}, u32[]{:S(2)}, u32[]{:S(2)}) collective-permute-start(bf16[588,512]{1,0:T(8,128)(2,1)S(1)} %copy-done.23), channel_id=1, source_target_pairs={{0,2},{1,3},{2,0},{3,1},{4,6},{5,7},{6,4},{7,5},{8,10},{9,11},{10,... | collective-permute-start | bytes 1806344 | tf_op jit(solution)/shard_map/ppermute | solution.py:82
  6.1 51.4 %copy-start.26 = (bf16[1296,128]{1,0:T(8,128)(2,1)}, bf16[1296,128]{1,0:T(8,128)(2,1)S(1)}, u32[]{:S(2)}) copy-start(bf16[1296,128]{1,0:T(8,128)(2,1)S(1)} %fusion.1.refs_2_) | copy-start | bytes 995332
  6.1 9.9 %collective-permute-start.2 = (bf16[1296,128]{1,0:T(8,128)(2,1)S(1)}, bf16[1296,128]{1,0:T(8,128)(2,1)S(1)}, u32[]{:S(2)}, u32[]{:S(2)}) collective-permute-start(bf16[1296,128]{1,0:T(8,128)(2,1)S(1)} %fusion.1.refs_2_), channel_id=1, source_target_pairs={{0,4},{4,0},{8,12},{12,8},{16,20},{20,16},{24,28},{28,24},{1,5},{5... | collective-permute-start | bytes 995336 | tf_op jit(solution)/shard_map/ppermute | solution.py:99
  7.7 11.8 %collective-permute-start.1 = (bf16[1296,128]{1,0:T(8,128)(2,1)S(1)}, bf16[1296,128]{1,0:T(8,128)(2,1)}, u32[]{:S(2)}, u32[]{:S(2)}) collective-permute-start(bf16[1296,128]{1,0:T(8,128)(2,1)S(1)} %fusion.1.refs_2_), channel_id=1, source_target_pairs={{0,24},{4,28},{8,0},{12,4},{16,8},{20,12},{24,16},{28,20},{1,25},{... | collective-permute-start | bytes 995336 | tf_op jit(solution)/shard_map/ppermute | solution.py:96
  11.3 15.2 %collective-permute-start = (bf16[1296,128]{1,0:T(8,128)(2,1)S(1)}, bf16[1296,128]{1,0:T(8,128)(2,1)}, u32[]{:S(2)}, u32[]{:S(2)}) collective-permute-start(bf16[1296,128]{1,0:T(8,128)(2,1)S(1)} %fusion.1.refs_2_), channel_id=1, source_target_pairs={{0,8},{4,12},{8,16},{12,20},{16,24},{20,28},{24,0},{28,4},{1,9},{5... | collective-permute-start | bytes 995336 | tf_op jit(solution)/shard_map/ppermute | solution.py:96
  11.6 40.2 %copy-start.37 = (s32[8]{0:T(128)}, s32[8]{0:T(128)S(1)}, u32[]{:S(2)}) copy-start(s32[8]{0:T(128)S(1)} %stack.73.refs_1_) | copy-start | bytes 100
  16.0 41.4 %copy-start.32 = (bf16[1296,128]{1,0:T(8,128)(2,1)}, bf16[1296,128]{1,0:T(8,128)(2,1)S(1)}, u32[]{:S(2)}) copy-start(bf16[1296,128]{1,0:T(8,128)(2,1)S(1)} %collective-permute-done.2.refs_6_) | copy-start | bytes 995332
  26.5 21.6 %copy-start.20 = (bf16[972,512]{1,0:T(8,128)(2,1)}, bf16[972,512]{1,0:T(8,128)(2,1)S(1)}, u32[]{:S(2)}) copy-start(bf16[972,512]{1,0:T(8,128)(2,1)S(1)} %collective-permute-done.4.refs_1_) | copy-start | bytes 2985988
  26.5 18.6 %collective-permute-start.9 = (bf16[588,512]{1,0:T(8,128)(2,1)}, bf16[588,512]{1,0:T(8,128)(2,1)S(1)}, u32[]{:S(2)}, u32[]{:S(2)}) collective-permute-start(bf16[588,512]{1,0:T(8,128)(2,1)} %collective-permute-done.3.refs_2_), channel_id=1, source_target_pairs={{0,1},{1,0},{2,3},{3,2},{4,5},{5,4},{6,7},{7,6},{8,9},{9,8},{10,11... | collective-permute-start | bytes 1806344 | tf_op jit(solution)/shard_map/ppermute | solution.py:79
  26.6 18.5 %collective-permute-start.8 = (bf16[384,512]{1,0:T(8,128)(2,1)S(1)}, bf16[384,512]{1,0:T(8,128)(2,1)S(1)}, u32[]{:S(2)}, u32[]{:S(2)}) collective-permute-start(bf16[384,512]{1,0:T(8,128)(2,1)S(1)} %copy-done.25), channel_id=1, source_target_pairs={{0,2},{1,3},{2,0},{3,1},{4,6},{5,7},{6,4},{7,5},{8,10},{9,11},{10,... | collective-permute-start | bytes 1179656 | tf_op jit(solution)/shard_map/ppermute | solution.py:82
  27.2 17.9 %collective-permute-start.5 = (bf16[1296,128]{1,0:T(8,128)(2,1)S(1)}, bf16[1296,128]{1,0:T(8,128)(2,1)S(1)}, u32[]{:S(2)}, u32[]{:S(2)}) collective-permute-start(bf16[1296,128]{1,0:T(8,128)(2,1)S(1)} %fusion.1.refs_2_), channel_id=1, source_target_pairs={{0,16},{4,20},{8,24},{12,28},{16,0},{20,4},{24,8},{28,12},{1,17},{... | collective-permute-start | bytes 995336 | tf_op jit(solution)/shard_map/ppermute | solution.py:96
  28.0 17.1 %collective-permute-start.6 = (bf16[1296,128]{1,0:T(8,128)(2,1)}, bf16[1296,128]{1,0:T(8,128)(2,1)S(1)}, u32[]{:S(2)}, u32[]{:S(2)}) collective-permute-start(bf16[1296,128]{1,0:T(8,128)(2,1)} %collective-permute-done.refs_3_), channel_id=1, source_target_pairs={{0,4},{4,0},{8,12},{12,8},{16,20},{20,16},{24,28},{28,24},{1,5},{5... | collective-permute-start | bytes 995336 | tf_op jit(solution)/shard_map/ppermute | solution.py:99
  28.5 16.6 %collective-permute-start.7 = (bf16[1296,128]{1,0:T(8,128)(2,1)}, bf16[1296,128]{1,0:T(8,128)(2,1)S(1)}, u32[]{:S(2)}, u32[]{:S(2)}) collective-permute-start(bf16[1296,128]{1,0:T(8,128)(2,1)} %collective-permute-done.1.refs_5_), channel_id=1, source_target_pairs={{0,4},{4,0},{8,12},{12,8},{16,20},{20,16},{24,28},{28,24},{1,5},{5... | collective-permute-start | bytes 995336 | tf_op jit(solution)/shard_map/ppermute | solution.py:99
  45.1 17.3 %copy-start.30 = (bf16[384,512]{1,0:T(8,128)(2,1)}, bf16[384,512]{1,0:T(8,128)(2,1)S(1)}, u32[]{:S(2)}) copy-start(bf16[384,512]{1,0:T(8,128)(2,1)S(1)} %collective-permute-done.8.refs_2_) | copy-start | bytes 1179652
  45.2 12.3 %collective-permute-start.12 = (bf16[384,512]{1,0:T(8,128)(2,1)}, bf16[384,512]{1,0:T(8,128)(2,1)S(1)}, u32[]{:S(2)}, u32[]{:S(2)}) collective-permute-start(bf16[384,512]{1,0:T(8,128)(2,1)} %refs_7_.2), channel_id=1, source_target_pairs={{1,0},{2,1},{3,2},{5,4},{6,5},{7,6},{9,8},{10,9},{11,10},{13,12},{... | collective-permute-start | bytes 1179656 | tf_op jit(solution)/shard_map/ppermute | solution.py:85
  46.5 11.0 %collective-permute-start.11 = (bf16[384,512]{1,0:T(8,128)(2,1)S(1)}, bf16[384,512]{1,0:T(8,128)(2,1)S(1)}, u32[]{:S(2)}, u32[]{:S(2)}) collective-permute-start(bf16[384,512]{1,0:T(8,128)(2,1)S(1)} %collective-permute-done.8.refs_2_), channel_id=1, source_target_pairs={{0,1},{1,0},{2,3},{3,2},{4,5},{5,4},{6,7},{7,6},{8,9},{9,8},{10,11... | collective-permute-start | bytes 1179656 | tf_op jit(solution)/shard_map/ppermute | solution.py:79
  47.7 9.8 %collective-permute-start.10 = (bf16[1296,128]{1,0:T(8,128)(2,1)S(1)}, bf16[1296,128]{1,0:T(8,128)(2,1)S(1)}, u32[]{:S(2)}, u32[]{:S(2)}) collective-permute-start(bf16[1296,128]{1,0:T(8,128)(2,1)S(1)} %collective-permute-done.5.refs_4_), channel_id=1, source_target_pairs={{0,4},{4,0},{8,12},{12,8},{16,20},{20,16},{24,28},{28,24},{1,5},{5... | collective-permute-start | bytes 995336 | tf_op jit(solution)/shard_map/ppermute | solution.py:99
  62.3 20.3 %collective-permute-start.13 = (bf16[10240,128]{1,0:T(8,128)(2,1)}, bf16[10240,128]{1,0:T(8,128)(2,1)}, u32[]{:S(2)}, u32[]{:S(2)}) collective-permute-start(bf16[10240,128]{1,0:T(8,128)(2,1)} %get-tuple-element.265.refs_1_.refs_5_.refs_2_.refs_15_.refs_7_.refs_13_), channel_id=1, source_target_pairs={{0,1},{1,0},{2,3},{3,2},{4,5},{5,4},{6,7},{7,6},{8,9},{9,8},{10,11... | collective-permute-start | bytes 7864328 | tf_op jit(solution)/shard_map/ppermute | solution.py:1274
  65.5 17.1 %collective-permute-start.14 = (bf16[2560,128]{1,0:T(8,128)(2,1)S(1)}, bf16[2560,128]{1,0:T(8,128)(2,1)S(1)}, u32[]{:S(2)}, u32[]{:S(2)}) collective-permute-start(bf16[2560,128]{1,0:T(8,128)(2,1)S(1)} %get-tuple-element.273), channel_id=1, source_target_pairs={{0,2},{1,3},{2,0},{3,1},{4,6},{5,7},{6,4},{7,5},{8,10},{9,11},{10,... | collective-permute-start | bytes 1966088 | tf_op jit(solution)/shard_map/ppermute | solution.py:1143
  82.6 14.7 %copy-start.16 = (bf16[2560,128]{1,0:T(8,128)(2,1)}, bf16[2560,128]{1,0:T(8,128)(2,1)S(1)}, u32[]{:S(2)}) copy-start(bf16[2560,128]{1,0:T(8,128)(2,1)S(1)} %collective-permute-done.14.refs_7_.refs_9_) | copy-start | bytes 1966084
  82.6 9.6 %collective-permute-start.15 = (bf16[784,128]{1,0:T(8,128)(2,1)S(1)}, bf16[784,128]{1,0:T(8,128)(2,1)S(1)}, u32[]{:S(2)}, u32[]{:S(2)}) collective-permute-start(bf16[784,128]{1,0:T(8,128)(2,1)S(1)} %get-tuple-element.285), channel_id=1, source_target_pairs={{0,1},{1,0},{2,3},{3,2},{4,5},{5,4},{6,7},{7,6},{8,9},{9,8},{10,11... | collective-permute-start | bytes 602120 | tf_op jit(solution)/shard_map/ppermute | solution.py:156
  82.6 9.6 %collective-permute-start.16 = (bf16[784,128]{1,0:T(8,128)(2,1)S(1)}, bf16[784,128]{1,0:T(8,128)(2,1)S(1)}, u32[]{:S(2)}, u32[]{:S(2)}) collective-permute-start(bf16[784,128]{1,0:T(8,128)(2,1)S(1)} %get-tuple-element.286), channel_id=1, source_target_pairs={{0,2},{1,3},{2,0},{3,1},{4,6},{5,7},{6,4},{7,5},{8,10},{9,11},{10,... | collective-permute-start | bytes 602120 | tf_op jit(solution)/shard_map/ppermute | solution.py:157
  84.2 9.7 %collective-permute-start.17 = (bf16[784,128]{1,0:T(8,128)(2,1)S(1)}, bf16[784,128]{1,0:T(8,128)(2,1)S(1)}, u32[]{:S(2)}, u32[]{:S(2)}) collective-permute-start(bf16[784,128]{1,0:T(8,128)(2,1)S(1)} %get-tuple-element.287), channel_id=1, source_target_pairs={{0,3},{1,2},{2,1},{3,0},{4,7},{5,6},{6,5},{7,4},{8,11},{9,10},{10,... | collective-permute-start | bytes 602120 | tf_op jit(solution)/shard_map/ppermute | solution.py:158
  84.5 9.4 %collective-permute-start.18 = (bf16[2560,128]{1,0:T(8,128)(2,1)S(1)}, bf16[2560,128]{1,0:T(8,128)(2,1)S(1)}, u32[]{:S(2)}, u32[]{:S(2)}) collective-permute-start(bf16[2560,128]{1,0:T(8,128)(2,1)S(1)} %collective-permute-done.14.refs_7_.refs_9_), channel_id=1, source_target_pairs={{0,1},{1,0},{2,3},{3,2},{4,5},{5,4},{6,7},{7,6},{8,9},{9,8},{10,11... | collective-permute-start | bytes 1966088 | tf_op jit(solution)/shard_map/ppermute | solution.py:1146
  93.9 12.7 %collective-permute-start.19 = (bf16[512,128]{1,0:T(8,128)(2,1)S(1)}, bf16[512,128]{1,0:T(8,128)(2,1)S(1)}, u32[]{:S(2)}, u32[]{:S(2)}) collective-permute-start(bf16[512,128]{1,0:T(8,128)(2,1)S(1)} %get-tuple-element.307), channel_id=1, source_target_pairs={{0,1},{1,0},{2,3},{3,2},{4,5},{5,4},{6,7},{7,6},{8,9},{9,8},{10,11... | collective-permute-start | bytes 393224 | tf_op jit(solution)/shard_map/ppermute | solution.py:156
  94.2 12.4 %collective-permute-start.20 = (bf16[512,128]{1,0:T(8,128)(2,1)S(1)}, bf16[512,128]{1,0:T(8,128)(2,1)S(1)}, u32[]{:S(2)}, u32[]{:S(2)}) collective-permute-start(bf16[512,128]{1,0:T(8,128)(2,1)S(1)} %get-tuple-element.308), channel_id=1, source_target_pairs={{0,2},{1,3},{2,0},{3,1},{4,6},{5,7},{6,4},{7,5},{8,10},{9,11},{10,... | collective-permute-start | bytes 393224 | tf_op jit(solution)/shard_map/ppermute | solution.py:157
  95.7 10.9 %collective-permute-start.21 = (bf16[512,128]{1,0:T(8,128)(2,1)S(1)}, bf16[512,128]{1,0:T(8,128)(2,1)S(1)}, u32[]{:S(2)}, u32[]{:S(2)}) collective-permute-start(bf16[512,128]{1,0:T(8,128)(2,1)S(1)} %get-tuple-element.309), channel_id=1, source_target_pairs={{0,3},{1,2},{2,1},{3,0},{4,7},{5,6},{6,5},{7,4},{8,11},{9,10},{10,... | collective-permute-start | bytes 393224 | tf_op jit(solution)/shard_map/ppermute | solution.py:158
  95.8 20.9 %collective-permute-start.22 = (bf16[2560,128]{1,0:T(8,128)(2,1)S(1)}, bf16[2560,128]{1,0:T(8,128)(2,1)S(1)}, u32[]{:S(2)}, u32[]{:S(2)}) collective-permute-start(bf16[2560,128]{1,0:T(8,128)(2,1)S(1)} %get-tuple-element.311), channel_id=1, source_target_pairs={{0,2},{1,3},{2,0},{3,1},{4,6},{5,7},{6,4},{7,5},{8,10},{9,11},{10,... | collective-permute-start | bytes 1966088 | tf_op jit(solution)/shard_map/ppermute | solution.py:1143
  116.7 16.4 %copy-start.18 = (bf16[2560,128]{1,0:T(8,128)(2,1)}, bf16[2560,128]{1,0:T(8,128)(2,1)S(1)}, u32[]{:S(2)}) copy-start(bf16[2560,128]{1,0:T(8,128)(2,1)S(1)} %collective-permute-done.22.refs_7_.refs_17_) | copy-start | bytes 1966084
  116.7 2.1 collective-permute-start.23
  118.8 14.4 %copy-start.41 = (bf16[588,512]{1,0:T(8,128)(2,1)S(1)}, bf16[588,512]{1,0:T(8,128)(2,1)}, u32[]{:S(2)}) copy-start(bf16[588,512]{1,0:T(8,128)(2,1)} %refs_2_) | copy-start | bytes 1806340
  118.8 14.3 %collective-permute-start.24 = (bf16[2048,128]{1,0:T(8,128)(2,1)S(1)}, bf16[2048,128]{1,0:T(8,128)(2,1)S(1)}, u32[]{:S(2)}, u32[]{:S(2)}) collective-permute-start(bf16[2048,128]{1,0:T(8,128)(2,1)S(1)} %get-tuple-element.329), channel_id=1, source_target_pairs={{0,2},{1,3},{2,0},{3,1},{4,6},{5,7},{6,4},{7,5},{8,10},{9,11},{10,... | collective-permute-start | bytes 1572872 | tf_op jit(solution)/shard_map/ppermute | solution.py:1143
  133.2 2.0 collective-permute-start.25
  133.2 11.9 %collective-permute-start.26 = (bf16[588,512]{1,0:T(8,128)(2,1)S(1)}, bf16[588,512]{1,0:T(8,128)(2,1)S(1)}, u32[]{:S(2)}, u32[]{:S(2)}) collective-permute-start(bf16[588,512]{1,0:T(8,128)(2,1)S(1)} %copy-done.41), channel_id=1, source_target_pairs={{1,0},{2,1},{3,2},{5,4},{6,5},{7,6},{9,8},{10,9},{11,10},{13,12},{... | collective-permute-start | bytes 1806344 | tf_op jit(solution)/shard_map/ppermute | solution.py:1164
  145.2 22.0 %copy-start.42 = (bf16[588,512]{1,0:T(8,128)(2,1)}, bf16[588,512]{1,0:T(8,128)(2,1)S(1)}, u32[]{:S(2)}) copy-start(bf16[588,512]{1,0:T(8,128)(2,1)S(1)} %collective-permute-done.26.refs_3_) | copy-start | bytes 1806340
  145.2 22.0 %collective-permute-start.28 = (bf16[976,512]{1,0:T(8,128)(2,1)}, bf16[976,512]{1,0:T(8,128)(2,1)S(1)}, u32[]{:S(2)}, u32[]{:S(2)}) collective-permute-start(bf16[976,512]{1,0:T(8,128)(2,1)} %get-tuple-element.365), channel_id=1, source_target_pairs={{0,1},{1,2},{2,3},{4,5},{5,6},{6,7},{8,9},{9,10},{10,11},{12,13},{... | collective-permute-start | bytes 2998280 | tf_op jit(solution)/shard_map/ppermute | solution.py:203
  148.1 19.1 %collective-permute-start.27 = (bf16[4096,128]{1,0:T(8,128)(2,1)S(1)}, bf16[4096,128]{1,0:T(8,128)(2,1)S(1)}, u32[]{:S(2)}, u32[]{:S(2)}) collective-permute-start(bf16[4096,128]{1,0:T(8,128)(2,1)S(1)} %get-tuple-element.364), channel_id=1, source_target_pairs={{0,1},{1,0},{2,3},{3,2},{4,5},{5,4},{6,7},{7,6},{8,9},{9,8},{10,11... | collective-permute-start | bytes 3145736 | tf_op jit(solution)/shard_map/ppermute | solution.py:141
  167.2 19.8 %collective-permute-start.32 = (bf16[5120,128]{1,0:T(8,128)(2,1)S(1)}, bf16[5120,128]{1,0:T(8,128)(2,1)S(1)}, u32[]{:S(2)}, u32[]{:S(2)}) collective-permute-start(bf16[5120,128]{1,0:T(8,128)(2,1)S(1)} %get-tuple-element.398), channel_id=1, source_target_pairs={{0,1},{1,0},{2,3},{3,2},{4,5},{5,4},{6,7},{7,6},{8,9},{9,8},{10,11... | collective-permute-start | bytes 3932168 | tf_op jit(solution)/shard_map/ppermute | solution.py:141
  167.5 19.5 %collective-permute-start.33 = (bf16[2048,128]{1,0:T(8,128)(2,1)S(1)}, bf16[2048,128]{1,0:T(8,128)(2,1)S(1)}, u32[]{:S(2)}, u32[]{:S(2)}) collective-permute-start(bf16[2048,128]{1,0:T(8,128)(2,1)S(1)} %add_convert_fusion.3), channel_id=1, source_target_pairs={{0,2},{1,3},{2,0},{3,1},{4,6},{5,7},{6,4},{7,5},{8,10},{9,11},{10,... | collective-permute-start | bytes 1572872 | tf_op jit(solution)/shard_map/ppermute | solution.py:150
  167.9 13.8 %collective-permute-start.29 = (bf16[512,128]{1,0:T(8,128)(2,1)S(1)}, bf16[512,128]{1,0:T(8,128)(2,1)S(1)}, u32[]{:S(2)}, u32[]{:S(2)}) collective-permute-start(bf16[512,128]{1,0:T(8,128)(2,1)S(1)} %get-tuple-element.395), channel_id=1, source_target_pairs={{0,1},{1,0},{2,3},{3,2},{4,5},{5,4},{6,7},{7,6},{8,9},{9,8},{10,11... | collective-permute-start | bytes 393224 | tf_op jit(solution)/shard_map/ppermute | solution.py:156
  168.3 16.8 %collective-permute-start.30 = (bf16[512,128]{1,0:T(8,128)(2,1)S(1)}, bf16[512,128]{1,0:T(8,128)(2,1)S(1)}, u32[]{:S(2)}, u32[]{:S(2)}) collective-permute-start(bf16[512,128]{1,0:T(8,128)(2,1)S(1)} %get-tuple-element.396), channel_id=1, source_target_pairs={{0,2},{1,3},{2,0},{3,1},{4,6},{5,7},{6,4},{7,5},{8,10},{9,11},{10,... | collective-permute-start | bytes 393224 | tf_op jit(solution)/shard_map/ppermute | solution.py:157
  170.0 17.0 %collective-permute-start.31 = (bf16[512,128]{1,0:T(8,128)(2,1)S(1)}, bf16[512,128]{1,0:T(8,128)(2,1)S(1)}, u32[]{:S(2)}, u32[]{:S(2)}) collective-permute-start(bf16[512,128]{1,0:T(8,128)(2,1)S(1)} %get-tuple-element.397), channel_id=1, source_target_pairs={{0,3},{1,2},{2,1},{3,0},{4,7},{5,6},{6,5},{7,4},{8,11},{9,10},{10,... | collective-permute-start | bytes 393224 | tf_op jit(solution)/shard_map/ppermute | solution.py:158
  187.2 48.0 %collective-permute-start.40 = (bf16[2560,128]{1,0:T(8,128)(2,1)S(1)}, bf16[2560,128]{1,0:T(8,128)(2,1)}, u32[]{:S(2)}, u32[]{:S(2)}) collective-permute-start(bf16[2560,128]{1,0:T(8,128)(2,1)S(1)} %add_convert_fusion.1), channel_id=1, source_target_pairs={{0,2},{1,3},{2,0},{3,1},{4,6},{5,7},{6,4},{7,5},{8,10},{9,11},{10,... | collective-permute-start | bytes 1966088 | tf_op jit(solution)/shard_map/ppermute | solution.py:150
  187.5 15.3 %collective-permute-start.34 = (bf16[784,128]{1,0:T(8,128)(2,1)S(1)}, bf16[784,128]{1,0:T(8,128)(2,1)S(1)}, u32[]{:S(2)}, u32[]{:S(2)}) collective-permute-start(bf16[784,128]{1,0:T(8,128)(2,1)S(1)} %get-tuple-element.414), channel_id=1, source_target_pairs={{0,1},{1,0},{2,3},{3,2},{4,5},{5,4},{6,7},{7,6},{8,9},{9,8},{10,11... | collective-permute-start | bytes 602120 | tf_op jit(solution)/shard_map/ppermute | solution.py:156
  187.6 21.5 %collective-permute-start.35 = (bf16[784,128]{1,0:T(8,128)(2,1)S(1)}, bf16[784,128]{1,0:T(8,128)(2,1)S(1)}, u32[]{:S(2)}, u32[]{:S(2)}) collective-permute-start(bf16[784,128]{1,0:T(8,128)(2,1)S(1)} %get-tuple-element.415), channel_id=1, source_target_pairs={{0,2},{1,3},{2,0},{3,1},{4,6},{5,7},{6,4},{7,5},{8,10},{9,11},{10,... | collective-permute-start | bytes 602120 | tf_op jit(solution)/shard_map/ppermute | solution.py:157
  189.3 22.8 %collective-permute-start.36 = (bf16[784,128]{1,0:T(8,128)(2,1)S(1)}, bf16[784,128]{1,0:T(8,128)(2,1)S(1)}, u32[]{:S(2)}, u32[]{:S(2)}) collective-permute-start(bf16[784,128]{1,0:T(8,128)(2,1)S(1)} %get-tuple-element.416), channel_id=1, source_target_pairs={{0,3},{1,2},{2,1},{3,0},{4,7},{5,6},{6,5},{7,4},{8,11},{9,10},{10,... | collective-permute-start | bytes 602120 | tf_op jit(solution)/shard_map/ppermute | solution.py:158
  189.5 22.7 %collective-permute-start.37 = (bf16[5184,128]{1,0:T(8,128)(2,1)S(1)}, bf16[5184,128]{1,0:T(8,128)(2,1)S(1)}, u32[]{:S(2)}, u32[]{:S(2)}) collective-permute-start(bf16[5184,128]{1,0:T(8,128)(2,1)S(1)} %get-tuple-element.417), channel_id=1, source_target_pairs={{0,1},{1,0},{2,3},{3,2},{4,5},{5,4},{6,7},{7,6},{8,9},{9,8},{10,11... | collective-permute-start | bytes 3981320 | tf_op jit(solution)/shard_map/ppermute | solution.py:141
  212.2 23.1 %copy-start.19 = (bf16[5184,128]{1,0:T(8,128)(2,1)}, bf16[5184,128]{1,0:T(8,128)(2,1)S(1)}, u32[]{:S(2)}) copy-start(bf16[5184,128]{1,0:T(8,128)(2,1)S(1)} %collective-permute-done.37.refs_9_.refs_11_) | copy-start | bytes 3981316
  212.3 22.9 %collective-permute-start.39 = (bf16[2624,128]{1,0:T(8,128)(2,1)S(1)}, bf16[2624,128]{1,0:T(8,128)(2,1)S(1)}, u32[]{:S(2)}, u32[]{:S(2)}) collective-permute-start(bf16[2624,128]{1,0:T(8,128)(2,1)S(1)} %add_convert_fusion), channel_id=1, source_target_pairs={{0,2},{1,3},{2,0},{3,1},{4,6},{5,7},{6,4},{7,5},{8,10},{9,11},{10,... | collective-permute-start | bytes 2015240 | tf_op jit(solution)/shard_map/ppermute | solution.py:150
  212.8 22.5 %collective-permute-start.38 = (bf16[768,512]{1,0:T(8,128)(2,1)S(1)}, bf16[768,512]{1,0:T(8,128)(2,1)S(1)}, u32[]{:S(2)}, u32[]{:S(2)}) collective-permute-start(bf16[768,512]{1,0:T(8,128)(2,1)S(1)} %get-tuple-element.433), channel_id=1, source_target_pairs={{0,1},{1,0},{2,3},{3,2},{4,5},{5,4},{6,7},{7,6},{8,9},{9,8},{10,11... | collective-permute-start | bytes 2359304 | tf_op jit(solution)/shard_map/ppermute | solution.py:1196
  213.0 22.3 %collective-permute-start.41 = (bf16[976,512]{1,0:T(8,128)(2,1)}, bf16[976,512]{1,0:T(8,128)(2,1)S(1)}, u32[]{:S(2)}, u32[]{:S(2)}) collective-permute-start(bf16[976,512]{1,0:T(8,128)(2,1)} %get-tuple-element.436), channel_id=1, source_target_pairs={{0,1},{1,2},{2,3},{4,5},{5,6},{6,7},{8,9},{9,10},{10,11},{12,13},{... | collective-permute-start | bytes 2998280 | tf_op jit(solution)/shard_map/ppermute | solution.py:203
  235.3 7.3 %collective-permute-start.42 = (bf16[1216,512]{1,0:T(8,128)(2,1)S(1)}, bf16[1216,512]{1,0:T(8,128)(2,1)S(1)}, u32[]{:S(2)}, u32[]{:S(2)}) collective-permute-start(bf16[1216,512]{1,0:T(8,128)(2,1)S(1)} %get-tuple-element.456), channel_id=1, source_target_pairs={{0,1},{1,0},{2,3},{3,2},{4,5},{5,4},{6,7},{7,6},{8,9},{9,8},{10,11... | collective-permute-start | bytes 3735560 | tf_op jit(solution)/shard_map/ppermute | solution.py:1279
  242.6 10.7 %collective-permute-start.44 = (bf16[1296,128]{1,0:T(8,128)(2,1)S(1)}, bf16[1296,128]{1,0:T(8,128)(2,1)S(1)}, u32[]{:S(2)}, u32[]{:S(2)}) collective-permute-start(bf16[1296,128]{1,0:T(8,128)(2,1)S(1)} %get-tuple-element.467), channel_id=1, source_target_pairs={{0,4},{4,0},{8,12},{12,8},{16,20},{20,16},{24,28},{28,24},{1,5},{5... | collective-permute-start | bytes 995336 | tf_op jit(solution)/shard_map/ppermute | solution.py:127
  243.8 26.9 %copy-start.1 = (bf16[784,512]{1,0:T(8,128)(2,1)S(1)}, bf16[784,512]{1,0:T(8,128)(2,1)}, u32[]{:S(2)}) copy-start(bf16[784,512]{1,0:T(8,128)(2,1)} %get-tuple-element.312.refs_10_.refs_14_.refs_0_) | copy-start | bytes 2408452
  243.8 26.9 %copy-start.8 = (bf16[512,512]{1,0:T(8,128)(2,1)S(1)}, bf16[512,512]{1,0:T(8,128)(2,1)}, u32[]{:S(2)}) copy-start(bf16[512,512]{1,0:T(8,128)(2,1)} %get-tuple-element.342.refs_1_) | copy-start | bytes 1572868
  243.9 16.6 %collective-permute-start.46 = (bf16[1296,128]{1,0:T(8,128)(2,1)S(1)}, bf16[1296,128]{1,0:T(8,128)(2,1)S(1)}, u32[]{:S(2)}, u32[]{:S(2)}) collective-permute-start(bf16[1296,128]{1,0:T(8,128)(2,1)S(1)} %get-tuple-element.469), channel_id=1, source_target_pairs={{0,4},{4,0},{8,12},{12,8},{16,20},{20,16},{24,28},{28,24},{1,5},{5... | collective-permute-start | bytes 995336 | tf_op jit(solution)/shard_map/ppermute | solution.py:127
  245.1 27.3 %collective-permute-start.43 = (bf16[992,512]{1,0:T(8,128)(2,1)S(1)}, bf16[992,512]{1,0:T(8,128)(2,1)S(1)}, u32[]{:S(2)}, u32[]{:S(2)}) collective-permute-start(bf16[992,512]{1,0:T(8,128)(2,1)S(1)} %pad_maximum_fusion), channel_id=1, source_target_pairs={{0,2},{1,3},{2,0},{3,1},{4,6},{5,7},{6,4},{7,5},{8,10},{9,11},{10,... | collective-permute-start | bytes 3047432 | tf_op jit(solution)/shard_map/ppermute | solution.py:1288
  253.4 24.3 %collective-permute-start.45 = (bf16[1296,128]{1,0:T(8,128)(2,1)S(1)}, bf16[1296,128]{1,0:T(8,128)(2,1)S(1)}, u32[]{:S(2)}, u32[]{:S(2)}) collective-permute-start(bf16[1296,128]{1,0:T(8,128)(2,1)S(1)} %add_convert_fusion.7), channel_id=1, source_target_pairs={{0,16},{4,20},{8,24},{12,28},{16,0},{20,4},{24,8},{28,12},{1,17},{... | collective-permute-start | bytes 995336 | tf_op jit(solution)/shard_map/ppermute | solution.py:133
  255.5 12.1 %collective-permute-start.48 = (bf16[1296,128]{1,0:T(8,128)(2,1)S(1)}, bf16[1296,128]{1,0:T(8,128)(2,1)S(1)}, u32[]{:S(2)}, u32[]{:S(2)}) collective-permute-start(bf16[1296,128]{1,0:T(8,128)(2,1)S(1)} %get-tuple-element.472), channel_id=1, source_target_pairs={{0,4},{4,0},{8,12},{12,8},{16,20},{20,16},{24,28},{28,24},{1,5},{5... | collective-permute-start | bytes 995336 | tf_op jit(solution)/shard_map/ppermute | solution.py:127
  260.6 17.2 %collective-permute-start.47 = (bf16[1296,128]{1,0:T(8,128)(2,1)S(1)}, bf16[1296,128]{1,0:T(8,128)(2,1)S(1)}, u32[]{:S(2)}, u32[]{:S(2)}) collective-permute-start(bf16[1296,128]{1,0:T(8,128)(2,1)S(1)} %add_convert_fusion.6), channel_id=1, source_target_pairs={{0,8},{4,12},{8,16},{12,20},{16,24},{20,28},{24,0},{28,4},{1,9},{5... | collective-permute-start | bytes 995336 | tf_op jit(solution)/shard_map/ppermute | solution.py:133
  261.9 12.8 %collective-permute-start.50 = (bf16[1296,128]{1,0:T(8,128)(2,1)S(1)}, bf16[1296,128]{1,0:T(8,128)(2,1)S(1)}, u32[]{:S(2)}, u32[]{:S(2)}) collective-permute-start(bf16[1296,128]{1,0:T(8,128)(2,1)S(1)} %get-tuple-element.474), channel_id=1, source_target_pairs={{0,4},{4,0},{8,12},{12,8},{16,20},{20,16},{24,28},{28,24},{1,5},{5... | collective-permute-start | bytes 995336 | tf_op jit(solution)/shard_map/ppermute | solution.py:127
  267.7 16.2 %collective-permute-start.49 = (bf16[1296,128]{1,0:T(8,128)(2,1)S(1)}, bf16[1296,128]{1,0:T(8,128)(2,1)S(1)}, u32[]{:S(2)}, u32[]{:S(2)}) collective-permute-start(bf16[1296,128]{1,0:T(8,128)(2,1)S(1)} %add_convert_fusion.5), channel_id=1, source_target_pairs={{0,24},{4,28},{8,0},{12,4},{16,8},{20,12},{24,16},{28,20},{1,25},{... | collective-permute-start | bytes 995336 | tf_op jit(solution)/shard_map/ppermute | solution.py:133
  (45 other events, 312.9 us)

commit v5 on v4

--- a/solution.py
+++ b/solution.py
@@ -1184,7 +1184,7 @@
     d_mixed0, extra, part_a = rest[:4], rest[4], rest[5:]
     d_mixed0 = spread(d_mixed0)
     near_a = send_near(part_a)
-    far_sum_b = sum_far(part_b, near_b)
+    far_sum_b = sum_far(part_b, after(near_b, d_mixed0[1]))
     outs = heads_backward(
         "heads_backward_2", info, after(y_all, far_sum_b), tiles, 32, qkv2, mixed2[0], stats2, d_mixed2, True, piece_size(tag_rows)
     )

time: 294 us -> 291 us (0.990)
  waiting for transfers between devices: 89.7 us -> 80.4 us
  starting transfers between devices: 52.5 us -> 59.1 us
    ppermute x4, waiting for transfers between devices: 9.7 us -> 3.38 us  [spread(): lax.ppermute(pieces[2], 'tensor', chip_pairs())]
    ppermute x1, starting transfers between devices: 3.3 us -> 8.35 us  [local(): came_x = lax.ppermute(dx[1], 'tensor', core_pairs())]
    ppermute x4, waiting for transfers between devices: 6.53 us -> 3.53 us  [spread(): lax.ppermute(pieces[3], 'tensor', diagonal_pairs())]
  transfers between devices with their start and end apart: 51 -> 51, of which waited for: 19 -> 17; matrix products, arithmetic and copies ran while one was open for 1% -> 1% of each run, Pallas kernels for 44% -> 45%
where the time goes in v5:
time: 291 us; the launch traced here: 286 us
  Pallas kernels  136 us (47%)
  waiting for transfers between devices  80.4 us (28%)
  starting transfers between devices  59.1 us (20%)
  other arithmetic  4.86 us (2%)
  local copies, waits for them, and re-layouts  3.58 us (1%)
    pallas_call x12, Pallas kernels, call(): pl.pallas_call(body, out_shape=shapes, in_specs=[SM if a.dtype == jnp.int...  121 us
    ppermute x3, waiting for transfers between devices, column(): return lax.ppermute(part, 'dp', z_shift(step))  25.6 us
    ppermute x4, waiting for transfers between devices, sum_pieces(): other = lax.ppermute(piece, 'dp', y_pairs())  15.5 us
    ppermute x3, waiting for transfers between devices, far_part(): lax.ppermute(after(part, *others) if others else part, 'tensor', chip_pai...  13 us
    ppermute x3, waiting for transfers between devices, sum_pieces(): column.append(lax.ppermute(both, 'dp', z_shift(step)))  9.26 us
    ppermute x1, starting transfers between devices, local(): came_x = lax.ppermute(dx[1], 'tensor', core_pairs())  8.35 us
    ppermute x4, waiting for transfers between devices, row(): return lax.ppermute(part, 'dp', y_pairs())  7.49 us
    pallas_call x2, Pallas kernels, whole_group(): pl.pallas_call(kernel, out_shape=jax.ShapeDtypeStruct((count * shards, D)...  6.65 us
  transfers between devices with their start and end apart: 51, of which 17 were waited for; matrix products, arithmetic and copies ran while one was open for 1% of the time, Pallas kernels for 45%

profile of v5, /device:TPU:0, one launch (start us, length us, event | category | flops | bytes accessed | tf_op | source)
XLA Modules:
  0.0 286.4 jit_solution(5973061024404297812)
XLA Ops:
  0.7 2.3 pad_maximum_fusion.1
  3.4 2.6 collective-permute-start.3
  6.1 1.6 collective-permute-start.2
  7.7 3.6 %collective-permute-start.1 = (bf16[1296,128]{1,0:T(8,128)(2,1)S(1)}, bf16[1296,128]{1,0:T(8,128)(2,1)}, u32[]{:S(2)}, u32[]{:S(2)}) collective-permute-start(bf16[1296,128]{1,0:T(8,128)(2,1)S(1)} %fusion.1.refs_2_), channel_id=1, source_target_pairs={{0,24},{4,28},{8,0},{12,4},{16,8},{20,12},{24,16},{28,20},{1,25},{... | collective-permute-start | bytes 995336 | tf_op jit(solution)/shard_map/ppermute | solution.py:96
  11.6 0.6 fusion.4
  12.2 1.3 concatenate.14
  13.6 0.7 multiply_reduce_fusion
  14.2 1.8 collective-permute-done.2.refs_6_
  16.0 3.5 %collective-permute-done.1.refs_5_ = bf16[1296,128]{1,0:T(8,128)(2,1)} collective-permute-done((bf16[1296,128]{1,0:T(8,128)(2,1)S(1)}, bf16[1296,128]{1,0:T(8,128)(2,1)}, u32[]{:S(2)}, u32[]{:S(2)}) %collective-permute-start.1) | collective-permute-done | bytes 331808 | tf_op jit(solution)/shard_map/ppermute | solution.py:96
  19.5 7.0 %collective-permute-done.refs_3_ = bf16[1296,128]{1,0:T(8,128)(2,1)} collective-permute-done((bf16[1296,128]{1,0:T(8,128)(2,1)S(1)}, bf16[1296,128]{1,0:T(8,128)(2,1)}, u32[]{:S(2)}, u32[]{:S(2)}) %collective-permute-start) | collective-permute-done | bytes 331808 | tf_op jit(solution)/shard_map/ppermute | solution.py:96
  27.2 0.7 collective-permute-start.5
  28.5 1.5 collective-permute-start.7
  30.0 15.1 %collective-permute-done.5.refs_4_ = bf16[1296,128]{1,0:T(8,128)(2,1)S(1)} collective-permute-done((bf16[1296,128]{1,0:T(8,128)(2,1)S(1)}, bf16[1296,128]{1,0:T(8,128)(2,1)S(1)}, u32[]{:S(2)}, u32[]{:S(2)}) %collective-permute-start.5) | collective-permute-done | bytes 331808 | tf_op jit(solution)/shard_map/ppermute | solution.py:96
  45.2 1.3 collective-permute-start.12
  46.5 1.2 collective-permute-start.11
  48.2 3.6 %whole_images.1.refs_2_.refs_3_.refs_4_.refs_9_.refs_10_.refs_11_.refs_12_ = bf16[2352,512]{1,0:T(8,128)(2,1)} custom-call(s32[1,16]{1,0:T(1,128)} %bitcast.18, bf16[588,512]{1,0:T(8,128)(2,1)} %refs_0_.2, bf16[972,512]{1,0:T(8,128)(2,1)} %copy-done.20, bf16[588,512]{1,0:T(8,128)(2,1)} %collective-permute-done.3.refs_2_, bf16[588,512]{1,0:T(8,128)(2,1)} %copy-done.28), custom_call_target="tpu_custom_call" | custom-call | tf_op jit(solution)/shard_map/whole_images/pallas_call | solution.py:175
  51.8 5.7 %collective-permute-done.10.refs_8_ = bf16[1296,128]{1,0:T(8,128)(2,1)S(1)} collective-permute-done((bf16[1296,128]{1,0:T(8,128)(2,1)S(1)}, bf16[1296,128]{1,0:T(8,128)(2,1)S(1)}, u32[]{:S(2)}, u32[]{:S(2)}) %collective-permute-start.10) | collective-permute-done | bytes 331808 | tf_op jit(solution)/shard_map/ppermute | solution.py:99
  57.5 0.7 copy-done.36
  58.2 4.2 %order_tiles.1 = (bf16[10240,128]{1,0:T(8,128)(2,1)}, bf16[2560,128]{1,0:T(8,128)(2,1)S(1)}, bf16[2560,128]{1,0:T(8,128)(2,1)S(1)}, bf16[2048,128]{1,0:T(8,128)(2,1)S(1)}, f32[16,512]{1,0:T(8,128)}) custom-call(s32[8,10]{1,0:T(8,128)S(1)} %get-tuple-element.250.refs_0_, s32[8]{0:T(128)S(1)} %stack.70.refs_1_, bf16[1296,128]{1,0:T(8,128)(2,1)} %copy-done.26, ...), custom_call_target="tpu_custom_call" | custom-call | bytes 4000000 | tf_op jit(solution)/shard_map/order_tiles/pallas_call | solution.py:723
  62.4 3.1 %whole_sequences.1.refs_2_.refs_3_.refs_4_.refs_9_.refs_10_.refs_11_.refs_12_ = bf16[1536,512]{1,0:T(8,128)(2,1)} custom-call(s32[1,16]{1,0:T(1,128)} %bitcast.19, bf16[384,512]{1,0:T(8,128)(2,1)} %refs_0_.3, bf16[972,512]{1,0:T(8,128)(2,1)} %copy-done.20, bf16[384,512]{1,0:T(8,128)(2,1)} %copy-done.30, bf16[384,512]{1,0:T(8,128)(2,1)} %copy-done.31), custom_call_target="tpu_custom_call" | custom-call | tf_op jit(solution)/shard_map/whole_sequences/pallas_call | solution.py:175
  65.5 1.5 collective-permute-start.14
  67.0 12.7 %heads_forward_0.1 = (bf16[2352,384]{1,0:T(8,128)(2,1)}, bf16[2352,128]{1,0:T(8,128)(2,1)}, f32[48,784]{1,0:T(8,128)}, bf16[784,128]{1,0:T(8,128)(2,1)S(1)}, bf1...) custom-call(s32[1,16]{1,0:T(1,128)S(1)} %bitcast.23, ...), custom_call_target="tpu_custom_call" | custom-call | flops 10000000000 | bytes 4000000 | tf_op jit(solution)/shard_map/heads_forward_0/pallas_call | solution.py:723
  79.7 2.9 %collective-permute-done.14.refs_7_.refs_9_ = bf16[2560,128]{1,0:T(8,128)(2,1)S(1)} collective-permute-done((bf16[2560,128]{1,0:T(8,128)(2,1)S(1)}, bf16[2560,128]{1,0:T(8,128)(2,1)S(1)}, u32[]{:S(2)}, u32[]{:S(2)}) %collective-permute-start.14) | collective-permute-done | bytes 655392 | tf_op jit(solution)/shard_map/ppermute | solution.py:1143
  82.6 1.6 collective-permute-start.16
  84.9 7.3 %heads_forward_2.1 = (bf16[1536,384]{1,0:T(8,128)(2,1)}, bf16[1536,128]{1,0:T(8,128)(2,1)}, f32[48,512]{1,0:T(8,128)}, bf16[512,128]{1,0:T(8,128)(2,1)S(1)}, bf1...) custom-call(s32[1,16]{1,0:T(1,128)S(1)} %bitcast.24, ...), custom_call_target="tpu_custom_call" | custom-call | flops 10000000000 | bytes 4000000 | tf_op jit(solution)/shard_map/heads_forward_2/pallas_call | solution.py:723
  92.3 1.6 collective-permute-done.17.refs_4_.refs_18_
  94.2 1.5 collective-permute-start.20
  95.8 1.5 collective-permute-start.22
  97.3 9.2 %ffn_forward.1 = (bf16[784,512]{1,0:T(8,128)(2,1)}, bf16[784,512]{1,0:T(8,128)(2,1)}, bf16[784,512]{1,0:T(8,128)(2,1)}, f32[16,784]{1,0:T(8,128)}, bf16[784,512]...) custom-call(s32[1,16]{1,0:T(1,128)S(1)} %bitcast.25, ...), custom_call_target="tpu_custom_call" | custom-call | flops 8000000000 | bytes 4000000 | tf_op jit(solution)/shard_map/ffn_forward/pallas_call | solution.py:723
  106.6 10.1 %collective-permute-done.22.refs_7_.refs_17_ = bf16[2560,128]{1,0:T(8,128)(2,1)S(1)} collective-permute-done((bf16[2560,128]{1,0:T(8,128)(2,1)S(1)}, bf16[2560,128]{1,0:T(8,128)(2,1)S(1)}, u32[]{:S(2)}, u32[]{:S(2)}) %collective-permute-start.22) | collective-permute-done | bytes 655392 | tf_op jit(solution)/shard_map/ppermute | solution.py:1143
  116.7 2.1 collective-permute-done.23.refs_8_.refs_18_
  118.8 1.5 collective-permute-start.24
  120.3 12.8 %cross_forward.1 = (f32[512,512]{1,0:T(8,128)S(1)}, bf16[512,512]{1,0:T(8,128)(2,1)}, bf16[512,512]{1,0:T(8,128)(2,1)}, bf16[512,512]{1,0:T(8,128)(2,1)}, bf16[5...) custom-call(s32[1,16]{1,0:T(1,128)S(1)} %bitcast.26, ...), custom_call_target="tpu_custom_call" | custom-call | flops 8000000000 | bytes 4000000 | tf_op jit(solution)/shard_map/cross_forward/pallas_call | solution.py:723
  133.2 1.3 collective-permute-start.26
  135.1 0.8 copy-done.44
  135.9 9.2 %ffn_both.1 = (bf16[512,512]{1,0:T(8,128)(2,1)}, bf16[976,512]{1,0:T(8,128)(2,1)}, f32[512,512]{1,0:T(8,128)S(1)}, f32[8,512]{1,0:T(8,128)}, bf16[2048,128]{1,0:...) custom-call(s32[1,16]{1,0:T(1,128)} %bitcast.20, f32[512,512]{1,0:T(8,128)S(1)} %get-tuple-element.331.refs_1_, ...), custom_call_target="tpu_custom_call" | custom-call | flops 10000000000 | bytes 4000000 | tf_op jit(solution)/shard_map/ffn_both/pallas_call | solution.py:723
  145.2 2.9 %collective-permute-start.28 = (bf16[976,512]{1,0:T(8,128)(2,1)}, bf16[976,512]{1,0:T(8,128)(2,1)S(1)}, u32[]{:S(2)}, u32[]{:S(2)}) collective-permute-start(bf16[976,512]{1,0:T(8,128)(2,1)} %get-tuple-element.366), channel_id=1, source_target_pairs={{0,1},{1,2},{2,3},{4,5},{5,6},{6,7},{8,9},{9,10},{10,11},{12,13},{... | collective-permute-start | bytes 2998280 | tf_op jit(solution)/shard_map/ppermute | solution.py:203
  148.1 1.7 collective-permute-start.27
  149.9 17.3 %cross_backward.1 = (f32[784,512]{1,0:T(8,128)S(1)}, bf16[512,512]{1,0:T(8,128)(2,1)}, bf16[384,512]{1,0:T(8,128)(2,1)}, bf16[512,128]{1,0:T(8,128)(2,1)}, bf16[...) custom-call(s32[1,16]{1,0:T(1,128)} %bitcast.21, ...), custom_call_target="tpu_custom_call" | custom-call | flops 20000000000 | bytes 4000000 | tf_op jit(solution)/shard_map/cross_backward/pallas_call | solution.py:723
  168.3 1.7 collective-permute-start.30
  170.0 11.7 %ffn_backward.1 = (bf16[784,512]{1,0:T(8,128)(2,1)}, bf16[976,512]{1,0:T(8,128)(2,1)}, bf16[784,128]{1,0:T(8,128)(2,1)}, bf16[784,128]{1,0:T(8,128)(2,1)S(1)}, b...) custom-call(s32[1,16]{1,0:T(1,128)} %bitcast.22, ...), custom_call_target="tpu_custom_call" | custom-call | flops 12000000000 | bytes 4000000 | tf_op jit(solution)/shard_map/ffn_backward/pallas_call | solution.py:723
  181.7 3.4 %collective-permute-done.30.refs_3_ = bf16[512,128]{1,0:T(8,128)(2,1)S(1)} collective-permute-done((bf16[512,128]{1,0:T(8,128)(2,1)S(1)}, bf16[512,128]{1,0:T(8,128)(2,1)S(1)}, u32[]{:S(2)}, u32[]{:S(2)}) %collective-permute-start.30) | collective-permute-done | bytes 131104 | tf_op jit(solution)/shard_map/ppermute | solution.py:157
  185.1 1.9 collective-permute-done.31.refs_4_
  187.7 1.3 collective-permute-start.36
  190.1 10.8 %heads_backward_2.1 = (bf16[384,512]{1,0:T(8,128)(2,1)}, bf16[768,512]{1,0:T(8,128)(2,1)S(1)}, bf16[384,512]{1,0:T(8,128)(2,1)}, bf16[1536,128]{1,0:T(8,128)(2,1)}) custom-call(s32[1,16]{1,0:T(1,128)S(1)} %bitcast.27, bf16[512,128]{1,0:T(8,128)(2,1)} %get-tuple-element.402.refs_1_, bf16[512,128]{1,0:T(8,128)(2,1)} %copy-done.55, ...), custom_call_target="tpu_custom_call" | custom-call | flops 20000000000 | bytes 4000000 | tf_op jit(solution)/shard_map/heads_backward_2/pallas_call | solution.py:723
  200.9 2.2 sum_group.1.refs_2_
  203.3 1.8 collective-permute-start.39
  205.1 2.5 collective-permute-start.41
  207.6 19.9 %heads_backward_0.1 = (bf16[608,512]{1,0:T(8,128)(2,1)}, bf16[1216,512]{1,0:T(8,128)(2,1)S(1)}, bf16[608,512]{1,0:T(8,128)(2,1)}, bf16[1536,128]{1,0:T(8,128)(2,1)}) custom-call(s32[1,16]{1,0:T(1,128)S(1)} %bitcast.28, bf16[784,128]{1,0:T(8,128)(2,1)} %get-tuple-element.423.refs_1_, bf16[784,128]{1,0:T(8,128)(2,1)} %copy-done.49, ...), custom_call_target="tpu_custom_call" | custom-call | flops 20000000000 | bytes 4000000 | tf_op jit(solution)/shard_map/heads_backward_0/pallas_call | solution.py:723
  227.6 8.3 %collective-permute-start.42 = (bf16[1216,512]{1,0:T(8,128)(2,1)S(1)}, bf16[1216,512]{1,0:T(8,128)(2,1)S(1)}, u32[]{:S(2)}, u32[]{:S(2)}) collective-permute-start(bf16[1216,512]{1,0:T(8,128)(2,1)S(1)} %get-tuple-element.458), channel_id=1, source_target_pairs={{0,1},{1,0},{2,3},{3,2},{4,5},{5,4},{6,7},{7,6},{8,9},{9,8},{10,11... | collective-permute-start | bytes 3735560 | tf_op jit(solution)/shard_map/ppermute | solution.py:1279
  236.0 3.9 %deal_tiles.1 = (bf16[1296,128]{1,0:T(8,128)(2,1)S(1)}, bf16[1296,128]{1,0:T(8,128)(2,1)S(1)}, bf16[1296,128]{1,0:T(8,128)(2,1)S(1)}, bf16[1296,128]{1,0:T(8,128...) custom-call(s32[8,10]{1,0:T(8,128)} %get-tuple-element.441.refs_0_, ...), custom_call_target="tpu_custom_call" | custom-call | bytes 4000000 | tf_op jit(solution)/shard_map/deal_tiles/pallas_call | solution.py:723
  241.2 1.2 collective-permute-start.46
  242.4 2.4 collective-permute-start.43
  244.9 5.9 %collective-permute-done.44 = bf16[1296,128]{1,0:T(8,128)(2,1)S(1)} collective-permute-done((bf16[1296,128]{1,0:T(8,128)(2,1)S(1)}, bf16[1296,128]{1,0:T(8,128)(2,1)S(1)}, u32[]{:S(2)}, u32[]{:S(2)}) %collective-permute-start.44) | collective-permute-done | bytes 331808 | tf_op jit(solution)/shard_map/ppermute | solution.py:127
  250.8 2.0 collective-permute-start.45
  253.3 4.5 %collective-permute-done.46 = bf16[1296,128]{1,0:T(8,128)(2,1)S(1)} collective-permute-done((bf16[1296,128]{1,0:T(8,128)(2,1)S(1)}, bf16[1296,128]{1,0:T(8,128)(2,1)S(1)}, u32[]{:S(2)}, u32[]{:S(2)}) %collective-permute-start.46) | collective-permute-done | bytes 331808 | tf_op jit(solution)/shard_map/ppermute | solution.py:127
  257.9 1.3 collective-permute-start.47
  259.8 5.1 %collective-permute-done.48 = bf16[1296,128]{1,0:T(8,128)(2,1)S(1)} collective-permute-done((bf16[1296,128]{1,0:T(8,128)(2,1)S(1)}, bf16[1296,128]{1,0:T(8,128)(2,1)S(1)}, u32[]{:S(2)}, u32[]{:S(2)}) %collective-permute-start.48) | collective-permute-done | bytes 331808 | tf_op jit(solution)/shard_map/ppermute | solution.py:127
  265.1 3.0 %collective-permute-start.49 = (bf16[1296,128]{1,0:T(8,128)(2,1)S(1)}, bf16[1296,128]{1,0:T(8,128)(2,1)S(1)}, u32[]{:S(2)}, u32[]{:S(2)}) collective-permute-start(bf16[1296,128]{1,0:T(8,128)(2,1)S(1)} %add_convert_fusion.5), channel_id=1, source_target_pairs={{0,24},{4,28},{8,0},{12,4},{16,8},{20,12},{24,16},{28,20},{1,25},{... | collective-permute-start | bytes 995336 | tf_op jit(solution)/shard_map/ppermute | solution.py:133
  268.1 1.6 push_outputs.1
  269.7 2.3 push_gradients.1
  272.1 3.1 %collective-permute-done.45.refs_1_ = bf16[1296,128]{1,0:T(8,128)(2,1)S(1)} collective-permute-done((bf16[1296,128]{1,0:T(8,128)(2,1)S(1)}, bf16[1296,128]{1,0:T(8,128)(2,1)S(1)}, u32[]{:S(2)}, u32[]{:S(2)}) %collective-permute-start.45) | collective-permute-done | bytes 331808 | tf_op jit(solution)/shard_map/ppermute | solution.py:133
  275.1 6.2 %collective-permute-done.49.refs_3_ = bf16[1296,128]{1,0:T(8,128)(2,1)S(1)} collective-permute-done((bf16[1296,128]{1,0:T(8,128)(2,1)S(1)}, bf16[1296,128]{1,0:T(8,128)(2,1)S(1)}, u32[]{:S(2)}, u32[]{:S(2)}) %collective-permute-start.49) | collective-permute-done | bytes 331808 | tf_op jit(solution)/shard_map/ppermute | solution.py:133
  281.3 4.5 %shampoo.1 = (f32[1,10,128,128]{3,2,1,0:T(8,128)}, f32[1,10,128,128]{3,2,1,0:T(8,128)}, f32[1,10,128,128]{3,2,1,0:T(8,128)}, f32[1,10,128,128]{3,2,1,0:T(8,128)}...) custom-call(bf16[1296,128]{1,0:T(8,128)(2,1)S(1)} %get-tuple-element.463.refs_0_, ...), custom_call_target="tpu_custom_call" | custom-call | tf_op jit(solution)/shard_map/shampoo/pallas_call | solution.py:397
  (192 shorter events, 10.2 us)
Async XLA Ops:
  3.0 23.6 %copy-start.25 = (bf16[384,512]{1,0:T(8,128)(2,1)S(1)}, bf16[384,512]{1,0:T(8,128)(2,1)}, u32[]{:S(2)}) copy-start(bf16[384,512]{1,0:T(8,128)(2,1)} %refs_0_.3) | copy-start | bytes 1179652
  3.0 23.6 %collective-permute-start.4 = (bf16[972,512]{1,0:T(8,128)(2,1)}, bf16[972,512]{1,0:T(8,128)(2,1)S(1)}, u32[]{:S(2)}, u32[]{:S(2)}) collective-permute-start(bf16[972,512]{1,0:T(8,128)(2,1)} %pad_maximum_fusion.1), channel_id=1, source_target_pairs={{0,1},{1,0},{2,3},{3,2},{4,5},{5,4},{6,7},{7,6},{8,9},{9,8},{10,11... | collective-permute-start | bytes 2985992 | tf_op jit(solution)/shard_map/ppermute | solution.py:79
  3.4 23.1 %collective-permute-start.3 = (bf16[588,512]{1,0:T(8,128)(2,1)S(1)}, bf16[588,512]{1,0:T(8,128)(2,1)}, u32[]{:S(2)}, u32[]{:S(2)}) collective-permute-start(bf16[588,512]{1,0:T(8,128)(2,1)S(1)} %copy-done.23), channel_id=1, source_target_pairs={{0,2},{1,3},{2,0},{3,1},{4,6},{5,7},{6,4},{7,5},{8,10},{9,11},{10,... | collective-permute-start | bytes 1806344 | tf_op jit(solution)/shard_map/ppermute | solution.py:82
  6.1 51.4 %copy-start.26 = (bf16[1296,128]{1,0:T(8,128)(2,1)}, bf16[1296,128]{1,0:T(8,128)(2,1)S(1)}, u32[]{:S(2)}) copy-start(bf16[1296,128]{1,0:T(8,128)(2,1)S(1)} %fusion.1.refs_2_) | copy-start | bytes 995332
  6.1 9.9 %collective-permute-start.2 = (bf16[1296,128]{1,0:T(8,128)(2,1)S(1)}, bf16[1296,128]{1,0:T(8,128)(2,1)S(1)}, u32[]{:S(2)}, u32[]{:S(2)}) collective-permute-start(bf16[1296,128]{1,0:T(8,128)(2,1)S(1)} %fusion.1.refs_2_), channel_id=1, source_target_pairs={{0,4},{4,0},{8,12},{12,8},{16,20},{20,16},{24,28},{28,24},{1,5},{5... | collective-permute-start | bytes 995336 | tf_op jit(solution)/shard_map/ppermute | solution.py:99
  7.7 11.8 %collective-permute-start.1 = (bf16[1296,128]{1,0:T(8,128)(2,1)S(1)}, bf16[1296,128]{1,0:T(8,128)(2,1)}, u32[]{:S(2)}, u32[]{:S(2)}) collective-permute-start(bf16[1296,128]{1,0:T(8,128)(2,1)S(1)} %fusion.1.refs_2_), channel_id=1, source_target_pairs={{0,24},{4,28},{8,0},{12,4},{16,8},{20,12},{24,16},{28,20},{1,25},{... | collective-permute-start | bytes 995336 | tf_op jit(solution)/shard_map/ppermute | solution.py:96
  11.3 15.2 %collective-permute-start = (bf16[1296,128]{1,0:T(8,128)(2,1)S(1)}, bf16[1296,128]{1,0:T(8,128)(2,1)}, u32[]{:S(2)}, u32[]{:S(2)}) collective-permute-start(bf16[1296,128]{1,0:T(8,128)(2,1)S(1)} %fusion.1.refs_2_), channel_id=1, source_target_pairs={{0,8},{4,12},{8,16},{12,20},{16,24},{20,28},{24,0},{28,4},{1,9},{5... | collective-permute-start | bytes 995336 | tf_op jit(solution)/shard_map/ppermute | solution.py:96
  11.6 40.2 %copy-start.37 = (s32[8]{0:T(128)}, s32[8]{0:T(128)S(1)}, u32[]{:S(2)}) copy-start(s32[8]{0:T(128)S(1)} %stack.73.refs_1_) | copy-start | bytes 100
  16.0 41.4 %copy-start.32 = (bf16[1296,128]{1,0:T(8,128)(2,1)}, bf16[1296,128]{1,0:T(8,128)(2,1)S(1)}, u32[]{:S(2)}) copy-start(bf16[1296,128]{1,0:T(8,128)(2,1)S(1)} %collective-permute-done.2.refs_6_) | copy-start | bytes 995332
  26.5 21.6 %copy-start.20 = (bf16[972,512]{1,0:T(8,128)(2,1)}, bf16[972,512]{1,0:T(8,128)(2,1)S(1)}, u32[]{:S(2)}) copy-start(bf16[972,512]{1,0:T(8,128)(2,1)S(1)} %collective-permute-done.4.refs_1_) | copy-start | bytes 2985988
  26.5 18.6 %collective-permute-start.9 = (bf16[588,512]{1,0:T(8,128)(2,1)}, bf16[588,512]{1,0:T(8,128)(2,1)S(1)}, u32[]{:S(2)}, u32[]{:S(2)}) collective-permute-start(bf16[588,512]{1,0:T(8,128)(2,1)} %collective-permute-done.3.refs_2_), channel_id=1, source_target_pairs={{0,1},{1,0},{2,3},{3,2},{4,5},{5,4},{6,7},{7,6},{8,9},{9,8},{10,11... | collective-permute-start | bytes 1806344 | tf_op jit(solution)/shard_map/ppermute | solution.py:79
  26.6 18.5 %collective-permute-start.8 = (bf16[384,512]{1,0:T(8,128)(2,1)S(1)}, bf16[384,512]{1,0:T(8,128)(2,1)S(1)}, u32[]{:S(2)}, u32[]{:S(2)}) collective-permute-start(bf16[384,512]{1,0:T(8,128)(2,1)S(1)} %copy-done.25), channel_id=1, source_target_pairs={{0,2},{1,3},{2,0},{3,1},{4,6},{5,7},{6,4},{7,5},{8,10},{9,11},{10,... | collective-permute-start | bytes 1179656 | tf_op jit(solution)/shard_map/ppermute | solution.py:82
  27.2 17.9 %collective-permute-start.5 = (bf16[1296,128]{1,0:T(8,128)(2,1)S(1)}, bf16[1296,128]{1,0:T(8,128)(2,1)S(1)}, u32[]{:S(2)}, u32[]{:S(2)}) collective-permute-start(bf16[1296,128]{1,0:T(8,128)(2,1)S(1)} %fusion.1.refs_2_), channel_id=1, source_target_pairs={{0,16},{4,20},{8,24},{12,28},{16,0},{20,4},{24,8},{28,12},{1,17},{... | collective-permute-start | bytes 995336 | tf_op jit(solution)/shard_map/ppermute | solution.py:96
  28.0 17.1 %collective-permute-start.6 = (bf16[1296,128]{1,0:T(8,128)(2,1)}, bf16[1296,128]{1,0:T(8,128)(2,1)S(1)}, u32[]{:S(2)}, u32[]{:S(2)}) collective-permute-start(bf16[1296,128]{1,0:T(8,128)(2,1)} %collective-permute-done.refs_3_), channel_id=1, source_target_pairs={{0,4},{4,0},{8,12},{12,8},{16,20},{20,16},{24,28},{28,24},{1,5},{5... | collective-permute-start | bytes 995336 | tf_op jit(solution)/shard_map/ppermute | solution.py:99
  28.5 16.6 %collective-permute-start.7 = (bf16[1296,128]{1,0:T(8,128)(2,1)}, bf16[1296,128]{1,0:T(8,128)(2,1)S(1)}, u32[]{:S(2)}, u32[]{:S(2)}) collective-permute-start(bf16[1296,128]{1,0:T(8,128)(2,1)} %collective-permute-done.1.refs_5_), channel_id=1, source_target_pairs={{0,4},{4,0},{8,12},{12,8},{16,20},{20,16},{24,28},{28,24},{1,5},{5... | collective-permute-start | bytes 995336 | tf_op jit(solution)/shard_map/ppermute | solution.py:99
  45.1 17.3 %copy-start.30 = (bf16[384,512]{1,0:T(8,128)(2,1)}, bf16[384,512]{1,0:T(8,128)(2,1)S(1)}, u32[]{:S(2)}) copy-start(bf16[384,512]{1,0:T(8,128)(2,1)S(1)} %collective-permute-done.8.refs_2_) | copy-start | bytes 1179652
  45.2 12.3 %collective-permute-start.12 = (bf16[384,512]{1,0:T(8,128)(2,1)}, bf16[384,512]{1,0:T(8,128)(2,1)S(1)}, u32[]{:S(2)}, u32[]{:S(2)}) collective-permute-start(bf16[384,512]{1,0:T(8,128)(2,1)} %refs_7_.2), channel_id=1, source_target_pairs={{1,0},{2,1},{3,2},{5,4},{6,5},{7,6},{9,8},{10,9},{11,10},{13,12},{... | collective-permute-start | bytes 1179656 | tf_op jit(solution)/shard_map/ppermute | solution.py:85
  46.5 11.0 %collective-permute-start.11 = (bf16[384,512]{1,0:T(8,128)(2,1)S(1)}, bf16[384,512]{1,0:T(8,128)(2,1)S(1)}, u32[]{:S(2)}, u32[]{:S(2)}) collective-permute-start(bf16[384,512]{1,0:T(8,128)(2,1)S(1)} %collective-permute-done.8.refs_2_), channel_id=1, source_target_pairs={{0,1},{1,0},{2,3},{3,2},{4,5},{5,4},{6,7},{7,6},{8,9},{9,8},{10,11... | collective-permute-start | bytes 1179656 | tf_op jit(solution)/shard_map/ppermute | solution.py:79
  47.7 9.8 %collective-permute-start.10 = (bf16[1296,128]{1,0:T(8,128)(2,1)S(1)}, bf16[1296,128]{1,0:T(8,128)(2,1)S(1)}, u32[]{:S(2)}, u32[]{:S(2)}) collective-permute-start(bf16[1296,128]{1,0:T(8,128)(2,1)S(1)} %collective-permute-done.5.refs_4_), channel_id=1, source_target_pairs={{0,4},{4,0},{8,12},{12,8},{16,20},{20,16},{24,28},{28,24},{1,5},{5... | collective-permute-start | bytes 995336 | tf_op jit(solution)/shard_map/ppermute | solution.py:99
  62.3 20.3 %collective-permute-start.13 = (bf16[10240,128]{1,0:T(8,128)(2,1)}, bf16[10240,128]{1,0:T(8,128)(2,1)}, u32[]{:S(2)}, u32[]{:S(2)}) collective-permute-start(bf16[10240,128]{1,0:T(8,128)(2,1)} %get-tuple-element.266.refs_1_.refs_5_.refs_2_.refs_15_.refs_7_.refs_13_), channel_id=1, source_target_pairs={{0,1},{1,0},{2,3},{3,2},{4,5},{5,4},{6,7},{7,6},{8,9},{9,8},{10,11... | collective-permute-start | bytes 7864328 | tf_op jit(solution)/shard_map/ppermute | solution.py:1274
  65.5 17.1 %collective-permute-start.14 = (bf16[2560,128]{1,0:T(8,128)(2,1)S(1)}, bf16[2560,128]{1,0:T(8,128)(2,1)S(1)}, u32[]{:S(2)}, u32[]{:S(2)}) collective-permute-start(bf16[2560,128]{1,0:T(8,128)(2,1)S(1)} %get-tuple-element.274), channel_id=1, source_target_pairs={{0,2},{1,3},{2,0},{3,1},{4,6},{5,7},{6,4},{7,5},{8,10},{9,11},{10,... | collective-permute-start | bytes 1966088 | tf_op jit(solution)/shard_map/ppermute | solution.py:1143
  82.6 14.7 %copy-start.16 = (bf16[2560,128]{1,0:T(8,128)(2,1)}, bf16[2560,128]{1,0:T(8,128)(2,1)S(1)}, u32[]{:S(2)}) copy-start(bf16[2560,128]{1,0:T(8,128)(2,1)S(1)} %collective-permute-done.14.refs_7_.refs_9_) | copy-start | bytes 1966084
  82.6 9.6 %collective-permute-start.15 = (bf16[784,128]{1,0:T(8,128)(2,1)S(1)}, bf16[784,128]{1,0:T(8,128)(2,1)S(1)}, u32[]{:S(2)}, u32[]{:S(2)}) collective-permute-start(bf16[784,128]{1,0:T(8,128)(2,1)S(1)} %get-tuple-element.286), channel_id=1, source_target_pairs={{0,1},{1,0},{2,3},{3,2},{4,5},{5,4},{6,7},{7,6},{8,9},{9,8},{10,11... | collective-permute-start | bytes 602120 | tf_op jit(solution)/shard_map/ppermute | solution.py:156
  82.6 9.6 %collective-permute-start.16 = (bf16[784,128]{1,0:T(8,128)(2,1)S(1)}, bf16[784,128]{1,0:T(8,128)(2,1)S(1)}, u32[]{:S(2)}, u32[]{:S(2)}) collective-permute-start(bf16[784,128]{1,0:T(8,128)(2,1)S(1)} %get-tuple-element.287), channel_id=1, source_target_pairs={{0,2},{1,3},{2,0},{3,1},{4,6},{5,7},{6,4},{7,5},{8,10},{9,11},{10,... | collective-permute-start | bytes 602120 | tf_op jit(solution)/shard_map/ppermute | solution.py:157
  84.2 9.7 %collective-permute-start.17 = (bf16[784,128]{1,0:T(8,128)(2,1)S(1)}, bf16[784,128]{1,0:T(8,128)(2,1)S(1)}, u32[]{:S(2)}, u32[]{:S(2)}) collective-permute-start(bf16[784,128]{1,0:T(8,128)(2,1)S(1)} %get-tuple-element.288), channel_id=1, source_target_pairs={{0,3},{1,2},{2,1},{3,0},{4,7},{5,6},{6,5},{7,4},{8,11},{9,10},{10,... | collective-permute-start | bytes 602120 | tf_op jit(solution)/shard_map/ppermute | solution.py:158
  84.5 9.4 %collective-permute-start.18 = (bf16[2560,128]{1,0:T(8,128)(2,1)S(1)}, bf16[2560,128]{1,0:T(8,128)(2,1)S(1)}, u32[]{:S(2)}, u32[]{:S(2)}) collective-permute-start(bf16[2560,128]{1,0:T(8,128)(2,1)S(1)} %collective-permute-done.14.refs_7_.refs_9_), channel_id=1, source_target_pairs={{0,1},{1,0},{2,3},{3,2},{4,5},{5,4},{6,7},{7,6},{8,9},{9,8},{10,11... | collective-permute-start | bytes 1966088 | tf_op jit(solution)/shard_map/ppermute | solution.py:1146
  93.9 12.7 %collective-permute-start.19 = (bf16[512,128]{1,0:T(8,128)(2,1)S(1)}, bf16[512,128]{1,0:T(8,128)(2,1)S(1)}, u32[]{:S(2)}, u32[]{:S(2)}) collective-permute-start(bf16[512,128]{1,0:T(8,128)(2,1)S(1)} %get-tuple-element.308), channel_id=1, source_target_pairs={{0,1},{1,0},{2,3},{3,2},{4,5},{5,4},{6,7},{7,6},{8,9},{9,8},{10,11... | collective-permute-start | bytes 393224 | tf_op jit(solution)/shard_map/ppermute | solution.py:156
  94.2 12.4 %collective-permute-start.20 = (bf16[512,128]{1,0:T(8,128)(2,1)S(1)}, bf16[512,128]{1,0:T(8,128)(2,1)S(1)}, u32[]{:S(2)}, u32[]{:S(2)}) collective-permute-start(bf16[512,128]{1,0:T(8,128)(2,1)S(1)} %get-tuple-element.309), channel_id=1, source_target_pairs={{0,2},{1,3},{2,0},{3,1},{4,6},{5,7},{6,4},{7,5},{8,10},{9,11},{10,... | collective-permute-start | bytes 393224 | tf_op jit(solution)/shard_map/ppermute | solution.py:157
  95.7 10.9 %collective-permute-start.21 = (bf16[512,128]{1,0:T(8,128)(2,1)S(1)}, bf16[512,128]{1,0:T(8,128)(2,1)S(1)}, u32[]{:S(2)}, u32[]{:S(2)}) collective-permute-start(bf16[512,128]{1,0:T(8,128)(2,1)S(1)} %get-tuple-element.310), channel_id=1, source_target_pairs={{0,3},{1,2},{2,1},{3,0},{4,7},{5,6},{6,5},{7,4},{8,11},{9,10},{10,... | collective-permute-start | bytes 393224 | tf_op jit(solution)/shard_map/ppermute | solution.py:158
  95.8 20.9 %collective-permute-start.22 = (bf16[2560,128]{1,0:T(8,128)(2,1)S(1)}, bf16[2560,128]{1,0:T(8,128)(2,1)S(1)}, u32[]{:S(2)}, u32[]{:S(2)}) collective-permute-start(bf16[2560,128]{1,0:T(8,128)(2,1)S(1)} %get-tuple-element.312), channel_id=1, source_target_pairs={{0,2},{1,3},{2,0},{3,1},{4,6},{5,7},{6,4},{7,5},{8,10},{9,11},{10,... | collective-permute-start | bytes 1966088 | tf_op jit(solution)/shard_map/ppermute | solution.py:1143
  116.7 16.4 %copy-start.18 = (bf16[2560,128]{1,0:T(8,128)(2,1)}, bf16[2560,128]{1,0:T(8,128)(2,1)S(1)}, u32[]{:S(2)}) copy-start(bf16[2560,128]{1,0:T(8,128)(2,1)S(1)} %collective-permute-done.22.refs_7_.refs_17_) | copy-start | bytes 1966084
  116.7 2.1 collective-permute-start.23
  118.8 14.4 %copy-start.41 = (bf16[588,512]{1,0:T(8,128)(2,1)S(1)}, bf16[588,512]{1,0:T(8,128)(2,1)}, u32[]{:S(2)}) copy-start(bf16[588,512]{1,0:T(8,128)(2,1)} %refs_2_) | copy-start | bytes 1806340
  118.8 14.3 %collective-permute-start.24 = (bf16[2048,128]{1,0:T(8,128)(2,1)S(1)}, bf16[2048,128]{1,0:T(8,128)(2,1)S(1)}, u32[]{:S(2)}, u32[]{:S(2)}) collective-permute-start(bf16[2048,128]{1,0:T(8,128)(2,1)S(1)} %get-tuple-element.330), channel_id=1, source_target_pairs={{0,2},{1,3},{2,0},{3,1},{4,6},{5,7},{6,4},{7,5},{8,10},{9,11},{10,... | collective-permute-start | bytes 1572872 | tf_op jit(solution)/shard_map/ppermute | solution.py:1143
  133.2 2.0 collective-permute-start.25
  133.2 11.9 %collective-permute-start.26 = (bf16[588,512]{1,0:T(8,128)(2,1)S(1)}, bf16[588,512]{1,0:T(8,128)(2,1)S(1)}, u32[]{:S(2)}, u32[]{:S(2)}) collective-permute-start(bf16[588,512]{1,0:T(8,128)(2,1)S(1)} %copy-done.41), channel_id=1, source_target_pairs={{1,0},{2,1},{3,2},{5,4},{6,5},{7,6},{9,8},{10,9},{11,10},{13,12},{... | collective-permute-start | bytes 1806344 | tf_op jit(solution)/shard_map/ppermute | solution.py:1164
  145.2 22.0 %copy-start.42 = (bf16[588,512]{1,0:T(8,128)(2,1)}, bf16[588,512]{1,0:T(8,128)(2,1)S(1)}, u32[]{:S(2)}) copy-start(bf16[588,512]{1,0:T(8,128)(2,1)S(1)} %collective-permute-done.26.refs_3_) | copy-start | bytes 1806340
  145.2 22.0 %collective-permute-start.28 = (bf16[976,512]{1,0:T(8,128)(2,1)}, bf16[976,512]{1,0:T(8,128)(2,1)S(1)}, u32[]{:S(2)}, u32[]{:S(2)}) collective-permute-start(bf16[976,512]{1,0:T(8,128)(2,1)} %get-tuple-element.366), channel_id=1, source_target_pairs={{0,1},{1,2},{2,3},{4,5},{5,6},{6,7},{8,9},{9,10},{10,11},{12,13},{... | collective-permute-start | bytes 2998280 | tf_op jit(solution)/shard_map/ppermute | solution.py:203
  148.1 19.1 %collective-permute-start.27 = (bf16[4096,128]{1,0:T(8,128)(2,1)S(1)}, bf16[4096,128]{1,0:T(8,128)(2,1)S(1)}, u32[]{:S(2)}, u32[]{:S(2)}) collective-permute-start(bf16[4096,128]{1,0:T(8,128)(2,1)S(1)} %get-tuple-element.365), channel_id=1, source_target_pairs={{0,1},{1,0},{2,3},{3,2},{4,5},{5,4},{6,7},{7,6},{8,9},{9,8},{10,11... | collective-permute-start | bytes 3145736 | tf_op jit(solution)/shard_map/ppermute | solution.py:141
  167.2 19.8 %collective-permute-start.32 = (bf16[5120,128]{1,0:T(8,128)(2,1)S(1)}, bf16[5120,128]{1,0:T(8,128)(2,1)S(1)}, u32[]{:S(2)}, u32[]{:S(2)}) collective-permute-start(bf16[5120,128]{1,0:T(8,128)(2,1)S(1)} %get-tuple-element.399), channel_id=1, source_target_pairs={{0,1},{1,0},{2,3},{3,2},{4,5},{5,4},{6,7},{7,6},{8,9},{9,8},{10,11... | collective-permute-start | bytes 3932168 | tf_op jit(solution)/shard_map/ppermute | solution.py:141
  167.5 19.5 %collective-permute-start.33 = (bf16[2048,128]{1,0:T(8,128)(2,1)S(1)}, bf16[2048,128]{1,0:T(8,128)(2,1)S(1)}, u32[]{:S(2)}, u32[]{:S(2)}) collective-permute-start(bf16[2048,128]{1,0:T(8,128)(2,1)S(1)} %add_convert_fusion.3), channel_id=1, source_target_pairs={{0,2},{1,3},{2,0},{3,1},{4,6},{5,7},{6,4},{7,5},{8,10},{9,11},{10,... | collective-permute-start | bytes 1572872 | tf_op jit(solution)/shard_map/ppermute | solution.py:150
  167.9 13.8 %collective-permute-start.29 = (bf16[512,128]{1,0:T(8,128)(2,1)S(1)}, bf16[512,128]{1,0:T(8,128)(2,1)S(1)}, u32[]{:S(2)}, u32[]{:S(2)}) collective-permute-start(bf16[512,128]{1,0:T(8,128)(2,1)S(1)} %get-tuple-element.396), channel_id=1, source_target_pairs={{0,1},{1,0},{2,3},{3,2},{4,5},{5,4},{6,7},{7,6},{8,9},{9,8},{10,11... | collective-permute-start | bytes 393224 | tf_op jit(solution)/shard_map/ppermute | solution.py:156
  168.3 16.8 %collective-permute-start.30 = (bf16[512,128]{1,0:T(8,128)(2,1)S(1)}, bf16[512,128]{1,0:T(8,128)(2,1)S(1)}, u32[]{:S(2)}, u32[]{:S(2)}) collective-permute-start(bf16[512,128]{1,0:T(8,128)(2,1)S(1)} %get-tuple-element.397), channel_id=1, source_target_pairs={{0,2},{1,3},{2,0},{3,1},{4,6},{5,7},{6,4},{7,5},{8,10},{9,11},{10,... | collective-permute-start | bytes 393224 | tf_op jit(solution)/shard_map/ppermute | solution.py:157
  170.0 17.0 %collective-permute-start.31 = (bf16[512,128]{1,0:T(8,128)(2,1)S(1)}, bf16[512,128]{1,0:T(8,128)(2,1)S(1)}, u32[]{:S(2)}, u32[]{:S(2)}) collective-permute-start(bf16[512,128]{1,0:T(8,128)(2,1)S(1)} %get-tuple-element.398), channel_id=1, source_target_pairs={{0,3},{1,2},{2,1},{3,0},{4,7},{5,6},{6,5},{7,4},{8,11},{9,10},{10,... | collective-permute-start | bytes 393224 | tf_op jit(solution)/shard_map/ppermute | solution.py:158
  187.0 2.5 collective-permute-start.34
  187.4 15.7 %collective-permute-start.35 = (bf16[784,128]{1,0:T(8,128)(2,1)S(1)}, bf16[784,128]{1,0:T(8,128)(2,1)S(1)}, u32[]{:S(2)}, u32[]{:S(2)}) collective-permute-start(bf16[784,128]{1,0:T(8,128)(2,1)S(1)} %get-tuple-element.417), channel_id=1, source_target_pairs={{0,2},{1,3},{2,0},{3,1},{4,6},{5,7},{6,4},{7,5},{8,10},{9,11},{10,... | collective-permute-start | bytes 602120 | tf_op jit(solution)/shard_map/ppermute | solution.py:157
  187.7 15.4 %collective-permute-start.36 = (bf16[784,128]{1,0:T(8,128)(2,1)S(1)}, bf16[784,128]{1,0:T(8,128)(2,1)S(1)}, u32[]{:S(2)}, u32[]{:S(2)}) collective-permute-start(bf16[784,128]{1,0:T(8,128)(2,1)S(1)} %get-tuple-element.418), channel_id=1, source_target_pairs={{0,3},{1,2},{2,1},{3,0},{4,7},{5,6},{6,5},{7,4},{8,11},{9,10},{10,... | collective-permute-start | bytes 602120 | tf_op jit(solution)/shard_map/ppermute | solution.py:158
  189.0 14.2 %collective-permute-start.37 = (bf16[5184,128]{1,0:T(8,128)(2,1)S(1)}, bf16[5184,128]{1,0:T(8,128)(2,1)S(1)}, u32[]{:S(2)}, u32[]{:S(2)}) collective-permute-start(bf16[5184,128]{1,0:T(8,128)(2,1)S(1)} %get-tuple-element.419), channel_id=1, source_target_pairs={{0,1},{1,0},{2,3},{3,2},{4,5},{5,4},{6,7},{7,6},{8,9},{9,8},{10,11... | collective-permute-start | bytes 3981320 | tf_op jit(solution)/shard_map/ppermute | solution.py:141
  189.7 37.9 %collective-permute-start.40 = (bf16[2560,128]{1,0:T(8,128)(2,1)S(1)}, bf16[2560,128]{1,0:T(8,128)(2,1)}, u32[]{:S(2)}, u32[]{:S(2)}) collective-permute-start(bf16[2560,128]{1,0:T(8,128)(2,1)S(1)} %add_convert_fusion.1), channel_id=1, source_target_pairs={{0,2},{1,3},{2,0},{3,1},{4,6},{5,7},{6,4},{7,5},{8,10},{9,11},{10,... | collective-permute-start | bytes 1966088 | tf_op jit(solution)/shard_map/ppermute | solution.py:150
  203.1 24.4 %copy-start.19 = (bf16[5184,128]{1,0:T(8,128)(2,1)}, bf16[5184,128]{1,0:T(8,128)(2,1)S(1)}, u32[]{:S(2)}) copy-start(bf16[5184,128]{1,0:T(8,128)(2,1)S(1)} %collective-permute-done.37.refs_9_.refs_11_) | copy-start | bytes 3981316
  203.3 24.3 %collective-permute-start.39 = (bf16[2624,128]{1,0:T(8,128)(2,1)S(1)}, bf16[2624,128]{1,0:T(8,128)(2,1)S(1)}, u32[]{:S(2)}, u32[]{:S(2)}) collective-permute-start(bf16[2624,128]{1,0:T(8,128)(2,1)S(1)} %add_convert_fusion), channel_id=1, source_target_pairs={{0,2},{1,3},{2,0},{3,1},{4,6},{5,7},{6,4},{7,5},{8,10},{9,11},{10,... | collective-permute-start | bytes 2015240 | tf_op jit(solution)/shard_map/ppermute | solution.py:150
  205.1 22.5 %collective-permute-start.38 = (bf16[768,512]{1,0:T(8,128)(2,1)S(1)}, bf16[768,512]{1,0:T(8,128)(2,1)S(1)}, u32[]{:S(2)}, u32[]{:S(2)}) collective-permute-start(bf16[768,512]{1,0:T(8,128)(2,1)S(1)} %get-tuple-element.435), channel_id=1, source_target_pairs={{0,1},{1,0},{2,3},{3,2},{4,5},{5,4},{6,7},{7,6},{8,9},{9,8},{10,11... | collective-permute-start | bytes 2359304 | tf_op jit(solution)/shard_map/ppermute | solution.py:1196
  205.1 22.5 %collective-permute-start.41 = (bf16[976,512]{1,0:T(8,128)(2,1)}, bf16[976,512]{1,0:T(8,128)(2,1)S(1)}, u32[]{:S(2)}, u32[]{:S(2)}) collective-permute-start(bf16[976,512]{1,0:T(8,128)(2,1)} %get-tuple-element.438), channel_id=1, source_target_pairs={{0,1},{1,2},{2,3},{4,5},{5,6},{6,7},{8,9},{9,10},{10,11},{12,13},{... | collective-permute-start | bytes 2998280 | tf_op jit(solution)/shard_map/ppermute | solution.py:203
  227.6 12.4 %collective-permute-start.42 = (bf16[1216,512]{1,0:T(8,128)(2,1)S(1)}, bf16[1216,512]{1,0:T(8,128)(2,1)S(1)}, u32[]{:S(2)}, u32[]{:S(2)}) collective-permute-start(bf16[1216,512]{1,0:T(8,128)(2,1)S(1)} %get-tuple-element.458), channel_id=1, source_target_pairs={{0,1},{1,0},{2,3},{3,2},{4,5},{5,4},{6,7},{7,6},{8,9},{9,8},{10,11... | collective-permute-start | bytes 3735560 | tf_op jit(solution)/shard_map/ppermute | solution.py:1279
  240.0 10.7 %collective-permute-start.44 = (bf16[1296,128]{1,0:T(8,128)(2,1)S(1)}, bf16[1296,128]{1,0:T(8,128)(2,1)S(1)}, u32[]{:S(2)}, u32[]{:S(2)}) collective-permute-start(bf16[1296,128]{1,0:T(8,128)(2,1)S(1)} %get-tuple-element.469), channel_id=1, source_target_pairs={{0,4},{4,0},{8,12},{12,8},{16,20},{20,16},{24,28},{28,24},{1,5},{5... | collective-permute-start | bytes 995336 | tf_op jit(solution)/shard_map/ppermute | solution.py:127
  241.2 26.9 %copy-start.1 = (bf16[784,512]{1,0:T(8,128)(2,1)S(1)}, bf16[784,512]{1,0:T(8,128)(2,1)}, u32[]{:S(2)}) copy-start(bf16[784,512]{1,0:T(8,128)(2,1)} %get-tuple-element.313.refs_10_.refs_14_.refs_0_) | copy-start | bytes 2408452
  241.2 26.9 %copy-start.8 = (bf16[512,512]{1,0:T(8,128)(2,1)S(1)}, bf16[512,512]{1,0:T(8,128)(2,1)}, u32[]{:S(2)}) copy-start(bf16[512,512]{1,0:T(8,128)(2,1)} %get-tuple-element.343.refs_1_) | copy-start | bytes 1572868
  241.2 16.6 %collective-permute-start.46 = (bf16[1296,128]{1,0:T(8,128)(2,1)S(1)}, bf16[1296,128]{1,0:T(8,128)(2,1)S(1)}, u32[]{:S(2)}, u32[]{:S(2)}) collective-permute-start(bf16[1296,128]{1,0:T(8,128)(2,1)S(1)} %get-tuple-element.471), channel_id=1, source_target_pairs={{0,4},{4,0},{8,12},{12,8},{16,20},{20,16},{24,28},{28,24},{1,5},{5... | collective-permute-start | bytes 995336 | tf_op jit(solution)/shard_map/ppermute | solution.py:127
  242.4 27.3 %collective-permute-start.43 = (bf16[992,512]{1,0:T(8,128)(2,1)S(1)}, bf16[992,512]{1,0:T(8,128)(2,1)S(1)}, u32[]{:S(2)}, u32[]{:S(2)}) collective-permute-start(bf16[992,512]{1,0:T(8,128)(2,1)S(1)} %pad_maximum_fusion), channel_id=1, source_target_pairs={{0,2},{1,3},{2,0},{3,1},{4,6},{5,7},{6,4},{7,5},{8,10},{9,11},{10,... | collective-permute-start | bytes 3047432 | tf_op jit(solution)/shard_map/ppermute | solution.py:1288
  250.8 24.3 %collective-permute-start.45 = (bf16[1296,128]{1,0:T(8,128)(2,1)S(1)}, bf16[1296,128]{1,0:T(8,128)(2,1)S(1)}, u32[]{:S(2)}, u32[]{:S(2)}) collective-permute-start(bf16[1296,128]{1,0:T(8,128)(2,1)S(1)} %add_convert_fusion.7), channel_id=1, source_target_pairs={{0,16},{4,20},{8,24},{12,28},{16,0},{20,4},{24,8},{28,12},{1,17},{... | collective-permute-start | bytes 995336 | tf_op jit(solution)/shard_map/ppermute | solution.py:133
  252.8 12.1 %collective-permute-start.48 = (bf16[1296,128]{1,0:T(8,128)(2,1)S(1)}, bf16[1296,128]{1,0:T(8,128)(2,1)S(1)}, u32[]{:S(2)}, u32[]{:S(2)}) collective-permute-start(bf16[1296,128]{1,0:T(8,128)(2,1)S(1)} %get-tuple-element.474), channel_id=1, source_target_pairs={{0,4},{4,0},{8,12},{12,8},{16,20},{20,16},{24,28},{28,24},{1,5},{5... | collective-permute-start | bytes 995336 | tf_op jit(solution)/shard_map/ppermute | solution.py:127
  257.9 17.2 %collective-permute-start.47 = (bf16[1296,128]{1,0:T(8,128)(2,1)S(1)}, bf16[1296,128]{1,0:T(8,128)(2,1)S(1)}, u32[]{:S(2)}, u32[]{:S(2)}) collective-permute-start(bf16[1296,128]{1,0:T(8,128)(2,1)S(1)} %add_convert_fusion.6), channel_id=1, source_target_pairs={{0,8},{4,12},{8,16},{12,20},{16,24},{20,28},{24,0},{28,4},{1,9},{5... | collective-permute-start | bytes 995336 | tf_op jit(solution)/shard_map/ppermute | solution.py:133
  259.3 12.8 %collective-permute-start.50 = (bf16[1296,128]{1,0:T(8,128)(2,1)S(1)}, bf16[1296,128]{1,0:T(8,128)(2,1)S(1)}, u32[]{:S(2)}, u32[]{:S(2)}) collective-permute-start(bf16[1296,128]{1,0:T(8,128)(2,1)S(1)} %get-tuple-element.476), channel_id=1, source_target_pairs={{0,4},{4,0},{8,12},{12,8},{16,20},{20,16},{24,28},{28,24},{1,5},{5... | collective-permute-start | bytes 995336 | tf_op jit(solution)/shard_map/ppermute | solution.py:127
  265.1 16.2 %collective-permute-start.49 = (bf16[1296,128]{1,0:T(8,128)(2,1)S(1)}, bf16[1296,128]{1,0:T(8,128)(2,1)S(1)}, u32[]{:S(2)}, u32[]{:S(2)}) collective-permute-start(bf16[1296,128]{1,0:T(8,128)(2,1)S(1)} %add_convert_fusion.5), channel_id=1, source_target_pairs={{0,24},{4,28},{8,0},{12,4},{16,8},{20,12},{24,16},{28,20},{1,25},{... | collective-permute-start | bytes 995336 | tf_op jit(solution)/shard_map/ppermute | solution.py:133
  (45 other events, 320.6 us)
